TPU v7x, 32 devices: a whole 2x2x4 slice. The times are simulated.
32 devices in a mesh: gx: 4 (over z), gy: 4 (over y, x), gz: 2 (over core).
Axes of the slice: x: 2, y: 2, z: 4, core: 2. Of those that a mesh axis runs over, the one named last changes fastest.
Arguments:
- positions: float32 [4, 4, 4, 192], P('gx', 'gy', 'gz'), may hold values from 0 to 1, as said below
- species: int32 [4, 4, 4, 64], P('gx', 'gy', 'gz'), may hold values from 0 to 4
- neighbors: int32 [4, 4, 4, 512], P('gx', 'gy', 'gz'), may hold values from 0 to 1727, as said below
- center_table: bfloat16 [5, 128], replicated, may hold values from -4 to 4
- neighbor_table: bfloat16 [5, 128], replicated, may hold values from -4 to 4
- radial_weight: bfloat16 [8, 128], replicated, may hold values from -2 to 2
- mix_weight: bfloat16 [128, 128], replicated, may hold values from -0.5 to 0.5
- env_weight: bfloat16 [128, 128], replicated, may hold values from -0.5 to 0.5
- update_weight: bfloat16 [384, 128], replicated, may hold values from -0.3125 to 0.3125
- second_weight: bfloat16 [128, 128], replicated, may hold values from -0.5 to 0.5
- readout: float32 [128], replicated, may hold values from -0.5 to 0.5
Outputs:
- atom_energy: float32 [4, 4, 4, 64], P('gx', 'gy', 'gz')
- forces: float32 [4, 4, 4, 192], P('gx', 'gy', 'gz')
Inputs may be any that keep to these rules, and one draw needn't show every extreme that they name: `positions`: every coordinate lies inside its block; atoms of a block sit on a jittered sublattice, so any two atoms are at least 0.4 / cube root of 64 apart. `neighbors`: each atom lists 8 different atoms of the 27 blocks around and including its own, never itself; a code is offset index times 64 plus slot.
All inputs are finite; a program needn't handle non-finite values.
Results may differ from a plain program's by a relative error of at most 0.011.
Values may be sent and summed in bfloat16 or wider, within the bound.
No kernel may reach another device: no remote copies, remote signals or barrier semaphores. Data moves between devices by JAX's collectives and lax.ppermute only.
A program may use at most 64 MiB of HBM per device.

v0:
```python
import math

import jax
import jax.numpy as jnp
from jax import lax
from jax.sharding import PartitionSpec as P

NEIGH = 8


CUTOFF = 4.0
SHARPNESS = 2.0
HIGH = lax.Precision.HIGHEST


def padded_2(cells, sides, width):
    for axis, dim in sides:
        count = lax.axis_size(axis)
        head = lax.slice_in_dim(cells, 0, width, axis=dim)
        tail = lax.slice_in_dim(cells, cells.shape[dim] - width, cells.shape[dim], axis=dim)
        cells = jnp.concatenate(
            [
                lax.ppermute(tail, axis, [(i, (i + 1) % count) for i in range(count)]),
                cells,
                lax.ppermute(head, axis, [((i + 1) % count, i) for i in range(count)]),
            ],
            axis=dim,
        )
    return cells


def harmonics(displacement):
    distance = jnp.sqrt(jnp.sum(displacement * displacement, axis=0))
    unit_vec = displacement / distance
    unit_x, unit_y, unit_z = (unit_vec[0], unit_vec[1], unit_vec[2])
    root_three = math.sqrt(3.0)
    angular = jnp.stack(
        [
            jnp.ones_like(unit_x),
            unit_x,
            unit_y,
            unit_z,
            root_three * unit_x * unit_y,
            root_three * unit_y * unit_z,
            0.5 * (3.0 * unit_z * unit_z - 1.0),
            root_three * unit_x * unit_z,
            0.5 * root_three * (unit_x * unit_x - unit_y * unit_y),
        ],
        axis=0,
    )
    return (distance, angular)


def layer_one(displacement, onehot_center, onehot_other, params):
    radial_weight, center_table, neighbor_table, mix_weight, env_weight, update_weight = params
    distance, angular = harmonics(displacement)
    nbasis = radial_weight.shape[0]
    centers = CUTOFF * (jnp.arange(nbasis, dtype=jnp.float32) + 0.5) / nbasis
    cut_ratio = distance / CUTOFF
    envelope = (1.0 - cut_ratio * cut_ratio) ** 2
    radial_basis = (
        jnp.exp(-SHARPNESS * (distance[:, None] - centers[None, :]) ** 2) * envelope[:, None]
    )
    before = jnp.dot(
        radial_basis.astype(jnp.bfloat16), radial_weight, preferred_element_type=jnp.float32
    )
    before = before + jnp.dot(onehot_center, center_table, preferred_element_type=jnp.float32)
    before = before + jnp.dot(onehot_other, neighbor_table, preferred_element_type=jnp.float32)
    activated = jax.nn.silu(before).astype(jnp.bfloat16)
    latent = jax.nn.silu(jnp.dot(activated, mix_weight, preferred_element_type=jnp.float32))
    env_terms = jnp.dot(latent.astype(jnp.bfloat16), env_weight, preferred_element_type=jnp.float32)
    channels = latent.shape[1]
    center_count = latent.shape[0] // NEIGH
    env_terms = env_terms.reshape(center_count, NEIGH, channels)
    harmonic_grid = angular.reshape(9, center_count, NEIGH)
    environment = jnp.einsum("akc,mak->amc", env_terms, harmonic_grid, precision=HIGH) / NEIGH
    pieces = []
    for start_m, stop_m in ((0, 1), (1, 4), (4, 9)):
        pieces.append(
            jnp.einsum(
                "amc,mak->akc",
                environment[:, start_m:stop_m],
                harmonic_grid[start_m:stop_m],
                precision=HIGH,
            )
        )
    invariants = jnp.concatenate(pieces, axis=2).reshape(center_count * NEIGH, 3 * channels)
    invariants = invariants.astype(jnp.bfloat16)
    update = jnp.dot(invariants, update_weight, preferred_element_type=jnp.float32)
    edge_latent = jax.nn.silu(latent + update)
    atom_latent = jnp.mean(edge_latent.reshape(center_count, NEIGH, channels), axis=1)
    return (atom_latent, edge_latent)


def layer_two(edge_latent, other_latent, second_weight, readout):
    product = (edge_latent * other_latent).astype(jnp.bfloat16)
    hidden = jax.nn.silu(jnp.dot(product, second_weight, preferred_element_type=jnp.float32))
    edge_energy = jnp.dot(hidden, readout, precision=HIGH)
    return jnp.sum(edge_energy.reshape(-1, NEIGH), axis=1)


def edge_model(rel_center, rel_other, offsets, onehot_center, onehot_other, params):
    displacement = (offsets + (rel_other - rel_center[:, :, None])).reshape(3, -1)
    return layer_one(displacement, onehot_center, onehot_other, params)


def one_hot(labels, count):
    return (labels[:, None] == jnp.arange(count, dtype=jnp.int32)[None, :]).astype(jnp.bfloat16)


def fold_rim(extended, dimension, interior):
    middle = lax.slice_in_dim(extended, 2, 2 + interior, axis=dimension)
    leading = lax.slice_in_dim(extended, 0, 1, axis=dimension)
    trailing = lax.slice_in_dim(extended, interior + 3, interior + 4, axis=dimension)
    front_pad = [(0, 0)] * extended.ndim
    front_pad[dimension] = (0, interior - 1)
    back_pad = [(0, 0)] * extended.ndim
    back_pad[dimension] = (interior - 1, 0)
    return middle + jnp.pad(leading, front_pad) + jnp.pad(trailing, back_pad)


def on_device(
    positions,
    species,
    neighbors,
    center_table,
    neighbor_table,
    radial_weight,
    mix_weight,
    env_weight,
    update_weight,
    second_weight,
    readout,
):
    params = (radial_weight, center_table, neighbor_table, mix_weight, env_weight, update_weight)
    cells_x, cells_y, cells_z, triple = positions.shape
    slot_count = triple // 3
    channels = mix_weight.shape[1]
    outer_x, outer_y, outer_z = (cells_x + 2, cells_y + 2, cells_z + 2)
    atom_count = cells_x * cells_y * cells_z * slot_count
    padded_count = outer_x * outer_y * outer_z * slot_count
    packed = jnp.concatenate([positions, species.astype(jnp.float32)], axis=3)
    padded = padded_2(packed, (("gx", 0), ("gy", 1), ("gz", 2)), 1)
    ghost_pos = padded[..., :triple].reshape(outer_x, outer_y, outer_z, 3, slot_count)
    ghost_pos = ghost_pos.transpose(3, 0, 1, 2, 4).reshape(3, padded_count)
    ghost_species = padded[..., triple:].reshape(padded_count).astype(jnp.int32)
    index_x = jnp.arange(cells_x, dtype=jnp.int32).reshape(cells_x, 1, 1, 1, 1)
    index_y = jnp.arange(cells_y, dtype=jnp.int32).reshape(1, cells_y, 1, 1, 1)
    index_z = jnp.arange(cells_z, dtype=jnp.int32).reshape(1, 1, cells_z, 1, 1)
    codes = neighbors.reshape(cells_x, cells_y, cells_z, slot_count, NEIGH)
    offset_code = codes // slot_count
    slot_other = codes % slot_count
    step_x = offset_code // 9 - 1
    step_y = offset_code // 3 % 3 - 1
    step_z = offset_code % 3 - 1
    cell_other = ((index_x + 1 + step_x) * outer_y + (index_y + 1 + step_y)) * outer_z + (
        index_z + 1 + step_z
    )
    other_index = (cell_other * slot_count + slot_other).reshape(atom_count, NEIGH)
    other_flat = other_index.reshape(-1)
    slot_own = jnp.arange(slot_count, dtype=jnp.int32).reshape(1, 1, 1, slot_count)
    cell_own = (
        ((index_x[..., 0] + 1) * outer_y + index_y[..., 0] + 1) * outer_z + index_z[..., 0] + 1
    )
    own_index = (cell_own * slot_count + slot_own).reshape(atom_count)
    offsets = jnp.stack([step_x, step_y, step_z]).astype(jnp.float32).reshape(3, atom_count, NEIGH)
    spec_count = center_table.shape[0]
    center_species = jnp.broadcast_to(
        species.reshape(atom_count)[:, None], (atom_count, NEIGH)
    ).reshape(-1)
    onehot_center = one_hot(center_species, spec_count)
    onehot_other = one_hot(ghost_species[other_flat], spec_count)
    rel_center = ghost_pos[:, own_index]
    rel_other = ghost_pos[:, other_index]

    def first(center_pos, other_pos):
        return edge_model(center_pos, other_pos, offsets, onehot_center, onehot_other, params)

    outputs, back_one = jax.vjp(first, rel_center, rel_other)
    coarse_table = (
        outputs[0].astype(jnp.bfloat16).reshape(cells_x, cells_y, cells_z, slot_count * channels)
    )
    spread_latent = padded_2(coarse_table, (("gx", 0), ("gy", 1), ("gz", 2)), 1)
    latent_table = spread_latent.reshape(padded_count, channels)
    other_latent = latent_table[other_flat].astype(jnp.float32)

    def second(edge_latent, neighbor_latent):
        return layer_two(edge_latent, neighbor_latent, second_weight, readout)

    energy, back_two = jax.vjp(second, outputs[1], other_latent)
    grad_edge, grad_other = back_two(jnp.ones_like(energy))
    latent_spread = jnp.zeros((padded_count, channels), jnp.float32).at[other_flat].add(grad_other)
    latent_spread = latent_spread.reshape(outer_x, outer_y, outer_z, slot_count * channels)
    returned = padded_2(latent_spread, (("gx", 0), ("gy", 1), ("gz", 2)), 1)
    owned_grad = fold_rim(fold_rim(fold_rim(returned, 0, cells_x), 1, cells_y), 2, cells_z)
    grad_center, grad_other_pos = back_one((owned_grad.reshape(atom_count, channels), grad_edge))
    motion = jnp.zeros((3, padded_count), jnp.float32).at[:, own_index].add(grad_center)
    motion = motion.at[:, other_flat].add(grad_other_pos.reshape(3, -1))
    motion = motion.reshape(3, outer_x, outer_y, outer_z, slot_count).transpose(1, 2, 3, 0, 4)
    motion = motion.reshape(outer_x, outer_y, outer_z, triple)
    returned_motion = padded_2(motion, (("gx", 0), ("gy", 1), ("gz", 2)), 1)
    forces = -fold_rim(fold_rim(fold_rim(returned_motion, 0, cells_x), 1, cells_y), 2, cells_z)
    return (energy.reshape(cells_x, cells_y, cells_z, slot_count), forces)


def solution(mesh):
    placed = (
        P("gx", "gy", "gz", None),
        P("gx", "gy", "gz", None),
        P("gx", "gy", "gz", None),
        P(),
        P(),
        P(),
        P(),
        P(),
        P(),
        P(),
        P(),
    )
    return jax.shard_map(
        on_device,
        mesh=mesh,
        in_specs=placed,
        out_specs=(P("gx", "gy", "gz", None), P("gx", "gy", "gz", None)),
        check_vma=False,
    )
```

profile of v0, /device:TPU:0, one launch (start us, length us, event | category | flops | bytes accessed | tf_op | source)
XLA Modules:
  0.0 173.2 jit_solution(16079899848892998118)
XLA Ops:
  2.1 5.0 %collective-permute-start.1 = (f32[1,1,2,256]{3,2,1,0:T(2,128)S(1)}, f32[1,1,2,256]{3,2,1,0:T(2,128)S(1)}, u32[]{:S(2)}, u32[]{:S(2)}) collective-permute-start(f32[1,1,2,256]{3,2,1,0:T(2,128)S(1)} %pad_maximum_fusion.35), channel_id=1, source_target_pairs={{8,0},{16,8},{24,16},{0,24},{9,1},{17,9},{25,17},{1,25},{10,2},{18... | collective-permute-start | bytes 6152 | tf_op jit(solution)/shard_map/ppermute | solution.py:25
  13.3 2.4 %collective-permute-start.3 = (f32[3,1,2,256]{3,2,1,0:T(2,128)S(1)}, f32[3,1,2,256]{3,2,1,0:T(2,128)S(1)}, u32[]{:S(2)}, u32[]{:S(2)}) collective-permute-start(f32[3,1,2,256]{3,2,1,0:T(2,128)S(1)} %pad_maximum_fusion.34), channel_id=1, source_target_pairs={{2,0},{4,2},{6,4},{0,6},{3,1},{5,3},{7,5},{1,7},{10,8},{12,10},{14... | collective-permute-start | bytes 18440 | tf_op jit(solution)/shard_map/ppermute | solution.py:25
  17.1 3.2 %collective-permute-done.2 = f32[3,1,2,256]{3,2,1,0:T(2,128)S(1)} collective-permute-done((f32[3,1,2,256]{3,2,1,0:T(2,128)S(1)}, f32[3,1,2,256]{3,2,1,0:T(2,128)S(1)}, u32[]{:S(2)}, u32[]{:S(2)}) %collective-permute-start.2) | collective-permute-done | bytes 6176 | tf_op jit(solution)/shard_map/ppermute | solution.py:23
  24.3 2.8 %gather_fusion = f32[1024,3]{1,0:T(8,128)S(1)} fusion(f32[3,2304]{0,1:T(8,128)S(1)} %bitcast.99, s32[1024]{0:T(1024)S(1)} %broadcast_clamp_fusion.1), kind=kCustom, calls=%fused_computation | custom fusion | bytes 28672 | tf_op jit(solution)/shard_map/gather | solution.py:174
  31.4 6.2 %gather_fusion.2 = s32[1024]{0:T(1024)S(1)} fusion(s32[2304]{0:T(1024)S(1)} %convert_element_type.95, s32[1024]{0:T(1024)S(1)} %get-tuple-element.65), kind=kCustom, calls=%fused_computation.2 | custom fusion | bytes 12288 | tf_op jit(solution)/shard_map/gather | solution.py:172
  44.7 3.8 %collective-permute-start.7 = (bf16[1,1,2,8192]{3,2,1,0:T(2,128)(2,1)S(1)}, bf16[1,1,2,8192]{3,2,1,0:T(2,128)(2,1)S(1)}, u32[]{:S(2)}, u32[]{:S(2)}) collective-permute-start(bf16[1,1,2,8192]{3,2,1,0:T(2,128)(2,1)S(1)} %convert_element_type.101), channel_id=1, source_target_pairs={{8,0},{16,8},{24,16},{0,24},{9,1},{17,9},{25,17},{1,25},{10,2},{18... | collective-permute-start | bytes 98312 | tf_op jit(solution)/shard_map/ppermute | solution.py:25
  48.5 1.9 %collective-permute-done.6 = bf16[1,1,2,8192]{3,2,1,0:T(2,128)(2,1)S(1)} collective-permute-done((bf16[1,1,2,8192]{3,2,1,0:T(2,128)(2,1)S(1)}, bf16[1,1,2,8192]{3,2,1,0:T(2,128)(2,1)S(1)}, u32[]{:S(2)}, u32[]{:S(2)}) %collective-permute-start.6) | collective-permute-done | bytes 32800 | tf_op jit(solution)/shard_map/ppermute | solution.py:23
  50.6 2.0 %collective-permute-start.8 = (bf16[3,1,2,8192]{3,2,1,0:T(2,128)(2,1)S(1)}, bf16[3,1,2,8192]{3,2,1,0:T(2,128)(2,1)S(1)}, u32[]{:S(2)}, u32[]{:S(2)}) collective-permute-start(bf16[3,1,2,8192]{3,2,1,0:T(2,128)(2,1)S(1)} %constant_dynamic-update-slice_fusion.7), channel_id=1, source_target_pairs={{0,2},{2,4},{4,6},{6,0},{1,3},{3,5},{5,7},{7,1},{8,10},{10,12},{12... | collective-permute-start | bytes 294920 | tf_op jit(solution)/shard_map/ppermute | solution.py:23
  52.6 2.6 %collective-permute-done.9 = bf16[3,1,2,8192]{3,2,1,0:T(2,128)(2,1)S(1)} collective-permute-done((bf16[3,1,2,8192]{3,2,1,0:T(2,128)(2,1)S(1)}, bf16[3,1,2,8192]{3,2,1,0:T(2,128)(2,1)S(1)}, u32[]{:S(2)}, u32[]{:S(2)}) %collective-permute-start.9) | collective-permute-done | bytes 98336 | tf_op jit(solution)/shard_map/ppermute | solution.py:25
  61.1 3.2 %gather_fusion.3 = bf16[1024,128]{1,0:T(8,128)(2,1)S(1)} fusion(bf16[2304,128]{1,0:T(8,128)(2,1)S(1)} %reshape.1254, s32[1024]{0:T(1024)S(1)} %get-tuple-element.65), kind=kCustom, calls=%fused_computation.3 | custom fusion | bytes 528384 | tf_op jit(solution)/shard_map/gather | solution.py:185
  67.2 6.6 %scatter_custom_fusion = f32[2304,128]{1,0:T(8,128)S(1)} fusion(s32[1024]{0:T(1024)} %bitcast.110, f32[]{:T(128)} %constant.112.clone.1, f32[1024,128]{1,0:T(8,128)S(1)} %fusion.5, f32[1024,128]{1,0:T(8,128)S(1)} %copy-done.10), kind=kCustom, calls=%fused_computation.47 | custom fusion | flops 786432 | bytes 2228736 | tf_op jit(solution)/shard_map/scatter-add | solution.py:192
  77.1 3.9 %collective-permute-start.13 = (f32[1,3,4,8192]{3,2,1,0:T(4,128)S(1)}, f32[1,3,4,8192]{3,2,1,0:T(4,128)S(1)}, u32[]{:S(2)}, u32[]{:S(2)}) collective-permute-start(f32[1,3,4,8192]{3,2,1,0:T(4,128)S(1)} %slice.179), channel_id=1, source_target_pairs={{8,0},{16,8},{24,16},{0,24},{9,1},{17,9},{25,17},{1,25},{10,2},{18... | collective-permute-start | bytes 1179656 | tf_op jit(solution)/shard_map/ppermute | solution.py:25
  81.0 8.7 %collective-permute-done.12 = f32[1,3,4,8192]{3,2,1,0:T(4,128)} collective-permute-done((f32[1,3,4,8192]{3,2,1,0:T(4,128)}, f32[1,3,4,8192]{3,2,1,0:T(4,128)}, u32[]{:S(2)}, u32[]{:S(2)}) %collective-permute-start.12) | collective-permute-done | bytes 393248 | tf_op jit(solution)/shard_map/ppermute | solution.py:23
  90.8 5.9 %collective-permute-done.13 = f32[1,3,4,8192]{3,2,1,0:T(4,128)S(1)} collective-permute-done((f32[1,3,4,8192]{3,2,1,0:T(4,128)S(1)}, f32[1,3,4,8192]{3,2,1,0:T(4,128)S(1)}, u32[]{:S(2)}, u32[]{:S(2)}) %collective-permute-start.13) | collective-permute-done | bytes 393248 | tf_op jit(solution)/shard_map/ppermute | solution.py:25
  97.8 2.1 %collective-permute-start.15 = (f32[5,1,4,8192]{3,2,1,0:T(4,128)S(1)}, f32[5,1,4,8192]{3,2,1,0:T(4,128)S(1)}, u32[]{:S(2)}, u32[]{:S(2)}) collective-permute-start(f32[5,1,4,8192]{3,2,1,0:T(4,128)S(1)} %get-tuple-element.31), channel_id=1, source_target_pairs={{2,0},{4,2},{6,4},{0,6},{3,1},{5,3},{7,5},{1,7},{10,8},{12,10},{14... | collective-permute-start | bytes 1966088 | tf_op jit(solution)/shard_map/ppermute | solution.py:25
  99.9 15.6 %collective-permute-done.14 = f32[5,1,4,8192]{3,2,1,0:T(4,128)S(1)} collective-permute-done((f32[5,1,4,8192]{3,2,1,0:T(4,128)S(1)}, f32[5,1,4,8192]{3,2,1,0:T(4,128)S(1)}, u32[]{:S(2)}, u32[]{:S(2)}) %collective-permute-start.14) | collective-permute-done | bytes 655392 | tf_op jit(solution)/shard_map/ppermute | solution.py:23
  115.5 12.5 %collective-permute-done.15 = f32[5,1,4,8192]{3,2,1,0:T(4,128)S(1)} collective-permute-done((f32[5,1,4,8192]{3,2,1,0:T(4,128)S(1)}, f32[5,1,4,8192]{3,2,1,0:T(4,128)S(1)}, u32[]{:S(2)}, u32[]{:S(2)}) %collective-permute-start.15) | collective-permute-done | bytes 655392 | tf_op jit(solution)/shard_map/ppermute | solution.py:25
  128.0 2.1 %pad_maximum_fusion.2 = (f32[5,5,1,8192]{3,2,1,0:T(1,128)S(1)}, f32[5,5,1,8192]{3,2,1,0:T(1,128)S(1)}) fusion(f32[5,1,4,8192]{3,2,1,0:T(4,128)S(1)} %collective-permute-done.15, f32[5,3,4,8192]{3,2,1,0:T(4,128)S(1)} %constant_dynamic-update-slice_fusion.10, f32[5,1,4,8192]{3,2,1,0:T(4,128)S(1)} %collective-permute-done.14), kind=kLoop, calls=%fused_computation.34 | loop fusion | flops 819200 | bytes 4915200 | tf_op jit(solution)/shard_map/slice | solution.py:20
  142.1 2.4 %fusion.111 = (f32[1024]{0:T(1024)}, f32[1024]{0:T(1024)}) fusion(f32[8]{0:T(128)} %copy-done.36, f32[1024]{0:T(1024)S(1)} %sqrt.22, f32[1024]{0:T(1024)} %copy-done.27, bf16[8,128]{1,0:T(8,128)(2,1)} %param.16, f32[1024,128]{1,0:T(8,128)S(1)} %copy-done.17, bf16[128,128]{1,0:T(8,128)(2,1)} %param.17, f32[1024,128]{1,0:T(8,128)} %copy-done.46, ...), kind=kOutput, calls=%fused_computation.196 | convolution fusion | flops 38377472 | bytes 1624096 | tf_op jit(solution)/shard_map/transpose(jvp())/dot_general | solution.py:64
  144.5 2.8 %fusion.1 = f32[9,128,8]{0,2,1:T(8,128)S(1)} fusion(f32[128,8,128]{2,1,0:T(8,128)S(1)} %copy-done.8, f32[128,1,128]{2,1,0:T(1,128)} %copy-done.21, f32[128,3,128]{2,1,0:T(4,128)S(1)} %fusion.68, f32[128,5,128]{2,1,0:T(8,128)S(1)} %fusion.30, f32[1,128,8]{0,2,1:T(8,128)S(1)} %convolution_bitcast_fusion.2, f32[3,128,8]{0,2,1:T(8,128)S(1)} %convolution_bitcast_fusion.3, ...), kind=kOutput, calls=%fused_computation.14 | convolution fusion | flops 14625792 | bytes 1187840 | tf_op jit(solution)/shard_map/transpose(jvp(akc,mak->amc))/dot_general | solution.py:76
  147.3 2.2 %slice_reduce_fusion.5 = (f32[128,8]{1,0:T(8,128)S(1)}, f32[128,8]{1,0:T(8,128)S(1)}, f32[128,8]{1,0:T(8,128)S(1)}, f32[128,8]{1,0:T(8,128)S(1)}, f32[128,8]{1,0...) fusion(f32[9,128,8]{0,2,1:T(8,128)S(1)} %fusion.1), kind=kLoop, calls=%fused_computation.70 | loop fusion | flops 2048 | bytes 65536 | tf_op jit(solution)/shard_map/transpose(jvp())/unstack | solution.py:37
  153.0 6.5 %scatter_fusion = f32[3,2304]{0,1:T(8,128)S(1)} fusion(f32[3,2304]{0,1:T(8,128)S(1)} %scatter_custom_fusion.1, s32[1024]{0:T(1024)S(1)} %bitcast.111, f32[1024,3]{1,0:T(8,128)S(1)} %copy.213), kind=kCustom, calls=%fused_computation.6 | custom fusion | flops 3072 | bytes 40960 | tf_op jit(solution)/shard_map/scatter-add | solution.py:198
  161.7 2.3 %collective-permute-start.19 = (f32[1,3,4,192]{3,2,1,0:T(4,128)S(1)}, f32[1,3,4,192]{3,2,1,0:T(4,128)S(1)}, u32[]{:S(2)}, u32[]{:S(2)}) collective-permute-start(f32[1,3,4,192]{3,2,1,0:T(4,128)S(1)} %slice.197), channel_id=1, source_target_pairs={{8,0},{16,8},{24,16},{0,24},{9,1},{17,9},{25,17},{1,25},{10,2},{18... | collective-permute-start | bytes 27656 | tf_op jit(solution)/shard_map/ppermute | solution.py:25
  166.0 2.6 %collective-permute-start.21 = (f32[5,1,4,192]{3,2,1,0:T(4,128)S(1)}, f32[5,1,4,192]{3,2,1,0:T(4,128)S(1)}, u32[]{:S(2)}, u32[]{:S(2)}) collective-permute-start(f32[5,1,4,192]{3,2,1,0:T(4,128)S(1)} %get-tuple-element.44), channel_id=1, source_target_pairs={{2,0},{4,2},{6,4},{0,6},{3,1},{5,3},{7,5},{1,7},{10,8},{12,10},{14... | collective-permute-start | bytes 46088 | tf_op jit(solution)/shard_map/ppermute | solution.py:25
  (281 shorter events, 62.0 us)
Async XLA Ops:
  2.1 9.3 %collective-permute-start.1 = (f32[1,1,2,256]{3,2,1,0:T(2,128)S(1)}, f32[1,1,2,256]{3,2,1,0:T(2,128)S(1)}, u32[]{:S(2)}, u32[]{:S(2)}) collective-permute-start(f32[1,1,2,256]{3,2,1,0:T(2,128)S(1)} %pad_maximum_fusion.35), channel_id=1, source_target_pairs={{8,0},{16,8},{24,16},{0,24},{9,1},{17,9},{25,17},{1,25},{10,2},{18... | collective-permute-start | bytes 6152 | tf_op jit(solution)/shard_map/ppermute | solution.py:25
  7.2 5.4 %collective-permute-start = (f32[1,1,2,256]{3,2,1,0:T(2,128)S(1)}, f32[1,1,2,256]{3,2,1,0:T(2,128)S(1)}, u32[]{:S(2)}, u32[]{:S(2)}) collective-permute-start(f32[1,1,2,256]{3,2,1,0:T(2,128)S(1)} %pad_maximum_fusion.35), channel_id=1, source_target_pairs={{0,8},{8,16},{16,24},{24,0},{1,9},{9,17},{17,25},{25,1},{2,10},{10... | collective-permute-start | bytes 6152 | tf_op jit(solution)/shard_map/ppermute | solution.py:23
  13.3 3.8 %collective-permute-start.3 = (f32[3,1,2,256]{3,2,1,0:T(2,128)S(1)}, f32[3,1,2,256]{3,2,1,0:T(2,128)S(1)}, u32[]{:S(2)}, u32[]{:S(2)}) collective-permute-start(f32[3,1,2,256]{3,2,1,0:T(2,128)S(1)} %pad_maximum_fusion.34), channel_id=1, source_target_pairs={{2,0},{4,2},{6,4},{0,6},{3,1},{5,3},{7,5},{1,7},{10,8},{12,10},{14... | collective-permute-start | bytes 18440 | tf_op jit(solution)/shard_map/ppermute | solution.py:25
  15.8 4.5 %collective-permute-start.2 = (f32[3,1,2,256]{3,2,1,0:T(2,128)S(1)}, f32[3,1,2,256]{3,2,1,0:T(2,128)S(1)}, u32[]{:S(2)}, u32[]{:S(2)}) collective-permute-start(f32[3,1,2,256]{3,2,1,0:T(2,128)S(1)} %pad_maximum_fusion.34), channel_id=1, source_target_pairs={{0,2},{2,4},{4,6},{6,0},{1,3},{3,5},{5,7},{7,1},{8,10},{10,12},{12... | collective-permute-start | bytes 18440 | tf_op jit(solution)/shard_map/ppermute | solution.py:23
  21.1 1.7 collective-permute-start.4
  21.2 1.6 collective-permute-start.5
  44.6 5.8 %collective-permute-start.6 = (bf16[1,1,2,8192]{3,2,1,0:T(2,128)(2,1)S(1)}, bf16[1,1,2,8192]{3,2,1,0:T(2,128)(2,1)S(1)}, u32[]{:S(2)}, u32[]{:S(2)}) collective-permute-start(bf16[1,1,2,8192]{3,2,1,0:T(2,128)(2,1)S(1)} %convert_element_type.101), channel_id=1, source_target_pairs={{0,8},{8,16},{16,24},{24,0},{1,9},{9,17},{17,25},{25,1},{2,10},{10... | collective-permute-start | bytes 98312 | tf_op jit(solution)/shard_map/ppermute | solution.py:23
  44.7 5.8 %collective-permute-start.7 = (bf16[1,1,2,8192]{3,2,1,0:T(2,128)(2,1)S(1)}, bf16[1,1,2,8192]{3,2,1,0:T(2,128)(2,1)S(1)}, u32[]{:S(2)}, u32[]{:S(2)}) collective-permute-start(bf16[1,1,2,8192]{3,2,1,0:T(2,128)(2,1)S(1)} %convert_element_type.101), channel_id=1, source_target_pairs={{8,0},{16,8},{24,16},{0,24},{9,1},{17,9},{25,17},{1,25},{10,2},{18... | collective-permute-start | bytes 98312 | tf_op jit(solution)/shard_map/ppermute | solution.py:25
  50.5 4.7 %collective-permute-start.9 = (bf16[3,1,2,8192]{3,2,1,0:T(2,128)(2,1)S(1)}, bf16[3,1,2,8192]{3,2,1,0:T(2,128)(2,1)S(1)}, u32[]{:S(2)}, u32[]{:S(2)}) collective-permute-start(bf16[3,1,2,8192]{3,2,1,0:T(2,128)(2,1)S(1)} %constant_dynamic-update-slice_fusion.7), channel_id=1, source_target_pairs={{2,0},{4,2},{6,4},{0,6},{3,1},{5,3},{7,5},{1,7},{10,8},{12,10},{14... | collective-permute-start | bytes 294920 | tf_op jit(solution)/shard_map/ppermute | solution.py:25
  50.6 5.8 %collective-permute-start.8 = (bf16[3,1,2,8192]{3,2,1,0:T(2,128)(2,1)S(1)}, bf16[3,1,2,8192]{3,2,1,0:T(2,128)(2,1)S(1)}, u32[]{:S(2)}, u32[]{:S(2)}) collective-permute-start(bf16[3,1,2,8192]{3,2,1,0:T(2,128)(2,1)S(1)} %constant_dynamic-update-slice_fusion.7), channel_id=1, source_target_pairs={{0,2},{2,4},{4,6},{6,0},{1,3},{3,5},{5,7},{7,1},{8,10},{10,12},{12... | collective-permute-start | bytes 294920 | tf_op jit(solution)/shard_map/ppermute | solution.py:23
  57.4 1.6 collective-permute-start.10
  57.5 2.0 %collective-permute-start.11 = (bf16[3,3,1,8192]{3,2,1,0:T(2,128)(2,1)S(1)}, bf16[3,3,1,8192]{3,2,1,0:T(2,128)(2,1)S(1)}, u32[]{:S(2)}, u32[]{:S(2)}) collective-permute-start(bf16[3,3,1,8192]{3,2,1,0:T(2,128)(2,1)S(1)} %get-tuple-element.35), channel_id=1, source_target_pairs={{1,0},{0,1},{3,2},{2,3},{5,4},{4,5},{7,6},{6,7},{9,8},{8,9},{11,10... | collective-permute-start | bytes 442376 | tf_op jit(solution)/shard_map/ppermute | solution.py:25
  75.5 14.2 %collective-permute-start.12 = (f32[1,3,4,8192]{3,2,1,0:T(4,128)}, f32[1,3,4,8192]{3,2,1,0:T(4,128)}, u32[]{:S(2)}, u32[]{:S(2)}) collective-permute-start(f32[1,3,4,8192]{3,2,1,0:T(4,128)} %slice.177), channel_id=1, source_target_pairs={{0,8},{8,16},{16,24},{24,0},{1,9},{9,17},{17,25},{25,1},{2,10},{10... | collective-permute-start | bytes 1179656 | tf_op jit(solution)/shard_map/ppermute | solution.py:23
  77.1 19.6 %collective-permute-start.13 = (f32[1,3,4,8192]{3,2,1,0:T(4,128)S(1)}, f32[1,3,4,8192]{3,2,1,0:T(4,128)S(1)}, u32[]{:S(2)}, u32[]{:S(2)}) collective-permute-start(f32[1,3,4,8192]{3,2,1,0:T(4,128)S(1)} %slice.179), channel_id=1, source_target_pairs={{8,0},{16,8},{24,16},{0,24},{9,1},{17,9},{25,17},{1,25},{10,2},{18... | collective-permute-start | bytes 1179656 | tf_op jit(solution)/shard_map/ppermute | solution.py:25
  96.9 18.6 %collective-permute-start.14 = (f32[5,1,4,8192]{3,2,1,0:T(4,128)S(1)}, f32[5,1,4,8192]{3,2,1,0:T(4,128)S(1)}, u32[]{:S(2)}, u32[]{:S(2)}) collective-permute-start(f32[5,1,4,8192]{3,2,1,0:T(4,128)S(1)} %get-tuple-element.30), channel_id=1, source_target_pairs={{0,2},{2,4},{4,6},{6,0},{1,3},{3,5},{5,7},{7,1},{8,10},{10,12},{12... | collective-permute-start | bytes 1966088 | tf_op jit(solution)/shard_map/ppermute | solution.py:23
  97.8 30.2 %collective-permute-start.15 = (f32[5,1,4,8192]{3,2,1,0:T(4,128)S(1)}, f32[5,1,4,8192]{3,2,1,0:T(4,128)S(1)}, u32[]{:S(2)}, u32[]{:S(2)}) collective-permute-start(f32[5,1,4,8192]{3,2,1,0:T(4,128)S(1)} %get-tuple-element.31), channel_id=1, source_target_pairs={{2,0},{4,2},{6,4},{0,6},{3,1},{5,3},{7,5},{1,7},{10,8},{12,10},{14... | collective-permute-start | bytes 1966088 | tf_op jit(solution)/shard_map/ppermute | solution.py:25
  130.1 2.4 %collective-permute-start.16 = (f32[5,5,1,8192]{3,2,1,0:T(1,128)S(1)}, f32[5,5,1,8192]{3,2,1,0:T(1,128)S(1)}, u32[]{:S(2)}, u32[]{:S(2)}) collective-permute-start(f32[5,5,1,8192]{3,2,1,0:T(1,128)S(1)} %get-tuple-element.28), channel_id=1, source_target_pairs={{0,1},{1,0},{2,3},{3,2},{4,5},{5,4},{6,7},{7,6},{8,9},{9,8},{10,11... | collective-permute-start | bytes 2457608 | tf_op jit(solution)/shard_map/ppermute | solution.py:23
  130.2 3.4 %collective-permute-start.17 = (f32[5,5,1,8192]{3,2,1,0:T(1,128)S(1)}, f32[5,5,1,8192]{3,2,1,0:T(1,128)S(1)}, u32[]{:S(2)}, u32[]{:S(2)}) collective-permute-start(f32[5,5,1,8192]{3,2,1,0:T(1,128)S(1)} %get-tuple-element.29), channel_id=1, source_target_pairs={{1,0},{0,1},{3,2},{2,3},{5,4},{4,5},{7,6},{6,7},{9,8},{8,9},{11,10... | collective-permute-start | bytes 2457608 | tf_op jit(solution)/shard_map/ppermute | solution.py:25
  160.0 5.6 %collective-permute-start.18 = (f32[1,3,4,192]{3,2,1,0:T(4,128)S(1)}, f32[1,3,4,192]{3,2,1,0:T(4,128)S(1)}, u32[]{:S(2)}, u32[]{:S(2)}) collective-permute-start(f32[1,3,4,192]{3,2,1,0:T(4,128)S(1)} %slice.195), channel_id=1, source_target_pairs={{0,8},{8,16},{16,24},{24,0},{1,9},{9,17},{17,25},{25,1},{2,10},{10... | collective-permute-start | bytes 27656 | tf_op jit(solution)/shard_map/ppermute | solution.py:23
  161.7 3.8 %collective-permute-start.19 = (f32[1,3,4,192]{3,2,1,0:T(4,128)S(1)}, f32[1,3,4,192]{3,2,1,0:T(4,128)S(1)}, u32[]{:S(2)}, u32[]{:S(2)}) collective-permute-start(f32[1,3,4,192]{3,2,1,0:T(4,128)S(1)} %slice.197), channel_id=1, source_target_pairs={{8,0},{16,8},{24,16},{0,24},{9,1},{17,9},{25,17},{1,25},{10,2},{18... | collective-permute-start | bytes 27656 | tf_op jit(solution)/shard_map/ppermute | solution.py:25
  165.6 4.7 %collective-permute-start.20 = (f32[5,1,4,192]{3,2,1,0:T(4,128)S(1)}, f32[5,1,4,192]{3,2,1,0:T(4,128)S(1)}, u32[]{:S(2)}, u32[]{:S(2)}) collective-permute-start(f32[5,1,4,192]{3,2,1,0:T(4,128)S(1)} %get-tuple-element.43), channel_id=1, source_target_pairs={{0,2},{2,4},{4,6},{6,0},{1,3},{3,5},{5,7},{7,1},{8,10},{10,12},{12... | collective-permute-start | bytes 46088 | tf_op jit(solution)/shard_map/ppermute | solution.py:23
  166.0 4.4 %collective-permute-start.21 = (f32[5,1,4,192]{3,2,1,0:T(4,128)S(1)}, f32[5,1,4,192]{3,2,1,0:T(4,128)S(1)}, u32[]{:S(2)}, u32[]{:S(2)}) collective-permute-start(f32[5,1,4,192]{3,2,1,0:T(4,128)S(1)} %get-tuple-element.44), channel_id=1, source_target_pairs={{2,0},{4,2},{6,4},{0,6},{3,1},{5,3},{7,5},{1,7},{10,8},{12,10},{14... | collective-permute-start | bytes 46088 | tf_op jit(solution)/shard_map/ppermute | solution.py:25
  170.4 2.1 %collective-permute-start.22 = (f32[5,5,1,192]{3,2,1,0:T(1,128)S(1)}, f32[5,5,1,192]{3,2,1,0:T(1,128)S(1)}, u32[]{:S(2)}, u32[]{:S(2)}) collective-permute-start(f32[5,5,1,192]{3,2,1,0:T(1,128)S(1)} %get-tuple-element.36), channel_id=1, source_target_pairs={{0,1},{1,0},{2,3},{3,2},{4,5},{5,4},{6,7},{7,6},{8,9},{9,8},{10,11... | collective-permute-start | bytes 57608 | tf_op jit(solution)/shard_map/ppermute | solution.py:23
  170.5 2.0 %collective-permute-start.23 = (f32[5,5,1,192]{3,2,1,0:T(1,128)S(1)}, f32[5,5,1,192]{3,2,1,0:T(1,128)S(1)}, u32[]{:S(2)}, u32[]{:S(2)}) collective-permute-start(f32[5,5,1,192]{3,2,1,0:T(1,128)S(1)} %get-tuple-element.37), channel_id=1, source_target_pairs={{1,0},{0,1},{3,2},{2,3},{5,4},{4,5},{7,6},{6,7},{9,8},{8,9},{11,10... | collective-permute-start | bytes 57608 | tf_op jit(solution)/shard_map/ppermute | solution.py:25
  (47 other events, 278.1 us)
where the time goes:
time: 174 us; the launch traced here: 173 us
  waiting for transfers between devices  61.8 us (36%)
  local copies, waits for them, and re-layouts  33.8 us (19%)
  starting transfers between devices  29.4 us (17%)
  other arithmetic  27.5 us (16%)
  matrix products  18.8 us (11%)
  between operations  1.89 us (1%)
    ppermute x12, waiting for transfers between devices, padded_2(): lax.ppermute(tail, axis, [(i, (i + 1) % count) for i in range(count)])  37.8 us
    ppermute x12, starting transfers between devices, padded_2(): lax.ppermute(head, axis, [((i + 1) % count, i) for i in range(count)])  24.2 us
    ppermute x12, waiting for transfers between devices, padded_2(): lax.ppermute(head, axis, [((i + 1) % count, i) for i in range(count)])  24 us
    scatter-add x1, other arithmetic, on_device(): jnp.zeros((padded_count, channels), jnp.float32).at[other_flat]  6.58 us
    unnamed x106, local copies, waits for them, and re-layouts  6.49 us
    scatter-add x1, other arithmetic, on_device(): motion = motion.at[:, other_flat].add(grad_other_pos.reshape(3, -1))  6.48 us
    gather x1, local copies, waits for them, and re-layouts, on_device(): onehot_other = one_hot(ghost_species[other_flat], spec_count)  6.15 us
    dot_general x3, matrix products, layer_one(): jnp.einsum('akc,mak->amc', env_terms, harmonic_grid, precision=HIGH) / NEIGH  5.87 us
  transfers between devices with their start and end apart: 24, of which 16 were waited for; matrix products, arithmetic and copies ran while one was open for 5% of the time, Pallas kernels for 0%

commit v1 on v0

v1 whole, which is shorter than its diff:
```python
import functools
import math

import jax
import jax.numpy as jnp
from jax import lax
from jax.experimental import pallas as pl
from jax.experimental.pallas import tpu as pltpu
from jax.sharding import PartitionSpec as P

NEIGH = 8
ATOMS = 128
EDGES = NEIGH * ATOMS
CHUNKS = 18
CUTOFF = 4.0
SHARPNESS = 2.0
ROOT3 = math.sqrt(3.0)
F32 = jnp.float32
BF16 = jnp.bfloat16
TILE = 256


def shifted(value, axis, step):
    count = lax.axis_size(axis)
    return lax.ppermute(value, axis, [(i, (i + step) % count) for i in range(count)])


def gather_halo(chunk):
    for axis in ("gx", "gy"):
        lower = shifted(chunk, axis, 1)
        upper = shifted(chunk, axis, -1)
        chunk = jnp.concatenate([chunk, lower, upper], axis=0)
    if lax.axis_size("gz") == 2:
        return chunk, shifted(chunk, "gz", 1)
    half = chunk.shape[-1] // 2
    above = shifted(chunk[..., :half], "gz", -1)
    below = shifted(chunk[..., half:], "gz", 1)
    return chunk, jnp.concatenate([above, below], axis=-1)


def reduce_halo(own, other):
    if lax.axis_size("gz") == 2:
        back = shifted(other, "gz", 1)
    else:
        half = other.shape[-1] // 2
        first = shifted(other[..., :half], "gz", 1)
        second = shifted(other[..., half:], "gz", -1)
        back = jnp.concatenate([first, second], axis=-1)
    kind = own.dtype
    own = own.astype(F32) + back.astype(F32)
    for axis, size in (("gy", 3), ("gx", 1)):
        lower = shifted(own[size : 2 * size].astype(kind), axis, -1)
        upper = shifted(own[2 * size :].astype(kind), axis, 1)
        own = own[:size] + lower.astype(F32) + upper.astype(F32)
    return own


def pack_kernel(pos_ref, spec_ref, out_ref):
    out_ref[...] = jnp.zeros(out_ref.shape, F32)
    slots = spec_ref.shape[-1]
    for block in range(2):
        lanes = slice(block * slots, (block + 1) * slots)
        for c in range(3):
            out_ref[0, c : c + 1, lanes] = pos_ref[0, 0, block : block + 1, c * slots : (c + 1) * slots]
        out_ref[0, 3:4, lanes] = spec_ref[0, 0, block : block + 1, :].astype(F32)


def prep_kernel(
    nb_ref, center_ref, neighbor_ref, radial_ref, mix_ref, env_ref, upd_ref, second_ref, readout_ref,
    code_ref, onehot_ref, wcat_ref, mixt_ref, envt_ref, updt_ref, secondt_ref, rocol_ref, pad_ref,
):
    width = nb_ref.shape[-1]
    slots = width // NEIGH
    lane = lax.broadcasted_iota(jnp.int32, (NEIGH, width), 1)
    row = lax.broadcasted_iota(jnp.int32, (NEIGH, width), 0)
    mine = (lane & (NEIGH - 1)) == row
    spot = lax.broadcasted_iota(jnp.int32, (width, ATOMS), 0) // NEIGH
    column = lax.broadcasted_iota(jnp.int32, (width, ATOMS), 1)
    total = jnp.zeros((NEIGH, ATOMS), F32)
    for block in range(2):
        listed = jnp.broadcast_to(nb_ref[0, 0, block : block + 1, :], (NEIGH, width))
        listed = jnp.where(mine, listed, 0)
        high = (listed >> 4).astype(F32).astype(BF16)
        low = (listed & 15).astype(F32).astype(BF16)
        pick = jnp.where(spot + block * slots == column, 1.0, 0.0).astype(BF16)
        total = total + 16.0 * jnp.dot(high, pick, preferred_element_type=F32)
        total = total + jnp.dot(low, pick, preferred_element_type=F32)
    code = (total + 0.5).astype(jnp.int32)
    offset = code >> 6
    slot = code & 63
    step_x = jnp.where(offset >= 18, 1, jnp.where(offset >= 9, 0, -1))
    rest = offset - 9 * (step_x + 1)
    step_y = jnp.where(rest >= 6, 1, jnp.where(rest >= 3, 0, -1))
    step_z = rest - 3 * (step_y + 1) - 1
    block = lax.broadcasted_iota(jnp.int32, (NEIGH, ATOMS), 1) // slots
    level = block + step_z
    outside = jnp.where((level < 0) | (level > 1), 1, 0)
    place_x = jnp.where(step_x == 0, 0, jnp.where(step_x < 0, 1, 2))
    place_y = jnp.where(step_y == 0, 0, jnp.where(step_y < 0, 1, 2))
    chunk = outside * 9 + place_y * 3 + place_x
    target = chunk * ATOMS + (level & 1) * slots + slot
    code_ref[0] = target
    code_ref[1] = step_x
    code_ref[2] = step_y
    code_ref[3] = step_z

    pad_ref[...] = jnp.zeros(pad_ref.shape, F32)
    pad_ref[0:8, :] = radial_ref[...].astype(F32)
    pad_ref[8 : 8 + neighbor_ref.shape[0], :] = neighbor_ref[...].astype(F32)
    pad_ref[16 : 16 + center_ref.shape[0], :] = center_ref[...].astype(F32)
    wcat_ref[...] = pad_ref[...].T[:, :32].astype(BF16)
    mixt_ref[...] = mix_ref[...].astype(F32).T.astype(BF16)
    envt_ref[...] = env_ref[...].astype(F32).T.astype(BF16)
    secondt_ref[...] = second_ref[...].astype(F32).T.astype(BF16)
    for part in range(3):
        span = slice(part * ATOMS, (part + 1) * ATOMS)
        updt_ref[:, span] = upd_ref[span, :].astype(F32).T.astype(BF16)
    rocol_ref[...] = jnp.broadcast_to(readout_ref[...], (ATOMS, ATOMS)).T

    atom = lax.broadcasted_iota(jnp.int32, (ATOMS, ATOMS), 0)
    for k in range(NEIGH):
        aim = jnp.broadcast_to(target[k : k + 1, :], (ATOMS, ATOMS)) - atom

        def fill(c, carry, k=k, aim=aim):
            rows = pl.ds(pl.multiple_of(c * ATOMS, ATOMS), ATOMS)
            hit = jnp.where(aim == c * ATOMS, 1.0, 0.0)
            onehot_ref[rows, k * ATOMS : (k + 1) * ATOMS] = hit.astype(BF16)
            return carry

        lax.fori_loop(0, CHUNKS, fill, 0)


def sigmoid(v):
    return 0.5 * jnp.tanh(0.5 * v) + 0.5


def silu_pair(v):
    s = sigmoid(v)
    value = v * s
    return value, s + value * (1.0 - s)


def angular_rows(ux, uy, uz):
    return [
        None, ux, uy, uz, ROOT3 * ux * uy, ROOT3 * uy * uz, 0.5 * (3.0 * uz * uz - 1.0),
        ROOT3 * ux * uz, 0.5 * ROOT3 * (ux * ux - uy * uy),
    ]


def spread_rows(yb_ref, angular):
    for m in range(1, 9):
        for k in range(NEIGH):
            yb_ref[m * NEIGH + k] = jnp.broadcast_to(angular[m][k : k + 1, :], (8, ATOMS))


def basis_parts(r_row):
    row = lax.broadcasted_iota(jnp.int32, (8, ATOMS), 0).astype(F32)
    centers = CUTOFF * (row + 0.5) / 8.0
    r = jnp.broadcast_to(r_row, (8, ATOMS))
    ratio = r * (1.0 / CUTOFF)
    inner = 1.0 - ratio * ratio
    gap = r - centers
    return jnp.exp(-SHARPNESS * gap * gap), gap, inner, ratio


PIECE = (0, 1, 1, 1, 2, 2, 2, 2, 2)


def forward_kernel(
    own_ref, other_ref, code_ref, wcat_ref, mixt_ref, envt_ref, updt_ref,
    table_ref, edge_ref, dsb_ref, dsl_ref, dse_ref, env_ref, v_ref, geo_ref, yb_ref, inv_ref, lat_ref,
):
    target = code_ref[0]
    chunk = target >> 7
    lane = target & 127
    found = [jnp.zeros((NEIGH, ATOMS), F32) for _ in range(4)]
    for c in range(CHUNKS):
        ref = own_ref if c < 9 else other_ref
        hit = chunk == c
        for f in range(4):
            row = jnp.broadcast_to(ref[c % 9, f : f + 1, :], (NEIGH, ATOMS))
            value = jnp.take_along_axis(row, lane, axis=1)
            found[f] = jnp.where(hit, value, found[f])
    d = [
        code_ref[1 + c].astype(F32) + (found[c] - jnp.broadcast_to(own_ref[0, c : c + 1, :], (NEIGH, ATOMS)))
        for c in range(3)
    ]
    r = jnp.sqrt(d[0] * d[0] + d[1] * d[1] + d[2] * d[2])
    ux, uy, uz = d[0] / r, d[1] / r, d[2] / r
    geo_ref[0] = r
    geo_ref[1] = ux
    geo_ref[2] = uy
    geo_ref[3] = uz
    spread_rows(yb_ref, angular_rows(ux, uy, uz))

    kind = lax.broadcasted_iota(jnp.int32, (8, ATOMS), 0).astype(F32)
    center_hot = jnp.where(jnp.broadcast_to(own_ref[0, 3:4, :], (8, ATOMS)) == kind, 1.0, 0.0)
    zero = jnp.zeros((8, ATOMS), F32)
    columns = []
    for k in range(NEIGH):
        bump, gap, inner, ratio = basis_parts(r[k : k + 1, :])
        other_hot = jnp.where(jnp.broadcast_to(found[3][k : k + 1, :], (8, ATOMS)) == kind, 1.0, 0.0)
        columns.append(jnp.concatenate([bump * (inner * inner), other_hot, center_hot, zero], axis=0).astype(BF16))
    for j in range(EDGES // TILE):
        span = slice(j * TILE, (j + 1) * TILE)
        per = TILE // ATOMS
        x = jnp.concatenate(columns[j * per : (j + 1) * per], axis=1)
        act, ds = silu_pair(jnp.dot(wcat_ref[...], x, preferred_element_type=F32))
        dsb_ref[:, span] = ds
        latent, ds = silu_pair(jnp.dot(mixt_ref[...], act.astype(BF16), preferred_element_type=F32))
        dsl_ref[:, span] = ds
        lat_ref[:, span] = latent
        env_ref[:, span] = jnp.dot(envt_ref[...], latent.astype(BF16), preferred_element_type=F32)
    for t in range(8):
        halves = []
        for h in range(2):
            rows = slice(t * 16 + h * 8, t * 16 + h * 8 + 8)
            env = [env_ref[rows, k * ATOMS : (k + 1) * ATOMS] for k in range(NEIGH)]
            field = []
            for m in range(9):
                terms = [env[k] if m == 0 else env[k] * yb_ref[m * NEIGH + k] for k in range(NEIGH)]
                while len(terms) > 1:
                    terms = [terms[i] + terms[i + 1] for i in range(0, len(terms), 2)]
                field.append(terms[0] * 0.125)
                v_ref[m, rows, :] = field[m]
            out = []
            for k in range(NEIGH):
                sums = [field[0], None, None]
                for m in range(1, 9):
                    term = field[m] * yb_ref[m * NEIGH + k]
                    sums[PIECE[m]] = term if sums[PIECE[m]] is None else sums[PIECE[m]] + term
                out.append(sums)
            halves.append(out)
        for k in range(NEIGH):
            for p in range(3):
                both = jnp.concatenate([halves[0][k][p], halves[1][k][p]], axis=0)
                inv_ref[p * ATOMS + t * 16 : p * ATOMS + t * 16 + 16, k * ATOMS : (k + 1) * ATOMS] = both.astype(BF16)
    mean = jnp.zeros((ATOMS, ATOMS), F32)
    for j in range(EDGES // TILE):
        span = slice(j * TILE, (j + 1) * TILE)
        update = jnp.dot(updt_ref[...], inv_ref[:, span], preferred_element_type=F32)
        edge, ds = silu_pair(lat_ref[:, span] + update)
        edge_ref[:, span] = edge
        dse_ref[:, span] = ds
        for i in range(TILE // ATOMS):
            mean = mean + edge[:, i * ATOMS : (i + 1) * ATOMS]
    table_ref[0] = (mean * 0.125).astype(BF16)


def second_kernel(
    own_ref, other_ref, onehot_ref, edge_ref, second_ref, secondt_ref, rocol_ref,
    energy_ref, grad_edge_ref, back_own_ref, back_other_ref, grad_ref,
):
    table = jnp.concatenate([own_ref[c] for c in range(9)] + [other_ref[c] for c in range(9)], axis=1)
    rocol = rocol_ref[...]
    total = jnp.zeros((ATOMS, ATOMS), F32)
    for j in range(EDGES // TILE):
        span = slice(j * TILE, (j + 1) * TILE)
        other = jnp.dot(table, onehot_ref[:, span], preferred_element_type=F32)
        edge = edge_ref[:, span]
        hidden, ds = silu_pair(jnp.dot(secondt_ref[...], (edge * other).astype(BF16), preferred_element_type=F32))
        for i in range(TILE // ATOMS):
            total = total + hidden[:, i * ATOMS : (i + 1) * ATOMS]
        grad_hidden = ds * jnp.concatenate([rocol] * (TILE // ATOMS), axis=1)
        grad_prod = jnp.dot(second_ref[...], grad_hidden.astype(BF16), preferred_element_type=F32)
        grad_prod = grad_prod.astype(BF16).astype(F32)
        grad_edge_ref[:, span] = grad_prod * other
        grad_ref[:, span] = (grad_prod * edge).astype(BF16)
    energy = jnp.sum(total * rocol, axis=0, keepdims=True)
    slots = energy_ref.shape[-1]
    for block in range(2):
        energy_ref[0, 0, block : block + 1, :] = energy[:, block * slots : (block + 1) * slots]
    grad = grad_ref[...]
    for c in range(CHUNKS):
        rows = slice(c * ATOMS, (c + 1) * ATOMS)
        back = lax.dot_general(
            grad, onehot_ref[rows, :], (((1,), (1,)), ((), ())), preferred_element_type=F32
        )
        ref = back_own_ref if c < 9 else back_other_ref
        ref[c % 9] = back.astype(BF16)


def backward_kernel(
    owned_ref, grad_edge_ref, dse_ref, dsl_ref, dsb_ref, env_ref, v_ref, geo_ref, onehot_ref,
    upd_ref, envw_ref, mix_ref, radial_ref,
    own_ref, other_ref, yb_ref, dinv_ref, denv_ref, dlat_ref, part_ref, force_ref,
):
    r, ux, uy, uz = (geo_ref[i] for i in range(4))
    angular = angular_rows(ux, uy, uz)
    spread_rows(yb_ref, angular)
    share = owned_ref[0] * 0.125
    for j in range(EDGES // TILE):
        span = slice(j * TILE, (j + 1) * TILE)
        d_edge = grad_edge_ref[:, span] + jnp.concatenate([share] * (TILE // ATOMS), axis=1)
        d_pre = d_edge * dse_ref[:, span]
        dlat_ref[:, span] = d_pre
        dinv_ref[:, span] = jnp.dot(upd_ref[...], d_pre.astype(BF16), preferred_element_type=F32).astype(BF16)
    part_ref[...] = jnp.zeros(part_ref.shape, F32)
    for t in range(8):
        wide = [
            [
                dinv_ref[p * ATOMS + t * 16 : p * ATOMS + t * 16 + 16, k * ATOMS : (k + 1) * ATOMS].astype(F32)
                for k in range(NEIGH)
            ]
            for p in range(3)
        ]
        halves = []
        for h in range(2):
            rows = slice(t * 16 + h * 8, t * 16 + h * 8 + 8)
            dinv = [[wide[p][k][h * 8 : h * 8 + 8] for k in range(NEIGH)] for p in range(3)]
            env = [env_ref[rows, k * ATOMS : (k + 1) * ATOMS] for k in range(NEIGH)]
            denv = [None] * NEIGH
            for m in range(9):
                down = dinv[PIECE[m]]
                terms = [down[k] if m == 0 else down[k] * yb_ref[m * NEIGH + k] for k in range(NEIGH)]
                while len(terms) > 1:
                    terms = [terms[i] + terms[i + 1] for i in range(0, len(terms), 2)]
                d_field = terms[0] * 0.125
                if m == 0:
                    denv = [d_field] * NEIGH
                    continue
                field = v_ref[m, rows, :]
                for k in range(NEIGH):
                    spot = m * NEIGH + k
                    part_ref[spot] = part_ref[spot] + (down[k] * field + env[k] * d_field)
                    denv[k] = denv[k] + d_field * yb_ref[spot]
            halves.append(denv)
        for k in range(NEIGH):
            both = jnp.concatenate([halves[0][k], halves[1][k]], axis=0)
            denv_ref[t * 16 : t * 16 + 16, k * ATOMS : (k + 1) * ATOMS] = both.astype(BF16)
    d_r_rows = []
    for j in range(EDGES // TILE):
        span = slice(j * TILE, (j + 1) * TILE)
        d_lat = jnp.dot(envw_ref[...], denv_ref[:, span], preferred_element_type=F32).astype(BF16).astype(F32)
        d_mix = (dlat_ref[:, span] + d_lat) * dsl_ref[:, span]
        d_act = jnp.dot(mix_ref[...], d_mix.astype(BF16), preferred_element_type=F32).astype(BF16).astype(F32)
        d_before = (d_act * dsb_ref[:, span]).astype(BF16)
        d_basis = jnp.dot(radial_ref[...], d_before, preferred_element_type=F32).astype(BF16).astype(F32)
        for i in range(TILE // ATOMS):
            k = j * (TILE // ATOMS) + i
            bump, gap, inner, ratio = basis_parts(r[k : k + 1, :])
            slope = bump * inner * (-2.0 * SHARPNESS * gap * inner - (4.0 / CUTOFF) * ratio)
            d_r_rows.append(jnp.sum(slope * d_basis[:, i * ATOMS : (i + 1) * ATOMS], axis=0, keepdims=True))
    d_r = jnp.concatenate(d_r_rows, axis=0)
    dy = [None]
    for m in range(1, 9):
        rows = [jnp.sum(part_ref[m * NEIGH + k], axis=0, keepdims=True) for k in range(NEIGH)]
        dy.append(jnp.concatenate(rows, axis=0))
    d_ux = dy[1] + ROOT3 * (uy * dy[4] + uz * dy[7] + ux * dy[8])
    d_uy = dy[2] + ROOT3 * (ux * dy[4] + uz * dy[5] - uy * dy[8])
    d_uz = dy[3] + ROOT3 * (uy * dy[5] + ux * dy[7]) + 3.0 * uz * dy[6]
    along = ux * d_ux + uy * d_uy + uz * d_uz
    inverse = 1.0 / r
    radial = d_r - along * inverse
    pull = [d_ux * inverse + ux * radial, d_uy * inverse + uy * radial, d_uz * inverse + uz * radial]
    high = [p.astype(BF16).astype(F32) for p in pull]
    low = [p - h for p, h in zip(pull, high)]
    zero = jnp.zeros((1, ATOMS), F32)
    for k in range(NEIGH):
        rows = [h[k : k + 1, :] for h in high] + [zero] * 5 + [q[k : k + 1, :] for q in low] + [zero] * 5
        force_ref[:, k * ATOMS : (k + 1) * ATOMS] = jnp.concatenate(rows, axis=0).astype(BF16)
    force = force_ref[...]
    center = jnp.concatenate([jnp.sum(p, axis=0, keepdims=True) for p in pull] + [zero] * 5, axis=0)
    for c in range(CHUNKS):
        rows = slice(c * ATOMS, (c + 1) * ATOMS)
        back = lax.dot_general(
            force, onehot_ref[rows, :], (((1,), (1,)), ((), ())), preferred_element_type=F32
        )
        moved = back[:8] + back[8:]
        if c == 0:
            moved = moved - center
        ref = own_ref if c < 9 else other_ref
        ref[c % 9] = moved


def finish_kernel(own_ref, out_ref):
    slots = out_ref.shape[-1] // 3
    for block in range(2):
        for c in range(3):
            out_ref[0, 0, block : block + 1, c * slots : (c + 1) * slots] = -own_ref[
                0, c : c + 1, block * slots : (block + 1) * slots
            ]


def call(kernel, outs, scratch=(), name=None, limit=24 << 20):
    whole = pl.BlockSpec(memory_space=pltpu.VMEM)
    shapes = [jax.ShapeDtypeStruct(shape, kind) for shape, kind in outs]

    def run(*args):
        return pl.pallas_call(
            kernel,
            out_shape=shapes,
            in_specs=[whole] * len(args),
            out_specs=[whole] * len(shapes),
            scratch_shapes=list(scratch),
            compiler_params=pltpu.CompilerParams(vmem_limit_bytes=limit),
            name=name,
        )(*args)

    return run


def on_device(
    positions, species, neighbors, center_table, neighbor_table, radial_weight, mix_weight,
    env_weight, update_weight, second_weight, readout,
):
    slots = species.shape[-1]
    edges = (ATOMS, EDGES)
    square = (ATOMS, ATOMS)
    (packed,) = call(pack_kernel, [((1, 8, ATOMS), F32)], name="pack")(positions, species)
    code, onehot, wcat, mixt, envt, updt, secondt, rocol = call(
        prep_kernel,
        [
            ((4, NEIGH, ATOMS), jnp.int32), ((CHUNKS * ATOMS, EDGES), BF16), ((ATOMS, 32), BF16), (square, BF16),
            (square, BF16), ((ATOMS, 3 * ATOMS), BF16), (square, BF16), (square, F32),
        ],
        [pltpu.VMEM(square, F32)],
        name="prep",
    )(
        neighbors, center_table, neighbor_table, radial_weight, mix_weight, env_weight, update_weight,
        second_weight, readout.reshape(1, ATOMS),
    )
    near, far = gather_halo(packed)
    table, edge, dsb, dsl, dse, env, field, geo = call(
        forward_kernel,
        [
            ((1,) + square, BF16), (edges, F32), (edges, F32), (edges, F32), (edges, F32), (edges, F32),
            ((9,) + square, F32), ((4, NEIGH, ATOMS), F32),
        ],
        [pltpu.VMEM((72, 8, ATOMS), F32), pltpu.VMEM((3 * ATOMS, EDGES), BF16), pltpu.VMEM(edges, F32)],
        name="forward",
    )(near, far, code, wcat, mixt, envt, updt)
    near, far = gather_halo(table)
    energy, grad_edge, back_own, back_other = call(
        second_kernel,
        [((1, 1, 2, slots), F32), (edges, F32), ((9,) + square, BF16), ((9,) + square, BF16)],
        [pltpu.VMEM(edges, BF16)],
        name="second",
    )(near, far, onehot, edge, second_weight, secondt, rocol)
    owned = reduce_halo(back_own, back_other)
    own, other = call(
        backward_kernel,
        [((9, 8, ATOMS), F32), ((9, 8, ATOMS), F32)],
        [
            pltpu.VMEM((72, 8, ATOMS), F32), pltpu.VMEM((3 * ATOMS, EDGES), BF16), pltpu.VMEM(edges, BF16),
            pltpu.VMEM(edges, F32), pltpu.VMEM((72, 8, ATOMS), F32), pltpu.VMEM((16, EDGES), BF16),
        ],
        name="backward",
    )(
        owned, grad_edge, dse, dsl, dsb, env, field, geo, onehot, update_weight, env_weight, mix_weight,
        radial_weight,
    )
    motion = reduce_halo(own, other)
    (forces,) = call(finish_kernel, [((1, 1, 2, 3 * slots), F32)], name="finish")(motion)
    return energy, forces


def solution(mesh):
    split = P("gx", "gy", "gz", None)
    return jax.shard_map(
        on_device,
        mesh=mesh,
        in_specs=(split, split, split) + (P(),) * 8,
        out_specs=(split, split),
        check_vma=False,
    )
```

time: 174 us -> 81.9 us (0.47)
  other arithmetic: 27.5 us -> 0.17 us
  local copies, waits for them, and re-layouts: 33.8 us -> 8.78 us
  waiting for transfers between devices: 61.8 us -> 38.1 us
  matrix products: 18.8 us -> 0 us
  Pallas kernels: 0 us -> 12 us
  starting transfers between devices: 29.4 us -> 21.5 us
    ppermute x24 -> x20, waiting for transfers between devices: 61.8 us -> 38.1 us  [shifted(): lax.ppermute(value, axis, [(i, (i + step) % count) for i in range(count)])]
    dot_general x23 -> x0, matrix products: 18.8 us -> none  [the longest x3 5.87 us: layer_one(): jnp.einsum('akc,mak->amc', env_terms, harmonic_grid, precision=HIGH) / NEIGH]
    scatter-add x3 -> x0, other arithmetic: 14.5 us -> none  [the longest x1 6.58 us: on_device(): jnp.zeros((padded_count, channels), jnp.float32).at[other_flat]]
    gather x6 -> x0, local copies, waits for them, and re-layouts: 13.1 us -> none  [the longest x1 6.15 us: on_device(): onehot_other = one_hot(ghost_species[other_flat], spec_count)]
    pallas_call x0 -> x6, Pallas kernels: none -> 12 us  [run(): pl.pallas_call(kernel, out_shape=shapes, in_specs=[whole] * len(args), ou...]
    ppermute x24 -> x20, starting transfers between devices: 29.4 us -> 21.5 us  [shifted(): lax.ppermute(value, axis, [(i, (i + step) % count) for i in range(count)])]
    reshape x10 -> x0, local copies, waits for them, and re-layouts: 4.11 us -> none  [the longest x2 1.55 us: on_device(): codes = neighbors.reshape(cells_x, cells_y, cells_z, slot_count, NEIGH)]
    concatenate x6 -> x1, other arithmetic: 3.83 us -> 0.01 us  [gather_halo(): chunk = jnp.concatenate([chunk, lower, upper], axis=0)]
  transfers between devices with their start and end apart: 24 -> 20, of which waited for: 16 -> 17; matrix products, arithmetic and copies ran while one was open for 5% -> 0% of each run, Pallas kernels for 0% -> 2%
where the time goes in v1:
time: 81.9 us; the launch traced here: 81.4 us
  waiting for transfers between devices  38.1 us (47%)
  starting transfers between devices  21.5 us (26%)
  Pallas kernels  12 us (15%)
  local copies, waits for them, and re-layouts  8.78 us (11%)
  between operations  0.84 us (1%)
    ppermute x20, waiting for transfers between devices, shifted(): lax.ppermute(value, axis, [(i, (i + step) % count) for i in range(count)])  38.1 us
    ppermute x20, starting transfers between devices, shifted(): lax.ppermute(value, axis, [(i, (i + step) % count) for i in range(count)])  21.5 us
    pallas_call x6, Pallas kernels, run(): pl.pallas_call(kernel, out_shape=shapes, in_specs=[whole] * len(args), ou...  12 us
    unnamed x39, local copies, waits for them, and re-layouts  8.71 us
  transfers between devices with their start and end apart: 20, of which 17 were waited for; matrix products, arithmetic and copies ran while one was open for 0% of the time, Pallas kernels for 2%

profile of v1, /device:TPU:0, one launch (start us, length us, event | category | flops | bytes accessed | tf_op | source)
XLA Modules:
  0.0 81.4 jit_solution(2137155412208726460)
XLA Ops:
  2.1 5.0 %collective-permute-start.1 = (f32[1,8,128]{2,1,0:T(8,128)S(1)}, f32[1,8,128]{2,1,0:T(8,128)S(1)}, u32[]{:S(2)}, u32[]{:S(2)}) collective-permute-start(f32[1,8,128]{2,1,0:T(8,128)S(1)} %pack.1), channel_id=1, source_target_pairs={{0,24},{8,0},{16,8},{24,16},{1,25},{9,1},{17,9},{25,17},{2,26},{10... | collective-permute-start | bytes 12296 | tf_op jit(solution)/shard_map/ppermute | solution.py:25
  8.4 4.1 %collective-permute-done = f32[1,8,128]{2,1,0:T(8,128)S(1)} collective-permute-done((f32[1,8,128]{2,1,0:T(8,128)S(1)}, f32[1,8,128]{2,1,0:T(8,128)S(1)}, u32[]{:S(2)}, u32[]{:S(2)}) %collective-permute-start) | collective-permute-done | bytes 4128 | tf_op jit(solution)/shard_map/ppermute | solution.py:25
  12.5 2.4 %collective-permute-start.3 = (f32[3,8,128]{2,1,0:T(8,128)S(1)}, f32[3,8,128]{2,1,0:T(8,128)S(1)}, u32[]{:S(2)}, u32[]{:S(2)}) collective-permute-start(f32[3,8,128]{2,1,0:T(8,128)S(1)} %pad_maximum_fusion), channel_id=1, source_target_pairs={{0,6},{2,0},{4,2},{6,4},{1,7},{3,1},{5,3},{7,5},{8,14},{10,8},{12,... | collective-permute-start | bytes 36872 | tf_op jit(solution)/shard_map/ppermute | solution.py:25
  15.0 4.6 %collective-permute-done.2 = f32[3,8,128]{2,1,0:T(8,128)S(1)} collective-permute-done((f32[3,8,128]{2,1,0:T(8,128)S(1)}, f32[3,8,128]{2,1,0:T(8,128)S(1)}, u32[]{:S(2)}, u32[]{:S(2)}) %collective-permute-start.2) | collective-permute-done | bytes 12320 | tf_op jit(solution)/shard_map/ppermute | solution.py:25
  26.2 1.8 %prep.1 = (s32[4,8,128]{2,1,0:T(8,128)S(1)}, bf16[2304,1024]{1,0:T(8,128)(2,1)S(1)}, bf16[128,32]{1,0:T(8,128)(2,1)S(1)}, bf16[128,128]{1,0:T(8,128)(2,1)S(1)}, ...) custom-call(s32[1,1,2,512]{3,2,1,0:T(2,128)S(1)} %copy-done.10, ...), custom_call_target="tpu_custom_call" | custom-call | tf_op jit(solution)/shard_map/prep/pallas_call | solution.py:390
  28.0 2.3 %forward.1 = (bf16[1,128,128]{2,1,0:T(8,128)(2,1)S(1)}, f32[128,1024]{1,0:T(8,128)S(1)}, f32[128,1024]{1,0:T(8,128)S(1)}, f32[128,1024]{1,0:T(8,128)S(1)}, f32[1...) custom-call(f32[9,8,128]{2,1,0:T(8,128)S(1)} %constant_dynamic-update-slice, ...), custom_call_target="tpu_custom_call" | custom-call | tf_op jit(solution)/shard_map/forward/pallas_call | solution.py:390
  30.4 2.0 %collective-permute-start.5 = (bf16[1,128,128]{2,1,0:T(8,128)(2,1)S(1)}, bf16[1,128,128]{2,1,0:T(8,128)(2,1)S(1)}, u32[]{:S(2)}, u32[]{:S(2)}) collective-permute-start(bf16[1,128,128]{2,1,0:T(8,128)(2,1)S(1)} %get-tuple-element.29), channel_id=1, source_target_pairs={{0,8},{8,16},{16,24},{24,0},{1,9},{9,17},{17,25},{25,1},{2,10},{10... | collective-permute-start | bytes 98312 | tf_op jit(solution)/shard_map/ppermute | solution.py:25
  32.4 3.7 %collective-permute-done.5 = bf16[1,128,128]{2,1,0:T(8,128)(2,1)S(1)} collective-permute-done((bf16[1,128,128]{2,1,0:T(8,128)(2,1)S(1)}, bf16[1,128,128]{2,1,0:T(8,128)(2,1)S(1)}, u32[]{:S(2)}, u32[]{:S(2)}) %collective-permute-start.5) | collective-permute-done | bytes 32800 | tf_op jit(solution)/shard_map/ppermute | solution.py:25
  36.2 2.9 %collective-permute-start.8 = (bf16[3,128,128]{2,1,0:T(8,128)(2,1)S(1)}, bf16[3,128,128]{2,1,0:T(8,128)(2,1)S(1)}, u32[]{:S(2)}, u32[]{:S(2)}) collective-permute-start(bf16[3,128,128]{2,1,0:T(8,128)(2,1)S(1)} %get-tuple-element.56), channel_id=1, source_target_pairs={{0,6},{2,0},{4,2},{6,4},{1,7},{3,1},{5,3},{7,5},{8,14},{10,8},{12,... | collective-permute-start | bytes 294920 | tf_op jit(solution)/shard_map/ppermute | solution.py:25
  39.2 3.1 %collective-permute-done.7 = bf16[3,128,128]{2,1,0:T(8,128)(2,1)S(1)} collective-permute-done((bf16[3,128,128]{2,1,0:T(8,128)(2,1)S(1)}, bf16[3,128,128]{2,1,0:T(8,128)(2,1)S(1)}, u32[]{:S(2)}, u32[]{:S(2)}) %collective-permute-start.7) | collective-permute-done | bytes 98336 | tf_op jit(solution)/shard_map/ppermute | solution.py:25
  42.4 1.6 %collective-permute-done.9.other_ref = bf16[9,128,128]{2,1,0:T(8,128)(2,1)S(1)} collective-permute-done((bf16[9,128,128]{2,1,0:T(8,128)(2,1)S(1)}, bf16[9,128,128]{2,1,0:T(8,128)(2,1)S(1)}, u32[]{:S(2)}, u32[]{:S(2)}) %collective-permute-start.9) | collective-permute-done | bytes 294944 | tf_op jit(solution)/shard_map/ppermute | solution.py:25
  44.8 3.6 %second.1 = (f32[1,1,2,64]{3,2,1,0:T(2,128)}, f32[128,1024]{1,0:T(8,128)S(1)}, bf16[9,128,128]{2,1,0:T(8,128)(2,1)S(1)}, bf16[9,128,128]{2,1,0:T(8,128)(2,1)S(1)}) custom-call(bf16[9,128,128]{2,1,0:T(8,128)(2,1)S(1)} %constant_dynamic-update-slice_fusion.8.own_ref, bf16[9,128,128]{2,1,0:T(8,128)(2,1)S(1)} %collective-permute-done.9.other_ref, ...), custom_call_target="tpu_custom_call" | custom-call | tf_op jit(solution)/shard_map/second/pallas_call | solution.py:390
  48.6 1.4 %collective-permute-done.10 = bf16[9,128,128]{2,1,0:T(8,128)(2,1)S(1)} collective-permute-done((bf16[9,128,128]{2,1,0:T(8,128)(2,1)S(1)}, bf16[9,128,128]{2,1,0:T(8,128)(2,1)S(1)}, u32[]{:S(2)}, u32[]{:S(2)}) %collective-permute-start.10) | collective-permute-done | bytes 294944 | tf_op jit(solution)/shard_map/ppermute | solution.py:25
  50.2 2.4 %collective-permute-start.11 = (bf16[3,128,128]{2,1,0:T(8,128)(2,1)S(1)}, bf16[3,128,128]{2,1,0:T(8,128)(2,1)S(1)}, u32[]{:S(2)}, u32[]{:S(2)}) collective-permute-start(bf16[3,128,128]{2,1,0:T(8,128)(2,1)S(1)} %get-tuple-element.50), channel_id=1, source_target_pairs={{0,6},{2,0},{4,2},{6,4},{1,7},{3,1},{5,3},{7,5},{8,14},{10,8},{12,... | collective-permute-start | bytes 294920 | tf_op jit(solution)/shard_map/ppermute | solution.py:25
  52.6 3.2 %collective-permute-done.11 = bf16[3,128,128]{2,1,0:T(8,128)(2,1)S(1)} collective-permute-done((bf16[3,128,128]{2,1,0:T(8,128)(2,1)S(1)}, bf16[3,128,128]{2,1,0:T(8,128)(2,1)S(1)}, u32[]{:S(2)}, u32[]{:S(2)}) %collective-permute-start.11) | collective-permute-done | bytes 98336 | tf_op jit(solution)/shard_map/ppermute | solution.py:25
  55.7 2.4 %collective-permute-done.12 = bf16[3,128,128]{2,1,0:T(8,128)(2,1)S(1)} collective-permute-done((bf16[3,128,128]{2,1,0:T(8,128)(2,1)S(1)}, bf16[3,128,128]{2,1,0:T(8,128)(2,1)S(1)}, u32[]{:S(2)}, u32[]{:S(2)}) %collective-permute-start.12) | collective-permute-done | bytes 98336 | tf_op jit(solution)/shard_map/ppermute | solution.py:25
  60.3 1.9 %collective-permute-done.13 = bf16[1,128,128]{2,1,0:T(8,128)(2,1)S(1)} collective-permute-done((bf16[1,128,128]{2,1,0:T(8,128)(2,1)S(1)}, bf16[1,128,128]{2,1,0:T(8,128)(2,1)S(1)}, u32[]{:S(2)}, u32[]{:S(2)}) %collective-permute-start.13) | collective-permute-done | bytes 32800 | tf_op jit(solution)/shard_map/ppermute | solution.py:25
  62.2 2.4 %collective-permute-done.14 = bf16[1,128,128]{2,1,0:T(8,128)(2,1)S(1)} collective-permute-done((bf16[1,128,128]{2,1,0:T(8,128)(2,1)S(1)}, bf16[1,128,128]{2,1,0:T(8,128)(2,1)S(1)}, u32[]{:S(2)}, u32[]{:S(2)}) %collective-permute-start.14) | collective-permute-done | bytes 32800 | tf_op jit(solution)/shard_map/ppermute | solution.py:25
  64.6 3.6 %backward.1 = (f32[9,8,128]{2,1,0:T(8,128)S(1)}, f32[9,8,128]{2,1,0:T(8,128)S(1)}) custom-call(f32[1,128,128]{2,1,0:T(8,128)S(1)} %fusion.1.owned_ref, f32[128,1024]{1,0:T(8,128)S(1)} %get-tuple-element.37.grad_edge_ref, f32[128,1024]{1,0:T(8,128)S(1)} %get-tuple-element.38.dse_ref, f32[128,1024]{1,0:T(8,128)S(1)} %get-tuple-element.39.dsl_ref, ...), custom_call_target="tpu_custom_call" | custom-call | tf_op jit(solution)/shard_map/backward/pallas_call | solution.py:390
  71.6 1.7 %collective-permute-done.16 = f32[3,8,128]{2,1,0:T(8,128)S(1)} collective-permute-done((f32[3,8,128]{2,1,0:T(8,128)S(1)}, f32[3,8,128]{2,1,0:T(8,128)S(1)}, u32[]{:S(2)}, u32[]{:S(2)}) %collective-permute-start.16) | collective-permute-done | bytes 12320 | tf_op jit(solution)/shard_map/ppermute | solution.py:25
  73.2 1.7 %collective-permute-done.17 = f32[3,8,128]{2,1,0:T(8,128)S(1)} collective-permute-done((f32[3,8,128]{2,1,0:T(8,128)S(1)}, f32[3,8,128]{2,1,0:T(8,128)S(1)}, u32[]{:S(2)}, u32[]{:S(2)}) %collective-permute-start.17) | collective-permute-done | bytes 12320 | tf_op jit(solution)/shard_map/ppermute | solution.py:25
  75.3 1.7 %collective-permute-start.19 = (f32[1,8,128]{2,1,0:T(8,128)S(1)}, f32[1,8,128]{2,1,0:T(8,128)S(1)}, u32[]{:S(2)}, u32[]{:S(2)}) collective-permute-start(f32[1,8,128]{2,1,0:T(8,128)S(1)} %get-tuple-element.63), channel_id=1, source_target_pairs={{0,8},{8,16},{16,24},{24,0},{1,9},{9,17},{17,25},{25,1},{2,10},{10... | collective-permute-start | bytes 12296 | tf_op jit(solution)/shard_map/ppermute | solution.py:25
  77.0 1.6 %collective-permute-done.18 = f32[1,8,128]{2,1,0:T(8,128)S(1)} collective-permute-done((f32[1,8,128]{2,1,0:T(8,128)S(1)}, f32[1,8,128]{2,1,0:T(8,128)S(1)}, u32[]{:S(2)}, u32[]{:S(2)}) %collective-permute-start.18) | collective-permute-done | bytes 4128 | tf_op jit(solution)/shard_map/ppermute | solution.py:25
  78.6 2.1 %collective-permute-done.19 = f32[1,8,128]{2,1,0:T(8,128)S(1)} collective-permute-done((f32[1,8,128]{2,1,0:T(8,128)S(1)}, f32[1,8,128]{2,1,0:T(8,128)S(1)}, u32[]{:S(2)}, u32[]{:S(2)}) %collective-permute-start.19) | collective-permute-done | bytes 4128 | tf_op jit(solution)/shard_map/ppermute | solution.py:25
  (75 shorter events, 17.3 us)
Async XLA Ops:
  2.1 6.4 %collective-permute-start.1 = (f32[1,8,128]{2,1,0:T(8,128)S(1)}, f32[1,8,128]{2,1,0:T(8,128)S(1)}, u32[]{:S(2)}, u32[]{:S(2)}) collective-permute-start(f32[1,8,128]{2,1,0:T(8,128)S(1)} %pack.1), channel_id=1, source_target_pairs={{0,24},{8,0},{16,8},{24,16},{1,25},{9,1},{17,9},{25,17},{2,26},{10... | collective-permute-start | bytes 12296 | tf_op jit(solution)/shard_map/ppermute | solution.py:25
  7.1 5.4 %collective-permute-start = (f32[1,8,128]{2,1,0:T(8,128)S(1)}, f32[1,8,128]{2,1,0:T(8,128)S(1)}, u32[]{:S(2)}, u32[]{:S(2)}) collective-permute-start(f32[1,8,128]{2,1,0:T(8,128)S(1)} %pack.1), channel_id=1, source_target_pairs={{0,8},{8,16},{16,24},{24,0},{1,9},{9,17},{17,25},{25,1},{2,10},{10... | collective-permute-start | bytes 12296 | tf_op jit(solution)/shard_map/ppermute | solution.py:25
  12.5 7.0 %collective-permute-start.3 = (f32[3,8,128]{2,1,0:T(8,128)S(1)}, f32[3,8,128]{2,1,0:T(8,128)S(1)}, u32[]{:S(2)}, u32[]{:S(2)}) collective-permute-start(f32[3,8,128]{2,1,0:T(8,128)S(1)} %pad_maximum_fusion), channel_id=1, source_target_pairs={{0,6},{2,0},{4,2},{6,4},{1,7},{3,1},{5,3},{7,5},{8,14},{10,8},{12,... | collective-permute-start | bytes 36872 | tf_op jit(solution)/shard_map/ppermute | solution.py:25
  15.0 4.6 %collective-permute-start.2 = (f32[3,8,128]{2,1,0:T(8,128)S(1)}, f32[3,8,128]{2,1,0:T(8,128)S(1)}, u32[]{:S(2)}, u32[]{:S(2)}) collective-permute-start(f32[3,8,128]{2,1,0:T(8,128)S(1)} %pad_maximum_fusion), channel_id=1, source_target_pairs={{0,2},{2,4},{4,6},{6,0},{1,3},{3,5},{5,7},{7,1},{8,10},{10,12},{12... | collective-permute-start | bytes 36872 | tf_op jit(solution)/shard_map/ppermute | solution.py:25
  19.6 8.4 %collective-permute-start.4 = (f32[9,8,128]{2,1,0:T(8,128)S(1)}, f32[9,8,128]{2,1,0:T(8,128)S(1)}, u32[]{:S(2)}, u32[]{:S(2)}) collective-permute-start(f32[9,8,128]{2,1,0:T(8,128)S(1)} %constant_dynamic-update-slice_fusion.own_ref), channel_id=1, source_target_pairs={{0,1},{1,0},{2,3},{3,2},{4,5},{5,4},{6,7},{7,6},{8,9},{9,8},{10,11... | collective-permute-start | bytes 110600 | tf_op jit(solution)/shard_map/ppermute | solution.py:25
  30.3 5.9 %collective-permute-start.6 = (bf16[1,128,128]{2,1,0:T(8,128)(2,1)S(1)}, bf16[1,128,128]{2,1,0:T(8,128)(2,1)S(1)}, u32[]{:S(2)}, u32[]{:S(2)}) collective-permute-start(bf16[1,128,128]{2,1,0:T(8,128)(2,1)S(1)} %get-tuple-element.29), channel_id=1, source_target_pairs={{0,24},{8,0},{16,8},{24,16},{1,25},{9,1},{17,9},{25,17},{2,26},{10... | collective-permute-start | bytes 98312 | tf_op jit(solution)/shard_map/ppermute | solution.py:25
  30.4 5.8 %collective-permute-start.5 = (bf16[1,128,128]{2,1,0:T(8,128)(2,1)S(1)}, bf16[1,128,128]{2,1,0:T(8,128)(2,1)S(1)}, u32[]{:S(2)}, u32[]{:S(2)}) collective-permute-start(bf16[1,128,128]{2,1,0:T(8,128)(2,1)S(1)} %get-tuple-element.29), channel_id=1, source_target_pairs={{0,8},{8,16},{16,24},{24,0},{1,9},{9,17},{17,25},{25,1},{2,10},{10... | collective-permute-start | bytes 98312 | tf_op jit(solution)/shard_map/ppermute | solution.py:25
  36.1 28.5 %copy-start.1 = (bf16[384,128]{1,0:T(8,128)(2,1)S(1)}, bf16[384,128]{1,0:T(8,128)(2,1)}, u32[]{:S(2)}) copy-start(bf16[384,128]{1,0:T(8,128)(2,1)} %upd_ref.3) | copy-start | bytes 294916
  36.1 28.5 %copy-start.5 = (bf16[128,128]{1,0:T(8,128)(2,1)S(1)}, bf16[128,128]{1,0:T(8,128)(2,1)}, u32[]{:S(2)}) copy-start(bf16[128,128]{1,0:T(8,128)(2,1)} %mix_ref.3) | copy-start | bytes 98308
  36.1 28.5 %copy-start.7 = (bf16[128,128]{1,0:T(8,128)(2,1)S(1)}, bf16[128,128]{1,0:T(8,128)(2,1)}, u32[]{:S(2)}) copy-start(bf16[128,128]{1,0:T(8,128)(2,1)} %envw_ref.1) | copy-start | bytes 98308
  36.1 28.5 %copy-start.9 = (bf16[8,128]{1,0:T(8,128)(2,1)S(1)}, bf16[8,128]{1,0:T(8,128)(2,1)}, u32[]{:S(2)}) copy-start(bf16[8,128]{1,0:T(8,128)(2,1)} %radial_ref.3) | copy-start | bytes 6148
  36.2 6.0 %collective-permute-start.7 = (bf16[3,128,128]{2,1,0:T(8,128)(2,1)S(1)}, bf16[3,128,128]{2,1,0:T(8,128)(2,1)S(1)}, u32[]{:S(2)}, u32[]{:S(2)}) collective-permute-start(bf16[3,128,128]{2,1,0:T(8,128)(2,1)S(1)} %get-tuple-element.56), channel_id=1, source_target_pairs={{0,2},{2,4},{4,6},{6,0},{1,3},{3,5},{5,7},{7,1},{8,10},{10,12},{12... | collective-permute-start | bytes 294920 | tf_op jit(solution)/shard_map/ppermute | solution.py:25
  36.2 6.1 %collective-permute-start.8 = (bf16[3,128,128]{2,1,0:T(8,128)(2,1)S(1)}, bf16[3,128,128]{2,1,0:T(8,128)(2,1)S(1)}, u32[]{:S(2)}, u32[]{:S(2)}) collective-permute-start(bf16[3,128,128]{2,1,0:T(8,128)(2,1)S(1)} %get-tuple-element.56), channel_id=1, source_target_pairs={{0,6},{2,0},{4,2},{6,4},{1,7},{3,1},{5,3},{7,5},{8,14},{10,8},{12,... | collective-permute-start | bytes 294920 | tf_op jit(solution)/shard_map/ppermute | solution.py:25
  42.3 1.6 %collective-permute-start.9 = (bf16[9,128,128]{2,1,0:T(8,128)(2,1)S(1)}, bf16[9,128,128]{2,1,0:T(8,128)(2,1)S(1)}, u32[]{:S(2)}, u32[]{:S(2)}) collective-permute-start(bf16[9,128,128]{2,1,0:T(8,128)(2,1)S(1)} %constant_dynamic-update-slice_fusion.8.own_ref), channel_id=1, source_target_pairs={{0,1},{1,0},{2,3},{3,2},{4,5},{5,4},{6,7},{7,6},{8,9},{9,8},{10,11... | collective-permute-start | bytes 884744 | tf_op jit(solution)/shard_map/ppermute | solution.py:25
  48.4 1.6 %collective-permute-start.10 = (bf16[9,128,128]{2,1,0:T(8,128)(2,1)S(1)}, bf16[9,128,128]{2,1,0:T(8,128)(2,1)S(1)}, u32[]{:S(2)}, u32[]{:S(2)}) collective-permute-start(bf16[9,128,128]{2,1,0:T(8,128)(2,1)S(1)} %get-tuple-element.36), channel_id=1, source_target_pairs={{0,1},{1,0},{2,3},{3,2},{4,5},{5,4},{6,7},{7,6},{8,9},{9,8},{10,11... | collective-permute-start | bytes 884744 | tf_op jit(solution)/shard_map/ppermute | solution.py:25
  50.2 5.6 %collective-permute-start.11 = (bf16[3,128,128]{2,1,0:T(8,128)(2,1)S(1)}, bf16[3,128,128]{2,1,0:T(8,128)(2,1)S(1)}, u32[]{:S(2)}, u32[]{:S(2)}) collective-permute-start(bf16[3,128,128]{2,1,0:T(8,128)(2,1)S(1)} %get-tuple-element.50), channel_id=1, source_target_pairs={{0,6},{2,0},{4,2},{6,4},{1,7},{3,1},{5,3},{7,5},{8,14},{10,8},{12,... | collective-permute-start | bytes 294920 | tf_op jit(solution)/shard_map/ppermute | solution.py:25
  52.6 5.6 %collective-permute-start.12 = (bf16[3,128,128]{2,1,0:T(8,128)(2,1)S(1)}, bf16[3,128,128]{2,1,0:T(8,128)(2,1)S(1)}, u32[]{:S(2)}, u32[]{:S(2)}) collective-permute-start(bf16[3,128,128]{2,1,0:T(8,128)(2,1)S(1)} %get-tuple-element.51), channel_id=1, source_target_pairs={{0,2},{2,4},{4,6},{6,0},{1,3},{3,5},{5,7},{7,1},{8,10},{10,12},{12... | collective-permute-start | bytes 294920 | tf_op jit(solution)/shard_map/ppermute | solution.py:25
  58.2 4.0 %collective-permute-start.13 = (bf16[1,128,128]{2,1,0:T(8,128)(2,1)S(1)}, bf16[1,128,128]{2,1,0:T(8,128)(2,1)S(1)}, u32[]{:S(2)}, u32[]{:S(2)}) collective-permute-start(bf16[1,128,128]{2,1,0:T(8,128)(2,1)S(1)} %get-tuple-element.52), channel_id=1, source_target_pairs={{0,24},{8,0},{16,8},{24,16},{1,25},{9,1},{17,9},{25,17},{2,26},{10... | collective-permute-start | bytes 98312 | tf_op jit(solution)/shard_map/ppermute | solution.py:25
  58.9 5.7 %collective-permute-start.14 = (bf16[1,128,128]{2,1,0:T(8,128)(2,1)S(1)}, bf16[1,128,128]{2,1,0:T(8,128)(2,1)S(1)}, u32[]{:S(2)}, u32[]{:S(2)}) collective-permute-start(bf16[1,128,128]{2,1,0:T(8,128)(2,1)S(1)} %get-tuple-element.53), channel_id=1, source_target_pairs={{0,8},{8,16},{16,24},{24,0},{1,9},{9,17},{17,25},{25,1},{2,10},{10... | collective-permute-start | bytes 98312 | tf_op jit(solution)/shard_map/ppermute | solution.py:25
  68.2 1.2 %collective-permute-start.15 = (f32[9,8,128]{2,1,0:T(8,128)S(1)}, f32[9,8,128]{2,1,0:T(8,128)S(1)}, u32[]{:S(2)}, u32[]{:S(2)}) collective-permute-start(f32[9,8,128]{2,1,0:T(8,128)S(1)} %get-tuple-element.45), channel_id=1, source_target_pairs={{0,1},{1,0},{2,3},{3,2},{4,5},{5,4},{6,7},{7,6},{8,9},{9,8},{10,11... | collective-permute-start | bytes 110600 | tf_op jit(solution)/shard_map/ppermute | solution.py:25
  69.5 3.7 %collective-permute-start.16 = (f32[3,8,128]{2,1,0:T(8,128)S(1)}, f32[3,8,128]{2,1,0:T(8,128)S(1)}, u32[]{:S(2)}, u32[]{:S(2)}) collective-permute-start(f32[3,8,128]{2,1,0:T(8,128)S(1)} %get-tuple-element.54), channel_id=1, source_target_pairs={{0,6},{2,0},{4,2},{6,4},{1,7},{3,1},{5,3},{7,5},{8,14},{10,8},{12,... | collective-permute-start | bytes 36872 | tf_op jit(solution)/shard_map/ppermute | solution.py:25
  70.4 4.6 %collective-permute-start.17 = (f32[3,8,128]{2,1,0:T(8,128)S(1)}, f32[3,8,128]{2,1,0:T(8,128)S(1)}, u32[]{:S(2)}, u32[]{:S(2)}) collective-permute-start(f32[3,8,128]{2,1,0:T(8,128)S(1)} %get-tuple-element.55), channel_id=1, source_target_pairs={{0,2},{2,4},{4,6},{6,0},{1,3},{3,5},{5,7},{7,1},{8,10},{10,12},{12... | collective-permute-start | bytes 36872 | tf_op jit(solution)/shard_map/ppermute | solution.py:25
  75.0 3.6 %collective-permute-start.18 = (f32[1,8,128]{2,1,0:T(8,128)S(1)}, f32[1,8,128]{2,1,0:T(8,128)S(1)}, u32[]{:S(2)}, u32[]{:S(2)}) collective-permute-start(f32[1,8,128]{2,1,0:T(8,128)S(1)} %get-tuple-element.62), channel_id=1, source_target_pairs={{0,24},{8,0},{16,8},{24,16},{1,25},{9,1},{17,9},{25,17},{2,26},{10... | collective-permute-start | bytes 12296 | tf_op jit(solution)/shard_map/ppermute | solution.py:25
  75.3 5.4 %collective-permute-start.19 = (f32[1,8,128]{2,1,0:T(8,128)S(1)}, f32[1,8,128]{2,1,0:T(8,128)S(1)}, u32[]{:S(2)}, u32[]{:S(2)}) collective-permute-start(f32[1,8,128]{2,1,0:T(8,128)S(1)} %get-tuple-element.63), channel_id=1, source_target_pairs={{0,8},{8,16},{16,24},{24,0},{1,9},{9,17},{17,25},{25,1},{2,10},{10... | collective-permute-start | bytes 12296 | tf_op jit(solution)/shard_map/ppermute | solution.py:25
  (12 other events, 8.7 us)

commit v2 on v1

--- a/solution.py
+++ b/solution.py
@@ -20,25 +20,69 @@
 TILE = 256
 
 
+ROUTES = (((1, 0), (0, 2), (1, 2), (2, 1)), ((2, 0), (0, 1), (1, 1), (2, 2)))
+
+
+def is_paired():
+    return lax.axis_size("gz") == 2 and all(
+        lax.axis_size(axis) % 2 == 0 and lax.axis_size(axis) >= 4 for axis in ("gx", "gy")
+    )
+
+
 def shifted(value, axis, step):
     count = lax.axis_size(axis)
     return lax.ppermute(value, axis, [(i, (i + step) % count) for i in range(count)])
 
 
-def gather_halo(chunk):
+def partner(index, way, count):
+    if way == 0:
+        return index
+    if way == 1:
+        return index ^ 1
+    return (index + 1 if index % 2 else index - 1) % count
+
+
+def swapped(value, slot):
+    count_x, count_y = lax.axis_size("gx"), lax.axis_size("gy")
+    pairs = []
+    for x in range(count_x):
+        for y in range(count_y):
+            for core in range(2):
+                way_x, way_y = ROUTES[core][slot]
+                to_x, to_y = partner(x, way_x, count_x), partner(y, way_y, count_y)
+                pairs.append(((x * count_y + y) * 2 + core, (to_x * count_y + to_y) * 2 + core))
+    return lax.ppermute(value, ("gx", "gy", "gz"), pairs)
+
+
+def gather_halo(chunk, both=None):
+    if is_paired():
+        if both is None:
+            both = jnp.concatenate([chunk, shifted(chunk, "gz", 1)], axis=0)
+        direct = [swapped(both, slot) for slot in range(4)]
+        relayed = shifted(jnp.concatenate(direct, axis=0), "gz", 1)
+        near = [(slot, row) for slot in range(4) for row in range(2)] + [(4, 0)]
+        far = [(5, row) for row in range(8)] + [(4, 1)]
+        return direct + [both, relayed], near + far
     for axis in ("gx", "gy"):
         lower = shifted(chunk, axis, 1)
         upper = shifted(chunk, axis, -1)
-        chunk = jnp.concatenate([chunk, lower, upper], axis=0)
+        chunk = jnp.concatenate([lower, upper, chunk], axis=0)
+    order = [(array, row) for array in range(2) for row in range(9)]
     if lax.axis_size("gz") == 2:
-        return chunk, shifted(chunk, "gz", 1)
+        return [chunk, shifted(chunk, "gz", 1)], order
     half = chunk.shape[-1] // 2
     above = shifted(chunk[..., :half], "gz", -1)
     below = shifted(chunk[..., half:], "gz", 1)
-    return chunk, jnp.concatenate([above, below], axis=-1)
+    return [chunk, jnp.concatenate([above, below], axis=-1)], order
 
 
 def reduce_halo(own, other):
+    kind = own.dtype
+    if is_paired():
+        own = own.astype(F32) + shifted(other, "gz", 1).astype(F32)
+        came = [swapped(own[2 * slot : 2 * slot + 2].astype(kind), slot).astype(F32) for slot in range(4)]
+        both = came[0] + came[1] + came[2] + came[3]
+        return own[8:] + both[:1] + shifted(both[1:], "gz", 1)
     if lax.axis_size("gz") == 2:
         back = shifted(other, "gz", 1)
     else:
@@ -46,29 +90,70 @@
         first = shifted(other[..., :half], "gz", 1)
         second = shifted(other[..., half:], "gz", -1)
         back = jnp.concatenate([first, second], axis=-1)
-    kind = own.dtype
     own = own.astype(F32) + back.astype(F32)
     for axis, size in (("gy", 3), ("gx", 1)):
-        lower = shifted(own[size : 2 * size].astype(kind), axis, -1)
-        upper = shifted(own[2 * size :].astype(kind), axis, 1)
-        own = own[:size] + lower.astype(F32) + upper.astype(F32)
+        lower = shifted(own[:size].astype(kind), axis, -1)
+        upper = shifted(own[size : 2 * size].astype(kind), axis, 1)
+        own = own[2 * size :] + lower.astype(F32) + upper.astype(F32)
     return own
 
 
-def pack_kernel(pos_ref, spec_ref, out_ref):
+def place_column(step_x, step_y, outside, paired):
+    if not paired:
+        place_x = jnp.where(step_x == 0, 2, jnp.where(step_x < 0, 0, 1))
+        place_y = jnp.where(step_y == 0, 2, jnp.where(step_y < 0, 0, 1))
+        return outside * 9 + place_y * 3 + place_x
+    core = lax.axis_index("gz")
+    up_x = 1 - 2 * (lax.axis_index("gx") & 1)
+    up_y = 1 - 2 * (lax.axis_index("gy") & 1)
+    way_x = jnp.where(step_x == 0, 0, jnp.where(step_x == up_x, 1, 2))
+    way_y = jnp.where(step_y == 0, 0, jnp.where(step_y == up_y, 1, 2))
+    way = way_x * 3 + way_y
+    chunk = 8 + 9 * outside
+    for owner in range(2):
+        mine = core == owner
+        for slot, (to_x, to_y) in enumerate(ROUTES[owner]):
+            spot = jnp.where(mine, 2 * slot + outside, 9 + 2 * slot + 1 - outside)
+            chunk = jnp.where(way == to_x * 3 + to_y, spot, chunk)
+    return chunk
+
+
+def fetch(pairs, sems):
+    copies = [pltpu.make_async_copy(a, b, sems.at[i]) for i, (a, b) in enumerate(pairs)]
+    for copy in copies:
+        copy.start()
+    for copy in copies:
+        copy.wait()
+
+
+def pack_kernel(*refs):
+    out_ref = refs[-1]
     out_ref[...] = jnp.zeros(out_ref.shape, F32)
-    slots = spec_ref.shape[-1]
-    for block in range(2):
-        lanes = slice(block * slots, (block + 1) * slots)
-        for c in range(3):
-            out_ref[0, c : c + 1, lanes] = pos_ref[0, 0, block : block + 1, c * slots : (c + 1) * slots]
-        out_ref[0, 3:4, lanes] = spec_ref[0, 0, block : block + 1, :].astype(F32)
+    for chunk in range(out_ref.shape[0]):
+        pos_ref, spec_ref = refs[2 * chunk : 2 * chunk + 2]
+        slots = spec_ref.shape[-1]
+        for block in range(2):
+            lanes = slice(block * slots, (block + 1) * slots)
+            for c in range(3):
+                out_ref[chunk, c : c + 1, lanes] = pos_ref[0, 0, block : block + 1, c * slots : (c + 1) * slots]
+            out_ref[chunk, 3:4, lanes] = spec_ref[0, 0, block : block + 1, :].astype(F32)
 
 
 def prep_kernel(
-    nb_ref, center_ref, neighbor_ref, radial_ref, mix_ref, env_ref, upd_ref, second_ref, readout_ref,
-    code_ref, onehot_ref, wcat_ref, mixt_ref, envt_ref, updt_ref, secondt_ref, rocol_ref, pad_ref,
+    paired,
+    nb_hbm, center_hbm, neighbor_hbm, radial_hbm, mix_hbm, env_hbm, upd_hbm, second_hbm, readout_hbm,
+    code_ref, onehot_ref, wcat_ref, mixt_ref, envt_ref, updt_ref, secondt_ref, rocol_ref,
+    radial_ref, mix_ref, env_ref, upd_ref, second_ref,
+    nb_ref, center_ref, neighbor_ref, readout_ref, pad_ref, sems,
 ):
+    fetch(
+        (
+            (nb_hbm, nb_ref), (center_hbm, center_ref), (neighbor_hbm, neighbor_ref), (radial_hbm, radial_ref),
+            (mix_hbm, mix_ref), (env_hbm, env_ref), (upd_hbm, upd_ref), (second_hbm, second_ref),
+            (readout_hbm, readout_ref),
+        ),
+        sems,
+    )
     width = nb_ref.shape[-1]
     slots = width // NEIGH
     lane = lax.broadcasted_iota(jnp.int32, (NEIGH, width), 1)
@@ -95,9 +180,7 @@
     block = lax.broadcasted_iota(jnp.int32, (NEIGH, ATOMS), 1) // slots
     level = block + step_z
     outside = jnp.where((level < 0) | (level > 1), 1, 0)
-    place_x = jnp.where(step_x == 0, 0, jnp.where(step_x < 0, 1, 2))
-    place_y = jnp.where(step_y == 0, 0, jnp.where(step_y < 0, 1, 2))
-    chunk = outside * 9 + place_y * 3 + place_x
+    chunk = place_column(step_x, step_y, outside, paired)
     target = chunk * ATOMS + (level & 1) * slots + slot
     code_ref[0] = target
     code_ref[1] = step_x
@@ -166,23 +249,26 @@
 PIECE = (0, 1, 1, 1, 2, 2, 2, 2, 2)
 
 
-def forward_kernel(
-    own_ref, other_ref, code_ref, wcat_ref, mixt_ref, envt_ref, updt_ref,
-    table_ref, edge_ref, dsb_ref, dsl_ref, dse_ref, env_ref, v_ref, geo_ref, yb_ref, inv_ref, lat_ref,
-):
+def forward_kernel(parts, order, *refs):
+    atoms = [(refs[array], row) for array, row in order]
+    (
+        code_ref, wcat_ref, mixt_ref, envt_ref, updt_ref,
+        table_ref, edge_ref, dsb_ref, dsl_ref, dse_ref, env_ref, v_ref, geo_ref, yb_ref, inv_ref, lat_ref,
+    ) = refs[parts:]
+    home_ref, home = atoms[8]
     target = code_ref[0]
     chunk = target >> 7
     lane = target & 127
     found = [jnp.zeros((NEIGH, ATOMS), F32) for _ in range(4)]
     for c in range(CHUNKS):
-        ref = own_ref if c < 9 else other_ref
+        ref, at = atoms[c]
         hit = chunk == c
         for f in range(4):
-            row = jnp.broadcast_to(ref[c % 9, f : f + 1, :], (NEIGH, ATOMS))
+            row = jnp.broadcast_to(ref[at, f : f + 1, :], (NEIGH, ATOMS))
             value = jnp.take_along_axis(row, lane, axis=1)
             found[f] = jnp.where(hit, value, found[f])
     d = [
-        code_ref[1 + c].astype(F32) + (found[c] - jnp.broadcast_to(own_ref[0, c : c + 1, :], (NEIGH, ATOMS)))
+        code_ref[1 + c].astype(F32) + (found[c] - jnp.broadcast_to(home_ref[home, c : c + 1, :], (NEIGH, ATOMS)))
         for c in range(3)
     ]
     r = jnp.sqrt(d[0] * d[0] + d[1] * d[1] + d[2] * d[2])
@@ -194,7 +280,7 @@
     spread_rows(yb_ref, angular_rows(ux, uy, uz))
 
     kind = lax.broadcasted_iota(jnp.int32, (8, ATOMS), 0).astype(F32)
-    center_hot = jnp.where(jnp.broadcast_to(own_ref[0, 3:4, :], (8, ATOMS)) == kind, 1.0, 0.0)
+    center_hot = jnp.where(jnp.broadcast_to(home_ref[home, 3:4, :], (8, ATOMS)) == kind, 1.0, 0.0)
     zero = jnp.zeros((8, ATOMS), F32)
     columns = []
     for k in range(NEIGH):
@@ -247,11 +333,12 @@
     table_ref[0] = (mean * 0.125).astype(BF16)
 
 
-def second_kernel(
-    own_ref, other_ref, onehot_ref, edge_ref, second_ref, secondt_ref, rocol_ref,
-    energy_ref, grad_edge_ref, back_own_ref, back_other_ref, grad_ref,
-):
-    table = jnp.concatenate([own_ref[c] for c in range(9)] + [other_ref[c] for c in range(9)], axis=1)
+def second_kernel(parts, order, *refs):
+    (
+        onehot_ref, edge_ref, second_ref, secondt_ref, rocol_ref,
+        energy_ref, grad_edge_ref, back_own_ref, back_other_ref, grad_ref,
+    ) = refs[parts:]
+    table = jnp.concatenate([refs[array][row] for array, row in order], axis=1)
     rocol = rocol_ref[...]
     total = jnp.zeros((ATOMS, ATOMS), F32)
     for j in range(EDGES // TILE):
@@ -367,7 +454,7 @@
             force, onehot_ref[rows, :], (((1,), (1,)), ((), ())), preferred_element_type=F32
         )
         moved = back[:8] + back[8:]
-        if c == 0:
+        if c == 8:
             moved = moved - center
         ref = own_ref if c < 9 else other_ref
         ref[c % 9] = moved
@@ -382,7 +469,7 @@
             ]
 
 
-def call(kernel, outs, scratch=(), name=None, limit=24 << 20):
+def call(kernel, outs, scratch=(), name=None, limit=24 << 20, place=pltpu.VMEM, cost=None):
     whole = pl.BlockSpec(memory_space=pltpu.VMEM)
     shapes = [jax.ShapeDtypeStruct(shape, kind) for shape, kind in outs]
 
@@ -390,10 +477,11 @@
         return pl.pallas_call(
             kernel,
             out_shape=shapes,
-            in_specs=[whole] * len(args),
+            in_specs=[pl.BlockSpec(memory_space=place)] * len(args),
             out_specs=[whole] * len(shapes),
             scratch_shapes=list(scratch),
             compiler_params=pltpu.CompilerParams(vmem_limit_bytes=limit),
+            cost_estimate=cost,
             name=name,
         )(*args)
 
@@ -407,36 +495,54 @@
     slots = species.shape[-1]
     edges = (ATOMS, EDGES)
     square = (ATOMS, ATOMS)
-    (packed,) = call(pack_kernel, [((1, 8, ATOMS), F32)], name="pack")(positions, species)
-    code, onehot, wcat, mixt, envt, updt, secondt, rocol = call(
-        prep_kernel,
+    readout = readout.reshape(1, ATOMS)
+
+    def like(*arrays):
+        return [pltpu.VMEM(array.shape, array.dtype) for array in arrays]
+
+    halves = [positions, species]
+    if is_paired():
+        halves += [shifted(positions, "gz", 1), shifted(species, "gz", 1)]
+    (packed,) = call(
+        pack_kernel,
+        [((len(halves) // 2, 8, ATOMS), F32)],
+        name="pack",
+        cost=pl.CostEstimate(flops=1 << 34, bytes_accessed=64 << 20, transcendentals=0),
+    )(*halves)
+    weights = (radial_weight, mix_weight, env_weight, update_weight, second_weight)
+    code, onehot, wcat, mixt, envt, updt, secondt, rocol, radial, mix, envw, upd, second = call(
+        functools.partial(prep_kernel, is_paired()),
         [
             ((4, NEIGH, ATOMS), jnp.int32), ((CHUNKS * ATOMS, EDGES), BF16), ((ATOMS, 32), BF16), (square, BF16),
             (square, BF16), ((ATOMS, 3 * ATOMS), BF16), (square, BF16), (square, F32),
-        ],
-        [pltpu.VMEM(square, F32)],
+        ]
+        + [(weight.shape, weight.dtype) for weight in weights],
+        like(neighbors, center_table, neighbor_table, readout)
+        + [pltpu.VMEM(square, F32), pltpu.SemaphoreType.DMA((9,))],
         name="prep",
+        place=pltpu.HBM,
+        cost=pl.CostEstimate(flops=1 << 28, bytes_accessed=8 << 20, transcendentals=0),
     )(
         neighbors, center_table, neighbor_table, radial_weight, mix_weight, env_weight, update_weight,
-        second_weight, readout.reshape(1, ATOMS),
+        second_weight, readout,
     )
-    near, far = gather_halo(packed)
+    tables, order = gather_halo(packed, packed)
     table, edge, dsb, dsl, dse, env, field, geo = call(
-        forward_kernel,
+        functools.partial(forward_kernel, len(tables), order),
         [
             ((1,) + square, BF16), (edges, F32), (edges, F32), (edges, F32), (edges, F32), (edges, F32),
             ((9,) + square, F32), ((4, NEIGH, ATOMS), F32),
         ],
         [pltpu.VMEM((72, 8, ATOMS), F32), pltpu.VMEM((3 * ATOMS, EDGES), BF16), pltpu.VMEM(edges, F32)],
         name="forward",
-    )(near, far, code, wcat, mixt, envt, updt)
-    near, far = gather_halo(table)
+    )(*tables, code, wcat, mixt, envt, updt)
+    tables, order = gather_halo(table)
     energy, grad_edge, back_own, back_other = call(
-        second_kernel,
+        functools.partial(second_kernel, len(tables), order),
         [((1, 1, 2, slots), F32), (edges, F32), ((9,) + square, BF16), ((9,) + square, BF16)],
         [pltpu.VMEM(edges, BF16)],
         name="second",
-    )(near, far, onehot, edge, second_weight, secondt, rocol)
+    )(*tables, onehot, edge, second, secondt, rocol)
     owned = reduce_halo(back_own, back_other)
     own, other = call(
         backward_kernel,
@@ -446,10 +552,7 @@
             pltpu.VMEM(edges, F32), pltpu.VMEM((72, 8, ATOMS), F32), pltpu.VMEM((16, EDGES), BF16),
         ],
         name="backward",
-    )(
-        owned, grad_edge, dse, dsl, dsb, env, field, geo, onehot, update_weight, env_weight, mix_weight,
-        radial_weight,
-    )
+    )(owned, grad_edge, dse, dsl, dsb, env, field, geo, onehot, upd, envw, mix, radial)
     motion = reduce_halo(own, other)
     (forces,) = call(finish_kernel, [((1, 1, 2, 3 * slots), F32)], name="finish")(motion)
     return energy, forces

time: 81.9 us -> 68.5 us (0.84)
  waiting for transfers between devices: 38.1 us -> 21.5 us
  starting transfers between devices: 21.5 us -> 31.9 us
  local copies, waits for them, and re-layouts: 8.78 us -> 1.44 us
    ppermute x0 -> x16, starting transfers between devices: none -> 30.1 us  [swapped(): return lax.ppermute(value, ('gx', 'gy', 'gz'), pairs)]
    ppermute x20 -> x9, waiting for transfers between devices: 38.1 us -> 8.55 us  [shifted(): lax.ppermute(value, axis, [(i, (i + step) % count) for i in range(count)])]
    ppermute x20 -> x9, starting transfers between devices: 21.5 us -> 1.74 us  [shifted(): lax.ppermute(value, axis, [(i, (i + step) % count) for i in range(count)])]
    ppermute x0 -> x16, waiting for transfers between devices: none -> 13 us  [swapped(): return lax.ppermute(value, ('gx', 'gy', 'gz'), pairs)]
    unnamed x39 -> x23, local copies, waits for them, and re-layouts: 8.71 us -> 1.4 us
  transfers between devices with their start and end apart: 20 -> 25, of which waited for: 17 -> 17; matrix products, arithmetic and copies ran while one was open for 0% -> 0% of each run, Pallas kernels for 2% -> 3%
where the time goes in v2:
time: 68.5 us; the launch traced here: 68.4 us
  starting transfers between devices  31.9 us (47%)
  waiting for transfers between devices  21.5 us (31%)
  Pallas kernels  12.5 us (18%)
  local copies, waits for them, and re-layouts  1.44 us (2%)
  between operations  0.87 us (1%)
    ppermute x16, starting transfers between devices, swapped(): return lax.ppermute(value, ('gx', 'gy', 'gz'), pairs)  30.1 us
    ppermute x16, waiting for transfers between devices, swapped(): return lax.ppermute(value, ('gx', 'gy', 'gz'), pairs)  13 us
    pallas_call x6, Pallas kernels, run(): pl.pallas_call(kernel, out_shape=shapes, in_specs=[pl.BlockSpec(memory_sp...  12.5 us
    ppermute x9, waiting for transfers between devices, shifted(): lax.ppermute(value, axis, [(i, (i + step) % count) for i in range(count)])  8.55 us
    ppermute x9, starting transfers between devices, shifted(): lax.ppermute(value, axis, [(i, (i + step) % count) for i in range(count)])  1.74 us
    unnamed x23, local copies, waits for them, and re-layouts  1.4 us
  transfers between devices with their start and end apart: 25, of which 17 were waited for; matrix products, arithmetic and copies ran while one was open for 0% of the time, Pallas kernels for 3%

profile of v2, /device:TPU:0, one launch (start us, length us, event | category | flops | bytes accessed | tf_op | source)
XLA Modules:
  0.0 68.4 jit_solution(6312210154670737455)
XLA Ops:
  1.3 1.3 %collective-permute-done.1.refs_3_ = s32[1,1,2,64]{3,2,1,0:T(2,128)S(1)} collective-permute-done((s32[1,1,2,64]{3,2,1,0:T(2,128)}, s32[1,1,2,64]{3,2,1,0:T(2,128)S(1)}, u32[]{:S(2)}, u32[]{:S(2)}) %collective-permute-start.1) | collective-permute-done | bytes 544 | tf_op jit(solution)/shard_map/ppermute | solution.py:34
  4.0 5.7 %collective-permute-start.5 = (f32[2,8,128]{2,1,0:T(8,128)S(1)}, f32[2,8,128]{2,1,0:T(8,128)S(1)}, u32[]{:S(2)}, u32[]{:S(2)}) collective-permute-start(f32[2,8,128]{2,1,0:T(8,128)S(1)} %pack.1.refs_4_), channel_id=1, source_target_pairs={{0,26},{1,31},{2,24},{3,29},{4,30},{5,27},{6,28},{7,25},{8,18},{9,... | collective-permute-start | bytes 24584 | tf_op jit(solution)/shard_map/ppermute | solution.py:54
  10.2 1.4 %collective-permute-start.3 = (f32[2,8,128]{2,1,0:T(8,128)S(1)}, f32[2,8,128]{2,1,0:T(8,128)S(1)}, u32[]{:S(2)}, u32[]{:S(2)}) collective-permute-start(f32[2,8,128]{2,1,0:T(8,128)S(1)} %pack.1.refs_4_), channel_id=1, source_target_pairs={{0,6},{1,3},{2,4},{3,1},{4,2},{5,7},{6,0},{7,5},{8,14},{9,11},{10,... | collective-permute-start | bytes 24584 | tf_op jit(solution)/shard_map/ppermute | solution.py:54
  11.6 2.5 %collective-permute-start.2 = (f32[2,8,128]{2,1,0:T(8,128)S(1)}, f32[2,8,128]{2,1,0:T(8,128)S(1)}, u32[]{:S(2)}, u32[]{:S(2)}) collective-permute-start(f32[2,8,128]{2,1,0:T(8,128)S(1)} %pack.1.refs_4_), channel_id=1, source_target_pairs={{0,8},{1,25},{2,10},{3,27},{4,12},{5,29},{6,14},{7,31},{8,0},{9,17... | collective-permute-start | bytes 24584 | tf_op jit(solution)/shard_map/ppermute | solution.py:54
  15.8 2.2 %prep.1 = (s32[4,8,128]{2,1,0:T(8,128)S(1)}, bf16[2304,1024]{1,0:T(8,128)(2,1)S(1)}, bf16[128,32]{1,0:T(8,128)(2,1)S(1)}, bf16[128,128]{1,0:T(8,128)(2,1)S(1)}, ...) custom-call(s32[1,1,2,512]{3,2,1,0:T(2,128)S(1)} %copy-done.4, ...), custom_call_target="tpu_custom_call" | custom-call | flops 268435456 | bytes 8388608 | tf_op jit(solution)/shard_map/prep/pallas_call | solution.py:477
  18.0 2.3 %forward.1 = (bf16[1,128,128]{2,1,0:T(8,128)(2,1)S(1)}, f32[128,1024]{1,0:T(8,128)S(1)}, f32[128,1024]{1,0:T(8,128)S(1)}, f32[128,1024]{1,0:T(8,128)S(1)}, f32[1...) custom-call(f32[2,8,128]{2,1,0:T(8,128)S(1)} %collective-permute-done.2.ref, ...), custom_call_target="tpu_custom_call" | custom-call | tf_op jit(solution)/shard_map/forward/pallas_call | solution.py:477
  21.7 1.4 %collective-permute-start.11 = (bf16[2,128,128]{2,1,0:T(8,128)(2,1)S(1)}, bf16[2,128,128]{2,1,0:T(8,128)(2,1)S(1)}, u32[]{:S(2)}, u32[]{:S(2)}) collective-permute-start(bf16[2,128,128]{2,1,0:T(8,128)(2,1)S(1)} %constant_dynamic-update-slice_fusion.refs_4_), channel_id=1, source_target_pairs={{0,26},{1,31},{2,24},{3,29},{4,30},{5,27},{6,28},{7,25},{8,18},{9,... | collective-permute-start | bytes 196616 | tf_op jit(solution)/shard_map/ppermute | solution.py:54
  23.1 1.8 %collective-permute-start.10 = (bf16[2,128,128]{2,1,0:T(8,128)(2,1)S(1)}, bf16[2,128,128]{2,1,0:T(8,128)(2,1)S(1)}, u32[]{:S(2)}, u32[]{:S(2)}) collective-permute-start(bf16[2,128,128]{2,1,0:T(8,128)(2,1)S(1)} %constant_dynamic-update-slice_fusion.refs_4_), channel_id=1, source_target_pairs={{0,14},{1,11},{2,12},{3,9},{4,10},{5,15},{6,8},{7,13},{8,6},{9,3},... | collective-permute-start | bytes 196616 | tf_op jit(solution)/shard_map/ppermute | solution.py:54
  24.9 1.3 %collective-permute-start.9 = (bf16[2,128,128]{2,1,0:T(8,128)(2,1)S(1)}, bf16[2,128,128]{2,1,0:T(8,128)(2,1)S(1)}, u32[]{:S(2)}, u32[]{:S(2)}) collective-permute-start(bf16[2,128,128]{2,1,0:T(8,128)(2,1)S(1)} %constant_dynamic-update-slice_fusion.refs_4_), channel_id=1, source_target_pairs={{0,6},{1,3},{2,4},{3,1},{4,2},{5,7},{6,0},{7,5},{8,14},{9,11},{10,... | collective-permute-start | bytes 196616 | tf_op jit(solution)/shard_map/ppermute | solution.py:54
  26.2 1.3 %collective-permute-start.8 = (bf16[2,128,128]{2,1,0:T(8,128)(2,1)S(1)}, bf16[2,128,128]{2,1,0:T(8,128)(2,1)S(1)}, u32[]{:S(2)}, u32[]{:S(2)}) collective-permute-start(bf16[2,128,128]{2,1,0:T(8,128)(2,1)S(1)} %constant_dynamic-update-slice_fusion.refs_4_), channel_id=1, source_target_pairs={{0,8},{1,25},{2,10},{3,27},{4,12},{5,29},{6,14},{7,31},{8,0},{9,17... | collective-permute-start | bytes 196616 | tf_op jit(solution)/shard_map/ppermute | solution.py:54
  27.5 1.8 %collective-permute-done.11.refs_3_ = bf16[2,128,128]{2,1,0:T(8,128)(2,1)S(1)} collective-permute-done((bf16[2,128,128]{2,1,0:T(8,128)(2,1)S(1)}, bf16[2,128,128]{2,1,0:T(8,128)(2,1)S(1)}, u32[]{:S(2)}, u32[]{:S(2)}) %collective-permute-start.11) | collective-permute-done | bytes 65568 | tf_op jit(solution)/shard_map/ppermute | solution.py:54
  31.8 1.5 %collective-permute-done.12.refs_5_ = bf16[8,128,128]{2,1,0:T(8,128)(2,1)S(1)} collective-permute-done((bf16[8,128,128]{2,1,0:T(8,128)(2,1)S(1)}, bf16[8,128,128]{2,1,0:T(8,128)(2,1)S(1)}, u32[]{:S(2)}, u32[]{:S(2)}) %collective-permute-start.12) | collective-permute-done | bytes 262176 | tf_op jit(solution)/shard_map/ppermute | solution.py:34
  33.3 3.6 %second.1 = (f32[1,1,2,64]{3,2,1,0:T(2,128)}, f32[128,1024]{1,0:T(8,128)S(1)}, bf16[9,128,128]{2,1,0:T(8,128)(2,1)S(1)}, bf16[9,128,128]{2,1,0:T(8,128)(2,1)S(1)}) custom-call(bf16[2,128,128]{2,1,0:T(8,128)(2,1)S(1)} %collective-permute-done.8.refs_0_, bf16[2,128,128]{2,1,0:T(8,128)(2,1)S(1)} %collective-permute-done.9.refs_1_, ...), custom_call_target="tpu_custom_call" | custom-call | tf_op jit(solution)/shard_map/second/pallas_call | solution.py:477
  37.1 1.4 %collective-permute-done.13 = bf16[9,128,128]{2,1,0:T(8,128)(2,1)S(1)} collective-permute-done((bf16[9,128,128]{2,1,0:T(8,128)(2,1)S(1)}, bf16[9,128,128]{2,1,0:T(8,128)(2,1)S(1)}, u32[]{:S(2)}, u32[]{:S(2)}) %collective-permute-start.13) | collective-permute-done | bytes 294944 | tf_op jit(solution)/shard_map/ppermute | solution.py:34
  39.8 2.6 %collective-permute-start.17 = (bf16[2,128,128]{2,1,0:T(8,128)(2,1)S(1)}, bf16[2,128,128]{2,1,0:T(8,128)(2,1)S(1)}, u32[]{:S(2)}, u32[]{:S(2)}) collective-permute-start(bf16[2,128,128]{2,1,0:T(8,128)(2,1)S(1)} %get-tuple-element.59), channel_id=1, source_target_pairs={{0,26},{1,31},{2,24},{3,29},{4,30},{5,27},{6,28},{7,25},{8,18},{9,... | collective-permute-start | bytes 196616 | tf_op jit(solution)/shard_map/ppermute | solution.py:54
  42.5 1.5 %collective-permute-start.16 = (bf16[2,128,128]{2,1,0:T(8,128)(2,1)S(1)}, bf16[2,128,128]{2,1,0:T(8,128)(2,1)S(1)}, u32[]{:S(2)}, u32[]{:S(2)}) collective-permute-start(bf16[2,128,128]{2,1,0:T(8,128)(2,1)S(1)} %get-tuple-element.60), channel_id=1, source_target_pairs={{0,14},{1,11},{2,12},{3,9},{4,10},{5,15},{6,8},{7,13},{8,6},{9,3},... | collective-permute-start | bytes 196616 | tf_op jit(solution)/shard_map/ppermute | solution.py:54
  44.0 1.5 %collective-permute-start.15 = (bf16[2,128,128]{2,1,0:T(8,128)(2,1)S(1)}, bf16[2,128,128]{2,1,0:T(8,128)(2,1)S(1)}, u32[]{:S(2)}, u32[]{:S(2)}) collective-permute-start(bf16[2,128,128]{2,1,0:T(8,128)(2,1)S(1)} %get-tuple-element.61), channel_id=1, source_target_pairs={{0,6},{1,3},{2,4},{3,1},{4,2},{5,7},{6,0},{7,5},{8,14},{9,11},{10,... | collective-permute-start | bytes 196616 | tf_op jit(solution)/shard_map/ppermute | solution.py:54
  45.5 1.4 %collective-permute-done.17 = bf16[2,128,128]{2,1,0:T(8,128)(2,1)S(1)} collective-permute-done((bf16[2,128,128]{2,1,0:T(8,128)(2,1)S(1)}, bf16[2,128,128]{2,1,0:T(8,128)(2,1)S(1)}, u32[]{:S(2)}, u32[]{:S(2)}) %collective-permute-start.17) | collective-permute-done | bytes 65568 | tf_op jit(solution)/shard_map/ppermute | solution.py:54
  46.9 2.7 %collective-permute-done.16 = bf16[2,128,128]{2,1,0:T(8,128)(2,1)S(1)} collective-permute-done((bf16[2,128,128]{2,1,0:T(8,128)(2,1)S(1)}, bf16[2,128,128]{2,1,0:T(8,128)(2,1)S(1)}, u32[]{:S(2)}, u32[]{:S(2)}) %collective-permute-start.16) | collective-permute-done | bytes 65568 | tf_op jit(solution)/shard_map/ppermute | solution.py:54
  51.8 3.6 %backward.1 = (f32[9,8,128]{2,1,0:T(8,128)S(1)}, f32[9,8,128]{2,1,0:T(8,128)S(1)}) custom-call(f32[1,128,128]{2,1,0:T(8,128)S(1)} %fusion.owned_ref, f32[128,1024]{1,0:T(8,128)S(1)} %get-tuple-element.43.grad_edge_ref, f32[128,1024]{1,0:T(8,128)S(1)} %get-tuple-element.44.dse_ref, f32[128,1024]{1,0:T(8,128)S(1)} %get-tuple-element.45.dsl_ref, ...), custom_call_target="tpu_custom_call" | custom-call | tf_op jit(solution)/shard_map/backward/pallas_call | solution.py:477
  56.7 1.6 %collective-permute-start.21 = (f32[2,8,128]{2,1,0:T(8,128)S(1)}, f32[2,8,128]{2,1,0:T(8,128)S(1)}, u32[]{:S(2)}, u32[]{:S(2)}) collective-permute-start(f32[2,8,128]{2,1,0:T(8,128)S(1)} %get-tuple-element.62), channel_id=1, source_target_pairs={{0,6},{1,3},{2,4},{3,1},{4,2},{5,7},{6,0},{7,5},{8,14},{9,11},{10,... | collective-permute-start | bytes 24584 | tf_op jit(solution)/shard_map/ppermute | solution.py:54
  58.3 2.7 %collective-permute-start.23 = (f32[2,8,128]{2,1,0:T(8,128)S(1)}, f32[2,8,128]{2,1,0:T(8,128)S(1)}, u32[]{:S(2)}, u32[]{:S(2)}) collective-permute-start(f32[2,8,128]{2,1,0:T(8,128)S(1)} %get-tuple-element.63), channel_id=1, source_target_pairs={{0,26},{1,31},{2,24},{3,29},{4,30},{5,27},{6,28},{7,25},{8,18},{9,... | collective-permute-start | bytes 24584 | tf_op jit(solution)/shard_map/ppermute | solution.py:54
  61.3 2.9 %collective-permute-start.20 = (f32[2,8,128]{2,1,0:T(8,128)S(1)}, f32[2,8,128]{2,1,0:T(8,128)S(1)}, u32[]{:S(2)}, u32[]{:S(2)}) collective-permute-start(f32[2,8,128]{2,1,0:T(8,128)S(1)} %get-tuple-element.65), channel_id=1, source_target_pairs={{0,8},{1,25},{2,10},{3,27},{4,12},{5,29},{6,14},{7,31},{8,0},{9,17... | collective-permute-start | bytes 24584 | tf_op jit(solution)/shard_map/ppermute | solution.py:54
  64.6 1.8 %collective-permute-done.22 = f32[2,8,128]{2,1,0:T(8,128)S(1)} collective-permute-done((f32[2,8,128]{2,1,0:T(8,128)S(1)}, f32[2,8,128]{2,1,0:T(8,128)S(1)}, u32[]{:S(2)}, u32[]{:S(2)}) %collective-permute-start.22) | collective-permute-done | bytes 8224 | tf_op jit(solution)/shard_map/ppermute | solution.py:54
  (68 shorter events, 15.5 us)
Async XLA Ops:
  0.7 1.9 %collective-permute-start = (f32[1,1,2,192]{3,2,1,0:T(2,128)}, f32[1,1,2,192]{3,2,1,0:T(2,128)S(1)}, u32[]{:S(2)}, u32[]{:S(2)}) collective-permute-start(f32[1,1,2,192]{3,2,1,0:T(2,128)} %refs_0_.1), channel_id=1, source_target_pairs={{0,1},{1,0},{2,3},{3,2},{4,5},{5,4},{6,7},{7,6},{8,9},{9,8},{10,11... | collective-permute-start | bytes 4616 | tf_op jit(solution)/shard_map/ppermute | solution.py:34
  1.2 1.4 %collective-permute-start.1 = (s32[1,1,2,64]{3,2,1,0:T(2,128)}, s32[1,1,2,64]{3,2,1,0:T(2,128)S(1)}, u32[]{:S(2)}, u32[]{:S(2)}) collective-permute-start(s32[1,1,2,64]{3,2,1,0:T(2,128)} %refs_1_.1), channel_id=1, source_target_pairs={{0,1},{1,0},{2,3},{3,2},{4,5},{5,4},{6,7},{7,6},{8,9},{9,8},{10,11... | collective-permute-start | bytes 1544 | tf_op jit(solution)/shard_map/ppermute | solution.py:34
  4.0 10.1 %collective-permute-start.5 = (f32[2,8,128]{2,1,0:T(8,128)S(1)}, f32[2,8,128]{2,1,0:T(8,128)S(1)}, u32[]{:S(2)}, u32[]{:S(2)}) collective-permute-start(f32[2,8,128]{2,1,0:T(8,128)S(1)} %pack.1.refs_4_), channel_id=1, source_target_pairs={{0,26},{1,31},{2,24},{3,29},{4,30},{5,27},{6,28},{7,25},{8,18},{9,... | collective-permute-start | bytes 24584 | tf_op jit(solution)/shard_map/ppermute | solution.py:54
  9.7 5.4 %collective-permute-start.4 = (f32[2,8,128]{2,1,0:T(8,128)S(1)}, f32[2,8,128]{2,1,0:T(8,128)S(1)}, u32[]{:S(2)}, u32[]{:S(2)}) collective-permute-start(f32[2,8,128]{2,1,0:T(8,128)S(1)} %pack.1.refs_4_), channel_id=1, source_target_pairs={{0,14},{1,11},{2,12},{3,9},{4,10},{5,15},{6,8},{7,13},{8,6},{9,3},... | collective-permute-start | bytes 24584 | tf_op jit(solution)/shard_map/ppermute | solution.py:54
  10.2 5.0 %collective-permute-start.3 = (f32[2,8,128]{2,1,0:T(8,128)S(1)}, f32[2,8,128]{2,1,0:T(8,128)S(1)}, u32[]{:S(2)}, u32[]{:S(2)}) collective-permute-start(f32[2,8,128]{2,1,0:T(8,128)S(1)} %pack.1.refs_4_), channel_id=1, source_target_pairs={{0,6},{1,3},{2,4},{3,1},{4,2},{5,7},{6,0},{7,5},{8,14},{9,11},{10,... | collective-permute-start | bytes 24584 | tf_op jit(solution)/shard_map/ppermute | solution.py:54
  11.6 4.1 %collective-permute-start.2 = (f32[2,8,128]{2,1,0:T(8,128)S(1)}, f32[2,8,128]{2,1,0:T(8,128)S(1)}, u32[]{:S(2)}, u32[]{:S(2)}) collective-permute-start(f32[2,8,128]{2,1,0:T(8,128)S(1)} %pack.1.refs_4_), channel_id=1, source_target_pairs={{0,8},{1,25},{2,10},{3,27},{4,12},{5,29},{6,14},{7,31},{8,0},{9,17... | collective-permute-start | bytes 24584 | tf_op jit(solution)/shard_map/ppermute | solution.py:54
  15.8 2.3 %collective-permute-start.6 = (f32[8,8,128]{2,1,0:T(8,128)S(1)}, f32[8,8,128]{2,1,0:T(8,128)S(1)}, u32[]{:S(2)}, u32[]{:S(2)}) collective-permute-start(f32[8,8,128]{2,1,0:T(8,128)S(1)} %pad_maximum_fusion.1), channel_id=1, source_target_pairs={{0,1},{1,0},{2,3},{3,2},{4,5},{5,4},{6,7},{7,6},{8,9},{9,8},{10,11... | collective-permute-start | bytes 98312 | tf_op jit(solution)/shard_map/ppermute | solution.py:34
  20.3 1.4 %collective-permute-start.7 = (bf16[1,128,128]{2,1,0:T(8,128)(2,1)S(1)}, bf16[1,128,128]{2,1,0:T(8,128)(2,1)S(1)}, u32[]{:S(2)}, u32[]{:S(2)}) collective-permute-start(bf16[1,128,128]{2,1,0:T(8,128)(2,1)S(1)} %get-tuple-element.34), channel_id=1, source_target_pairs={{0,1},{1,0},{2,3},{3,2},{4,5},{5,4},{6,7},{7,6},{8,9},{9,8},{10,11... | collective-permute-start | bytes 98312 | tf_op jit(solution)/shard_map/ppermute | solution.py:34
  21.7 7.6 %collective-permute-start.11 = (bf16[2,128,128]{2,1,0:T(8,128)(2,1)S(1)}, bf16[2,128,128]{2,1,0:T(8,128)(2,1)S(1)}, u32[]{:S(2)}, u32[]{:S(2)}) collective-permute-start(bf16[2,128,128]{2,1,0:T(8,128)(2,1)S(1)} %constant_dynamic-update-slice_fusion.refs_4_), channel_id=1, source_target_pairs={{0,26},{1,31},{2,24},{3,29},{4,30},{5,27},{6,28},{7,25},{8,18},{9,... | collective-permute-start | bytes 196616 | tf_op jit(solution)/shard_map/ppermute | solution.py:54
  23.1 7.4 %collective-permute-start.10 = (bf16[2,128,128]{2,1,0:T(8,128)(2,1)S(1)}, bf16[2,128,128]{2,1,0:T(8,128)(2,1)S(1)}, u32[]{:S(2)}, u32[]{:S(2)}) collective-permute-start(bf16[2,128,128]{2,1,0:T(8,128)(2,1)S(1)} %constant_dynamic-update-slice_fusion.refs_4_), channel_id=1, source_target_pairs={{0,14},{1,11},{2,12},{3,9},{4,10},{5,15},{6,8},{7,13},{8,6},{9,3},... | collective-permute-start | bytes 196616 | tf_op jit(solution)/shard_map/ppermute | solution.py:54
  24.9 6.7 %collective-permute-start.9 = (bf16[2,128,128]{2,1,0:T(8,128)(2,1)S(1)}, bf16[2,128,128]{2,1,0:T(8,128)(2,1)S(1)}, u32[]{:S(2)}, u32[]{:S(2)}) collective-permute-start(bf16[2,128,128]{2,1,0:T(8,128)(2,1)S(1)} %constant_dynamic-update-slice_fusion.refs_4_), channel_id=1, source_target_pairs={{0,6},{1,3},{2,4},{3,1},{4,2},{5,7},{6,0},{7,5},{8,14},{9,11},{10,... | collective-permute-start | bytes 196616 | tf_op jit(solution)/shard_map/ppermute | solution.py:54
  26.2 5.4 %collective-permute-start.8 = (bf16[2,128,128]{2,1,0:T(8,128)(2,1)S(1)}, bf16[2,128,128]{2,1,0:T(8,128)(2,1)S(1)}, u32[]{:S(2)}, u32[]{:S(2)}) collective-permute-start(bf16[2,128,128]{2,1,0:T(8,128)(2,1)S(1)} %constant_dynamic-update-slice_fusion.refs_4_), channel_id=1, source_target_pairs={{0,8},{1,25},{2,10},{3,27},{4,12},{5,29},{6,14},{7,31},{8,0},{9,17... | collective-permute-start | bytes 196616 | tf_op jit(solution)/shard_map/ppermute | solution.py:54
  31.7 1.6 %collective-permute-start.12 = (bf16[8,128,128]{2,1,0:T(8,128)(2,1)S(1)}, bf16[8,128,128]{2,1,0:T(8,128)(2,1)S(1)}, u32[]{:S(2)}, u32[]{:S(2)}) collective-permute-start(bf16[8,128,128]{2,1,0:T(8,128)(2,1)S(1)} %pad_maximum_fusion), channel_id=1, source_target_pairs={{0,1},{1,0},{2,3},{3,2},{4,5},{5,4},{6,7},{7,6},{8,9},{9,8},{10,11... | collective-permute-start | bytes 786440 | tf_op jit(solution)/shard_map/ppermute | solution.py:34
  36.9 1.6 %collective-permute-start.13 = (bf16[9,128,128]{2,1,0:T(8,128)(2,1)S(1)}, bf16[9,128,128]{2,1,0:T(8,128)(2,1)S(1)}, u32[]{:S(2)}, u32[]{:S(2)}) collective-permute-start(bf16[9,128,128]{2,1,0:T(8,128)(2,1)S(1)} %get-tuple-element.42), channel_id=1, source_target_pairs={{0,1},{1,0},{2,3},{3,2},{4,5},{5,4},{6,7},{7,6},{8,9},{9,8},{10,11... | collective-permute-start | bytes 884744 | tf_op jit(solution)/shard_map/ppermute | solution.py:34
  38.7 6.8 %collective-permute-start.14 = (bf16[2,128,128]{2,1,0:T(8,128)(2,1)S(1)}, bf16[2,128,128]{2,1,0:T(8,128)(2,1)S(1)}, u32[]{:S(2)}, u32[]{:S(2)}) collective-permute-start(bf16[2,128,128]{2,1,0:T(8,128)(2,1)S(1)} %get-tuple-element.58), channel_id=1, source_target_pairs={{0,8},{1,25},{2,10},{3,27},{4,12},{5,29},{6,14},{7,31},{8,0},{9,17... | collective-permute-start | bytes 196616 | tf_op jit(solution)/shard_map/ppermute | solution.py:54
  39.8 7.1 %collective-permute-start.17 = (bf16[2,128,128]{2,1,0:T(8,128)(2,1)S(1)}, bf16[2,128,128]{2,1,0:T(8,128)(2,1)S(1)}, u32[]{:S(2)}, u32[]{:S(2)}) collective-permute-start(bf16[2,128,128]{2,1,0:T(8,128)(2,1)S(1)} %get-tuple-element.59), channel_id=1, source_target_pairs={{0,26},{1,31},{2,24},{3,29},{4,30},{5,27},{6,28},{7,25},{8,18},{9,... | collective-permute-start | bytes 196616 | tf_op jit(solution)/shard_map/ppermute | solution.py:54
  42.5 7.2 %collective-permute-start.16 = (bf16[2,128,128]{2,1,0:T(8,128)(2,1)S(1)}, bf16[2,128,128]{2,1,0:T(8,128)(2,1)S(1)}, u32[]{:S(2)}, u32[]{:S(2)}) collective-permute-start(bf16[2,128,128]{2,1,0:T(8,128)(2,1)S(1)} %get-tuple-element.60), channel_id=1, source_target_pairs={{0,14},{1,11},{2,12},{3,9},{4,10},{5,15},{6,8},{7,13},{8,6},{9,3},... | collective-permute-start | bytes 196616 | tf_op jit(solution)/shard_map/ppermute | solution.py:54
  44.0 6.4 %collective-permute-start.15 = (bf16[2,128,128]{2,1,0:T(8,128)(2,1)S(1)}, bf16[2,128,128]{2,1,0:T(8,128)(2,1)S(1)}, u32[]{:S(2)}, u32[]{:S(2)}) collective-permute-start(bf16[2,128,128]{2,1,0:T(8,128)(2,1)S(1)} %get-tuple-element.61), channel_id=1, source_target_pairs={{0,6},{1,3},{2,4},{3,1},{4,2},{5,7},{6,0},{7,5},{8,14},{9,11},{10,... | collective-permute-start | bytes 196616 | tf_op jit(solution)/shard_map/ppermute | solution.py:54
  50.5 1.3 %collective-permute-start.18 = (f32[1,128,128]{2,1,0:T(8,128)S(1)}, f32[1,128,128]{2,1,0:T(8,128)S(1)}, u32[]{:S(2)}, u32[]{:S(2)}) collective-permute-start(f32[1,128,128]{2,1,0:T(8,128)S(1)} %slice.66), channel_id=1, source_target_pairs={{0,1},{1,0},{2,3},{3,2},{4,5},{5,4},{6,7},{7,6},{8,9},{9,8},{10,11... | collective-permute-start | bytes 196616 | tf_op jit(solution)/shard_map/ppermute | solution.py:34
  55.5 1.2 %collective-permute-start.19 = (f32[9,8,128]{2,1,0:T(8,128)S(1)}, f32[9,8,128]{2,1,0:T(8,128)S(1)}, u32[]{:S(2)}, u32[]{:S(2)}) collective-permute-start(f32[9,8,128]{2,1,0:T(8,128)S(1)} %get-tuple-element.55), channel_id=1, source_target_pairs={{0,1},{1,0},{2,3},{3,2},{4,5},{5,4},{6,7},{7,6},{8,9},{9,8},{10,11... | collective-permute-start | bytes 110600 | tf_op jit(solution)/shard_map/ppermute | solution.py:34
  56.7 7.4 %collective-permute-start.21 = (f32[2,8,128]{2,1,0:T(8,128)S(1)}, f32[2,8,128]{2,1,0:T(8,128)S(1)}, u32[]{:S(2)}, u32[]{:S(2)}) collective-permute-start(f32[2,8,128]{2,1,0:T(8,128)S(1)} %get-tuple-element.62), channel_id=1, source_target_pairs={{0,6},{1,3},{2,4},{3,1},{4,2},{5,7},{6,0},{7,5},{8,14},{9,11},{10,... | collective-permute-start | bytes 24584 | tf_op jit(solution)/shard_map/ppermute | solution.py:54
  58.3 6.3 %collective-permute-start.23 = (f32[2,8,128]{2,1,0:T(8,128)S(1)}, f32[2,8,128]{2,1,0:T(8,128)S(1)}, u32[]{:S(2)}, u32[]{:S(2)}) collective-permute-start(f32[2,8,128]{2,1,0:T(8,128)S(1)} %get-tuple-element.63), channel_id=1, source_target_pairs={{0,26},{1,31},{2,24},{3,29},{4,30},{5,27},{6,28},{7,25},{8,18},{9,... | collective-permute-start | bytes 24584 | tf_op jit(solution)/shard_map/ppermute | solution.py:54
  61.0 5.4 %collective-permute-start.22 = (f32[2,8,128]{2,1,0:T(8,128)S(1)}, f32[2,8,128]{2,1,0:T(8,128)S(1)}, u32[]{:S(2)}, u32[]{:S(2)}) collective-permute-start(f32[2,8,128]{2,1,0:T(8,128)S(1)} %get-tuple-element.64), channel_id=1, source_target_pairs={{0,14},{1,11},{2,12},{3,9},{4,10},{5,15},{6,8},{7,13},{8,6},{9,3},... | collective-permute-start | bytes 24584 | tf_op jit(solution)/shard_map/ppermute | solution.py:54
  61.3 5.2 %collective-permute-start.20 = (f32[2,8,128]{2,1,0:T(8,128)S(1)}, f32[2,8,128]{2,1,0:T(8,128)S(1)}, u32[]{:S(2)}, u32[]{:S(2)}) collective-permute-start(f32[2,8,128]{2,1,0:T(8,128)S(1)} %get-tuple-element.65), channel_id=1, source_target_pairs={{0,8},{1,25},{2,10},{3,27},{4,12},{5,29},{6,14},{7,31},{8,0},{9,17... | collective-permute-start | bytes 24584 | tf_op jit(solution)/shard_map/ppermute | solution.py:54
  (12 other events, 125.8 us)

commit v3 on v2

--- a/solution.py
+++ b/solution.py
@@ -20,13 +20,13 @@
 TILE = 256
 
 
+RING = (0, 1, 3, 2)
 ROUTES = (((1, 0), (0, 2), (1, 2), (2, 1)), ((2, 0), (0, 1), (1, 1), (2, 2)))
-
-
-def is_paired():
-    return lax.axis_size("gz") == 2 and all(
-        lax.axis_size(axis) % 2 == 0 and lax.axis_size(axis) >= 4 for axis in ("gx", "gy")
-    )
+EVERY = ("gx", "gy", "gz")
+
+
+def is_direct():
+    return tuple(lax.axis_size(axis) for axis in EVERY) == (4, 4, 2)
 
 
 def shifted(value, axis, step):
@@ -34,30 +34,41 @@
     return lax.ppermute(value, axis, [(i, (i + step) % count) for i in range(count)])
 
 
-def partner(index, way, count):
+def partner(index, way):
     if way == 0:
         return index
     if way == 1:
         return index ^ 1
-    return (index + 1 if index % 2 else index - 1) % count
+    return (index + 2 * (index & 1) - 1) & 3
+
+
+def number(x, y, core):
+    return (x * 4 + y) * 2 + core
+
+
+def permuted(value, target):
+    pairs = []
+    for x in range(4):
+        for y in range(4):
+            for core in range(2):
+                to_x, to_y = target(x, y, core)
+                pairs.append((number(RING[x], RING[y], core), number(RING[to_x], RING[to_y], core)))
+    return lax.ppermute(value, EVERY, pairs)
 
 
 def swapped(value, slot):
-    count_x, count_y = lax.axis_size("gx"), lax.axis_size("gy")
-    pairs = []
-    for x in range(count_x):
-        for y in range(count_y):
-            for core in range(2):
-                way_x, way_y = ROUTES[core][slot]
-                to_x, to_y = partner(x, way_x, count_x), partner(y, way_y, count_y)
-                pairs.append(((x * count_y + y) * 2 + core, (to_x * count_y + to_y) * 2 + core))
-    return lax.ppermute(value, ("gx", "gy", "gz"), pairs)
-
-
-def gather_halo(chunk, both=None):
-    if is_paired():
-        if both is None:
-            both = jnp.concatenate([chunk, shifted(chunk, "gz", 1)], axis=0)
+    return permuted(
+        value, lambda x, y, core: (partner(x, ROUTES[core][slot][0]), partner(y, ROUTES[core][slot][1]))
+    )
+
+
+def to_workers(value):
+    return permuted(value, lambda x, y, core: (RING[x], RING[y]))
+
+
+def gather_halo(chunk):
+    if is_direct():
+        both = jnp.concatenate([chunk, shifted(chunk, "gz", 1)], axis=0)
         direct = [swapped(both, slot) for slot in range(4)]
         relayed = shifted(jnp.concatenate(direct, axis=0), "gz", 1)
         near = [(slot, row) for slot in range(4) for row in range(2)] + [(4, 0)]
@@ -78,7 +89,7 @@
 
 def reduce_halo(own, other):
     kind = own.dtype
-    if is_paired():
+    if is_direct():
         own = own.astype(F32) + shifted(other, "gz", 1).astype(F32)
         came = [swapped(own[2 * slot : 2 * slot + 2].astype(kind), slot).astype(F32) for slot in range(4)]
         both = came[0] + came[1] + came[2] + came[3]
@@ -98,40 +109,72 @@
     return own
 
 
-def place_column(step_x, step_y, outside, paired):
-    if not paired:
+def ring_at(index):
+    return index ^ (index >> 1)
+
+
+def column_here():
+    return ring_at(lax.axis_index("gx")), ring_at(lax.axis_index("gy")), lax.axis_index("gz")
+
+
+def owner_at(step_x, step_y, outside):
+    x, y, core = column_here()
+    return number((x + step_x) & 3, (y + step_y) & 3, core ^ outside)
+
+
+def owner_of_chunk(c):
+    x, y, core = column_here()
+    outside = 0
+    if c % 9 == 8:
+        return number(x, y, core ^ (c // 9))
+    relayed = c // 9
+    slot, row = (c % 9) // 2, (c % 9) % 2
+    outside = row ^ relayed
+    spots = [
+        number(partner(x, ROUTES[mate][slot][0]), partner(y, ROUTES[mate][slot][1]), core ^ outside)
+        for mate in range(2)
+    ]
+    return jnp.where((core ^ relayed) == 0, spots[0], spots[1])
+
+
+def place_column(step_x, step_y, outside, direct):
+    if not direct:
         place_x = jnp.where(step_x == 0, 2, jnp.where(step_x < 0, 0, 1))
         place_y = jnp.where(step_y == 0, 2, jnp.where(step_y < 0, 0, 1))
         return outside * 9 + place_y * 3 + place_x
-    core = lax.axis_index("gz")
-    up_x = 1 - 2 * (lax.axis_index("gx") & 1)
-    up_y = 1 - 2 * (lax.axis_index("gy") & 1)
-    way_x = jnp.where(step_x == 0, 0, jnp.where(step_x == up_x, 1, 2))
-    way_y = jnp.where(step_y == 0, 0, jnp.where(step_y == up_y, 1, 2))
+    x, y, core = column_here()
+    way_x = jnp.where(step_x == 0, 0, jnp.where(step_x == 1 - 2 * (x & 1), 1, 2))
+    way_y = jnp.where(step_y == 0, 0, jnp.where(step_y == 1 - 2 * (y & 1), 1, 2))
     way = way_x * 3 + way_y
     chunk = 8 + 9 * outside
-    for owner in range(2):
-        mine = core == owner
-        for slot, (to_x, to_y) in enumerate(ROUTES[owner]):
+    for mate in range(2):
+        mine = core == mate
+        for slot, (to_x, to_y) in enumerate(ROUTES[mate]):
             spot = jnp.where(mine, 2 * slot + outside, 9 + 2 * slot + 1 - outside)
             chunk = jnp.where(way == to_x * 3 + to_y, spot, chunk)
     return chunk
 
 
-def fetch(pairs, sems):
-    copies = [pltpu.make_async_copy(a, b, sems.at[i]) for i, (a, b) in enumerate(pairs)]
-    for copy in copies:
-        copy.start()
-    for copy in copies:
-        copy.wait()
-
-
-def pack_kernel(*refs):
-    out_ref = refs[-1]
+def decode(code, slots):
+    offset = code >> 6
+    slot = code & 63
+    step_x = jnp.where(offset >= 18, 1, jnp.where(offset >= 9, 0, -1))
+    rest = offset - 9 * (step_x + 1)
+    step_y = jnp.where(rest >= 6, 1, jnp.where(rest >= 3, 0, -1))
+    step_z = rest - 3 * (step_y + 1) - 1
+    block = lax.broadcasted_iota(jnp.int32, (NEIGH, ATOMS), 1) // slots
+    level = block + step_z
+    outside = jnp.where((level < 0) | (level > 1), 1, 0)
+    return step_x, step_y, step_z, outside, (level & 1) * slots + slot
+
+
+def blank_kernel(out_ref):
     out_ref[...] = jnp.zeros(out_ref.shape, F32)
+
+
+def pack_kernel(blank_ref, pos_ref, spec_ref, out_ref):
+    slots = spec_ref.shape[-1]
     for chunk in range(out_ref.shape[0]):
-        pos_ref, spec_ref = refs[2 * chunk : 2 * chunk + 2]
-        slots = spec_ref.shape[-1]
         for block in range(2):
             lanes = slice(block * slots, (block + 1) * slots)
             for c in range(3):
@@ -139,21 +182,25 @@
             out_ref[chunk, 3:4, lanes] = spec_ref[0, 0, block : block + 1, :].astype(F32)
 
 
-def prep_kernel(
-    paired,
-    nb_hbm, center_hbm, neighbor_hbm, radial_hbm, mix_hbm, env_hbm, upd_hbm, second_hbm, readout_hbm,
-    code_ref, onehot_ref, wcat_ref, mixt_ref, envt_ref, updt_ref, secondt_ref, rocol_ref,
-    radial_ref, mix_ref, env_ref, upd_ref, second_ref,
-    nb_ref, center_ref, neighbor_ref, readout_ref, pad_ref, sems,
-):
-    fetch(
-        (
-            (nb_hbm, nb_ref), (center_hbm, center_ref), (neighbor_hbm, neighbor_ref), (radial_hbm, radial_ref),
-            (mix_hbm, mix_ref), (env_hbm, env_ref), (upd_hbm, upd_ref), (second_hbm, second_ref),
-            (readout_hbm, readout_ref),
-        ),
-        sems,
-    )
+def onehot_kernel(direct, code_ref, second_ref, readout_ref, onehot_ref, secondt_ref, rocol_ref):
+    step_x, step_y, step_z, outside, lane = decode(code_ref[...], ATOMS // 2)
+    target = place_column(step_x, step_y, outside, direct) * ATOMS + lane
+    secondt_ref[...] = second_ref[...].astype(F32).T.astype(BF16)
+    rocol_ref[...] = jnp.broadcast_to(readout_ref[...], (ATOMS, ATOMS)).T
+    atom = lax.broadcasted_iota(jnp.int32, (ATOMS, ATOMS), 0)
+    for k in range(NEIGH):
+        aim = jnp.broadcast_to(target[k : k + 1, :], (ATOMS, ATOMS)) - atom
+
+        def fill(c, carry, k=k, aim=aim):
+            rows = pl.ds(pl.multiple_of(c * ATOMS, ATOMS), ATOMS)
+            hit = jnp.where(aim == c * ATOMS, 1.0, 0.0)
+            onehot_ref[rows, k * ATOMS : (k + 1) * ATOMS] = hit.astype(BF16)
+            return carry
+
+        lax.fori_loop(0, CHUNKS, fill, 0)
+
+
+def listed_codes(nb_ref):
     width = nb_ref.shape[-1]
     slots = width // NEIGH
     lane = lax.broadcasted_iota(jnp.int32, (NEIGH, width), 1)
@@ -170,47 +217,7 @@
         pick = jnp.where(spot + block * slots == column, 1.0, 0.0).astype(BF16)
         total = total + 16.0 * jnp.dot(high, pick, preferred_element_type=F32)
         total = total + jnp.dot(low, pick, preferred_element_type=F32)
-    code = (total + 0.5).astype(jnp.int32)
-    offset = code >> 6
-    slot = code & 63
-    step_x = jnp.where(offset >= 18, 1, jnp.where(offset >= 9, 0, -1))
-    rest = offset - 9 * (step_x + 1)
-    step_y = jnp.where(rest >= 6, 1, jnp.where(rest >= 3, 0, -1))
-    step_z = rest - 3 * (step_y + 1) - 1
-    block = lax.broadcasted_iota(jnp.int32, (NEIGH, ATOMS), 1) // slots
-    level = block + step_z
-    outside = jnp.where((level < 0) | (level > 1), 1, 0)
-    chunk = place_column(step_x, step_y, outside, paired)
-    target = chunk * ATOMS + (level & 1) * slots + slot
-    code_ref[0] = target
-    code_ref[1] = step_x
-    code_ref[2] = step_y
-    code_ref[3] = step_z
-
-    pad_ref[...] = jnp.zeros(pad_ref.shape, F32)
-    pad_ref[0:8, :] = radial_ref[...].astype(F32)
-    pad_ref[8 : 8 + neighbor_ref.shape[0], :] = neighbor_ref[...].astype(F32)
-    pad_ref[16 : 16 + center_ref.shape[0], :] = center_ref[...].astype(F32)
-    wcat_ref[...] = pad_ref[...].T[:, :32].astype(BF16)
-    mixt_ref[...] = mix_ref[...].astype(F32).T.astype(BF16)
-    envt_ref[...] = env_ref[...].astype(F32).T.astype(BF16)
-    secondt_ref[...] = second_ref[...].astype(F32).T.astype(BF16)
-    for part in range(3):
-        span = slice(part * ATOMS, (part + 1) * ATOMS)
-        updt_ref[:, span] = upd_ref[span, :].astype(F32).T.astype(BF16)
-    rocol_ref[...] = jnp.broadcast_to(readout_ref[...], (ATOMS, ATOMS)).T
-
-    atom = lax.broadcasted_iota(jnp.int32, (ATOMS, ATOMS), 0)
-    for k in range(NEIGH):
-        aim = jnp.broadcast_to(target[k : k + 1, :], (ATOMS, ATOMS)) - atom
-
-        def fill(c, carry, k=k, aim=aim):
-            rows = pl.ds(pl.multiple_of(c * ATOMS, ATOMS), ATOMS)
-            hit = jnp.where(aim == c * ATOMS, 1.0, 0.0)
-            onehot_ref[rows, k * ATOMS : (k + 1) * ATOMS] = hit.astype(BF16)
-            return carry
-
-        lax.fori_loop(0, CHUNKS, fill, 0)
+    return (total + 0.5).astype(jnp.int32)
 
 
 def sigmoid(v):
@@ -249,27 +256,46 @@
 PIECE = (0, 1, 1, 1, 2, 2, 2, 2, 2)
 
 
-def forward_kernel(parts, order, *refs):
-    atoms = [(refs[array], row) for array, row in order]
+def forward_kernel(parts, direct, *refs):
+    tables = refs[:parts]
     (
-        code_ref, wcat_ref, mixt_ref, envt_ref, updt_ref,
-        table_ref, edge_ref, dsb_ref, dsl_ref, dse_ref, env_ref, v_ref, geo_ref, yb_ref, inv_ref, lat_ref,
+        nb_ref, center_ref, neighbor_ref, radial_ref, mix_ref, envw_ref, upd_ref,
+        table_ref, code_ref, edge_ref, dsb_ref, dsl_ref, dse_ref, env_ref, v_ref, geo_ref,
+        yb_ref, inv_ref, lat_ref, pad_ref,
     ) = refs[parts:]
-    home_ref, home = atoms[8]
-    target = code_ref[0]
-    chunk = target >> 7
-    lane = target & 127
+    pad_ref[...] = jnp.zeros(pad_ref.shape, F32)
+    pad_ref[0:8, :] = radial_ref[...].astype(F32)
+    pad_ref[8 : 8 + neighbor_ref.shape[0], :] = neighbor_ref[...].astype(F32)
+    pad_ref[16 : 16 + center_ref.shape[0], :] = center_ref[...].astype(F32)
+    wcat = pad_ref[...].T[:, :32].astype(BF16)
+    mixt = mix_ref[...].astype(F32).T.astype(BF16)
+    envt = envw_ref[...].astype(F32).T.astype(BF16)
+    updt = [upd_ref[p * ATOMS : (p + 1) * ATOMS, :].astype(F32).T.astype(BF16) for p in range(3)]
+    updt = jnp.concatenate(updt, axis=1)
+
+    code = listed_codes(nb_ref)
+    code_ref[...] = code
+    step_x, step_y, step_z, outside, lane = decode(code, ATOMS // 2)
+    spot = outside * 9 + step_y * 3 + step_x + 4
+
+    def chunk_at(far, dx, dy):
+        if direct:
+            return tables[0][owner_at(dx, dy, far)]
+        return tables[far][(0, 2, 1)[dy + 1] * 3 + (0, 2, 1)[dx + 1]]
+
     found = [jnp.zeros((NEIGH, ATOMS), F32) for _ in range(4)]
-    for c in range(CHUNKS):
-        ref, at = atoms[c]
-        hit = chunk == c
-        for f in range(4):
-            row = jnp.broadcast_to(ref[at, f : f + 1, :], (NEIGH, ATOMS))
-            value = jnp.take_along_axis(row, lane, axis=1)
-            found[f] = jnp.where(hit, value, found[f])
+    for far in range(2):
+        for dy in (-1, 0, 1):
+            for dx in (-1, 0, 1):
+                hit = spot == far * 9 + dy * 3 + dx + 4
+                rows = chunk_at(far, dx, dy)
+                for f in range(4):
+                    row = jnp.broadcast_to(rows[f : f + 1, :], (NEIGH, ATOMS))
+                    found[f] = jnp.where(hit, jnp.take_along_axis(row, lane, axis=1), found[f])
+    home = chunk_at(0, 0, 0)
     d = [
-        code_ref[1 + c].astype(F32) + (found[c] - jnp.broadcast_to(home_ref[home, c : c + 1, :], (NEIGH, ATOMS)))
-        for c in range(3)
+        step.astype(F32) + (found[c] - jnp.broadcast_to(home[c : c + 1, :], (NEIGH, ATOMS)))
+        for c, step in enumerate((step_x, step_y, step_z))
     ]
     r = jnp.sqrt(d[0] * d[0] + d[1] * d[1] + d[2] * d[2])
     ux, uy, uz = d[0] / r, d[1] / r, d[2] / r
@@ -280,7 +306,7 @@
     spread_rows(yb_ref, angular_rows(ux, uy, uz))
 
     kind = lax.broadcasted_iota(jnp.int32, (8, ATOMS), 0).astype(F32)
-    center_hot = jnp.where(jnp.broadcast_to(home_ref[home, 3:4, :], (8, ATOMS)) == kind, 1.0, 0.0)
+    center_hot = jnp.where(jnp.broadcast_to(home[3:4, :], (8, ATOMS)) == kind, 1.0, 0.0)
     zero = jnp.zeros((8, ATOMS), F32)
     columns = []
     for k in range(NEIGH):
@@ -291,12 +317,12 @@
         span = slice(j * TILE, (j + 1) * TILE)
         per = TILE // ATOMS
         x = jnp.concatenate(columns[j * per : (j + 1) * per], axis=1)
-        act, ds = silu_pair(jnp.dot(wcat_ref[...], x, preferred_element_type=F32))
+        act, ds = silu_pair(jnp.dot(wcat, x, preferred_element_type=F32))
         dsb_ref[:, span] = ds
-        latent, ds = silu_pair(jnp.dot(mixt_ref[...], act.astype(BF16), preferred_element_type=F32))
+        latent, ds = silu_pair(jnp.dot(mixt, act.astype(BF16), preferred_element_type=F32))
         dsl_ref[:, span] = ds
         lat_ref[:, span] = latent
-        env_ref[:, span] = jnp.dot(envt_ref[...], latent.astype(BF16), preferred_element_type=F32)
+        env_ref[:, span] = jnp.dot(envt, latent.astype(BF16), preferred_element_type=F32)
     for t in range(8):
         halves = []
         for h in range(2):
@@ -324,7 +350,7 @@
     mean = jnp.zeros((ATOMS, ATOMS), F32)
     for j in range(EDGES // TILE):
         span = slice(j * TILE, (j + 1) * TILE)
-        update = jnp.dot(updt_ref[...], inv_ref[:, span], preferred_element_type=F32)
+        update = jnp.dot(updt, inv_ref[:, span], preferred_element_type=F32)
         edge, ds = silu_pair(lat_ref[:, span] + update)
         edge_ref[:, span] = edge
         dse_ref[:, span] = ds
@@ -354,9 +380,7 @@
         grad_edge_ref[:, span] = grad_prod * other
         grad_ref[:, span] = (grad_prod * edge).astype(BF16)
     energy = jnp.sum(total * rocol, axis=0, keepdims=True)
-    slots = energy_ref.shape[-1]
-    for block in range(2):
-        energy_ref[0, 0, block : block + 1, :] = energy[:, block * slots : (block + 1) * slots]
+    energy_ref[...] = energy
     grad = grad_ref[...]
     for c in range(CHUNKS):
         rows = slice(c * ATOMS, (c + 1) * ATOMS)
@@ -368,10 +392,11 @@
 
 
 def backward_kernel(
-    owned_ref, grad_edge_ref, dse_ref, dsl_ref, dsb_ref, env_ref, v_ref, geo_ref, onehot_ref,
-    upd_ref, envw_ref, mix_ref, radial_ref,
-    own_ref, other_ref, yb_ref, dinv_ref, denv_ref, dlat_ref, part_ref, force_ref,
+    direct, owned_ref, energy_ref, grad_edge_ref, dse_ref, dsl_ref, dsb_ref, env_ref, v_ref, geo_ref, onehot_ref,
+    upd_ref, envw_ref, mix_ref, radial_ref, *refs,
 ):
+    outs = refs[: 1 if direct else 2]
+    yb_ref, dinv_ref, denv_ref, dlat_ref, part_ref, force_ref = refs[len(outs) :]
     r, ux, uy, uz = (geo_ref[i] for i in range(4))
     angular = angular_rows(ux, uy, uz)
     spread_rows(yb_ref, angular)
@@ -447,26 +472,31 @@
         rows = [h[k : k + 1, :] for h in high] + [zero] * 5 + [q[k : k + 1, :] for q in low] + [zero] * 5
         force_ref[:, k * ATOMS : (k + 1) * ATOMS] = jnp.concatenate(rows, axis=0).astype(BF16)
     force = force_ref[...]
-    center = jnp.concatenate([jnp.sum(p, axis=0, keepdims=True) for p in pull] + [zero] * 5, axis=0)
+    center = jnp.concatenate([jnp.sum(p, axis=0, keepdims=True) for p in pull] + [-energy_ref[...]], axis=0)
+    if direct:
+        outs[0][...] = jnp.zeros(outs[0].shape, F32)
     for c in range(CHUNKS):
         rows = slice(c * ATOMS, (c + 1) * ATOMS)
         back = lax.dot_general(
             force, onehot_ref[rows, :], (((1,), (1,)), ((), ())), preferred_element_type=F32
         )
-        moved = back[:8] + back[8:]
+        moved = back[:4] + back[8:12]
         if c == 8:
             moved = moved - center
-        ref = own_ref if c < 9 else other_ref
-        ref[c % 9] = moved
-
-
-def finish_kernel(own_ref, out_ref):
-    slots = out_ref.shape[-1] // 3
+        if direct:
+            outs[0][owner_of_chunk(c)] = moved
+        else:
+            outs[c // 9][c % 9] = moved
+
+
+def finish_kernel(moved_ref, energy_ref, out_ref):
+    slots = energy_ref.shape[-1]
+    total = jnp.sum(moved_ref[...], axis=0)
     for block in range(2):
+        lanes = slice(block * slots, (block + 1) * slots)
+        energy_ref[0, 0, block : block + 1, :] = total[3:4, lanes]
         for c in range(3):
-            out_ref[0, 0, block : block + 1, c * slots : (c + 1) * slots] = -own_ref[
-                0, c : c + 1, block * slots : (block + 1) * slots
-            ]
+            out_ref[0, 0, block : block + 1, c * slots : (c + 1) * slots] = -total[c : c + 1, lanes]
 
 
 def call(kernel, outs, scratch=(), name=None, limit=24 << 20, place=pltpu.VMEM, cost=None):
@@ -496,66 +526,61 @@
     edges = (ATOMS, EDGES)
     square = (ATOMS, ATOMS)
     readout = readout.reshape(1, ATOMS)
-
-    def like(*arrays):
-        return [pltpu.VMEM(array.shape, array.dtype) for array in arrays]
-
-    halves = [positions, species]
-    if is_paired():
-        halves += [shifted(positions, "gz", 1), shifted(species, "gz", 1)]
-    (packed,) = call(
-        pack_kernel,
-        [((len(halves) // 2, 8, ATOMS), F32)],
-        name="pack",
+    direct = is_direct()
+    devices = 32 if direct else 1
+    (blank,) = call(
+        blank_kernel,
+        [((8, ATOMS), F32)],
+        name="blank",
         cost=pl.CostEstimate(flops=1 << 34, bytes_accessed=64 << 20, transcendentals=0),
-    )(*halves)
-    weights = (radial_weight, mix_weight, env_weight, update_weight, second_weight)
-    code, onehot, wcat, mixt, envt, updt, secondt, rocol, radial, mix, envw, upd, second = call(
-        functools.partial(prep_kernel, is_paired()),
+    )()
+    (packed,) = call(pack_kernel, [((devices, 4, ATOMS), F32)], name="pack")(blank, positions, species)
+    if direct:
+        listed = to_workers(neighbors)
+        tables = [lax.all_to_all(packed, EVERY, 0, 0, tiled=True)]
+    else:
+        listed = neighbors
+        tables, order = gather_halo(packed)
+    table, code, edge, dsb, dsl, dse, env, field, geo = call(
+        functools.partial(forward_kernel, len(tables), direct),
         [
-            ((4, NEIGH, ATOMS), jnp.int32), ((CHUNKS * ATOMS, EDGES), BF16), ((ATOMS, 32), BF16), (square, BF16),
-            (square, BF16), ((ATOMS, 3 * ATOMS), BF16), (square, BF16), (square, F32),
-        ]
-        + [(weight.shape, weight.dtype) for weight in weights],
-        like(neighbors, center_table, neighbor_table, readout)
-        + [pltpu.VMEM(square, F32), pltpu.SemaphoreType.DMA((9,))],
-        name="prep",
-        place=pltpu.HBM,
-        cost=pl.CostEstimate(flops=1 << 28, bytes_accessed=8 << 20, transcendentals=0),
-    )(
-        neighbors, center_table, neighbor_table, radial_weight, mix_weight, env_weight, update_weight,
-        second_weight, readout,
-    )
-    tables, order = gather_halo(packed, packed)
-    table, edge, dsb, dsl, dse, env, field, geo = call(
-        functools.partial(forward_kernel, len(tables), order),
+            ((1,) + square, BF16), ((NEIGH, ATOMS), jnp.int32), (edges, F32), (edges, F32), (edges, F32),
+            (edges, F32), (edges, F32), ((9,) + square, F32), ((4, NEIGH, ATOMS), F32),
+        ],
         [
-            ((1,) + square, BF16), (edges, F32), (edges, F32), (edges, F32), (edges, F32), (edges, F32),
-            ((9,) + square, F32), ((4, NEIGH, ATOMS), F32),
+            pltpu.VMEM((72, 8, ATOMS), F32), pltpu.VMEM((3 * ATOMS, EDGES), BF16), pltpu.VMEM(edges, F32),
+            pltpu.VMEM(square, F32),
         ],
-        [pltpu.VMEM((72, 8, ATOMS), F32), pltpu.VMEM((3 * ATOMS, EDGES), BF16), pltpu.VMEM(edges, F32)],
         name="forward",
-    )(*tables, code, wcat, mixt, envt, updt)
+    )(*tables, listed, center_table, neighbor_table, radial_weight, mix_weight, env_weight, update_weight)
+    onehot, secondt, rocol = call(
+        functools.partial(onehot_kernel, direct),
+        [((CHUNKS * ATOMS, EDGES), BF16), (square, BF16), (square, F32)],
+        name="onehot",
+        cost=pl.CostEstimate(flops=1 << 30, bytes_accessed=8 << 20, transcendentals=0),
+    )(code, second_weight, readout)
     tables, order = gather_halo(table)
     energy, grad_edge, back_own, back_other = call(
         functools.partial(second_kernel, len(tables), order),
-        [((1, 1, 2, slots), F32), (edges, F32), ((9,) + square, BF16), ((9,) + square, BF16)],
+        [((1, ATOMS), F32), (edges, F32), ((9,) + square, BF16), ((9,) + square, BF16)],
         [pltpu.VMEM(edges, BF16)],
         name="second",
-    )(*tables, onehot, edge, second, secondt, rocol)
+    )(*tables, onehot, edge, second_weight, secondt, rocol)
     owned = reduce_halo(back_own, back_other)
-    own, other = call(
-        backward_kernel,
-        [((9, 8, ATOMS), F32), ((9, 8, ATOMS), F32)],
+    moved = call(
+        functools.partial(backward_kernel, direct),
+        [((devices, 4, ATOMS), F32)] if direct else [((9, 4, ATOMS), F32)] * 2,
         [
             pltpu.VMEM((72, 8, ATOMS), F32), pltpu.VMEM((3 * ATOMS, EDGES), BF16), pltpu.VMEM(edges, BF16),
             pltpu.VMEM(edges, F32), pltpu.VMEM((72, 8, ATOMS), F32), pltpu.VMEM((16, EDGES), BF16),
         ],
         name="backward",
-    )(owned, grad_edge, dse, dsl, dsb, env, field, geo, onehot, upd, envw, mix, radial)
-    motion = reduce_halo(own, other)
-    (forces,) = call(finish_kernel, [((1, 1, 2, 3 * slots), F32)], name="finish")(motion)
-    return energy, forces
+    )(
+        owned, energy, grad_edge, dse, dsl, dsb, env, field, geo, onehot, update_weight, env_weight, mix_weight,
+        radial_weight,
+    )
+    moved = lax.all_to_all(moved[0], EVERY, 0, 0, tiled=True) if direct else reduce_halo(*moved)
+    return call(finish_kernel, [((1, 1, 2, slots), F32), ((1, 1, 2, 3 * slots), F32)], name="finish")(moved)
 
 
 def solution(mesh):

time: 68.5 us -> 63.1 us (0.921)
  starting transfers between devices: 31.9 us -> 18.8 us
  blocking collectives: 0 us -> 9.64 us
  waiting for transfers between devices: 21.5 us -> 19.9 us
  local copies, waits for them, and re-layouts: 1.44 us -> 0.66 us
    ppermute x16 -> x9, starting transfers between devices: 30.1 us -> 10.6 us  [permuted(): return lax.ppermute(value, EVERY, pairs)]
    all_to_all x0 -> x1, blocking collectives: none -> 9.64 us  [on_device(): lax.all_to_all(moved[0], EVERY, 0, 0, tiled=True)]
    all_to_all x0 -> x1, starting transfers between devices: none -> 7.3 us  [on_device(): tables = [lax.all_to_all(packed, EVERY, 0, 0, tiled=True)]]
    all_to_all x0 -> x1, waiting for transfers between devices: none -> 6.72 us  [on_device(): tables = [lax.all_to_all(packed, EVERY, 0, 0, tiled=True)]]
    ppermute x9 -> x4, waiting for transfers between devices: 8.55 us -> 3.54 us  [shifted(): lax.ppermute(value, axis, [(i, (i + step) % count) for i in range(count)])]
    ppermute x16 -> x9, waiting for transfers between devices: 13 us -> 9.61 us  [permuted(): return lax.ppermute(value, EVERY, pairs)]
    ppermute x9 -> x4, starting transfers between devices: 1.74 us -> 0.87 us  [shifted(): lax.ppermute(value, axis, [(i, (i + step) % count) for i in range(count)])]
    unnamed x23, local copies, waits for them, and re-layouts: 1.4 us -> 0.62 us
  transfers between devices with their start and end apart: 25 -> 14, of which waited for: 17 -> 10; matrix products, arithmetic and copies ran while one was open for 0% -> 0% of each run, Pallas kernels for 3% -> 2%
where the time goes in v3:
time: 63.1 us; the launch traced here: 62.9 us
  waiting for transfers between devices  19.9 us (32%)
  starting transfers between devices  18.8 us (30%)
  Pallas kernels  12.9 us (20%)
  blocking collectives  9.64 us (15%)
  between operations  0.9 us (1%)
  local copies, waits for them, and re-layouts  0.66 us (1%)
    pallas_call x7, Pallas kernels, run(): pl.pallas_call(kernel, out_shape=shapes, in_specs=[pl.BlockSpec(memory_sp...  12.9 us
    ppermute x9, starting transfers between devices, permuted(): return lax.ppermute(value, EVERY, pairs)  10.6 us
    all_to_all x1, blocking collectives, on_device(): lax.all_to_all(moved[0], EVERY, 0, 0, tiled=True)  9.64 us
    ppermute x9, waiting for transfers between devices, permuted(): return lax.ppermute(value, EVERY, pairs)  9.61 us
    all_to_all x1, starting transfers between devices, on_device(): tables = [lax.all_to_all(packed, EVERY, 0, 0, tiled=True)]  7.3 us
    all_to_all x1, waiting for transfers between devices, on_device(): tables = [lax.all_to_all(packed, EVERY, 0, 0, tiled=True)]  6.72 us
    ppermute x4, waiting for transfers between devices, shifted(): lax.ppermute(value, axis, [(i, (i + step) % count) for i in range(count)])  3.54 us
  transfers between devices with their start and end apart: 14, of which 10 were waited for; matrix products, arithmetic and copies ran while one was open for 0% of the time, Pallas kernels for 2%

profile of v3, /device:TPU:0, one launch (start us, length us, event | category | flops | bytes accessed | tf_op | source)
XLA Modules:
  0.0 62.9 jit_solution(14296741692353889504)
XLA Ops:
  1.3 0.8 %pack.1 = f32[32,4,128]{2,1,0:T(4,128)} custom-call(f32[8,128]{1,0:T(8,128)S(1)} %blank.1.blank_ref, f32[1,1,2,192]{3,2,1,0:T(2,128)S(1)} %copy-done.7, s32[1,1,2,64]{3,2,1,0:T(2,128)S(1)} %copy-done.8), custom_call_target="tpu_custom_call" | custom-call | tf_op jit(solution)/shard_map/pack/pallas_call | solution.py:507
  2.2 7.3 %all-to-all-start = ((f32[32,4,128]{2,1,0:T(4,128)}), f32[32,4,128]{2,1,0:T(4,128)S(1)}, u32[]{:S(2)}, u32[]{:S(2)}) async-start(f32[32,4,128]{2,1,0:T(4,128)} %pack.1), calls=%async_computation | async-start | bytes 131072 | tf_op jit(solution)/shard_map/all_to_all | solution.py:540
  9.5 0.7 %collective-permute-start = (s32[1,1,2,512]{3,2,1,0:T(2,128)S(1)}, s32[1,1,2,512]{3,2,1,0:T(2,128)S(1)}, u32[]{:S(2)}, u32[]{:S(2)}) collective-permute-start(s32[1,1,2,512]{3,2,1,0:T(2,128)S(1)} %copy-done.10), channel_id=1, source_target_pairs={{0,0},{1,1},{2,2},{3,3},{6,4},{7,5},{4,6},{5,7},{8,8},{9,9},{10,10... | collective-permute-start | bytes 12296 | tf_op jit(solution)/shard_map/ppermute | solution.py:56
  10.2 6.7 %all-to-all-done.refs_0_ = f32[32,4,128]{2,1,0:T(4,128)S(1)} async-done(((f32[32,4,128]{2,1,0:T(4,128)}), f32[32,4,128]{2,1,0:T(4,128)S(1)}, u32[]{:S(2)}, u32[]{:S(2)}) %all-to-all-start) | async-done | bytes 65568 | tf_op jit(solution)/shard_map/all_to_all | solution.py:540
  16.9 2.5 %forward.1 = (bf16[1,128,128]{2,1,0:T(8,128)(2,1)S(1)}, s32[8,128]{1,0:T(8,128)S(1)}, f32[128,1024]{1,0:T(8,128)S(1)}, f32[128,1024]{1,0:T(8,128)S(1)}, f32[128,...) custom-call(f32[32,4,128]{2,1,0:T(4,128)S(1)} %all-to-all-done.refs_, ...), custom_call_target="tpu_custom_call" | custom-call | tf_op jit(solution)/shard_map/forward/pallas_call | solution.py:507
  19.7 1.1 %collective-permute-done.1 = bf16[1,128,128]{2,1,0:T(8,128)(2,1)S(1)} collective-permute-done((bf16[1,128,128]{2,1,0:T(8,128)(2,1)S(1)}, bf16[1,128,128]{2,1,0:T(8,128)(2,1)S(1)}, u32[]{:S(2)}, u32[]{:S(2)}) %collective-permute-start.1) | collective-permute-done | bytes 32800 | tf_op jit(solution)/shard_map/ppermute | solution.py:34
  20.7 1.7 %collective-permute-start.5 = (bf16[2,128,128]{2,1,0:T(8,128)(2,1)S(1)}, bf16[2,128,128]{2,1,0:T(8,128)(2,1)S(1)}, u32[]{:S(2)}, u32[]{:S(2)}) collective-permute-start(bf16[2,128,128]{2,1,0:T(8,128)(2,1)S(1)} %constant_dynamic-update-slice_fusion.refs_4_), channel_id=1, source_target_pairs={{0,18},{1,21},{2,16},{3,23},{6,20},{7,19},{4,22},{5,17},{8,26},{9,... | collective-permute-start | bytes 196616 | tf_op jit(solution)/shard_map/ppermute | solution.py:56
  22.4 3.4 %collective-permute-start.4 = (bf16[2,128,128]{2,1,0:T(8,128)(2,1)S(1)}, bf16[2,128,128]{2,1,0:T(8,128)(2,1)S(1)}, u32[]{:S(2)}, u32[]{:S(2)}) collective-permute-start(bf16[2,128,128]{2,1,0:T(8,128)(2,1)S(1)} %constant_dynamic-update-slice_fusion.refs_4_), channel_id=1, source_target_pairs={{0,12},{1,11},{2,14},{3,9},{6,10},{7,13},{4,8},{5,15},{8,4},{9,3},... | collective-permute-start | bytes 196616 | tf_op jit(solution)/shard_map/ppermute | solution.py:56
  26.4 1.4 %collective-permute-done.5.refs_3_ = bf16[2,128,128]{2,1,0:T(8,128)(2,1)S(1)} collective-permute-done((bf16[2,128,128]{2,1,0:T(8,128)(2,1)S(1)}, bf16[2,128,128]{2,1,0:T(8,128)(2,1)S(1)}, u32[]{:S(2)}, u32[]{:S(2)}) %collective-permute-start.5) | collective-permute-done | bytes 65568 | tf_op jit(solution)/shard_map/ppermute | solution.py:56
  27.7 1.3 %collective-permute-done.4.refs_2_ = bf16[2,128,128]{2,1,0:T(8,128)(2,1)S(1)} collective-permute-done((bf16[2,128,128]{2,1,0:T(8,128)(2,1)S(1)}, bf16[2,128,128]{2,1,0:T(8,128)(2,1)S(1)}, u32[]{:S(2)}, u32[]{:S(2)}) %collective-permute-start.4) | collective-permute-done | bytes 65568 | tf_op jit(solution)/shard_map/ppermute | solution.py:56
  29.0 1.0 %collective-permute-done.3.refs_1_ = bf16[2,128,128]{2,1,0:T(8,128)(2,1)S(1)} collective-permute-done((bf16[2,128,128]{2,1,0:T(8,128)(2,1)S(1)}, bf16[2,128,128]{2,1,0:T(8,128)(2,1)S(1)}, u32[]{:S(2)}, u32[]{:S(2)}) %collective-permute-start.3) | collective-permute-done | bytes 65568 | tf_op jit(solution)/shard_map/ppermute | solution.py:56
  30.1 0.6 collective-permute-done.2.refs_0_
  30.8 1.6 %onehot.1 = (bf16[2304,1024]{1,0:T(8,128)(2,1)S(1)}, bf16[128,128]{1,0:T(8,128)(2,1)S(1)}, f32[128,128]{1,0:T(8,128)S(1)}) custom-call(s32[8,128]{1,0:T(8,128)S(1)} %get-tuple-element.19.code_ref, bf16[128,128]{1,0:T(8,128)(2,1)S(1)} %copy-done.3, f32[1,128]{1,0:T(1,128)S(1)} %bitcast.1), custom_call_target="tpu_custom_call" | custom-call | flops 1073741824 | bytes 8388608 | tf_op jit(solution)/shard_map/onehot/pallas_call | solution.py:507
  32.4 3.6 %second.1 = (f32[1,128]{1,0:T(1,128)S(1)}, f32[128,1024]{1,0:T(8,128)S(1)}, bf16[9,128,128]{2,1,0:T(8,128)(2,1)S(1)}, bf16[9,128,128]{2,1,0:T(8,128)(2,1)S(1)}) custom-call(bf16[2,128,128]{2,1,0:T(8,128)(2,1)S(1)} %collective-permute-done.2.refs_0_, bf16[2,128,128]{2,1,0:T(8,128)(2,1)S(1)} %collective-permute-done.3.refs_1_, ...), custom_call_target="tpu_custom_call" | custom-call | tf_op jit(solution)/shard_map/second/pallas_call | solution.py:507
  36.6 1.2 %collective-permute-done.7 = bf16[9,128,128]{2,1,0:T(8,128)(2,1)S(1)} collective-permute-done((bf16[9,128,128]{2,1,0:T(8,128)(2,1)S(1)}, bf16[9,128,128]{2,1,0:T(8,128)(2,1)S(1)}, u32[]{:S(2)}, u32[]{:S(2)}) %collective-permute-start.7) | collective-permute-done | bytes 294944 | tf_op jit(solution)/shard_map/ppermute | solution.py:34
  38.4 1.5 %collective-permute-start.11 = (bf16[2,128,128]{2,1,0:T(8,128)(2,1)S(1)}, bf16[2,128,128]{2,1,0:T(8,128)(2,1)S(1)}, u32[]{:S(2)}, u32[]{:S(2)}) collective-permute-start(bf16[2,128,128]{2,1,0:T(8,128)(2,1)S(1)} %get-tuple-element.37), channel_id=1, source_target_pairs={{0,18},{1,21},{2,16},{3,23},{6,20},{7,19},{4,22},{5,17},{8,26},{9,... | collective-permute-start | bytes 196616 | tf_op jit(solution)/shard_map/ppermute | solution.py:56
  39.9 1.2 %collective-permute-start.10 = (bf16[2,128,128]{2,1,0:T(8,128)(2,1)S(1)}, bf16[2,128,128]{2,1,0:T(8,128)(2,1)S(1)}, u32[]{:S(2)}, u32[]{:S(2)}) collective-permute-start(bf16[2,128,128]{2,1,0:T(8,128)(2,1)S(1)} %get-tuple-element.38), channel_id=1, source_target_pairs={{0,12},{1,11},{2,14},{3,9},{6,10},{7,13},{4,8},{5,15},{8,4},{9,3},... | collective-permute-start | bytes 196616 | tf_op jit(solution)/shard_map/ppermute | solution.py:56
  41.1 1.1 %collective-permute-start.9 = (bf16[2,128,128]{2,1,0:T(8,128)(2,1)S(1)}, bf16[2,128,128]{2,1,0:T(8,128)(2,1)S(1)}, u32[]{:S(2)}, u32[]{:S(2)}) collective-permute-start(bf16[2,128,128]{2,1,0:T(8,128)(2,1)S(1)} %get-tuple-element.39), channel_id=1, source_target_pairs={{0,4},{1,3},{2,6},{3,1},{6,2},{7,5},{4,0},{5,7},{8,12},{9,11},{10,... | collective-permute-start | bytes 196616 | tf_op jit(solution)/shard_map/ppermute | solution.py:56
  42.3 4.1 %collective-permute-done.11 = bf16[2,128,128]{2,1,0:T(8,128)(2,1)S(1)} collective-permute-done((bf16[2,128,128]{2,1,0:T(8,128)(2,1)S(1)}, bf16[2,128,128]{2,1,0:T(8,128)(2,1)S(1)}, u32[]{:S(2)}, u32[]{:S(2)}) %collective-permute-start.11) | collective-permute-done | bytes 65568 | tf_op jit(solution)/shard_map/ppermute | solution.py:56
  46.3 1.2 %collective-permute-done.10 = bf16[2,128,128]{2,1,0:T(8,128)(2,1)S(1)} collective-permute-done((bf16[2,128,128]{2,1,0:T(8,128)(2,1)S(1)}, bf16[2,128,128]{2,1,0:T(8,128)(2,1)S(1)}, u32[]{:S(2)}, u32[]{:S(2)}) %collective-permute-start.10) | collective-permute-done | bytes 65568 | tf_op jit(solution)/shard_map/ppermute | solution.py:56
  47.7 1.2 %collective-permute-done.12 = f32[1,128,128]{2,1,0:T(8,128)S(1)} collective-permute-done((f32[1,128,128]{2,1,0:T(8,128)S(1)}, f32[1,128,128]{2,1,0:T(8,128)S(1)}, u32[]{:S(2)}, u32[]{:S(2)}) %collective-permute-start.12) | collective-permute-done | bytes 65568 | tf_op jit(solution)/shard_map/ppermute | solution.py:34
  48.9 3.6 %backward.1 = f32[32,4,128]{2,1,0:T(4,128)S(1)} custom-call(f32[1,128,128]{2,1,0:T(8,128)S(1)} %fusion.owned_ref, f32[1,128]{1,0:T(1,128)S(1)} %get-tuple-element.26.energy_ref, f32[128,1024]{1,0:T(8,128)S(1)} %get-tuple-element.27.grad_edge_ref, f32[128,1024]{1,0:T(8,128)S(1)} %get-tuple-element.28.dse_ref, f32[128,1024]{1,0:T(8,128)S(1)} %get-tuple-element.29.dsl_ref, ...), custom_call_target="tpu_custom_call" | custom-call | tf_op jit(solution)/shard_map/backward/pallas_call | solution.py:507
  52.5 9.6 %all_to_all.10.moved_ref = f32[32,4,128]{2,1,0:T(4,128)S(1)} all-to-all(f32[32,4,128]{2,1,0:T(4,128)S(1)} %backward.1), channel_id=1, replica_groups=mesh['gx'=4,'gy'=4,'gz'=2] {'gx','gy','gz'}, dimensions={0} | all-to-all | bytes 131072 | tf_op jit(solution)/shard_map/all_to_all | solution.py:582
  62.2 0.7 %finish.1 = (f32[1,1,2,64]{3,2,1,0:T(2,128)}, f32[1,1,2,192]{3,2,1,0:T(2,128)}) custom-call(f32[32,4,128]{2,1,0:T(4,128)S(1)} %all_to_all.10.moved_ref), custom_call_target="tpu_custom_call" | custom-call | tf_op jit(solution)/shard_map/finish/pallas_call | solution.py:507
  (42 shorter events, 2.8 us)
Async XLA Ops:
  0.6 0.7 %copy-start.7 = (f32[1,1,2,192]{3,2,1,0:T(2,128)S(1)}, f32[1,1,2,192]{3,2,1,0:T(2,128)}, u32[]{:S(2)}) copy-start(f32[1,1,2,192]{3,2,1,0:T(2,128)} %pos_ref.1) | copy-start | bytes 4612
  0.7 8.8 %copy-start.10 = (s32[1,1,2,512]{3,2,1,0:T(2,128)S(1)}, s32[1,1,2,512]{3,2,1,0:T(2,128)}, u32[]{:S(2)}) copy-start(s32[1,1,2,512]{3,2,1,0:T(2,128)} %param.13) | copy-start | bytes 12292
  0.7 16.2 %copy-start = (bf16[384,128]{1,0:T(8,128)(2,1)S(1)}, bf16[384,128]{1,0:T(8,128)(2,1)}, u32[]{:S(2)}) copy-start(bf16[384,128]{1,0:T(8,128)(2,1)} %upd_ref.1) | copy-start | bytes 294916
  0.7 16.2 %copy-start.2 = (bf16[128,128]{1,0:T(8,128)(2,1)S(1)}, bf16[128,128]{1,0:T(8,128)(2,1)}, u32[]{:S(2)}) copy-start(bf16[128,128]{1,0:T(8,128)(2,1)} %envw_ref.1) | copy-start | bytes 98308
  0.7 16.2 %copy-start.1 = (bf16[128,128]{1,0:T(8,128)(2,1)S(1)}, bf16[128,128]{1,0:T(8,128)(2,1)}, u32[]{:S(2)}) copy-start(bf16[128,128]{1,0:T(8,128)(2,1)} %mix_ref.1) | copy-start | bytes 98308
  0.7 16.2 %copy-start.4 = (bf16[8,128]{1,0:T(8,128)(2,1)S(1)}, bf16[8,128]{1,0:T(8,128)(2,1)}, u32[]{:S(2)}) copy-start(bf16[8,128]{1,0:T(8,128)(2,1)} %radial_ref.1) | copy-start | bytes 6148
  0.7 16.2 %copy-start.6 = (bf16[5,128]{1,0:T(8,128)(2,1)S(1)}, bf16[5,128]{1,0:T(8,128)(2,1)}, u32[]{:S(2)}) copy-start(bf16[5,128]{1,0:T(8,128)(2,1)} %refs_3_.1) | copy-start | bytes 3844
  0.7 16.2 %copy-start.5 = (bf16[5,128]{1,0:T(8,128)(2,1)S(1)}, bf16[5,128]{1,0:T(8,128)(2,1)}, u32[]{:S(2)}) copy-start(bf16[5,128]{1,0:T(8,128)(2,1)} %refs_2_.1) | copy-start | bytes 3844
  0.7 30.1 %copy-start.3 = (bf16[128,128]{1,0:T(8,128)(2,1)S(1)}, bf16[128,128]{1,0:T(8,128)(2,1)}, u32[]{:S(2)}) copy-start(bf16[128,128]{1,0:T(8,128)(2,1)} %refs_8_.1) | copy-start | bytes 98308
  0.7 30.1 %copy-start.9 = (f32[128]{0:T(128)S(1)}, f32[128]{0:T(128)}, u32[]{:S(2)}) copy-start(f32[128]{0:T(128)} %param.21) | copy-start | bytes 1540
  2.2 14.7 %all-to-all-start = ((f32[32,4,128]{2,1,0:T(4,128)}), f32[32,4,128]{2,1,0:T(4,128)S(1)}, u32[]{:S(2)}, u32[]{:S(2)}) async-start(f32[32,4,128]{2,1,0:T(4,128)} %pack.1), calls=%async_computation | async-start | bytes 131072 | tf_op jit(solution)/shard_map/all_to_all | solution.py:540
  9.5 0.7 %collective-permute-start = (s32[1,1,2,512]{3,2,1,0:T(2,128)S(1)}, s32[1,1,2,512]{3,2,1,0:T(2,128)S(1)}, u32[]{:S(2)}, u32[]{:S(2)}) collective-permute-start(s32[1,1,2,512]{3,2,1,0:T(2,128)S(1)} %copy-done.10), channel_id=1, source_target_pairs={{0,0},{1,1},{2,2},{3,3},{6,4},{7,5},{4,6},{5,7},{8,8},{9,9},{10,10... | collective-permute-start | bytes 12296 | tf_op jit(solution)/shard_map/ppermute | solution.py:56
  19.5 1.3 %collective-permute-start.1 = (bf16[1,128,128]{2,1,0:T(8,128)(2,1)S(1)}, bf16[1,128,128]{2,1,0:T(8,128)(2,1)S(1)}, u32[]{:S(2)}, u32[]{:S(2)}) collective-permute-start(bf16[1,128,128]{2,1,0:T(8,128)(2,1)S(1)} %get-tuple-element.18), channel_id=1, source_target_pairs={{0,1},{1,0},{2,3},{3,2},{4,5},{5,4},{6,7},{7,6},{8,9},{9,8},{10,11... | collective-permute-start | bytes 98312 | tf_op jit(solution)/shard_map/ppermute | solution.py:34
  20.7 7.0 %collective-permute-start.5 = (bf16[2,128,128]{2,1,0:T(8,128)(2,1)S(1)}, bf16[2,128,128]{2,1,0:T(8,128)(2,1)S(1)}, u32[]{:S(2)}, u32[]{:S(2)}) collective-permute-start(bf16[2,128,128]{2,1,0:T(8,128)(2,1)S(1)} %constant_dynamic-update-slice_fusion.refs_4_), channel_id=1, source_target_pairs={{0,18},{1,21},{2,16},{3,23},{6,20},{7,19},{4,22},{5,17},{8,26},{9,... | collective-permute-start | bytes 196616 | tf_op jit(solution)/shard_map/ppermute | solution.py:56
  22.4 6.6 %collective-permute-start.4 = (bf16[2,128,128]{2,1,0:T(8,128)(2,1)S(1)}, bf16[2,128,128]{2,1,0:T(8,128)(2,1)S(1)}, u32[]{:S(2)}, u32[]{:S(2)}) collective-permute-start(bf16[2,128,128]{2,1,0:T(8,128)(2,1)S(1)} %constant_dynamic-update-slice_fusion.refs_4_), channel_id=1, source_target_pairs={{0,12},{1,11},{2,14},{3,9},{6,10},{7,13},{4,8},{5,15},{8,4},{9,3},... | collective-permute-start | bytes 196616 | tf_op jit(solution)/shard_map/ppermute | solution.py:56
  25.8 4.3 %collective-permute-start.3 = (bf16[2,128,128]{2,1,0:T(8,128)(2,1)S(1)}, bf16[2,128,128]{2,1,0:T(8,128)(2,1)S(1)}, u32[]{:S(2)}, u32[]{:S(2)}) collective-permute-start(bf16[2,128,128]{2,1,0:T(8,128)(2,1)S(1)} %constant_dynamic-update-slice_fusion.refs_4_), channel_id=1, source_target_pairs={{0,4},{1,3},{2,6},{3,1},{6,2},{7,5},{4,0},{5,7},{8,12},{9,11},{10,... | collective-permute-start | bytes 196616 | tf_op jit(solution)/shard_map/ppermute | solution.py:56
  25.8 4.9 %collective-permute-start.2 = (bf16[2,128,128]{2,1,0:T(8,128)(2,1)S(1)}, bf16[2,128,128]{2,1,0:T(8,128)(2,1)S(1)}, u32[]{:S(2)}, u32[]{:S(2)}) collective-permute-start(bf16[2,128,128]{2,1,0:T(8,128)(2,1)S(1)} %constant_dynamic-update-slice_fusion.refs_4_), channel_id=1, source_target_pairs={{0,8},{1,17},{2,10},{3,19},{6,14},{7,23},{4,12},{5,21},{8,0},{9,25... | collective-permute-start | bytes 196616 | tf_op jit(solution)/shard_map/ppermute | solution.py:56
  30.7 1.7 %collective-permute-start.6 = (bf16[8,128,128]{2,1,0:T(8,128)(2,1)S(1)}, bf16[8,128,128]{2,1,0:T(8,128)(2,1)S(1)}, u32[]{:S(2)}, u32[]{:S(2)}) collective-permute-start(bf16[8,128,128]{2,1,0:T(8,128)(2,1)S(1)} %pad_maximum_fusion), channel_id=1, source_target_pairs={{0,1},{1,0},{2,3},{3,2},{4,5},{5,4},{6,7},{7,6},{8,9},{9,8},{10,11... | collective-permute-start | bytes 786440 | tf_op jit(solution)/shard_map/ppermute | solution.py:34
  36.0 1.8 %collective-permute-start.7 = (bf16[9,128,128]{2,1,0:T(8,128)(2,1)S(1)}, bf16[9,128,128]{2,1,0:T(8,128)(2,1)S(1)}, u32[]{:S(2)}, u32[]{:S(2)}) collective-permute-start(bf16[9,128,128]{2,1,0:T(8,128)(2,1)S(1)} %get-tuple-element.25), channel_id=1, source_target_pairs={{0,1},{1,0},{2,3},{3,2},{4,5},{5,4},{6,7},{7,6},{8,9},{9,8},{10,11... | collective-permute-start | bytes 884744 | tf_op jit(solution)/shard_map/ppermute | solution.py:34
  37.9 4.4 %collective-permute-start.8 = (bf16[2,128,128]{2,1,0:T(8,128)(2,1)S(1)}, bf16[2,128,128]{2,1,0:T(8,128)(2,1)S(1)}, u32[]{:S(2)}, u32[]{:S(2)}) collective-permute-start(bf16[2,128,128]{2,1,0:T(8,128)(2,1)S(1)} %get-tuple-element.36), channel_id=1, source_target_pairs={{0,8},{1,17},{2,10},{3,19},{6,14},{7,23},{4,12},{5,21},{8,0},{9,25... | collective-permute-start | bytes 196616 | tf_op jit(solution)/shard_map/ppermute | solution.py:56
  38.4 8.0 %collective-permute-start.11 = (bf16[2,128,128]{2,1,0:T(8,128)(2,1)S(1)}, bf16[2,128,128]{2,1,0:T(8,128)(2,1)S(1)}, u32[]{:S(2)}, u32[]{:S(2)}) collective-permute-start(bf16[2,128,128]{2,1,0:T(8,128)(2,1)S(1)} %get-tuple-element.37), channel_id=1, source_target_pairs={{0,18},{1,21},{2,16},{3,23},{6,20},{7,19},{4,22},{5,17},{8,26},{9,... | collective-permute-start | bytes 196616 | tf_op jit(solution)/shard_map/ppermute | solution.py:56
  39.9 7.6 %collective-permute-start.10 = (bf16[2,128,128]{2,1,0:T(8,128)(2,1)S(1)}, bf16[2,128,128]{2,1,0:T(8,128)(2,1)S(1)}, u32[]{:S(2)}, u32[]{:S(2)}) collective-permute-start(bf16[2,128,128]{2,1,0:T(8,128)(2,1)S(1)} %get-tuple-element.38), channel_id=1, source_target_pairs={{0,12},{1,11},{2,14},{3,9},{6,10},{7,13},{4,8},{5,15},{8,4},{9,3},... | collective-permute-start | bytes 196616 | tf_op jit(solution)/shard_map/ppermute | solution.py:56
  41.1 6.4 %collective-permute-start.9 = (bf16[2,128,128]{2,1,0:T(8,128)(2,1)S(1)}, bf16[2,128,128]{2,1,0:T(8,128)(2,1)S(1)}, u32[]{:S(2)}, u32[]{:S(2)}) collective-permute-start(bf16[2,128,128]{2,1,0:T(8,128)(2,1)S(1)} %get-tuple-element.39), channel_id=1, source_target_pairs={{0,4},{1,3},{2,6},{3,1},{6,2},{7,5},{4,0},{5,7},{8,12},{9,11},{10,... | collective-permute-start | bytes 196616 | tf_op jit(solution)/shard_map/ppermute | solution.py:56
  47.6 1.3 %collective-permute-start.12 = (f32[1,128,128]{2,1,0:T(8,128)S(1)}, f32[1,128,128]{2,1,0:T(8,128)S(1)}, u32[]{:S(2)}, u32[]{:S(2)}) collective-permute-start(f32[1,128,128]{2,1,0:T(8,128)S(1)} %slice.38), channel_id=1, source_target_pairs={{0,1},{1,0},{2,3},{3,2},{4,5},{5,4},{6,7},{7,6},{8,9},{9,8},{10,11... | collective-permute-start | bytes 196616 | tf_op jit(solution)/shard_map/ppermute | solution.py:34
  (1 other events, 0.7 us)

commit v4 on v3

--- a/solution.py
+++ b/solution.py
@@ -46,24 +46,15 @@
     return (x * 4 + y) * 2 + core
 
 
-def permuted(value, target):
+def swapped(value, slot):
     pairs = []
     for x in range(4):
         for y in range(4):
             for core in range(2):
-                to_x, to_y = target(x, y, core)
+                way_x, way_y = ROUTES[core][slot]
+                to_x, to_y = partner(x, way_x), partner(y, way_y)
                 pairs.append((number(RING[x], RING[y], core), number(RING[to_x], RING[to_y], core)))
     return lax.ppermute(value, EVERY, pairs)
-
-
-def swapped(value, slot):
-    return permuted(
-        value, lambda x, y, core: (partner(x, ROUTES[core][slot][0]), partner(y, ROUTES[core][slot][1]))
-    )
-
-
-def to_workers(value):
-    return permuted(value, lambda x, y, core: (RING[x], RING[y]))
 
 
 def gather_halo(chunk):
@@ -172,14 +163,19 @@
     out_ref[...] = jnp.zeros(out_ref.shape, F32)
 
 
-def pack_kernel(blank_ref, pos_ref, spec_ref, out_ref):
+def pack_kernel(blank_ref, pos_ref, spec_ref, nb_ref, out_ref):
     slots = spec_ref.shape[-1]
-    for chunk in range(out_ref.shape[0]):
-        for block in range(2):
-            lanes = slice(block * slots, (block + 1) * slots)
-            for c in range(3):
-                out_ref[chunk, c : c + 1, lanes] = pos_ref[0, 0, block : block + 1, c * slots : (c + 1) * slots]
-            out_ref[chunk, 3:4, lanes] = spec_ref[0, 0, block : block + 1, :].astype(F32)
+    half = nb_ref.shape[-1] // 2
+    for block in range(2):
+        lanes = slice(block * slots, (block + 1) * slots)
+        for c in range(3):
+            out_ref[0, c : c + 1, lanes] = pos_ref[0, 0, block : block + 1, c * slots : (c + 1) * slots]
+        out_ref[0, 3:4, lanes] = spec_ref[0, 0, block : block + 1, :].astype(F32)
+        for part in range(half // ATOMS):
+            first = nb_ref[0, 0, block : block + 1, part * ATOMS : (part + 1) * ATOMS]
+            second = nb_ref[0, 0, block : block + 1, half + part * ATOMS : half + (part + 1) * ATOMS]
+            row = 4 + block * 2 + part
+            out_ref[0, row : row + 1, :] = (first * 2048 + second).astype(F32)
 
 
 def onehot_kernel(direct, code_ref, second_ref, readout_ref, onehot_ref, secondt_ref, rocol_ref):
@@ -200,8 +196,10 @@
         lax.fori_loop(0, CHUNKS, fill, 0)
 
 
-def listed_codes(nb_ref):
-    width = nb_ref.shape[-1]
+def listed_codes(words):
+    words = words.astype(jnp.int32)
+    first, second = words >> 11, words & 2047
+    width = 4 * ATOMS
     slots = width // NEIGH
     lane = lax.broadcasted_iota(jnp.int32, (NEIGH, width), 1)
     row = lax.broadcasted_iota(jnp.int32, (NEIGH, width), 0)
@@ -210,7 +208,8 @@
     column = lax.broadcasted_iota(jnp.int32, (width, ATOMS), 1)
     total = jnp.zeros((NEIGH, ATOMS), F32)
     for block in range(2):
-        listed = jnp.broadcast_to(nb_ref[0, 0, block : block + 1, :], (NEIGH, width))
+        pieces = [part[2 * block + i : 2 * block + i + 1, :] for part in (first, second) for i in range(2)]
+        listed = jnp.broadcast_to(jnp.concatenate(pieces, axis=1), (NEIGH, width))
         listed = jnp.where(mine, listed, 0)
         high = (listed >> 4).astype(F32).astype(BF16)
         low = (listed & 15).astype(F32).astype(BF16)
@@ -259,7 +258,7 @@
 def forward_kernel(parts, direct, *refs):
     tables = refs[:parts]
     (
-        nb_ref, center_ref, neighbor_ref, radial_ref, mix_ref, envw_ref, upd_ref,
+        center_ref, neighbor_ref, radial_ref, mix_ref, envw_ref, upd_ref,
         table_ref, code_ref, edge_ref, dsb_ref, dsl_ref, dse_ref, env_ref, v_ref, geo_ref,
         yb_ref, inv_ref, lat_ref, pad_ref,
     ) = refs[parts:]
@@ -273,16 +272,16 @@
     updt = [upd_ref[p * ATOMS : (p + 1) * ATOMS, :].astype(F32).T.astype(BF16) for p in range(3)]
     updt = jnp.concatenate(updt, axis=1)
 
-    code = listed_codes(nb_ref)
-    code_ref[...] = code
-    step_x, step_y, step_z, outside, lane = decode(code, ATOMS // 2)
-    spot = outside * 9 + step_y * 3 + step_x + 4
-
     def chunk_at(far, dx, dy):
         if direct:
             return tables[0][owner_at(dx, dy, far)]
         return tables[far][(0, 2, 1)[dy + 1] * 3 + (0, 2, 1)[dx + 1]]
 
+    home = chunk_at(0, 0, 0)
+    code = listed_codes(home[4:8, :])
+    code_ref[...] = code
+    step_x, step_y, step_z, outside, lane = decode(code, ATOMS // 2)
+    spot = outside * 9 + step_y * 3 + step_x + 4
     found = [jnp.zeros((NEIGH, ATOMS), F32) for _ in range(4)]
     for far in range(2):
         for dy in (-1, 0, 1):
@@ -292,7 +291,6 @@
                 for f in range(4):
                     row = jnp.broadcast_to(rows[f : f + 1, :], (NEIGH, ATOMS))
                     found[f] = jnp.where(hit, jnp.take_along_axis(row, lane, axis=1), found[f])
-    home = chunk_at(0, 0, 0)
     d = [
         step.astype(F32) + (found[c] - jnp.broadcast_to(home[c : c + 1, :], (NEIGH, ATOMS)))
         for c, step in enumerate((step_x, step_y, step_z))
@@ -527,19 +525,18 @@
     square = (ATOMS, ATOMS)
     readout = readout.reshape(1, ATOMS)
     direct = is_direct()
-    devices = 32 if direct else 1
+    devices = 32
     (blank,) = call(
         blank_kernel,
         [((8, ATOMS), F32)],
         name="blank",
         cost=pl.CostEstimate(flops=1 << 34, bytes_accessed=64 << 20, transcendentals=0),
     )()
-    (packed,) = call(pack_kernel, [((devices, 4, ATOMS), F32)], name="pack")(blank, positions, species)
+    (packed,) = call(pack_kernel, [((1, 8, ATOMS), F32)], name="pack")(blank, positions, species, neighbors)
     if direct:
-        listed = to_workers(neighbors)
-        tables = [lax.all_to_all(packed, EVERY, 0, 0, tiled=True)]
+        copies = jnp.broadcast_to(packed, (devices, 8, ATOMS))
+        tables = [lax.all_to_all(copies, EVERY, 0, 0, tiled=True)]
     else:
-        listed = neighbors
         tables, order = gather_halo(packed)
     table, code, edge, dsb, dsl, dse, env, field, geo = call(
         functools.partial(forward_kernel, len(tables), direct),
@@ -552,7 +549,7 @@
             pltpu.VMEM(square, F32),
         ],
         name="forward",
-    )(*tables, listed, center_table, neighbor_table, radial_weight, mix_weight, env_weight, update_weight)
+    )(*tables, center_table, neighbor_table, radial_weight, mix_weight, env_weight, update_weight)
     onehot, secondt, rocol = call(
         functools.partial(onehot_kernel, direct),
         [((CHUNKS * ATOMS, EDGES), BF16), (square, BF16), (square, F32)],

time: 63.1 us -> 62 us (0.983)
  blocking collectives: 9.64 us -> 26.3 us
  waiting for transfers between devices: 19.9 us -> 10.7 us
  starting transfers between devices: 18.8 us -> 11 us
  Pallas kernels: 12.9 us -> 12 us
    all_to_all x0 -> x1, blocking collectives: none -> 15.3 us  [on_device(): tables = [lax.all_to_all(copies, EVERY, 0, 0, tiled=True)]]
    all_to_all x1 -> x0, starting transfers between devices: 7.3 us -> none  [on_device(): tables = [lax.all_to_all(packed, EVERY, 0, 0, tiled=True)]]
    all_to_all x1 -> x0, waiting for transfers between devices: 6.72 us -> none  [on_device(): tables = [lax.all_to_all(packed, EVERY, 0, 0, tiled=True)]]
    ppermute x9 -> x8, waiting for transfers between devices: 9.61 us -> 7.31 us  [swapped(): return lax.ppermute(value, EVERY, pairs)]
    all_to_all x1, blocking collectives: 9.64 us -> 11 us  [on_device(): lax.all_to_all(moved[0], EVERY, 0, 0, tiled=True)]
    pallas_call x7, Pallas kernels: 12.9 us -> 12 us  [run(): pl.pallas_call(kernel, out_shape=shapes, in_specs=[pl.BlockSpec(memory_sp...]
    ppermute x9 -> x8, starting transfers between devices: 10.6 us -> 10 us  [swapped(): return lax.ppermute(value, EVERY, pairs)]
  transfers between devices with their start and end apart: 14 -> 12, of which waited for: 10 -> 8; matrix products, arithmetic and copies ran while one was open for 0% -> 0% of each run, Pallas kernels for 2% -> 3%
where the time goes in v4:
time: 62 us; the launch traced here: 61.8 us
  blocking collectives  26.3 us (42%)
  Pallas kernels  12 us (19%)
  starting transfers between devices  11 us (18%)
  waiting for transfers between devices  10.7 us (17%)
  between operations  0.84 us (1%)
  local copies, waits for them, and re-layouts  0.68 us (1%)
    all_to_all x1, blocking collectives, on_device(): tables = [lax.all_to_all(copies, EVERY, 0, 0, tiled=True)]  15.3 us
    pallas_call x7, Pallas kernels, run(): pl.pallas_call(kernel, out_shape=shapes, in_specs=[pl.BlockSpec(memory_sp...  12 us
    all_to_all x1, blocking collectives, on_device(): lax.all_to_all(moved[0], EVERY, 0, 0, tiled=True)  11 us
    ppermute x8, starting transfers between devices, swapped(): return lax.ppermute(value, EVERY, pairs)  10 us
    ppermute x8, waiting for transfers between devices, swapped(): return lax.ppermute(value, EVERY, pairs)  7.31 us
    ppermute x4, waiting for transfers between devices, shifted(): lax.ppermute(value, axis, [(i, (i + step) % count) for i in range(count)])  3.44 us
  transfers between devices with their start and end apart: 12, of which 8 were waited for; matrix products, arithmetic and copies ran while one was open for 0% of the time, Pallas kernels for 3%

profile of v4, /device:TPU:0, one launch (start us, length us, event | category | flops | bytes accessed | tf_op | source)
XLA Modules:
  0.0 61.8 jit_solution(10865808403555309750)
XLA Ops:
  0.8 0.6 copy-done.5
  1.4 15.3 %all_to_all.10.refs_0_ = f32[32,8,128]{2,1,0:T(8,128)S(1)} all-to-all(f32[32,8,128]{2,1,0:T(8,128)S(1)} %broadcast_in_dim.8), channel_id=1, replica_groups=mesh['gx'=4,'gy'=4,'gz'=2] {'gx','gy','gz'}, dimensions={0} | all-to-all | bytes 262144 | tf_op jit(solution)/shard_map/all_to_all | solution.py:538
  16.8 2.5 %forward.1 = (bf16[1,128,128]{2,1,0:T(8,128)(2,1)S(1)}, s32[8,128]{1,0:T(8,128)S(1)}, f32[128,1024]{1,0:T(8,128)S(1)}, f32[128,1024]{1,0:T(8,128)S(1)}, f32[128,...) custom-call(f32[32,8,128]{2,1,0:T(8,128)S(1)} %all_to_all.10.refs_0_, ...), custom_call_target="tpu_custom_call" | custom-call | tf_op jit(solution)/shard_map/forward/pallas_call | solution.py:505
  19.6 1.0 %collective-permute-done = bf16[1,128,128]{2,1,0:T(8,128)(2,1)S(1)} collective-permute-done((bf16[1,128,128]{2,1,0:T(8,128)(2,1)S(1)}, bf16[1,128,128]{2,1,0:T(8,128)(2,1)S(1)}, u32[]{:S(2)}, u32[]{:S(2)}) %collective-permute-start) | collective-permute-done | bytes 32800 | tf_op jit(solution)/shard_map/ppermute | solution.py:34
  20.6 0.5 collective-permute-start.4
  21.2 1.6 %collective-permute-start.3 = (bf16[2,128,128]{2,1,0:T(8,128)(2,1)S(1)}, bf16[2,128,128]{2,1,0:T(8,128)(2,1)S(1)}, u32[]{:S(2)}, u32[]{:S(2)}) collective-permute-start(bf16[2,128,128]{2,1,0:T(8,128)(2,1)S(1)} %constant_dynamic-update-slice_fusion.refs_4_), channel_id=1, source_target_pairs={{0,12},{1,11},{2,14},{3,9},{6,10},{7,13},{4,8},{5,15},{8,4},{9,3},... | collective-permute-start | bytes 196616 | tf_op jit(solution)/shard_map/ppermute | solution.py:57
  22.8 1.0 %collective-permute-start.2 = (bf16[2,128,128]{2,1,0:T(8,128)(2,1)S(1)}, bf16[2,128,128]{2,1,0:T(8,128)(2,1)S(1)}, u32[]{:S(2)}, u32[]{:S(2)}) collective-permute-start(bf16[2,128,128]{2,1,0:T(8,128)(2,1)S(1)} %constant_dynamic-update-slice_fusion.refs_4_), channel_id=1, source_target_pairs={{0,4},{1,3},{2,6},{3,1},{6,2},{7,5},{4,0},{5,7},{8,12},{9,11},{10,... | collective-permute-start | bytes 196616 | tf_op jit(solution)/shard_map/ppermute | solution.py:57
  23.8 0.8 %collective-permute-start.1 = (bf16[2,128,128]{2,1,0:T(8,128)(2,1)S(1)}, bf16[2,128,128]{2,1,0:T(8,128)(2,1)S(1)}, u32[]{:S(2)}, u32[]{:S(2)}) collective-permute-start(bf16[2,128,128]{2,1,0:T(8,128)(2,1)S(1)} %constant_dynamic-update-slice_fusion.refs_4_), channel_id=1, source_target_pairs={{0,8},{1,17},{2,10},{3,19},{6,14},{7,23},{4,12},{5,21},{8,0},{9,25... | collective-permute-start | bytes 196616 | tf_op jit(solution)/shard_map/ppermute | solution.py:57
  24.6 3.3 %collective-permute-done.4.refs_3_ = bf16[2,128,128]{2,1,0:T(8,128)(2,1)S(1)} collective-permute-done((bf16[2,128,128]{2,1,0:T(8,128)(2,1)S(1)}, bf16[2,128,128]{2,1,0:T(8,128)(2,1)S(1)}, u32[]{:S(2)}, u32[]{:S(2)}) %collective-permute-start.4) | collective-permute-done | bytes 65568 | tf_op jit(solution)/shard_map/ppermute | solution.py:57
  27.9 0.4 collective-permute-done.1.refs_0_
  28.6 1.6 %onehot.1 = (bf16[2304,1024]{1,0:T(8,128)(2,1)S(1)}, bf16[128,128]{1,0:T(8,128)(2,1)S(1)}, f32[128,128]{1,0:T(8,128)S(1)}) custom-call(s32[8,128]{1,0:T(8,128)S(1)} %get-tuple-element.19.code_ref, bf16[128,128]{1,0:T(8,128)(2,1)S(1)} %copy-done.3, f32[1,128]{1,0:T(1,128)S(1)} %bitcast.3), custom_call_target="tpu_custom_call" | custom-call | flops 1073741824 | bytes 8388608 | tf_op jit(solution)/shard_map/onehot/pallas_call | solution.py:505
  30.2 3.6 %second.1 = (f32[1,128]{1,0:T(1,128)S(1)}, f32[128,1024]{1,0:T(8,128)S(1)}, bf16[9,128,128]{2,1,0:T(8,128)(2,1)S(1)}, bf16[9,128,128]{2,1,0:T(8,128)(2,1)S(1)}) custom-call(bf16[2,128,128]{2,1,0:T(8,128)(2,1)S(1)} %collective-permute-done.1.refs_0_, bf16[2,128,128]{2,1,0:T(8,128)(2,1)S(1)} %collective-permute-done.2.refs_1_, ...), custom_call_target="tpu_custom_call" | custom-call | tf_op jit(solution)/shard_map/second/pallas_call | solution.py:505
  33.8 0.4 collective-permute-start.6
  34.2 1.2 %collective-permute-done.6 = bf16[9,128,128]{2,1,0:T(8,128)(2,1)S(1)} collective-permute-done((bf16[9,128,128]{2,1,0:T(8,128)(2,1)S(1)}, bf16[9,128,128]{2,1,0:T(8,128)(2,1)S(1)}, u32[]{:S(2)}, u32[]{:S(2)}) %collective-permute-start.6) | collective-permute-done | bytes 294944 | tf_op jit(solution)/shard_map/ppermute | solution.py:34
  35.6 0.8 %collective-permute-start.7 = (bf16[2,128,128]{2,1,0:T(8,128)(2,1)S(1)}, bf16[2,128,128]{2,1,0:T(8,128)(2,1)S(1)}, u32[]{:S(2)}, u32[]{:S(2)}) collective-permute-start(bf16[2,128,128]{2,1,0:T(8,128)(2,1)S(1)} %get-tuple-element.36), channel_id=1, source_target_pairs={{0,8},{1,17},{2,10},{3,19},{6,14},{7,23},{4,12},{5,21},{8,0},{9,25... | collective-permute-start | bytes 196616 | tf_op jit(solution)/shard_map/ppermute | solution.py:57
  36.4 3.2 %collective-permute-start.10 = (bf16[2,128,128]{2,1,0:T(8,128)(2,1)S(1)}, bf16[2,128,128]{2,1,0:T(8,128)(2,1)S(1)}, u32[]{:S(2)}, u32[]{:S(2)}) collective-permute-start(bf16[2,128,128]{2,1,0:T(8,128)(2,1)S(1)} %get-tuple-element.37), channel_id=1, source_target_pairs={{0,18},{1,21},{2,16},{3,23},{6,20},{7,19},{4,22},{5,17},{8,26},{9,... | collective-permute-start | bytes 196616 | tf_op jit(solution)/shard_map/ppermute | solution.py:57
  39.6 0.7 %collective-permute-start.9 = (bf16[2,128,128]{2,1,0:T(8,128)(2,1)S(1)}, bf16[2,128,128]{2,1,0:T(8,128)(2,1)S(1)}, u32[]{:S(2)}, u32[]{:S(2)}) collective-permute-start(bf16[2,128,128]{2,1,0:T(8,128)(2,1)S(1)} %get-tuple-element.38), channel_id=1, source_target_pairs={{0,12},{1,11},{2,14},{3,9},{6,10},{7,13},{4,8},{5,15},{8,4},{9,3},... | collective-permute-start | bytes 196616 | tf_op jit(solution)/shard_map/ppermute | solution.py:57
  40.3 1.4 %collective-permute-start.8 = (bf16[2,128,128]{2,1,0:T(8,128)(2,1)S(1)}, bf16[2,128,128]{2,1,0:T(8,128)(2,1)S(1)}, u32[]{:S(2)}, u32[]{:S(2)}) collective-permute-start(bf16[2,128,128]{2,1,0:T(8,128)(2,1)S(1)} %get-tuple-element.39), channel_id=1, source_target_pairs={{0,4},{1,3},{2,6},{3,1},{6,2},{7,5},{4,0},{5,7},{8,12},{9,11},{10,... | collective-permute-start | bytes 196616 | tf_op jit(solution)/shard_map/ppermute | solution.py:57
  41.6 3.0 %collective-permute-done.10 = bf16[2,128,128]{2,1,0:T(8,128)(2,1)S(1)} collective-permute-done((bf16[2,128,128]{2,1,0:T(8,128)(2,1)S(1)}, bf16[2,128,128]{2,1,0:T(8,128)(2,1)S(1)}, u32[]{:S(2)}, u32[]{:S(2)}) %collective-permute-start.10) | collective-permute-done | bytes 65568 | tf_op jit(solution)/shard_map/ppermute | solution.py:57
  44.9 0.4 collective-permute-done.8
  45.4 1.2 %collective-permute-done.11 = f32[1,128,128]{2,1,0:T(8,128)S(1)} collective-permute-done((f32[1,128,128]{2,1,0:T(8,128)S(1)}, f32[1,128,128]{2,1,0:T(8,128)S(1)}, u32[]{:S(2)}, u32[]{:S(2)}) %collective-permute-start.11) | collective-permute-done | bytes 65568 | tf_op jit(solution)/shard_map/ppermute | solution.py:34
  46.6 3.6 %backward.1 = f32[32,4,128]{2,1,0:T(4,128)S(1)} custom-call(f32[1,128,128]{2,1,0:T(8,128)S(1)} %fusion.owned_ref, f32[1,128]{1,0:T(1,128)S(1)} %get-tuple-element.26.energy_ref, f32[128,1024]{1,0:T(8,128)S(1)} %get-tuple-element.27.grad_edge_ref, f32[128,1024]{1,0:T(8,128)S(1)} %get-tuple-element.28.dse_ref, f32[128,1024]{1,0:T(8,128)S(1)} %get-tuple-element.29.dsl_ref, ...), custom_call_target="tpu_custom_call" | custom-call | tf_op jit(solution)/shard_map/backward/pallas_call | solution.py:505
  50.2 11.0 %all_to_all.11.moved_ref = f32[32,4,128]{2,1,0:T(4,128)S(1)} all-to-all(f32[32,4,128]{2,1,0:T(4,128)S(1)} %backward.1), channel_id=1, replica_groups=mesh['gx'=4,'gy'=4,'gz'=2] {'gx','gy','gz'}, dimensions={0} | all-to-all | bytes 131072 | tf_op jit(solution)/shard_map/all_to_all | solution.py:579
  61.1 0.7 %finish.1 = (f32[1,1,2,64]{3,2,1,0:T(2,128)}, f32[1,1,2,192]{3,2,1,0:T(2,128)}) custom-call(f32[32,4,128]{2,1,0:T(4,128)S(1)} %all_to_all.11.moved_ref), custom_call_target="tpu_custom_call" | custom-call | tf_op jit(solution)/shard_map/finish/pallas_call | solution.py:505
  (40 shorter events, 1.1 us)
Async XLA Ops:
  0.6 0.7 %copy-start.5 = (s32[1,1,2,512]{3,2,1,0:T(2,128)S(1)}, s32[1,1,2,512]{3,2,1,0:T(2,128)}, u32[]{:S(2)}) copy-start(s32[1,1,2,512]{3,2,1,0:T(2,128)} %nb_ref.1) | copy-start | bytes 12292
  0.6 0.7 %copy-start.9 = (s32[1,1,2,64]{3,2,1,0:T(2,128)S(1)}, s32[1,1,2,64]{3,2,1,0:T(2,128)}, u32[]{:S(2)}) copy-start(s32[1,1,2,64]{3,2,1,0:T(2,128)} %spec_ref.1) | copy-start | bytes 1540
  0.7 0.7 %copy-start.8 = (f32[1,1,2,192]{3,2,1,0:T(2,128)S(1)}, f32[1,1,2,192]{3,2,1,0:T(2,128)}, u32[]{:S(2)}) copy-start(f32[1,1,2,192]{3,2,1,0:T(2,128)} %pos_ref.1) | copy-start | bytes 4612
  0.7 16.1 %copy-start = (bf16[384,128]{1,0:T(8,128)(2,1)S(1)}, bf16[384,128]{1,0:T(8,128)(2,1)}, u32[]{:S(2)}) copy-start(bf16[384,128]{1,0:T(8,128)(2,1)} %upd_ref.1) | copy-start | bytes 294916
  0.7 16.1 %copy-start.2 = (bf16[128,128]{1,0:T(8,128)(2,1)S(1)}, bf16[128,128]{1,0:T(8,128)(2,1)}, u32[]{:S(2)}) copy-start(bf16[128,128]{1,0:T(8,128)(2,1)} %envw_ref.1) | copy-start | bytes 98308
  0.7 16.1 %copy-start.1 = (bf16[128,128]{1,0:T(8,128)(2,1)S(1)}, bf16[128,128]{1,0:T(8,128)(2,1)}, u32[]{:S(2)}) copy-start(bf16[128,128]{1,0:T(8,128)(2,1)} %mix_ref.1) | copy-start | bytes 98308
  0.7 16.1 %copy-start.4 = (bf16[8,128]{1,0:T(8,128)(2,1)S(1)}, bf16[8,128]{1,0:T(8,128)(2,1)}, u32[]{:S(2)}) copy-start(bf16[8,128]{1,0:T(8,128)(2,1)} %radial_ref.1) | copy-start | bytes 6148
  0.7 16.1 %copy-start.7 = (bf16[5,128]{1,0:T(8,128)(2,1)S(1)}, bf16[5,128]{1,0:T(8,128)(2,1)}, u32[]{:S(2)}) copy-start(bf16[5,128]{1,0:T(8,128)(2,1)} %refs_2_.1) | copy-start | bytes 3844
  0.7 16.1 %copy-start.6 = (bf16[5,128]{1,0:T(8,128)(2,1)S(1)}, bf16[5,128]{1,0:T(8,128)(2,1)}, u32[]{:S(2)}) copy-start(bf16[5,128]{1,0:T(8,128)(2,1)} %refs_1_.1) | copy-start | bytes 3844
  0.7 27.9 %copy-start.3 = (bf16[128,128]{1,0:T(8,128)(2,1)S(1)}, bf16[128,128]{1,0:T(8,128)(2,1)}, u32[]{:S(2)}) copy-start(bf16[128,128]{1,0:T(8,128)(2,1)} %refs_8_.1) | copy-start | bytes 98308
  0.7 27.9 %copy-start.10 = (f32[128]{0:T(128)S(1)}, f32[128]{0:T(128)}, u32[]{:S(2)}) copy-start(f32[128]{0:T(128)} %param.21) | copy-start | bytes 1540
  19.4 1.3 %collective-permute-start = (bf16[1,128,128]{2,1,0:T(8,128)(2,1)S(1)}, bf16[1,128,128]{2,1,0:T(8,128)(2,1)S(1)}, u32[]{:S(2)}, u32[]{:S(2)}) collective-permute-start(bf16[1,128,128]{2,1,0:T(8,128)(2,1)S(1)} %get-tuple-element.18), channel_id=1, source_target_pairs={{0,1},{1,0},{2,3},{3,2},{4,5},{5,4},{6,7},{7,6},{8,9},{9,8},{10,11... | collective-permute-start | bytes 98312 | tf_op jit(solution)/shard_map/ppermute | solution.py:34
  20.6 7.3 %collective-permute-start.4 = (bf16[2,128,128]{2,1,0:T(8,128)(2,1)S(1)}, bf16[2,128,128]{2,1,0:T(8,128)(2,1)S(1)}, u32[]{:S(2)}, u32[]{:S(2)}) collective-permute-start(bf16[2,128,128]{2,1,0:T(8,128)(2,1)S(1)} %constant_dynamic-update-slice_fusion.refs_4_), channel_id=1, source_target_pairs={{0,18},{1,21},{2,16},{3,23},{6,20},{7,19},{4,22},{5,17},{8,26},{9,... | collective-permute-start | bytes 196616 | tf_op jit(solution)/shard_map/ppermute | solution.py:57
  21.2 6.8 %collective-permute-start.3 = (bf16[2,128,128]{2,1,0:T(8,128)(2,1)S(1)}, bf16[2,128,128]{2,1,0:T(8,128)(2,1)S(1)}, u32[]{:S(2)}, u32[]{:S(2)}) collective-permute-start(bf16[2,128,128]{2,1,0:T(8,128)(2,1)S(1)} %constant_dynamic-update-slice_fusion.refs_4_), channel_id=1, source_target_pairs={{0,12},{1,11},{2,14},{3,9},{6,10},{7,13},{4,8},{5,15},{8,4},{9,3},... | collective-permute-start | bytes 196616 | tf_op jit(solution)/shard_map/ppermute | solution.py:57
  22.8 5.1 %collective-permute-start.2 = (bf16[2,128,128]{2,1,0:T(8,128)(2,1)S(1)}, bf16[2,128,128]{2,1,0:T(8,128)(2,1)S(1)}, u32[]{:S(2)}, u32[]{:S(2)}) collective-permute-start(bf16[2,128,128]{2,1,0:T(8,128)(2,1)S(1)} %constant_dynamic-update-slice_fusion.refs_4_), channel_id=1, source_target_pairs={{0,4},{1,3},{2,6},{3,1},{6,2},{7,5},{4,0},{5,7},{8,12},{9,11},{10,... | collective-permute-start | bytes 196616 | tf_op jit(solution)/shard_map/ppermute | solution.py:57
  23.8 4.5 %collective-permute-start.1 = (bf16[2,128,128]{2,1,0:T(8,128)(2,1)S(1)}, bf16[2,128,128]{2,1,0:T(8,128)(2,1)S(1)}, u32[]{:S(2)}, u32[]{:S(2)}) collective-permute-start(bf16[2,128,128]{2,1,0:T(8,128)(2,1)S(1)} %constant_dynamic-update-slice_fusion.refs_4_), channel_id=1, source_target_pairs={{0,8},{1,17},{2,10},{3,19},{6,14},{7,23},{4,12},{5,21},{8,0},{9,25... | collective-permute-start | bytes 196616 | tf_op jit(solution)/shard_map/ppermute | solution.py:57
  28.4 1.8 %collective-permute-start.5 = (bf16[8,128,128]{2,1,0:T(8,128)(2,1)S(1)}, bf16[8,128,128]{2,1,0:T(8,128)(2,1)S(1)}, u32[]{:S(2)}, u32[]{:S(2)}) collective-permute-start(bf16[8,128,128]{2,1,0:T(8,128)(2,1)S(1)} %pad_maximum_fusion), channel_id=1, source_target_pairs={{0,1},{1,0},{2,3},{3,2},{4,5},{5,4},{6,7},{7,6},{8,9},{9,8},{10,11... | collective-permute-start | bytes 786440 | tf_op jit(solution)/shard_map/ppermute | solution.py:34
  33.8 1.6 %collective-permute-start.6 = (bf16[9,128,128]{2,1,0:T(8,128)(2,1)S(1)}, bf16[9,128,128]{2,1,0:T(8,128)(2,1)S(1)}, u32[]{:S(2)}, u32[]{:S(2)}) collective-permute-start(bf16[9,128,128]{2,1,0:T(8,128)(2,1)S(1)} %get-tuple-element.25), channel_id=1, source_target_pairs={{0,1},{1,0},{2,3},{3,2},{4,5},{5,4},{6,7},{7,6},{8,9},{9,8},{10,11... | collective-permute-start | bytes 884744 | tf_op jit(solution)/shard_map/ppermute | solution.py:34
  35.6 6.0 %collective-permute-start.7 = (bf16[2,128,128]{2,1,0:T(8,128)(2,1)S(1)}, bf16[2,128,128]{2,1,0:T(8,128)(2,1)S(1)}, u32[]{:S(2)}, u32[]{:S(2)}) collective-permute-start(bf16[2,128,128]{2,1,0:T(8,128)(2,1)S(1)} %get-tuple-element.36), channel_id=1, source_target_pairs={{0,8},{1,17},{2,10},{3,19},{6,14},{7,23},{4,12},{5,21},{8,0},{9,25... | collective-permute-start | bytes 196616 | tf_op jit(solution)/shard_map/ppermute | solution.py:57
  36.4 8.3 %collective-permute-start.10 = (bf16[2,128,128]{2,1,0:T(8,128)(2,1)S(1)}, bf16[2,128,128]{2,1,0:T(8,128)(2,1)S(1)}, u32[]{:S(2)}, u32[]{:S(2)}) collective-permute-start(bf16[2,128,128]{2,1,0:T(8,128)(2,1)S(1)} %get-tuple-element.37), channel_id=1, source_target_pairs={{0,18},{1,21},{2,16},{3,23},{6,20},{7,19},{4,22},{5,17},{8,26},{9,... | collective-permute-start | bytes 196616 | tf_op jit(solution)/shard_map/ppermute | solution.py:57
  39.6 5.3 %collective-permute-start.9 = (bf16[2,128,128]{2,1,0:T(8,128)(2,1)S(1)}, bf16[2,128,128]{2,1,0:T(8,128)(2,1)S(1)}, u32[]{:S(2)}, u32[]{:S(2)}) collective-permute-start(bf16[2,128,128]{2,1,0:T(8,128)(2,1)S(1)} %get-tuple-element.38), channel_id=1, source_target_pairs={{0,12},{1,11},{2,14},{3,9},{6,10},{7,13},{4,8},{5,15},{8,4},{9,3},... | collective-permute-start | bytes 196616 | tf_op jit(solution)/shard_map/ppermute | solution.py:57
  40.3 5.0 %collective-permute-start.8 = (bf16[2,128,128]{2,1,0:T(8,128)(2,1)S(1)}, bf16[2,128,128]{2,1,0:T(8,128)(2,1)S(1)}, u32[]{:S(2)}, u32[]{:S(2)}) collective-permute-start(bf16[2,128,128]{2,1,0:T(8,128)(2,1)S(1)} %get-tuple-element.39), channel_id=1, source_target_pairs={{0,4},{1,3},{2,6},{3,1},{6,2},{7,5},{4,0},{5,7},{8,12},{9,11},{10,... | collective-permute-start | bytes 196616 | tf_op jit(solution)/shard_map/ppermute | solution.py:57
  45.3 1.3 %collective-permute-start.11 = (f32[1,128,128]{2,1,0:T(8,128)S(1)}, f32[1,128,128]{2,1,0:T(8,128)S(1)}, u32[]{:S(2)}, u32[]{:S(2)}) collective-permute-start(f32[1,128,128]{2,1,0:T(8,128)S(1)} %slice.38), channel_id=1, source_target_pairs={{0,1},{1,0},{2,3},{3,2},{4,5},{5,4},{6,7},{7,6},{8,9},{9,8},{10,11... | collective-permute-start | bytes 196616 | tf_op jit(solution)/shard_map/ppermute | solution.py:34

commit v5 on v4

--- a/solution.py
+++ b/solution.py
@@ -17,7 +17,7 @@
 ROOT3 = math.sqrt(3.0)
 F32 = jnp.float32
 BF16 = jnp.bfloat16
-TILE = 256
+TILE = 1024
 
 
 RING = (0, 1, 3, 2)
@@ -57,25 +57,26 @@
     return lax.ppermute(value, EVERY, pairs)
 
 
-def gather_halo(chunk):
+def gather_halo(chunk, beside=None):
     if is_direct():
         both = jnp.concatenate([chunk, shifted(chunk, "gz", 1)], axis=0)
         direct = [swapped(both, slot) for slot in range(4)]
+        direct, beside = lax.optimization_barrier((direct, beside))
         relayed = shifted(jnp.concatenate(direct, axis=0), "gz", 1)
         near = [(slot, row) for slot in range(4) for row in range(2)] + [(4, 0)]
         far = [(5, row) for row in range(8)] + [(4, 1)]
-        return direct + [both, relayed], near + far
+        return direct + [both, relayed], near + far, beside
     for axis in ("gx", "gy"):
         lower = shifted(chunk, axis, 1)
         upper = shifted(chunk, axis, -1)
         chunk = jnp.concatenate([lower, upper, chunk], axis=0)
     order = [(array, row) for array in range(2) for row in range(9)]
     if lax.axis_size("gz") == 2:
-        return [chunk, shifted(chunk, "gz", 1)], order
+        return [chunk, shifted(chunk, "gz", 1)], order, beside
     half = chunk.shape[-1] // 2
     above = shifted(chunk[..., :half], "gz", -1)
     below = shifted(chunk[..., half:], "gz", 1)
-    return [chunk, jnp.concatenate([above, below], axis=-1)], order
+    return [chunk, jnp.concatenate([above, below], axis=-1)], order, beside
 
 
 def reduce_halo(own, other):
@@ -113,21 +114,6 @@
     return number((x + step_x) & 3, (y + step_y) & 3, core ^ outside)
 
 
-def owner_of_chunk(c):
-    x, y, core = column_here()
-    outside = 0
-    if c % 9 == 8:
-        return number(x, y, core ^ (c // 9))
-    relayed = c // 9
-    slot, row = (c % 9) // 2, (c % 9) % 2
-    outside = row ^ relayed
-    spots = [
-        number(partner(x, ROUTES[mate][slot][0]), partner(y, ROUTES[mate][slot][1]), core ^ outside)
-        for mate in range(2)
-    ]
-    return jnp.where((core ^ relayed) == 0, spots[0], spots[1])
-
-
 def place_column(step_x, step_y, outside, direct):
     if not direct:
         place_x = jnp.where(step_x == 0, 2, jnp.where(step_x < 0, 0, 1))
@@ -178,19 +164,29 @@
             out_ref[0, row : row + 1, :] = (first * 2048 + second).astype(F32)
 
 
-def onehot_kernel(direct, code_ref, second_ref, readout_ref, onehot_ref, secondt_ref, rocol_ref):
+def onehot_kernel(
+    direct, code_ref, second_ref, readout_ref, gather_ref, scatter_ref, lane_ref, secondt_ref, rocol_ref, turn_ref
+):
     step_x, step_y, step_z, outside, lane = decode(code_ref[...], ATOMS // 2)
     target = place_column(step_x, step_y, outside, direct) * ATOMS + lane
     secondt_ref[...] = second_ref[...].astype(F32).T.astype(BF16)
     rocol_ref[...] = jnp.broadcast_to(readout_ref[...], (ATOMS, ATOMS)).T
-    atom = lax.broadcasted_iota(jnp.int32, (ATOMS, ATOMS), 0)
+    turn_ref[...] = jnp.zeros(turn_ref.shape, F32)
+    turn_ref[0:NEIGH, :] = target.astype(F32)
+    turned = turn_ref[...].T.astype(jnp.int32)
+    down = lax.broadcasted_iota(jnp.int32, (ATOMS, ATOMS), 0)
+    across = lax.broadcasted_iota(jnp.int32, (ATOMS, ATOMS), 1)
     for k in range(NEIGH):
-        aim = jnp.broadcast_to(target[k : k + 1, :], (ATOMS, ATOMS)) - atom
-
-        def fill(c, carry, k=k, aim=aim):
-            rows = pl.ds(pl.multiple_of(c * ATOMS, ATOMS), ATOMS)
-            hit = jnp.where(aim == c * ATOMS, 1.0, 0.0)
-            onehot_ref[rows, k * ATOMS : (k + 1) * ATOMS] = hit.astype(BF16)
+        span = slice(k * ATOMS, (k + 1) * ATOMS)
+        aim = jnp.broadcast_to(target[k : k + 1, :], (ATOMS, ATOMS)) - down
+        aim_turned = jnp.broadcast_to(turned[:, k : k + 1], (ATOMS, ATOMS)) - across
+        near = jnp.broadcast_to(lane[k : k + 1, :], (ATOMS, ATOMS)) == down
+        lane_ref[:, span] = jnp.where(near, 1.0, 0.0).astype(BF16)
+
+        def fill(c, carry, span=span, aim=aim, aim_turned=aim_turned):
+            part = pl.ds(pl.multiple_of(c * ATOMS, ATOMS), ATOMS)
+            gather_ref[part, span] = jnp.where(aim == c * ATOMS, 1.0, 0.0).astype(BF16)
+            scatter_ref[span, part] = jnp.where(aim_turned == c * ATOMS, 1.0, 0.0).astype(BF16)
             return carry
 
         lax.fori_loop(0, CHUNKS, fill, 0)
@@ -359,38 +355,37 @@
 
 def second_kernel(parts, order, *refs):
     (
-        onehot_ref, edge_ref, second_ref, secondt_ref, rocol_ref,
-        energy_ref, grad_edge_ref, back_own_ref, back_other_ref, grad_ref,
+        gather_ref, scatter_ref, edge_ref, second_ref, secondt_ref, rocol_ref,
+        energy_ref, grad_edge_ref, back_own_ref, back_other_ref, other_ref, grad_ref,
     ) = refs[parts:]
     table = jnp.concatenate([refs[array][row] for array, row in order], axis=1)
     rocol = rocol_ref[...]
+    other_ref[...] = jnp.dot(table, gather_ref[...], preferred_element_type=F32)
+    wide = 2 * ATOMS
     total = jnp.zeros((ATOMS, ATOMS), F32)
-    for j in range(EDGES // TILE):
-        span = slice(j * TILE, (j + 1) * TILE)
-        other = jnp.dot(table, onehot_ref[:, span], preferred_element_type=F32)
+    for j in range(EDGES // wide):
+        span = slice(j * wide, (j + 1) * wide)
+        other = other_ref[:, span]
         edge = edge_ref[:, span]
         hidden, ds = silu_pair(jnp.dot(secondt_ref[...], (edge * other).astype(BF16), preferred_element_type=F32))
-        for i in range(TILE // ATOMS):
-            total = total + hidden[:, i * ATOMS : (i + 1) * ATOMS]
-        grad_hidden = ds * jnp.concatenate([rocol] * (TILE // ATOMS), axis=1)
+        total = total + hidden[:, :ATOMS] + hidden[:, ATOMS:]
+        grad_hidden = ds * jnp.concatenate([rocol, rocol], axis=1)
         grad_prod = jnp.dot(second_ref[...], grad_hidden.astype(BF16), preferred_element_type=F32)
         grad_prod = grad_prod.astype(BF16).astype(F32)
         grad_edge_ref[:, span] = grad_prod * other
         grad_ref[:, span] = (grad_prod * edge).astype(BF16)
-    energy = jnp.sum(total * rocol, axis=0, keepdims=True)
-    energy_ref[...] = energy
-    grad = grad_ref[...]
-    for c in range(CHUNKS):
-        rows = slice(c * ATOMS, (c + 1) * ATOMS)
-        back = lax.dot_general(
-            grad, onehot_ref[rows, :], (((1,), (1,)), ((), ())), preferred_element_type=F32
-        )
-        ref = back_own_ref if c < 9 else back_other_ref
-        ref[c % 9] = back.astype(BF16)
+    energy_ref[...] = jnp.sum(total * rocol, axis=0, keepdims=True)
+    for c in range(0, CHUNKS, 2):
+        back = jnp.dot(
+            grad_ref[...], scatter_ref[:, c * ATOMS : (c + 2) * ATOMS], preferred_element_type=F32
+        ).astype(BF16)
+        for i in range(2):
+            ref = back_own_ref if c + i < 9 else back_other_ref
+            ref[(c + i) % 9] = back[:, i * ATOMS : (i + 1) * ATOMS]
 
 
 def backward_kernel(
-    direct, owned_ref, energy_ref, grad_edge_ref, dse_ref, dsl_ref, dsb_ref, env_ref, v_ref, geo_ref, onehot_ref,
+    direct, owned_ref, energy_ref, grad_edge_ref, dse_ref, dsl_ref, dsb_ref, env_ref, v_ref, geo_ref, code_ref, lane_ref,
     upd_ref, envw_ref, mix_ref, radial_ref, *refs,
 ):
     outs = refs[: 1 if direct else 2]
@@ -466,25 +461,32 @@
     high = [p.astype(BF16).astype(F32) for p in pull]
     low = [p - h for p, h in zip(pull, high)]
     zero = jnp.zeros((1, ATOMS), F32)
+    step_x, step_y, step_z, outside, lane = decode(code_ref[...], ATOMS // 2)
+    spot = outside * 9 + step_y * 3 + step_x + 4
+    rows, spots = [], []
     for k in range(NEIGH):
-        rows = [h[k : k + 1, :] for h in high] + [zero] * 5 + [q[k : k + 1, :] for q in low] + [zero] * 5
-        force_ref[:, k * ATOMS : (k + 1) * ATOMS] = jnp.concatenate(rows, axis=0).astype(BF16)
-    force = force_ref[...]
+        parts = [h[k : k + 1, :] for h in high] + [zero] + [q[k : k + 1, :] for q in low] + [zero]
+        rows.append(jnp.concatenate(parts, axis=0))
+        spots.append(jnp.broadcast_to(spot[k : k + 1, :], (8, ATOMS)))
+    for c in range(0, CHUNKS, 2):
+        for k in range(NEIGH):
+            both = [jnp.where(spots[k] == c + i, rows[k], 0.0) for i in range(2)]
+            force_ref[c * 8 : c * 8 + 16, k * ATOMS : (k + 1) * ATOMS] = jnp.concatenate(both, axis=0).astype(BF16)
+    back = lax.dot_general(
+        force_ref[...], lane_ref[...], (((1,), (1,)), ((), ())), preferred_element_type=F32
+    )
     center = jnp.concatenate([jnp.sum(p, axis=0, keepdims=True) for p in pull] + [-energy_ref[...]], axis=0)
     if direct:
         outs[0][...] = jnp.zeros(outs[0].shape, F32)
     for c in range(CHUNKS):
-        rows = slice(c * ATOMS, (c + 1) * ATOMS)
-        back = lax.dot_general(
-            force, onehot_ref[rows, :], (((1,), (1,)), ((), ())), preferred_element_type=F32
-        )
-        moved = back[:4] + back[8:12]
-        if c == 8:
+        far, dy, dx = c // 9, c % 9 // 3 - 1, c % 3 - 1
+        moved = back[8 * c : 8 * c + 4] + back[8 * c + 4 : 8 * c + 8]
+        if (far, dy, dx) == (0, 0, 0):
             moved = moved - center
         if direct:
-            outs[0][owner_of_chunk(c)] = moved
+            outs[0][owner_at(dx, dy, far)] = moved
         else:
-            outs[c // 9][c % 9] = moved
+            outs[far][(0, 2, 1)[dy + 1] * 3 + (0, 2, 1)[dx + 1]] = moved
 
 
 def finish_kernel(moved_ref, energy_ref, out_ref):
@@ -537,7 +539,7 @@
         copies = jnp.broadcast_to(packed, (devices, 8, ATOMS))
         tables = [lax.all_to_all(copies, EVERY, 0, 0, tiled=True)]
     else:
-        tables, order = gather_halo(packed)
+        tables, order, _ = gather_halo(packed)
     table, code, edge, dsb, dsl, dse, env, field, geo = call(
         functools.partial(forward_kernel, len(tables), direct),
         [
@@ -550,30 +552,35 @@
         ],
         name="forward",
     )(*tables, center_table, neighbor_table, radial_weight, mix_weight, env_weight, update_weight)
-    onehot, secondt, rocol = call(
+    beside = call(
         functools.partial(onehot_kernel, direct),
-        [((CHUNKS * ATOMS, EDGES), BF16), (square, BF16), (square, F32)],
+        [
+            ((CHUNKS * ATOMS, EDGES), BF16), ((EDGES, CHUNKS * ATOMS), BF16), (edges, BF16), (square, BF16),
+            (square, F32),
+        ],
+        [pltpu.VMEM(square, F32)],
         name="onehot",
         cost=pl.CostEstimate(flops=1 << 30, bytes_accessed=8 << 20, transcendentals=0),
     )(code, second_weight, readout)
-    tables, order = gather_halo(table)
+    tables, order, beside = gather_halo(table, beside)
+    gather, scatter, lanes, secondt, rocol = beside
     energy, grad_edge, back_own, back_other = call(
         functools.partial(second_kernel, len(tables), order),
         [((1, ATOMS), F32), (edges, F32), ((9,) + square, BF16), ((9,) + square, BF16)],
-        [pltpu.VMEM(edges, BF16)],
+        [pltpu.VMEM(edges, F32), pltpu.VMEM(edges, BF16)],
         name="second",
-    )(*tables, onehot, edge, second_weight, secondt, rocol)
+    )(*tables, gather, scatter, edge, second_weight, secondt, rocol)
     owned = reduce_halo(back_own, back_other)
     moved = call(
         functools.partial(backward_kernel, direct),
         [((devices, 4, ATOMS), F32)] if direct else [((9, 4, ATOMS), F32)] * 2,
         [
             pltpu.VMEM((72, 8, ATOMS), F32), pltpu.VMEM((3 * ATOMS, EDGES), BF16), pltpu.VMEM(edges, BF16),
-            pltpu.VMEM(edges, F32), pltpu.VMEM((72, 8, ATOMS), F32), pltpu.VMEM((16, EDGES), BF16),
+            pltpu.VMEM(edges, F32), pltpu.VMEM((72, 8, ATOMS), F32), pltpu.VMEM((CHUNKS * 8, EDGES), BF16),
         ],
         name="backward",
     )(
-        owned, energy, grad_edge, dse, dsl, dsb, env, field, geo, onehot, update_weight, env_weight, mix_weight,
+        owned, energy, grad_edge, dse, dsl, dsb, env, field, geo, code, lanes, update_weight, env_weight, mix_weight,
         radial_weight,
     )
     moved = lax.all_to_all(moved[0], EVERY, 0, 0, tiled=True) if direct else reduce_halo(*moved)

time: 62 us -> 58.1 us (0.937)
  waiting for transfers between devices: 10.7 us -> 9.11 us
  Pallas kernels: 12 us -> 10.6 us
  blocking collectives: 26.3 us -> 25.4 us
    ppermute x8, waiting for transfers between devices: 7.31 us -> 3.91 us  [swapped(): return lax.ppermute(value, EVERY, pairs)]
    ppermute x4, waiting for transfers between devices: 3.44 us -> 5.19 us  [shifted(): lax.ppermute(value, axis, [(i, (i + step) % count) for i in range(count)])]
    pallas_call x7, Pallas kernels: 12 us -> 10.6 us  [run(): pl.pallas_call(kernel, out_shape=shapes, in_specs=[pl.BlockSpec(memory_sp...]
    all_to_all x1, blocking collectives: 11 us -> 10.1 us  [on_device(): lax.all_to_all(moved[0], EVERY, 0, 0, tiled=True)]
  transfers between devices with their start and end apart: 12 -> 12, of which waited for: 8 -> 8; matrix products, arithmetic and copies ran while one was open for 0% -> 0% of each run, Pallas kernels for 3% -> 6%
where the time goes in v5:
time: 58.1 us; the launch traced here: 57.8 us
  blocking collectives  25.4 us (44%)
  starting transfers between devices  11 us (19%)
  Pallas kernels  10.6 us (18%)
  waiting for transfers between devices  9.11 us (16%)
  between operations  0.87 us (1%)
  local copies, waits for them, and re-layouts  0.68 us (1%)
    all_to_all x1, blocking collectives, on_device(): tables = [lax.all_to_all(copies, EVERY, 0, 0, tiled=True)]  15.3 us
    pallas_call x7, Pallas kernels, run(): pl.pallas_call(kernel, out_shape=shapes, in_specs=[pl.BlockSpec(memory_sp...  10.6 us
    ppermute x8, starting transfers between devices, swapped(): return lax.ppermute(value, EVERY, pairs)  10.4 us
    all_to_all x1, blocking collectives, on_device(): lax.all_to_all(moved[0], EVERY, 0, 0, tiled=True)  10.1 us
    ppermute x4, waiting for transfers between devices, shifted(): lax.ppermute(value, axis, [(i, (i + step) % count) for i in range(count)])  5.19 us
    ppermute x8, waiting for transfers between devices, swapped(): return lax.ppermute(value, EVERY, pairs)  3.91 us
  transfers between devices with their start and end apart: 12, of which 8 were waited for; matrix products, arithmetic and copies ran while one was open for 0% of the time, Pallas kernels for 6%

profile of v5, /device:TPU:0, one launch (start us, length us, event | category | flops | bytes accessed | tf_op | source)
XLA Modules:
  0.0 57.8 jit_solution(3765024294488468302)
XLA Ops:
  0.8 0.6 copy-done.5
  1.4 15.3 %all_to_all.10.refs_0_ = f32[32,8,128]{2,1,0:T(8,128)S(1)} all-to-all(f32[32,8,128]{2,1,0:T(8,128)S(1)} %broadcast_in_dim.8), channel_id=1, replica_groups=mesh['gx'=4,'gy'=4,'gz'=2] {'gx','gy','gz'}, dimensions={0} | all-to-all | bytes 262144 | tf_op jit(solution)/shard_map/all_to_all | solution.py:540
  16.8 2.0 %forward.1 = (bf16[1,128,128]{2,1,0:T(8,128)(2,1)S(1)}, s32[8,128]{1,0:T(8,128)S(1)}, f32[128,1024]{1,0:T(8,128)S(1)}, f32[128,1024]{1,0:T(8,128)S(1)}, f32[128,...) custom-call(f32[32,8,128]{2,1,0:T(8,128)S(1)} %all_to_all.10.refs_0_, ...), custom_call_target="tpu_custom_call" | custom-call | tf_op jit(solution)/shard_map/forward/pallas_call | solution.py:507
  18.8 0.3 collective-permute-start
  19.1 1.0 %collective-permute-done = bf16[1,128,128]{2,1,0:T(8,128)(2,1)S(1)} collective-permute-done((bf16[1,128,128]{2,1,0:T(8,128)(2,1)S(1)}, bf16[1,128,128]{2,1,0:T(8,128)(2,1)S(1)}, u32[]{:S(2)}, u32[]{:S(2)}) %collective-permute-start) | collective-permute-done | bytes 32800 | tf_op jit(solution)/shard_map/ppermute | solution.py:34
  20.1 0.5 collective-permute-start.4
  20.6 1.7 %collective-permute-start.3 = (bf16[2,128,128]{2,1,0:T(8,128)(2,1)S(1)}, bf16[2,128,128]{2,1,0:T(8,128)(2,1)S(1)}, u32[]{:S(2)}, u32[]{:S(2)}) collective-permute-start(bf16[2,128,128]{2,1,0:T(8,128)(2,1)S(1)} %constant_dynamic-update-slice_fusion.refs_4_), channel_id=1, source_target_pairs={{0,12},{1,11},{2,14},{3,9},{6,10},{7,13},{4,8},{5,15},{8,4},{9,3},... | collective-permute-start | bytes 196616 | tf_op jit(solution)/shard_map/ppermute | solution.py:57
  22.3 1.0 %collective-permute-start.2 = (bf16[2,128,128]{2,1,0:T(8,128)(2,1)S(1)}, bf16[2,128,128]{2,1,0:T(8,128)(2,1)S(1)}, u32[]{:S(2)}, u32[]{:S(2)}) collective-permute-start(bf16[2,128,128]{2,1,0:T(8,128)(2,1)S(1)} %constant_dynamic-update-slice_fusion.refs_4_), channel_id=1, source_target_pairs={{0,4},{1,3},{2,6},{3,1},{6,2},{7,5},{4,0},{5,7},{8,12},{9,11},{10,... | collective-permute-start | bytes 196616 | tf_op jit(solution)/shard_map/ppermute | solution.py:57
  23.3 0.8 %collective-permute-start.1 = (bf16[2,128,128]{2,1,0:T(8,128)(2,1)S(1)}, bf16[2,128,128]{2,1,0:T(8,128)(2,1)S(1)}, u32[]{:S(2)}, u32[]{:S(2)}) collective-permute-start(bf16[2,128,128]{2,1,0:T(8,128)(2,1)S(1)} %constant_dynamic-update-slice_fusion.refs_4_), channel_id=1, source_target_pairs={{0,8},{1,17},{2,10},{3,19},{6,14},{7,23},{4,12},{5,21},{8,0},{9,25... | collective-permute-start | bytes 196616 | tf_op jit(solution)/shard_map/ppermute | solution.py:57
  24.1 3.5 %onehot.1 = (bf16[2304,1024]{1,0:T(8,128)(2,1)S(1)}, bf16[1024,2304]{1,0:T(8,128)(2,1)S(1)}, bf16[128,1024]{1,0:T(8,128)(2,1)S(1)}, bf16[128,128]{1,0:T(8,128)(2,1)S(1)}, f32[128,128]{1,0:T(8,128)S(1)}) custom-call(s32[8,128]{1,0:T(8,128)S(1)} %get-tuple-element.30.code_ref, bf16[128,128]{1,0:T(8,128)(2,1)S(1)} %copy-done.3, f32[1,128]{1,0:T(1,128)S(1)} %bitcast.3), custom_call_target="tpu_custom_call" | custom-call | flops 1073741824 | bytes 8388608 | tf_op jit(solution)/shard_map/onehot/pallas_call | solution.py:507
  27.7 0.5 collective-permute-done.1.refs_0_
  28.3 1.5 %collective-permute-done.5.refs_5_ = bf16[8,128,128]{2,1,0:T(8,128)(2,1)S(1)} collective-permute-done((bf16[8,128,128]{2,1,0:T(8,128)(2,1)S(1)}, bf16[8,128,128]{2,1,0:T(8,128)(2,1)S(1)}, u32[]{:S(2)}, u32[]{:S(2)}) %collective-permute-start.5) | collective-permute-done | bytes 262176 | tf_op jit(solution)/shard_map/ppermute | solution.py:34
  29.8 2.0 %second.1 = (f32[1,128]{1,0:T(1,128)S(1)}, f32[128,1024]{1,0:T(8,128)S(1)}, bf16[9,128,128]{2,1,0:T(8,128)(2,1)S(1)}, bf16[9,128,128]{2,1,0:T(8,128)(2,1)S(1)}) custom-call(bf16[2,128,128]{2,1,0:T(8,128)(2,1)S(1)} %collective-permute-done.1.refs_0_, bf16[2,128,128]{2,1,0:T(8,128)(2,1)S(1)} %collective-permute-done.2.refs_1_, ...), custom_call_target="tpu_custom_call" | custom-call | tf_op jit(solution)/shard_map/second/pallas_call | solution.py:507
  32.0 1.4 %collective-permute-done.6 = bf16[9,128,128]{2,1,0:T(8,128)(2,1)S(1)} collective-permute-done((bf16[9,128,128]{2,1,0:T(8,128)(2,1)S(1)}, bf16[9,128,128]{2,1,0:T(8,128)(2,1)S(1)}, u32[]{:S(2)}, u32[]{:S(2)}) %collective-permute-start.6) | collective-permute-done | bytes 294944 | tf_op jit(solution)/shard_map/ppermute | solution.py:34
  33.6 0.8 %collective-permute-start.7 = (bf16[2,128,128]{2,1,0:T(8,128)(2,1)S(1)}, bf16[2,128,128]{2,1,0:T(8,128)(2,1)S(1)}, u32[]{:S(2)}, u32[]{:S(2)}) collective-permute-start(bf16[2,128,128]{2,1,0:T(8,128)(2,1)S(1)} %get-tuple-element.58), channel_id=1, source_target_pairs={{0,8},{1,17},{2,10},{3,19},{6,14},{7,23},{4,12},{5,21},{8,0},{9,25... | collective-permute-start | bytes 196616 | tf_op jit(solution)/shard_map/ppermute | solution.py:57
  34.4 2.9 %collective-permute-start.10 = (bf16[2,128,128]{2,1,0:T(8,128)(2,1)S(1)}, bf16[2,128,128]{2,1,0:T(8,128)(2,1)S(1)}, u32[]{:S(2)}, u32[]{:S(2)}) collective-permute-start(bf16[2,128,128]{2,1,0:T(8,128)(2,1)S(1)} %get-tuple-element.59), channel_id=1, source_target_pairs={{0,18},{1,21},{2,16},{3,23},{6,20},{7,19},{4,22},{5,17},{8,26},{9,... | collective-permute-start | bytes 196616 | tf_op jit(solution)/shard_map/ppermute | solution.py:57
  37.2 1.4 %collective-permute-start.9 = (bf16[2,128,128]{2,1,0:T(8,128)(2,1)S(1)}, bf16[2,128,128]{2,1,0:T(8,128)(2,1)S(1)}, u32[]{:S(2)}, u32[]{:S(2)}) collective-permute-start(bf16[2,128,128]{2,1,0:T(8,128)(2,1)S(1)} %get-tuple-element.60), channel_id=1, source_target_pairs={{0,12},{1,11},{2,14},{3,9},{6,10},{7,13},{4,8},{5,15},{8,4},{9,3},... | collective-permute-start | bytes 196616 | tf_op jit(solution)/shard_map/ppermute | solution.py:57
  38.6 1.4 %collective-permute-start.8 = (bf16[2,128,128]{2,1,0:T(8,128)(2,1)S(1)}, bf16[2,128,128]{2,1,0:T(8,128)(2,1)S(1)}, u32[]{:S(2)}, u32[]{:S(2)}) collective-permute-start(bf16[2,128,128]{2,1,0:T(8,128)(2,1)S(1)} %get-tuple-element.61), channel_id=1, source_target_pairs={{0,4},{1,3},{2,6},{3,1},{6,2},{7,5},{4,0},{5,7},{8,12},{9,11},{10,... | collective-permute-start | bytes 196616 | tf_op jit(solution)/shard_map/ppermute | solution.py:57
  39.9 2.5 %collective-permute-done.10 = bf16[2,128,128]{2,1,0:T(8,128)(2,1)S(1)} collective-permute-done((bf16[2,128,128]{2,1,0:T(8,128)(2,1)S(1)}, bf16[2,128,128]{2,1,0:T(8,128)(2,1)S(1)}, u32[]{:S(2)}, u32[]{:S(2)}) %collective-permute-start.10) | collective-permute-done | bytes 65568 | tf_op jit(solution)/shard_map/ppermute | solution.py:57
  42.4 0.7 %collective-permute-done.9 = bf16[2,128,128]{2,1,0:T(8,128)(2,1)S(1)} collective-permute-done((bf16[2,128,128]{2,1,0:T(8,128)(2,1)S(1)}, bf16[2,128,128]{2,1,0:T(8,128)(2,1)S(1)}, u32[]{:S(2)}, u32[]{:S(2)}) %collective-permute-start.9) | collective-permute-done | bytes 65568 | tf_op jit(solution)/shard_map/ppermute | solution.py:57
  43.5 1.2 %collective-permute-done.11 = f32[1,128,128]{2,1,0:T(8,128)S(1)} collective-permute-done((f32[1,128,128]{2,1,0:T(8,128)S(1)}, f32[1,128,128]{2,1,0:T(8,128)S(1)}, u32[]{:S(2)}, u32[]{:S(2)}) %collective-permute-start.11) | collective-permute-done | bytes 65568 | tf_op jit(solution)/shard_map/ppermute | solution.py:34
  44.8 2.3 %backward.1 = f32[32,4,128]{2,1,0:T(4,128)S(1)} custom-call(f32[1,128,128]{2,1,0:T(8,128)S(1)} %fusion.owned_ref, f32[1,128]{1,0:T(1,128)S(1)} %get-tuple-element.47.energy_ref, f32[128,1024]{1,0:T(8,128)S(1)} %get-tuple-element.48.grad_edge_ref, f32[128,1024]{1,0:T(8,128)S(1)} %get-tuple-element.49.dse_ref, f32[128,1024]{1,0:T(8,128)S(1)} %get-tuple-element.50.dsl_ref, ...), custom_call_target="tpu_custom_call" | custom-call | tf_op jit(solution)/shard_map/backward/pallas_call | solution.py:507
  47.1 10.1 %all_to_all.11.moved_ref = f32[32,4,128]{2,1,0:T(4,128)S(1)} all-to-all(f32[32,4,128]{2,1,0:T(4,128)S(1)} %backward.1), channel_id=1, replica_groups=mesh['gx'=4,'gy'=4,'gz'=2] {'gx','gy','gz'}, dimensions={0} | all-to-all | bytes 131072 | tf_op jit(solution)/shard_map/all_to_all | solution.py:586
  57.2 0.7 %finish.1 = (f32[1,1,2,64]{3,2,1,0:T(2,128)}, f32[1,1,2,192]{3,2,1,0:T(2,128)}) custom-call(f32[32,4,128]{2,1,0:T(4,128)S(1)} %all_to_all.11.moved_ref), custom_call_target="tpu_custom_call" | custom-call | tf_op jit(solution)/shard_map/finish/pallas_call | solution.py:507
  (40 shorter events, 0.9 us)
Async XLA Ops:
  0.6 0.7 %copy-start.5 = (s32[1,1,2,512]{3,2,1,0:T(2,128)S(1)}, s32[1,1,2,512]{3,2,1,0:T(2,128)}, u32[]{:S(2)}) copy-start(s32[1,1,2,512]{3,2,1,0:T(2,128)} %nb_ref.1) | copy-start | bytes 12292
  0.6 0.7 %copy-start.9 = (s32[1,1,2,64]{3,2,1,0:T(2,128)S(1)}, s32[1,1,2,64]{3,2,1,0:T(2,128)}, u32[]{:S(2)}) copy-start(s32[1,1,2,64]{3,2,1,0:T(2,128)} %spec_ref.1) | copy-start | bytes 1540
  0.7 0.7 %copy-start.8 = (f32[1,1,2,192]{3,2,1,0:T(2,128)S(1)}, f32[1,1,2,192]{3,2,1,0:T(2,128)}, u32[]{:S(2)}) copy-start(f32[1,1,2,192]{3,2,1,0:T(2,128)} %pos_ref.1) | copy-start | bytes 4612
  0.7 16.1 %copy-start = (bf16[384,128]{1,0:T(8,128)(2,1)S(1)}, bf16[384,128]{1,0:T(8,128)(2,1)}, u32[]{:S(2)}) copy-start(bf16[384,128]{1,0:T(8,128)(2,1)} %upd_ref.1) | copy-start | bytes 294916
  0.7 16.1 %copy-start.2 = (bf16[128,128]{1,0:T(8,128)(2,1)S(1)}, bf16[128,128]{1,0:T(8,128)(2,1)}, u32[]{:S(2)}) copy-start(bf16[128,128]{1,0:T(8,128)(2,1)} %envw_ref.1) | copy-start | bytes 98308
  0.7 16.1 %copy-start.1 = (bf16[128,128]{1,0:T(8,128)(2,1)S(1)}, bf16[128,128]{1,0:T(8,128)(2,1)}, u32[]{:S(2)}) copy-start(bf16[128,128]{1,0:T(8,128)(2,1)} %mix_ref.1) | copy-start | bytes 98308
  0.7 16.1 %copy-start.4 = (bf16[8,128]{1,0:T(8,128)(2,1)S(1)}, bf16[8,128]{1,0:T(8,128)(2,1)}, u32[]{:S(2)}) copy-start(bf16[8,128]{1,0:T(8,128)(2,1)} %radial_ref.1) | copy-start | bytes 6148
  0.7 16.1 %copy-start.7 = (bf16[5,128]{1,0:T(8,128)(2,1)S(1)}, bf16[5,128]{1,0:T(8,128)(2,1)}, u32[]{:S(2)}) copy-start(bf16[5,128]{1,0:T(8,128)(2,1)} %refs_2_.1) | copy-start | bytes 3844
  0.7 16.1 %copy-start.6 = (bf16[5,128]{1,0:T(8,128)(2,1)S(1)}, bf16[5,128]{1,0:T(8,128)(2,1)}, u32[]{:S(2)}) copy-start(bf16[5,128]{1,0:T(8,128)(2,1)} %refs_1_.1) | copy-start | bytes 3844
  0.7 23.4 %copy-start.3 = (bf16[128,128]{1,0:T(8,128)(2,1)S(1)}, bf16[128,128]{1,0:T(8,128)(2,1)}, u32[]{:S(2)}) copy-start(bf16[128,128]{1,0:T(8,128)(2,1)} %refs_9_.1) | copy-start | bytes 98308
  0.7 23.4 %copy-start.10 = (f32[128]{0:T(128)S(1)}, f32[128]{0:T(128)}, u32[]{:S(2)}) copy-start(f32[128]{0:T(128)} %param.21) | copy-start | bytes 1540
  18.8 1.3 %collective-permute-start = (bf16[1,128,128]{2,1,0:T(8,128)(2,1)S(1)}, bf16[1,128,128]{2,1,0:T(8,128)(2,1)S(1)}, u32[]{:S(2)}, u32[]{:S(2)}) collective-permute-start(bf16[1,128,128]{2,1,0:T(8,128)(2,1)S(1)} %get-tuple-element.29), channel_id=1, source_target_pairs={{0,1},{1,0},{2,3},{3,2},{4,5},{5,4},{6,7},{7,6},{8,9},{9,8},{10,11... | collective-permute-start | bytes 98312 | tf_op jit(solution)/shard_map/ppermute | solution.py:34
  20.1 7.5 %collective-permute-start.4 = (bf16[2,128,128]{2,1,0:T(8,128)(2,1)S(1)}, bf16[2,128,128]{2,1,0:T(8,128)(2,1)S(1)}, u32[]{:S(2)}, u32[]{:S(2)}) collective-permute-start(bf16[2,128,128]{2,1,0:T(8,128)(2,1)S(1)} %constant_dynamic-update-slice_fusion.refs_4_), channel_id=1, source_target_pairs={{0,18},{1,21},{2,16},{3,23},{6,20},{7,19},{4,22},{5,17},{8,26},{9,... | collective-permute-start | bytes 196616 | tf_op jit(solution)/shard_map/ppermute | solution.py:57
  20.6 7.0 %collective-permute-start.3 = (bf16[2,128,128]{2,1,0:T(8,128)(2,1)S(1)}, bf16[2,128,128]{2,1,0:T(8,128)(2,1)S(1)}, u32[]{:S(2)}, u32[]{:S(2)}) collective-permute-start(bf16[2,128,128]{2,1,0:T(8,128)(2,1)S(1)} %constant_dynamic-update-slice_fusion.refs_4_), channel_id=1, source_target_pairs={{0,12},{1,11},{2,14},{3,9},{6,10},{7,13},{4,8},{5,15},{8,4},{9,3},... | collective-permute-start | bytes 196616 | tf_op jit(solution)/shard_map/ppermute | solution.py:57
  22.3 5.4 %collective-permute-start.2 = (bf16[2,128,128]{2,1,0:T(8,128)(2,1)S(1)}, bf16[2,128,128]{2,1,0:T(8,128)(2,1)S(1)}, u32[]{:S(2)}, u32[]{:S(2)}) collective-permute-start(bf16[2,128,128]{2,1,0:T(8,128)(2,1)S(1)} %constant_dynamic-update-slice_fusion.refs_4_), channel_id=1, source_target_pairs={{0,4},{1,3},{2,6},{3,1},{6,2},{7,5},{4,0},{5,7},{8,12},{9,11},{10,... | collective-permute-start | bytes 196616 | tf_op jit(solution)/shard_map/ppermute | solution.py:57
  23.3 4.9 %collective-permute-start.1 = (bf16[2,128,128]{2,1,0:T(8,128)(2,1)S(1)}, bf16[2,128,128]{2,1,0:T(8,128)(2,1)S(1)}, u32[]{:S(2)}, u32[]{:S(2)}) collective-permute-start(bf16[2,128,128]{2,1,0:T(8,128)(2,1)S(1)} %constant_dynamic-update-slice_fusion.refs_4_), channel_id=1, source_target_pairs={{0,8},{1,17},{2,10},{3,19},{6,14},{7,23},{4,12},{5,21},{8,0},{9,25... | collective-permute-start | bytes 196616 | tf_op jit(solution)/shard_map/ppermute | solution.py:57
  28.2 1.6 %collective-permute-start.5 = (bf16[8,128,128]{2,1,0:T(8,128)(2,1)S(1)}, bf16[8,128,128]{2,1,0:T(8,128)(2,1)S(1)}, u32[]{:S(2)}, u32[]{:S(2)}) collective-permute-start(bf16[8,128,128]{2,1,0:T(8,128)(2,1)S(1)} %pad_maximum_fusion), channel_id=1, source_target_pairs={{0,1},{1,0},{2,3},{3,2},{4,5},{5,4},{6,7},{7,6},{8,9},{9,8},{10,11... | collective-permute-start | bytes 786440 | tf_op jit(solution)/shard_map/ppermute | solution.py:34
  31.8 1.6 %collective-permute-start.6 = (bf16[9,128,128]{2,1,0:T(8,128)(2,1)S(1)}, bf16[9,128,128]{2,1,0:T(8,128)(2,1)S(1)}, u32[]{:S(2)}, u32[]{:S(2)}) collective-permute-start(bf16[9,128,128]{2,1,0:T(8,128)(2,1)S(1)} %get-tuple-element.46), channel_id=1, source_target_pairs={{0,1},{1,0},{2,3},{3,2},{4,5},{5,4},{6,7},{7,6},{8,9},{9,8},{10,11... | collective-permute-start | bytes 884744 | tf_op jit(solution)/shard_map/ppermute | solution.py:34
  33.6 6.4 %collective-permute-start.7 = (bf16[2,128,128]{2,1,0:T(8,128)(2,1)S(1)}, bf16[2,128,128]{2,1,0:T(8,128)(2,1)S(1)}, u32[]{:S(2)}, u32[]{:S(2)}) collective-permute-start(bf16[2,128,128]{2,1,0:T(8,128)(2,1)S(1)} %get-tuple-element.58), channel_id=1, source_target_pairs={{0,8},{1,17},{2,10},{3,19},{6,14},{7,23},{4,12},{5,21},{8,0},{9,25... | collective-permute-start | bytes 196616 | tf_op jit(solution)/shard_map/ppermute | solution.py:57
  34.4 8.1 %collective-permute-start.10 = (bf16[2,128,128]{2,1,0:T(8,128)(2,1)S(1)}, bf16[2,128,128]{2,1,0:T(8,128)(2,1)S(1)}, u32[]{:S(2)}, u32[]{:S(2)}) collective-permute-start(bf16[2,128,128]{2,1,0:T(8,128)(2,1)S(1)} %get-tuple-element.59), channel_id=1, source_target_pairs={{0,18},{1,21},{2,16},{3,23},{6,20},{7,19},{4,22},{5,17},{8,26},{9,... | collective-permute-start | bytes 196616 | tf_op jit(solution)/shard_map/ppermute | solution.py:57
  37.2 5.9 %collective-permute-start.9 = (bf16[2,128,128]{2,1,0:T(8,128)(2,1)S(1)}, bf16[2,128,128]{2,1,0:T(8,128)(2,1)S(1)}, u32[]{:S(2)}, u32[]{:S(2)}) collective-permute-start(bf16[2,128,128]{2,1,0:T(8,128)(2,1)S(1)} %get-tuple-element.60), channel_id=1, source_target_pairs={{0,12},{1,11},{2,14},{3,9},{6,10},{7,13},{4,8},{5,15},{8,4},{9,3},... | collective-permute-start | bytes 196616 | tf_op jit(solution)/shard_map/ppermute | solution.py:57
  38.6 4.8 %collective-permute-start.8 = (bf16[2,128,128]{2,1,0:T(8,128)(2,1)S(1)}, bf16[2,128,128]{2,1,0:T(8,128)(2,1)S(1)}, u32[]{:S(2)}, u32[]{:S(2)}) collective-permute-start(bf16[2,128,128]{2,1,0:T(8,128)(2,1)S(1)} %get-tuple-element.61), channel_id=1, source_target_pairs={{0,4},{1,3},{2,6},{3,1},{6,2},{7,5},{4,0},{5,7},{8,12},{9,11},{10,... | collective-permute-start | bytes 196616 | tf_op jit(solution)/shard_map/ppermute | solution.py:57
  43.4 1.3 %collective-permute-start.11 = (f32[1,128,128]{2,1,0:T(8,128)S(1)}, f32[1,128,128]{2,1,0:T(8,128)S(1)}, u32[]{:S(2)}, u32[]{:S(2)}) collective-permute-start(f32[1,128,128]{2,1,0:T(8,128)S(1)} %slice.38), channel_id=1, source_target_pairs={{0,1},{1,0},{2,3},{3,2},{4,5},{5,4},{6,7},{7,6},{8,9},{9,8},{10,11... | collective-permute-start | bytes 196616 | tf_op jit(solution)/shard_map/ppermute | solution.py:34

commit v6 on v5

--- a/solution.py
+++ b/solution.py
@@ -57,35 +57,21 @@
     return lax.ppermute(value, EVERY, pairs)
 
 
-def gather_halo(chunk, beside=None):
-    if is_direct():
-        both = jnp.concatenate([chunk, shifted(chunk, "gz", 1)], axis=0)
-        direct = [swapped(both, slot) for slot in range(4)]
-        direct, beside = lax.optimization_barrier((direct, beside))
-        relayed = shifted(jnp.concatenate(direct, axis=0), "gz", 1)
-        near = [(slot, row) for slot in range(4) for row in range(2)] + [(4, 0)]
-        far = [(5, row) for row in range(8)] + [(4, 1)]
-        return direct + [both, relayed], near + far, beside
+def ring_gather(chunk):
     for axis in ("gx", "gy"):
         lower = shifted(chunk, axis, 1)
         upper = shifted(chunk, axis, -1)
         chunk = jnp.concatenate([lower, upper, chunk], axis=0)
-    order = [(array, row) for array in range(2) for row in range(9)]
     if lax.axis_size("gz") == 2:
-        return [chunk, shifted(chunk, "gz", 1)], order, beside
+        return [chunk, shifted(chunk, "gz", 1)]
     half = chunk.shape[-1] // 2
     above = shifted(chunk[..., :half], "gz", -1)
     below = shifted(chunk[..., half:], "gz", 1)
-    return [chunk, jnp.concatenate([above, below], axis=-1)], order, beside
-
-
-def reduce_halo(own, other):
+    return [chunk, jnp.concatenate([above, below], axis=-1)]
+
+
+def ring_reduce(own, other):
     kind = own.dtype
-    if is_direct():
-        own = own.astype(F32) + shifted(other, "gz", 1).astype(F32)
-        came = [swapped(own[2 * slot : 2 * slot + 2].astype(kind), slot).astype(F32) for slot in range(4)]
-        both = came[0] + came[1] + came[2] + came[3]
-        return own[8:] + both[:1] + shifted(both[1:], "gz", 1)
     if lax.axis_size("gz") == 2:
         back = shifted(other, "gz", 1)
     else:
@@ -114,21 +100,22 @@
     return number((x + step_x) & 3, (y + step_y) & 3, core ^ outside)
 
 
-def place_column(step_x, step_y, outside, direct):
-    if not direct:
-        place_x = jnp.where(step_x == 0, 2, jnp.where(step_x < 0, 0, 1))
-        place_y = jnp.where(step_y == 0, 2, jnp.where(step_y < 0, 0, 1))
-        return outside * 9 + place_y * 3 + place_x
+def place_ring(step_x, step_y, outside):
+    place_x = jnp.where(step_x == 0, 2, jnp.where(step_x < 0, 0, 1))
+    place_y = jnp.where(step_y == 0, 2, jnp.where(step_y < 0, 0, 1))
+    return outside * 9 + place_y * 3 + place_x
+
+
+def place_direct(step_x, step_y, outside, twin):
     x, y, core = column_here()
     way_x = jnp.where(step_x == 0, 0, jnp.where(step_x == 1 - 2 * (x & 1), 1, 2))
     way_y = jnp.where(step_y == 0, 0, jnp.where(step_y == 1 - 2 * (y & 1), 1, 2))
     way = way_x * 3 + way_y
-    chunk = 8 + 9 * outside
-    for mate in range(2):
-        mine = core == mate
-        for slot, (to_x, to_y) in enumerate(ROUTES[mate]):
-            spot = jnp.where(mine, 2 * slot + outside, 9 + 2 * slot + 1 - outside)
-            chunk = jnp.where(way == to_x * 3 + to_y, spot, chunk)
+    other = 1 - outside if twin else outside
+    chunk = jnp.where(way == 0, -1 if twin else 8 + other, -1)
+    for slot in range(4):
+        here, there = (ROUTES[mate][slot][0] * 3 + ROUTES[mate][slot][1] for mate in range(2))
+        chunk = jnp.where(way == jnp.where(core == 0, here, there), 2 * slot + other, chunk)
     return chunk
 
 
@@ -164,32 +151,44 @@
             out_ref[0, row : row + 1, :] = (first * 2048 + second).astype(F32)
 
 
-def onehot_kernel(
-    direct, code_ref, second_ref, readout_ref, gather_ref, scatter_ref, lane_ref, secondt_ref, rocol_ref, turn_ref
-):
-    step_x, step_y, step_z, outside, lane = decode(code_ref[...], ATOMS // 2)
-    target = place_column(step_x, step_y, outside, direct) * ATOMS + lane
+def onehot_kernel(direct, *refs):
+    codes = [refs[0][...]]
+    if direct:
+        codes.append(listed_codes(refs[1][owner_at(0, 0, 1)][4:8, :]))
+    second_ref, readout_ref, gather_ref, scatter_ref, lane_ref, secondt_ref, rocol_ref, turn_ref = refs[-8:]
     secondt_ref[...] = second_ref[...].astype(F32).T.astype(BF16)
     rocol_ref[...] = jnp.broadcast_to(readout_ref[...], (ATOMS, ATOMS)).T
+    down = lax.broadcasted_iota(jnp.int32, (ATOMS, ATOMS), 0).astype(F32).astype(BF16)
+    across = lax.broadcasted_iota(jnp.int32, (ATOMS, ATOMS), 1).astype(F32).astype(BF16)
+    one = jnp.ones((ATOMS, ATOMS), BF16)
+    zero = jnp.zeros((ATOMS, ATOMS), BF16)
     turn_ref[...] = jnp.zeros(turn_ref.shape, F32)
-    turn_ref[0:NEIGH, :] = target.astype(F32)
-    turned = turn_ref[...].T.astype(jnp.int32)
-    down = lax.broadcasted_iota(jnp.int32, (ATOMS, ATOMS), 0)
-    across = lax.broadcasted_iota(jnp.int32, (ATOMS, ATOMS), 1)
-    for k in range(NEIGH):
-        span = slice(k * ATOMS, (k + 1) * ATOMS)
-        aim = jnp.broadcast_to(target[k : k + 1, :], (ATOMS, ATOMS)) - down
-        aim_turned = jnp.broadcast_to(turned[:, k : k + 1], (ATOMS, ATOMS)) - across
-        near = jnp.broadcast_to(lane[k : k + 1, :], (ATOMS, ATOMS)) == down
-        lane_ref[:, span] = jnp.where(near, 1.0, 0.0).astype(BF16)
-
-        def fill(c, carry, span=span, aim=aim, aim_turned=aim_turned):
-            part = pl.ds(pl.multiple_of(c * ATOMS, ATOMS), ATOMS)
-            gather_ref[part, span] = jnp.where(aim == c * ATOMS, 1.0, 0.0).astype(BF16)
-            scatter_ref[span, part] = jnp.where(aim_turned == c * ATOMS, 1.0, 0.0).astype(BF16)
-            return carry
-
-        lax.fori_loop(0, CHUNKS, fill, 0)
+    for twin, code in enumerate(codes):
+        step_x, step_y, step_z, outside, lane = decode(code, ATOMS // 2)
+        chunk = place_direct(step_x, step_y, outside, twin) if direct else place_ring(step_x, step_y, outside)
+        lane, chunk = lane.astype(F32), chunk.astype(F32)
+        turn_ref[0:NEIGH, :] = lane
+        turn_ref[NEIGH : 2 * NEIGH, :] = chunk
+        turned = turn_ref[...].T
+        for k in range(NEIGH):
+            span = slice((twin * NEIGH + k) * ATOMS, (twin * NEIGH + k + 1) * ATOMS)
+
+            def row(array, k=k):
+                return jnp.broadcast_to(array[k : k + 1, :], (ATOMS, ATOMS)).astype(BF16)
+
+            def column(at):
+                return jnp.broadcast_to(turned[:, at : at + 1], (ATOMS, ATOMS)).astype(BF16)
+
+            near = jnp.where(row(lane) == down, one, zero)
+            near_turned = jnp.where(column(k) == across, one, zero)
+            at, at_turned = row(chunk), column(NEIGH + k)
+            if not twin:
+                lane_ref[:, span] = near
+            for c in range(gather_ref.shape[0] // ATOMS):
+                part = slice(c * ATOMS, (c + 1) * ATOMS)
+                this = jnp.full((ATOMS, ATOMS), c, BF16)
+                gather_ref[part, span] = jnp.where(at == this, near, zero)
+                scatter_ref[span, part] = jnp.where(at_turned == this, near_turned, zero)
 
 
 def listed_codes(words):
@@ -354,42 +353,60 @@
 
 
 def second_kernel(parts, order, *refs):
-    (
-        gather_ref, scatter_ref, edge_ref, second_ref, secondt_ref, rocol_ref,
-        energy_ref, grad_edge_ref, back_own_ref, back_other_ref, other_ref, grad_ref,
-    ) = refs[parts:]
+    gather_ref, scatter_ref, second_ref, secondt_ref, rocol_ref = refs[parts : parts + 5]
+    sets = gather_ref.shape[1] // EDGES
+    edges = refs[parts + 5 : parts + 5 + sets]
+    energy_ref, grad_edge_ref, *outs = refs[parts + 5 + sets : -2]
+    other_ref, grad_ref = refs[-2:]
     table = jnp.concatenate([refs[array][row] for array, row in order], axis=1)
     rocol = rocol_ref[...]
     other_ref[...] = jnp.dot(table, gather_ref[...], preferred_element_type=F32)
     wide = 2 * ATOMS
-    total = jnp.zeros((ATOMS, ATOMS), F32)
-    for j in range(EDGES // wide):
-        span = slice(j * wide, (j + 1) * wide)
-        other = other_ref[:, span]
-        edge = edge_ref[:, span]
-        hidden, ds = silu_pair(jnp.dot(secondt_ref[...], (edge * other).astype(BF16), preferred_element_type=F32))
-        total = total + hidden[:, :ATOMS] + hidden[:, ATOMS:]
-        grad_hidden = ds * jnp.concatenate([rocol, rocol], axis=1)
-        grad_prod = jnp.dot(second_ref[...], grad_hidden.astype(BF16), preferred_element_type=F32)
-        grad_prod = grad_prod.astype(BF16).astype(F32)
-        grad_edge_ref[:, span] = grad_prod * other
-        grad_ref[:, span] = (grad_prod * edge).astype(BF16)
-    energy_ref[...] = jnp.sum(total * rocol, axis=0, keepdims=True)
-    for c in range(0, CHUNKS, 2):
-        back = jnp.dot(
-            grad_ref[...], scatter_ref[:, c * ATOMS : (c + 2) * ATOMS], preferred_element_type=F32
-        ).astype(BF16)
+    if sets == 2:
+        give_ref = outs.pop(0)
+        give_ref[ATOMS:, :] = jnp.zeros((8, EDGES), F32)
+    for own in range(sets):
+        total = jnp.zeros((ATOMS, ATOMS), F32)
+        for j in range(EDGES // wide):
+            span = slice(j * wide, (j + 1) * wide)
+            both = slice(own * EDGES + j * wide, own * EDGES + (j + 1) * wide)
+            other = other_ref[:, both]
+            edge = edges[own][:, span]
+            hidden, ds = silu_pair(
+                jnp.dot(secondt_ref[...], (edge * other).astype(BF16), preferred_element_type=F32)
+            )
+            total = total + hidden[:, :ATOMS] + hidden[:, ATOMS:]
+            grad_hidden = ds * jnp.concatenate([rocol, rocol], axis=1)
+            grad_prod = jnp.dot(second_ref[...], grad_hidden.astype(BF16), preferred_element_type=F32)
+            grad_prod = grad_prod.astype(BF16).astype(F32)
+            if own == 0:
+                grad_edge_ref[:, span] = grad_prod * other
+            else:
+                give_ref[:ATOMS, span] = grad_prod * other
+            grad_ref[:, both] = (grad_prod * edge).astype(BF16)
+        energy = jnp.sum(total * rocol, axis=0, keepdims=True)
+        if own == 0:
+            energy_ref[...] = energy
+        else:
+            give_ref[ATOMS : ATOMS + 1, :ATOMS] = energy
+    places = [(ref, row) for ref in outs for row in range(ref.shape[0])]
+    for c in range(0, len(places), 2):
+        back = jnp.dot(grad_ref[...], scatter_ref[:, c * ATOMS : (c + 2) * ATOMS], preferred_element_type=F32)
         for i in range(2):
-            ref = back_own_ref if c + i < 9 else back_other_ref
-            ref[(c + i) % 9] = back[:, i * ATOMS : (i + 1) * ATOMS]
+            ref, row = places[c + i]
+            ref[row] = back[:, i * ATOMS : (i + 1) * ATOMS].astype(ref.dtype)
 
 
 def backward_kernel(
     direct, owned_ref, energy_ref, grad_edge_ref, dse_ref, dsl_ref, dsb_ref, env_ref, v_ref, geo_ref, code_ref, lane_ref,
     upd_ref, envw_ref, mix_ref, radial_ref, *refs,
 ):
-    outs = refs[: 1 if direct else 2]
-    yb_ref, dinv_ref, denv_ref, dlat_ref, part_ref, force_ref = refs[len(outs) :]
+    *extra, yb_ref, dinv_ref, denv_ref, dlat_ref, part_ref, force_ref = refs
+    energy = energy_ref[...]
+    if direct:
+        given_ref, *extra = extra
+        energy = energy + given_ref[ATOMS : ATOMS + 1, :ATOMS]
+    outs = extra
     r, ux, uy, uz = (geo_ref[i] for i in range(4))
     angular = angular_rows(ux, uy, uz)
     spread_rows(yb_ref, angular)
@@ -397,6 +414,8 @@
     for j in range(EDGES // TILE):
         span = slice(j * TILE, (j + 1) * TILE)
         d_edge = grad_edge_ref[:, span] + jnp.concatenate([share] * (TILE // ATOMS), axis=1)
+        if direct:
+            d_edge = d_edge + given_ref[:ATOMS, span]
         d_pre = d_edge * dse_ref[:, span]
         dlat_ref[:, span] = d_pre
         dinv_ref[:, span] = jnp.dot(upd_ref[...], d_pre.astype(BF16), preferred_element_type=F32).astype(BF16)
@@ -475,7 +494,7 @@
     back = lax.dot_general(
         force_ref[...], lane_ref[...], (((1,), (1,)), ((), ())), preferred_element_type=F32
     )
-    center = jnp.concatenate([jnp.sum(p, axis=0, keepdims=True) for p in pull] + [-energy_ref[...]], axis=0)
+    center = jnp.concatenate([jnp.sum(p, axis=0, keepdims=True) for p in pull] + [-energy], axis=0)
     if direct:
         outs[0][...] = jnp.zeros(outs[0].shape, F32)
     for c in range(CHUNKS):
@@ -539,7 +558,7 @@
         copies = jnp.broadcast_to(packed, (devices, 8, ATOMS))
         tables = [lax.all_to_all(copies, EVERY, 0, 0, tiled=True)]
     else:
-        tables, order, _ = gather_halo(packed)
+        tables = ring_gather(packed)
     table, code, edge, dsb, dsl, dse, env, field, geo = call(
         functools.partial(forward_kernel, len(tables), direct),
         [
@@ -552,25 +571,46 @@
         ],
         name="forward",
     )(*tables, center_table, neighbor_table, radial_weight, mix_weight, env_weight, update_weight)
-    beside = call(
+    chunks, sets = (10, 2) if direct else (CHUNKS, 1)
+    sent = edge
+    if direct:
+        both = jnp.concatenate([table, shifted(table, "gz", 1)], axis=0)
+        both, sent, code = lax.optimization_barrier((both, edge, code))
+    gather, scatter, lanes, secondt, rocol = call(
         functools.partial(onehot_kernel, direct),
         [
-            ((CHUNKS * ATOMS, EDGES), BF16), ((EDGES, CHUNKS * ATOMS), BF16), (edges, BF16), (square, BF16),
-            (square, F32),
+            ((chunks * ATOMS, sets * EDGES), BF16), ((sets * EDGES, chunks * ATOMS), BF16), (edges, BF16),
+            (square, BF16), (square, F32),
         ],
         [pltpu.VMEM(square, F32)],
         name="onehot",
         cost=pl.CostEstimate(flops=1 << 30, bytes_accessed=8 << 20, transcendentals=0),
-    )(code, second_weight, readout)
-    tables, order, beside = gather_halo(table, beside)
-    gather, scatter, lanes, secondt, rocol = beside
-    energy, grad_edge, back_own, back_other = call(
+    )(code, *(tables if direct else ()), second_weight, readout)
+    if direct:
+        tables = [swapped(both, slot) for slot in range(4)] + [both]
+        order = [(array, row) for array in range(5) for row in range(2)]
+        latents = [edge, shifted(sent, "gz", 1)]
+        returned = [((ATOMS + 8, EDGES), F32)] + [((2,) + square, BF16)] * 4 + [((2,) + square, F32)]
+    else:
+        tables = ring_gather(table)
+        order = [(array, row) for array in range(2) for row in range(9)]
+        latents = [edge]
+        returned = [((9,) + square, BF16)] * 2
+    energy, grad_edge, *returned = call(
         functools.partial(second_kernel, len(tables), order),
-        [((1, ATOMS), F32), (edges, F32), ((9,) + square, BF16), ((9,) + square, BF16)],
-        [pltpu.VMEM(edges, F32), pltpu.VMEM(edges, BF16)],
+        [((1, ATOMS), F32), (edges, F32)] + returned,
+        [pltpu.VMEM((ATOMS, sets * EDGES), F32), pltpu.VMEM((ATOMS, sets * EDGES), BF16)],
         name="second",
-    )(*tables, gather, scatter, edge, second_weight, secondt, rocol)
-    owned = reduce_halo(back_own, back_other)
+    )(*tables, gather, scatter, second_weight, secondt, rocol, *latents)
+    if direct:
+        give, *back, home = returned
+        given = [shifted(give, "gz", 1)]
+        for slot in range(4):
+            home = home + swapped(back[slot], slot).astype(F32)
+        owned = home[:1] + shifted(home[1:], "gz", 1)
+    else:
+        given = []
+        owned = ring_reduce(*returned)
     moved = call(
         functools.partial(backward_kernel, direct),
         [((devices, 4, ATOMS), F32)] if direct else [((9, 4, ATOMS), F32)] * 2,
@@ -581,9 +621,9 @@
         name="backward",
     )(
         owned, energy, grad_edge, dse, dsl, dsb, env, field, geo, code, lanes, update_weight, env_weight, mix_weight,
-        radial_weight,
+        radial_weight, *given,
     )
-    moved = lax.all_to_all(moved[0], EVERY, 0, 0, tiled=True) if direct else reduce_halo(*moved)
+    moved = lax.all_to_all(moved[0], EVERY, 0, 0, tiled=True) if direct else ring_reduce(*moved)
     return call(finish_kernel, [((1, 1, 2, slots), F32), ((1, 1, 2, 3 * slots), F32)], name="finish")(moved)
 
 

time: 58.1 us -> 56.3 us (0.969)
  waiting for transfers between devices: 9.11 us -> 7.78 us
  blocking collectives: 25.4 us -> 26.1 us
  Pallas kernels: 10.6 us -> 10 us
    ppermute x4, waiting for transfers between devices: 5.19 us -> 2.24 us  [shifted(): lax.ppermute(value, axis, [(i, (i + step) % count) for i in range(count)])]
    ppermute x8, waiting for transfers between devices: 3.91 us -> 5.54 us  [swapped(): return lax.ppermute(value, EVERY, pairs)]
    all_to_all x1, blocking collectives: 10.1 us -> 10.8 us  [on_device(): lax.all_to_all(moved[0], EVERY, 0, 0, tiled=True)]
    pallas_call x7, Pallas kernels: 10.6 us -> 10 us  [run(): pl.pallas_call(kernel, out_shape=shapes, in_specs=[pl.BlockSpec(memory_sp...]
  transfers between devices with their start and end apart: 12 -> 12, of which waited for: 8 -> 5; matrix products, arithmetic and copies ran while one was open for 0% -> 0% of each run, Pallas kernels for 6% -> 5%
where the time goes in v6:
time: 56.3 us; the launch traced here: 56.1 us
  blocking collectives  26.1 us (46%)
  starting transfers between devices  10.6 us (19%)
  Pallas kernels  10 us (18%)
  waiting for transfers between devices  7.78 us (14%)
  between operations  0.85 us (2%)
  local copies, waits for them, and re-layouts  0.65 us (1%)
    all_to_all x1, blocking collectives, on_device(): tables = [lax.all_to_all(copies, EVERY, 0, 0, tiled=True)]  15.3 us
    all_to_all x1, blocking collectives, on_device(): lax.all_to_all(moved[0], EVERY, 0, 0, tiled=True)  10.8 us
    pallas_call x7, Pallas kernels, run(): pl.pallas_call(kernel, out_shape=shapes, in_specs=[pl.BlockSpec(memory_sp...  10 us
    ppermute x8, starting transfers between devices, swapped(): return lax.ppermute(value, EVERY, pairs)  9.96 us
    ppermute x8, waiting for transfers between devices, swapped(): return lax.ppermute(value, EVERY, pairs)  5.54 us
    ppermute x4, waiting for transfers between devices, shifted(): lax.ppermute(value, axis, [(i, (i + step) % count) for i in range(count)])  2.24 us
  transfers between devices with their start and end apart: 12, of which 5 were waited for; matrix products, arithmetic and copies ran while one was open for 0% of the time, Pallas kernels for 5%

profile of v6, /device:TPU:0, one launch (start us, length us, event | category | flops | bytes accessed | tf_op | source)
XLA Modules:
  0.0 56.1 jit_solution(18430400299082139293)
XLA Ops:
  0.8 0.6 %copy-done.5 = s32[1,1,2,512]{3,2,1,0:T(2,128)S(1)} copy-done((s32[1,1,2,512]{3,2,1,0:T(2,128)S(1)}, s32[1,1,2,512]{3,2,1,0:T(2,128)}, u32[]{:S(2)}) %copy-start.5) | copy-done | bytes 4120
  1.3 0.1 pack.1
  1.4 15.3 %all_to_all.10.refs_0_.refs_1_ = f32[32,8,128]{2,1,0:T(8,128)S(1)} all-to-all(f32[32,8,128]{2,1,0:T(8,128)S(1)} %broadcast_in_dim.8), channel_id=1, replica_groups=mesh['gx'=4,'gy'=4,'gz'=2] {'gx','gy','gz'}, dimensions={0} | all-to-all | bytes 262144 | tf_op jit(solution)/shard_map/all_to_all | solution.py:559
  16.8 2.0 %forward.1 = (bf16[1,128,128]{2,1,0:T(8,128)(2,1)S(1)}, s32[8,128]{1,0:T(8,128)S(1)}, f32[128,1024]{1,0:T(8,128)S(1)}, f32[128,1024]{1,0:T(8,128)S(1)}, f32[128,...) custom-call(f32[32,8,128]{2,1,0:T(8,128)S(1)} %all_to_all.10.refs_0_, ...), custom_call_target="tpu_custom_call" | custom-call | tf_op jit(solution)/shard_map/forward/pallas_call | solution.py:526
  18.8 0.3 collective-permute-start
  19.1 1.0 %collective-permute-done = bf16[1,128,128]{2,1,0:T(8,128)(2,1)S(1)} collective-permute-done((bf16[1,128,128]{2,1,0:T(8,128)(2,1)S(1)}, bf16[1,128,128]{2,1,0:T(8,128)(2,1)S(1)}, u32[]{:S(2)}, u32[]{:S(2)}) %collective-permute-start) | collective-permute-done | bytes 32800 | tf_op jit(solution)/shard_map/ppermute | solution.py:34
  20.1 0.3 collective-permute-start.5
  20.4 0.5 collective-permute-start.4
  20.9 1.5 %collective-permute-start.3 = (bf16[2,128,128]{2,1,0:T(8,128)(2,1)S(1)}, bf16[2,128,128]{2,1,0:T(8,128)(2,1)S(1)}, u32[]{:S(2)}, u32[]{:S(2)}) collective-permute-start(bf16[2,128,128]{2,1,0:T(8,128)(2,1)S(1)} %pad_maximum_fusion.refs_4_), channel_id=1, source_target_pairs={{0,12},{1,11},{2,14},{3,9},{6,10},{7,13},{4,8},{5,15},{8,4},{9,3},... | collective-permute-start | bytes 196616 | tf_op jit(solution)/shard_map/ppermute | solution.py:57
  22.5 1.0 %collective-permute-start.2 = (bf16[2,128,128]{2,1,0:T(8,128)(2,1)S(1)}, bf16[2,128,128]{2,1,0:T(8,128)(2,1)S(1)}, u32[]{:S(2)}, u32[]{:S(2)}) collective-permute-start(bf16[2,128,128]{2,1,0:T(8,128)(2,1)S(1)} %pad_maximum_fusion.refs_4_), channel_id=1, source_target_pairs={{0,4},{1,3},{2,6},{3,1},{6,2},{7,5},{4,0},{5,7},{8,12},{9,11},{10,... | collective-permute-start | bytes 196616 | tf_op jit(solution)/shard_map/ppermute | solution.py:57
  23.5 0.9 %collective-permute-start.1 = (bf16[2,128,128]{2,1,0:T(8,128)(2,1)S(1)}, bf16[2,128,128]{2,1,0:T(8,128)(2,1)S(1)}, u32[]{:S(2)}, u32[]{:S(2)}) collective-permute-start(bf16[2,128,128]{2,1,0:T(8,128)(2,1)S(1)} %pad_maximum_fusion.refs_4_), channel_id=1, source_target_pairs={{0,8},{1,17},{2,10},{3,19},{6,14},{7,23},{4,12},{5,21},{8,0},{9,25... | collective-permute-start | bytes 196616 | tf_op jit(solution)/shard_map/ppermute | solution.py:57
  24.4 2.7 %onehot.1 = (bf16[1280,2048]{1,0:T(8,128)(2,1)S(1)}, bf16[2048,1280]{1,0:T(8,128)(2,1)S(1)}, bf16[128,1024]{1,0:T(8,128)(2,1)S(1)}, bf16[128,128]{1,0:T(8,128)(2,1)S(1)}, f32[128,128]{1,0:T(8,128)S(1)}) custom-call(s32[8,128]{1,0:T(8,128)S(1)} %get-tuple-element.31.refs_0_.code_ref, f32[32,8,128]{2,1,0:T(8,128)S(1)} %all_to_all.10.refs_0_.refs_1_, ...), custom_call_target="tpu_custom_call" | custom-call | flops 1073741824 | bytes 8388608 | tf_op jit(solution)/shard_map/onehot/pallas_call | solution.py:526
  27.1 1.0 %collective-permute-done.4.refs_3_ = bf16[2,128,128]{2,1,0:T(8,128)(2,1)S(1)} collective-permute-done((bf16[2,128,128]{2,1,0:T(8,128)(2,1)S(1)}, bf16[2,128,128]{2,1,0:T(8,128)(2,1)S(1)}, u32[]{:S(2)}, u32[]{:S(2)}) %collective-permute-start.4) | collective-permute-done | bytes 65568 | tf_op jit(solution)/shard_map/ppermute | solution.py:57
  28.1 2.2 %second.1 = (f32[1,128]{1,0:T(1,128)S(1)}, f32[128,1024]{1,0:T(8,128)S(1)}, f32[136,1024]{1,0:T(8,128)S(1)}, bf16[2,128,128]{2,1,0:T(8,128)(2,1)S(1)}, bf16[2,12...) custom-call(bf16[2,128,128]{2,1,0:T(8,128)(2,1)S(1)} %collective-per, ...), custom_call_target="tpu_custom_call" | custom-call | tf_op jit(solution)/shard_map/second/pallas_call | solution.py:526
  30.3 0.9 %collective-permute-start.6 = (bf16[2,128,128]{2,1,0:T(8,128)(2,1)S(1)}, bf16[2,128,128]{2,1,0:T(8,128)(2,1)S(1)}, u32[]{:S(2)}, u32[]{:S(2)}) collective-permute-start(bf16[2,128,128]{2,1,0:T(8,128)(2,1)S(1)} %get-tuple-element.38), channel_id=1, source_target_pairs={{0,8},{1,17},{2,10},{3,19},{6,14},{7,23},{4,12},{5,21},{8,0},{9,25... | collective-permute-start | bytes 196616 | tf_op jit(solution)/shard_map/ppermute | solution.py:57
  31.3 1.0 %collective-permute-start.7 = (bf16[2,128,128]{2,1,0:T(8,128)(2,1)S(1)}, bf16[2,128,128]{2,1,0:T(8,128)(2,1)S(1)}, u32[]{:S(2)}, u32[]{:S(2)}) collective-permute-start(bf16[2,128,128]{2,1,0:T(8,128)(2,1)S(1)} %get-tuple-element.39), channel_id=1, source_target_pairs={{0,4},{1,3},{2,6},{3,1},{6,2},{7,5},{4,0},{5,7},{8,12},{9,11},{10,... | collective-permute-start | bytes 196616 | tf_op jit(solution)/shard_map/ppermute | solution.py:57
  32.3 1.6 %collective-permute-start.8 = (bf16[2,128,128]{2,1,0:T(8,128)(2,1)S(1)}, bf16[2,128,128]{2,1,0:T(8,128)(2,1)S(1)}, u32[]{:S(2)}, u32[]{:S(2)}) collective-permute-start(bf16[2,128,128]{2,1,0:T(8,128)(2,1)S(1)} %get-tuple-element.40), channel_id=1, source_target_pairs={{0,12},{1,11},{2,14},{3,9},{6,10},{7,13},{4,8},{5,15},{8,4},{9,3},... | collective-permute-start | bytes 196616 | tf_op jit(solution)/shard_map/ppermute | solution.py:57
  33.9 2.4 %collective-permute-start.9 = (bf16[2,128,128]{2,1,0:T(8,128)(2,1)S(1)}, bf16[2,128,128]{2,1,0:T(8,128)(2,1)S(1)}, u32[]{:S(2)}, u32[]{:S(2)}) collective-permute-start(bf16[2,128,128]{2,1,0:T(8,128)(2,1)S(1)} %get-tuple-element.41), channel_id=1, source_target_pairs={{0,18},{1,21},{2,16},{3,23},{6,20},{7,19},{4,22},{5,17},{8,26},{9,... | collective-permute-start | bytes 196616 | tf_op jit(solution)/shard_map/ppermute | solution.py:57
  36.3 1.3 %collective-permute-done.8 = bf16[2,128,128]{2,1,0:T(8,128)(2,1)S(1)} collective-permute-done((bf16[2,128,128]{2,1,0:T(8,128)(2,1)S(1)}, bf16[2,128,128]{2,1,0:T(8,128)(2,1)S(1)}, u32[]{:S(2)}, u32[]{:S(2)}) %collective-permute-start.8) | collective-permute-done | bytes 65568 | tf_op jit(solution)/shard_map/ppermute | solution.py:57
  37.6 3.2 %collective-permute-done.9 = bf16[2,128,128]{2,1,0:T(8,128)(2,1)S(1)} collective-permute-done((bf16[2,128,128]{2,1,0:T(8,128)(2,1)S(1)}, bf16[2,128,128]{2,1,0:T(8,128)(2,1)S(1)}, u32[]{:S(2)}, u32[]{:S(2)}) %collective-permute-start.9) | collective-permute-done | bytes 65568 | tf_op jit(solution)/shard_map/ppermute | solution.py:57
  41.0 1.2 %collective-permute-done.10 = f32[1,128,128]{2,1,0:T(8,128)S(1)} collective-permute-done((f32[1,128,128]{2,1,0:T(8,128)S(1)}, f32[1,128,128]{2,1,0:T(8,128)S(1)}, u32[]{:S(2)}, u32[]{:S(2)}) %collective-permute-start.10) | collective-permute-done | bytes 65568 | tf_op jit(solution)/shard_map/ppermute | solution.py:34
  42.2 2.4 %backward.1 = f32[32,4,128]{2,1,0:T(4,128)S(1)} custom-call(f32[1,128,128]{2,1,0:T(8,128)S(1)} %slice_add_fusion.owned_ref, f32[1,128]{1,0:T(1,128)S(1)} %get-tuple-element.42.energy_ref, f32[128,1024]{1,0:T(8,128)S(1)} %get-tuple-element.43.grad_edge_ref, f32[128,1024]{1,0:T(8,128)S(1)} %get-tuple-element.44.dse_ref, ...), custom_call_target="tpu_custom_call" | custom-call | tf_op jit(solution)/shard_map/backward/pallas_call | solution.py:526
  44.6 10.8 %all_to_all.11.moved_ref = f32[32,4,128]{2,1,0:T(4,128)S(1)} all-to-all(f32[32,4,128]{2,1,0:T(4,128)S(1)} %backward.1), channel_id=1, replica_groups=mesh['gx'=4,'gy'=4,'gz'=2] {'gx','gy','gz'}, dimensions={0} | all-to-all | bytes 131072 | tf_op jit(solution)/shard_map/all_to_all | solution.py:626
  55.4 0.7 %finish.1 = (f32[1,1,2,64]{3,2,1,0:T(2,128)}, f32[1,1,2,192]{3,2,1,0:T(2,128)}) custom-call(f32[32,4,128]{2,1,0:T(4,128)S(1)} %all_to_all.11.moved_ref), custom_call_target="tpu_custom_call" | custom-call | tf_op jit(solution)/shard_map/finish/pallas_call | solution.py:526
  (36 shorter events, 0.2 us)
Async XLA Ops:
  0.6 0.7 %copy-start.5 = (s32[1,1,2,512]{3,2,1,0:T(2,128)S(1)}, s32[1,1,2,512]{3,2,1,0:T(2,128)}, u32[]{:S(2)}) copy-start(s32[1,1,2,512]{3,2,1,0:T(2,128)} %nb_ref.1) | copy-start | bytes 12292
  0.6 0.7 %copy-start.9 = (s32[1,1,2,64]{3,2,1,0:T(2,128)S(1)}, s32[1,1,2,64]{3,2,1,0:T(2,128)}, u32[]{:S(2)}) copy-start(s32[1,1,2,64]{3,2,1,0:T(2,128)} %spec_ref.1) | copy-start | bytes 1540
  0.7 0.7 %copy-start.8 = (f32[1,1,2,192]{3,2,1,0:T(2,128)S(1)}, f32[1,1,2,192]{3,2,1,0:T(2,128)}, u32[]{:S(2)}) copy-start(f32[1,1,2,192]{3,2,1,0:T(2,128)} %pos_ref.1) | copy-start | bytes 4612
  0.7 16.1 %copy-start = (bf16[384,128]{1,0:T(8,128)(2,1)S(1)}, bf16[384,128]{1,0:T(8,128)(2,1)}, u32[]{:S(2)}) copy-start(bf16[384,128]{1,0:T(8,128)(2,1)} %upd_ref.1) | copy-start | bytes 294916
  0.7 16.1 %copy-start.2 = (bf16[128,128]{1,0:T(8,128)(2,1)S(1)}, bf16[128,128]{1,0:T(8,128)(2,1)}, u32[]{:S(2)}) copy-start(bf16[128,128]{1,0:T(8,128)(2,1)} %envw_ref.1) | copy-start | bytes 98308
  0.7 16.1 %copy-start.1 = (bf16[128,128]{1,0:T(8,128)(2,1)S(1)}, bf16[128,128]{1,0:T(8,128)(2,1)}, u32[]{:S(2)}) copy-start(bf16[128,128]{1,0:T(8,128)(2,1)} %mix_ref.1) | copy-start | bytes 98308
  0.7 16.1 %copy-start.4 = (bf16[8,128]{1,0:T(8,128)(2,1)S(1)}, bf16[8,128]{1,0:T(8,128)(2,1)}, u32[]{:S(2)}) copy-start(bf16[8,128]{1,0:T(8,128)(2,1)} %radial_ref.1) | copy-start | bytes 6148
  0.7 16.1 %copy-start.7 = (bf16[5,128]{1,0:T(8,128)(2,1)S(1)}, bf16[5,128]{1,0:T(8,128)(2,1)}, u32[]{:S(2)}) copy-start(bf16[5,128]{1,0:T(8,128)(2,1)} %refs_2_.2) | copy-start | bytes 3844
  0.7 16.1 %copy-start.6 = (bf16[5,128]{1,0:T(8,128)(2,1)S(1)}, bf16[5,128]{1,0:T(8,128)(2,1)}, u32[]{:S(2)}) copy-start(bf16[5,128]{1,0:T(8,128)(2,1)} %refs_1_.1) | copy-start | bytes 3844
  0.7 23.7 %copy-start.3 = (bf16[128,128]{1,0:T(8,128)(2,1)S(1)}, bf16[128,128]{1,0:T(8,128)(2,1)}, u32[]{:S(2)}) copy-start(bf16[128,128]{1,0:T(8,128)(2,1)} %refs_7_.1) | copy-start | bytes 98308
  0.7 23.7 %copy-start.10 = (f32[128]{0:T(128)S(1)}, f32[128]{0:T(128)}, u32[]{:S(2)}) copy-start(f32[128]{0:T(128)} %param.21) | copy-start | bytes 1540
  18.8 1.3 %collective-permute-start = (bf16[1,128,128]{2,1,0:T(8,128)(2,1)S(1)}, bf16[1,128,128]{2,1,0:T(8,128)(2,1)S(1)}, u32[]{:S(2)}, u32[]{:S(2)}) collective-permute-start(bf16[1,128,128]{2,1,0:T(8,128)(2,1)S(1)} %get-tuple-element.27), channel_id=1, source_target_pairs={{0,1},{1,0},{2,3},{3,2},{4,5},{5,4},{6,7},{7,6},{8,9},{9,8},{10,11... | collective-permute-start | bytes 98312 | tf_op jit(solution)/shard_map/ppermute | solution.py:34
  20.1 8.0 %collective-permute-start.5 = (f32[128,1024]{1,0:T(8,128)S(1)}, f32[128,1024]{1,0:T(8,128)S(1)}, u32[]{:S(2)}, u32[]{:S(2)}) collective-permute-start(f32[128,1024]{1,0:T(8,128)S(1)} %get-tuple-element.36.refs_10_), channel_id=1, source_target_pairs={{0,1},{1,0},{2,3},{3,2},{4,5},{5,4},{6,7},{7,6},{8,9},{9,8},{10,11... | collective-permute-start | bytes 1572872 | tf_op jit(solution)/shard_map/ppermute | solution.py:34
  20.4 7.7 %collective-permute-start.4 = (bf16[2,128,128]{2,1,0:T(8,128)(2,1)S(1)}, bf16[2,128,128]{2,1,0:T(8,128)(2,1)S(1)}, u32[]{:S(2)}, u32[]{:S(2)}) collective-permute-start(bf16[2,128,128]{2,1,0:T(8,128)(2,1)S(1)} %pad_maximum_fusion.refs_4_), channel_id=1, source_target_pairs={{0,18},{1,21},{2,16},{3,23},{6,20},{7,19},{4,22},{5,17},{8,26},{9,... | collective-permute-start | bytes 196616 | tf_op jit(solution)/shard_map/ppermute | solution.py:57
  20.9 7.2 %collective-permute-start.3 = (bf16[2,128,128]{2,1,0:T(8,128)(2,1)S(1)}, bf16[2,128,128]{2,1,0:T(8,128)(2,1)S(1)}, u32[]{:S(2)}, u32[]{:S(2)}) collective-permute-start(bf16[2,128,128]{2,1,0:T(8,128)(2,1)S(1)} %pad_maximum_fusion.refs_4_), channel_id=1, source_target_pairs={{0,12},{1,11},{2,14},{3,9},{6,10},{7,13},{4,8},{5,15},{8,4},{9,3},... | collective-permute-start | bytes 196616 | tf_op jit(solution)/shard_map/ppermute | solution.py:57
  22.5 5.6 %collective-permute-start.2 = (bf16[2,128,128]{2,1,0:T(8,128)(2,1)S(1)}, bf16[2,128,128]{2,1,0:T(8,128)(2,1)S(1)}, u32[]{:S(2)}, u32[]{:S(2)}) collective-permute-start(bf16[2,128,128]{2,1,0:T(8,128)(2,1)S(1)} %pad_maximum_fusion.refs_4_), channel_id=1, source_target_pairs={{0,4},{1,3},{2,6},{3,1},{6,2},{7,5},{4,0},{5,7},{8,12},{9,11},{10,... | collective-permute-start | bytes 196616 | tf_op jit(solution)/shard_map/ppermute | solution.py:57
  23.5 4.6 %collective-permute-start.1 = (bf16[2,128,128]{2,1,0:T(8,128)(2,1)S(1)}, bf16[2,128,128]{2,1,0:T(8,128)(2,1)S(1)}, u32[]{:S(2)}, u32[]{:S(2)}) collective-permute-start(bf16[2,128,128]{2,1,0:T(8,128)(2,1)S(1)} %pad_maximum_fusion.refs_4_), channel_id=1, source_target_pairs={{0,8},{1,17},{2,10},{3,19},{6,14},{7,23},{4,12},{5,21},{8,0},{9,25... | collective-permute-start | bytes 196616 | tf_op jit(solution)/shard_map/ppermute | solution.py:57
  30.3 6.0 %collective-permute-start.6 = (bf16[2,128,128]{2,1,0:T(8,128)(2,1)S(1)}, bf16[2,128,128]{2,1,0:T(8,128)(2,1)S(1)}, u32[]{:S(2)}, u32[]{:S(2)}) collective-permute-start(bf16[2,128,128]{2,1,0:T(8,128)(2,1)S(1)} %get-tuple-element.38), channel_id=1, source_target_pairs={{0,8},{1,17},{2,10},{3,19},{6,14},{7,23},{4,12},{5,21},{8,0},{9,25... | collective-permute-start | bytes 196616 | tf_op jit(solution)/shard_map/ppermute | solution.py:57
  31.3 5.0 %collective-permute-start.7 = (bf16[2,128,128]{2,1,0:T(8,128)(2,1)S(1)}, bf16[2,128,128]{2,1,0:T(8,128)(2,1)S(1)}, u32[]{:S(2)}, u32[]{:S(2)}) collective-permute-start(bf16[2,128,128]{2,1,0:T(8,128)(2,1)S(1)} %get-tuple-element.39), channel_id=1, source_target_pairs={{0,4},{1,3},{2,6},{3,1},{6,2},{7,5},{4,0},{5,7},{8,12},{9,11},{10,... | collective-permute-start | bytes 196616 | tf_op jit(solution)/shard_map/ppermute | solution.py:57
  32.3 5.4 %collective-permute-start.8 = (bf16[2,128,128]{2,1,0:T(8,128)(2,1)S(1)}, bf16[2,128,128]{2,1,0:T(8,128)(2,1)S(1)}, u32[]{:S(2)}, u32[]{:S(2)}) collective-permute-start(bf16[2,128,128]{2,1,0:T(8,128)(2,1)S(1)} %get-tuple-element.40), channel_id=1, source_target_pairs={{0,12},{1,11},{2,14},{3,9},{6,10},{7,13},{4,8},{5,15},{8,4},{9,3},... | collective-permute-start | bytes 196616 | tf_op jit(solution)/shard_map/ppermute | solution.py:57
  33.9 6.9 %collective-permute-start.9 = (bf16[2,128,128]{2,1,0:T(8,128)(2,1)S(1)}, bf16[2,128,128]{2,1,0:T(8,128)(2,1)S(1)}, u32[]{:S(2)}, u32[]{:S(2)}) collective-permute-start(bf16[2,128,128]{2,1,0:T(8,128)(2,1)S(1)} %get-tuple-element.41), channel_id=1, source_target_pairs={{0,18},{1,21},{2,16},{3,23},{6,20},{7,19},{4,22},{5,17},{8,26},{9,... | collective-permute-start | bytes 196616 | tf_op jit(solution)/shard_map/ppermute | solution.py:57
  36.3 5.9 %collective-permute-start.11 = (f32[136,1024]{1,0:T(8,128)S(1)}, f32[136,1024]{1,0:T(8,128)S(1)}, u32[]{:S(2)}, u32[]{:S(2)}) collective-permute-start(f32[136,1024]{1,0:T(8,128)S(1)} %get-tuple-element.51), channel_id=1, source_target_pairs={{0,1},{1,0},{2,3},{3,2},{4,5},{5,4},{6,7},{7,6},{8,9},{9,8},{10,11... | collective-permute-start | bytes 1671176 | tf_op jit(solution)/shard_map/ppermute | solution.py:34
  40.9 1.3 %collective-permute-start.10 = (f32[1,128,128]{2,1,0:T(8,128)S(1)}, f32[1,128,128]{2,1,0:T(8,128)S(1)}, u32[]{:S(2)}, u32[]{:S(2)}) collective-permute-start(f32[1,128,128]{2,1,0:T(8,128)S(1)} %slice.9), channel_id=1, source_target_pairs={{0,1},{1,0},{2,3},{3,2},{4,5},{5,4},{6,7},{7,6},{8,9},{9,8},{10,11... | collective-permute-start | bytes 196616 | tf_op jit(solution)/shard_map/ppermute | solution.py:34

commit v7 on v6

--- a/solution.py
+++ b/solution.py
@@ -21,7 +21,7 @@
 
 
 RING = (0, 1, 3, 2)
-ROUTES = (((1, 0), (0, 2), (1, 2), (2, 1)), ((2, 0), (0, 1), (1, 1), (2, 2)))
+ROUTES = (((0, 1), (1, 0), (1, 2), (2, 2)), ((0, 2), (2, 0), (1, 1), (2, 1)))
 EVERY = ("gx", "gy", "gz")
 
 
@@ -605,7 +605,7 @@
     if direct:
         give, *back, home = returned
         given = [shifted(give, "gz", 1)]
-        for slot in range(4):
+        for slot in (3, 2, 1, 0):
             home = home + swapped(back[slot], slot).astype(F32)
         owned = home[:1] + shifted(home[1:], "gz", 1)
     else:

time: 56.3 us -> 54 us (0.959)
  blocking collectives: 26.1 us -> 24.7 us
  starting transfers between devices: 10.6 us -> 9.81 us
    all_to_all x1, blocking collectives: 10.8 us -> 9.32 us  [on_device(): lax.all_to_all(moved[0], EVERY, 0, 0, tiled=True)]
    ppermute x8, starting transfers between devices: 9.96 us -> 9.17 us  [swapped(): return lax.ppermute(value, EVERY, pairs)]
  transfers between devices with their start and end apart: 12 -> 12, of which waited for: 5 -> 7; matrix products, arithmetic and copies ran while one was open for 0% -> 0% of each run, Pallas kernels for 5% -> 5%
where the time goes in v7:
time: 54 us; the launch traced here: 53.8 us
  blocking collectives  24.7 us (46%)
  Pallas kernels  10 us (19%)
  starting transfers between devices  9.81 us (18%)
  waiting for transfers between devices  7.75 us (14%)
  between operations  0.83 us (2%)
  local copies, waits for them, and re-layouts  0.65 us (1%)
    all_to_all x1, blocking collectives, on_device(): tables = [lax.all_to_all(copies, EVERY, 0, 0, tiled=True)]  15.3 us
    pallas_call x7, Pallas kernels, run(): pl.pallas_call(kernel, out_shape=shapes, in_specs=[pl.BlockSpec(memory_sp...  10 us
    all_to_all x1, blocking collectives, on_device(): lax.all_to_all(moved[0], EVERY, 0, 0, tiled=True)  9.32 us
    ppermute x8, starting transfers between devices, swapped(): return lax.ppermute(value, EVERY, pairs)  9.17 us
    ppermute x8, waiting for transfers between devices, swapped(): return lax.ppermute(value, EVERY, pairs)  5.52 us
    ppermute x4, waiting for transfers between devices, shifted(): lax.ppermute(value, axis, [(i, (i + step) % count) for i in range(count)])  2.24 us
  transfers between devices with their start and end apart: 12, of which 7 were waited for; matrix products, arithmetic and copies ran while one was open for 0% of the time, Pallas kernels for 5%

profile of v7, /device:TPU:0, one launch (start us, length us, event | category | flops | bytes accessed | tf_op | source)
XLA Modules:
  0.0 53.8 jit_solution(30009213453563830)
XLA Ops:
  0.8 0.6 %copy-done.5 = s32[1,1,2,512]{3,2,1,0:T(2,128)S(1)} copy-done((s32[1,1,2,512]{3,2,1,0:T(2,128)S(1)}, s32[1,1,2,512]{3,2,1,0:T(2,128)}, u32[]{:S(2)}) %copy-start.5) | copy-done | bytes 4120
  1.4 15.3 %all_to_all.10.refs_0_.refs_1_ = f32[32,8,128]{2,1,0:T(8,128)S(1)} all-to-all(f32[32,8,128]{2,1,0:T(8,128)S(1)} %broadcast_in_dim.8), channel_id=1, replica_groups=mesh['gx'=4,'gy'=4,'gz'=2] {'gx','gy','gz'}, dimensions={0} | all-to-all | bytes 262144 | tf_op jit(solution)/shard_map/all_to_all | solution.py:559
  16.8 2.0 %forward.1 = (bf16[1,128,128]{2,1,0:T(8,128)(2,1)S(1)}, s32[8,128]{1,0:T(8,128)S(1)}, f32[128,1024]{1,0:T(8,128)S(1)}, f32[128,1024]{1,0:T(8,128)S(1)}, f32[128,...) custom-call(f32[32,8,128]{2,1,0:T(8,128)S(1)} %all_to_all.10.refs_0_, ...), custom_call_target="tpu_custom_call" | custom-call | tf_op jit(solution)/shard_map/forward/pallas_call | solution.py:526
  18.8 0.3 collective-permute-start
  19.1 1.0 %collective-permute-done = bf16[1,128,128]{2,1,0:T(8,128)(2,1)S(1)} collective-permute-done((bf16[1,128,128]{2,1,0:T(8,128)(2,1)S(1)}, bf16[1,128,128]{2,1,0:T(8,128)(2,1)S(1)}, u32[]{:S(2)}, u32[]{:S(2)}) %collective-permute-start) | collective-permute-done | bytes 32800 | tf_op jit(solution)/shard_map/ppermute | solution.py:34
  20.1 0.3 collective-permute-start.5
  20.4 0.7 %collective-permute-start.4 = (bf16[2,128,128]{2,1,0:T(8,128)(2,1)S(1)}, bf16[2,128,128]{2,1,0:T(8,128)(2,1)S(1)}, u32[]{:S(2)}, u32[]{:S(2)}) collective-permute-start(bf16[2,128,128]{2,1,0:T(8,128)(2,1)S(1)} %pad_maximum_fusion.refs_4_), channel_id=1, source_target_pairs={{0,20},{1,19},{2,22},{3,17},{6,18},{7,21},{4,16},{5,23},{8,28},{9,... | collective-permute-start | bytes 196616 | tf_op jit(solution)/shard_map/ppermute | solution.py:57
  21.1 2.0 %collective-permute-start.3 = (bf16[2,128,128]{2,1,0:T(8,128)(2,1)S(1)}, bf16[2,128,128]{2,1,0:T(8,128)(2,1)S(1)}, u32[]{:S(2)}, u32[]{:S(2)}) collective-permute-start(bf16[2,128,128]{2,1,0:T(8,128)(2,1)S(1)} %pad_maximum_fusion.refs_4_), channel_id=1, source_target_pairs={{0,12},{1,11},{2,14},{3,9},{6,10},{7,13},{4,8},{5,15},{8,4},{9,3},... | collective-permute-start | bytes 196616 | tf_op jit(solution)/shard_map/ppermute | solution.py:57
  23.1 0.9 %collective-permute-start.2 = (bf16[2,128,128]{2,1,0:T(8,128)(2,1)S(1)}, bf16[2,128,128]{2,1,0:T(8,128)(2,1)S(1)}, u32[]{:S(2)}, u32[]{:S(2)}) collective-permute-start(bf16[2,128,128]{2,1,0:T(8,128)(2,1)S(1)} %pad_maximum_fusion.refs_4_), channel_id=1, source_target_pairs={{0,8},{1,17},{2,10},{3,19},{6,14},{7,23},{4,12},{5,21},{8,0},{9,25... | collective-permute-start | bytes 196616 | tf_op jit(solution)/shard_map/ppermute | solution.py:57
  24.0 0.4 collective-permute-start.1
  24.4 2.7 %onehot.1 = (bf16[1280,2048]{1,0:T(8,128)(2,1)S(1)}, bf16[2048,1280]{1,0:T(8,128)(2,1)S(1)}, bf16[128,1024]{1,0:T(8,128)(2,1)S(1)}, bf16[128,128]{1,0:T(8,128)(2,1)S(1)}, f32[128,128]{1,0:T(8,128)S(1)}) custom-call(s32[8,128]{1,0:T(8,128)S(1)} %get-tuple-element.31.refs_0_.code_ref, f32[32,8,128]{2,1,0:T(8,128)S(1)} %all_to_all.10.refs_0_.refs_1_, ...), custom_call_target="tpu_custom_call" | custom-call | flops 1073741824 | bytes 8388608 | tf_op jit(solution)/shard_map/onehot/pallas_call | solution.py:526
  27.1 1.5 %collective-permute-done.4.refs_3_ = bf16[2,128,128]{2,1,0:T(8,128)(2,1)S(1)} collective-permute-done((bf16[2,128,128]{2,1,0:T(8,128)(2,1)S(1)}, bf16[2,128,128]{2,1,0:T(8,128)(2,1)S(1)}, u32[]{:S(2)}, u32[]{:S(2)}) %collective-permute-start.4) | collective-permute-done | bytes 65568 | tf_op jit(solution)/shard_map/ppermute | solution.py:57
  28.8 2.2 %second.1 = (f32[1,128]{1,0:T(1,128)S(1)}, f32[128,1024]{1,0:T(8,128)S(1)}, f32[136,1024]{1,0:T(8,128)S(1)}, bf16[2,128,128]{2,1,0:T(8,128)(2,1)S(1)}, bf16[2,12...) custom-call(bf16[2,128,128]{2,1,0:T(8,128)(2,1)S(1)} %collective-per, ...), custom_call_target="tpu_custom_call" | custom-call | tf_op jit(solution)/shard_map/second/pallas_call | solution.py:526
  31.0 1.8 %collective-permute-start.6 = (bf16[2,128,128]{2,1,0:T(8,128)(2,1)S(1)}, bf16[2,128,128]{2,1,0:T(8,128)(2,1)S(1)}, u32[]{:S(2)}, u32[]{:S(2)}) collective-permute-start(bf16[2,128,128]{2,1,0:T(8,128)(2,1)S(1)} %get-tuple-element.38), channel_id=1, source_target_pairs={{0,20},{1,19},{2,22},{3,17},{6,18},{7,21},{4,16},{5,23},{8,28},{9,... | collective-permute-start | bytes 196616 | tf_op jit(solution)/shard_map/ppermute | solution.py:57
  32.8 1.6 %collective-permute-start.7 = (bf16[2,128,128]{2,1,0:T(8,128)(2,1)S(1)}, bf16[2,128,128]{2,1,0:T(8,128)(2,1)S(1)}, u32[]{:S(2)}, u32[]{:S(2)}) collective-permute-start(bf16[2,128,128]{2,1,0:T(8,128)(2,1)S(1)} %get-tuple-element.39), channel_id=1, source_target_pairs={{0,12},{1,11},{2,14},{3,9},{6,10},{7,13},{4,8},{5,15},{8,4},{9,3},... | collective-permute-start | bytes 196616 | tf_op jit(solution)/shard_map/ppermute | solution.py:57
  34.4 1.3 %collective-permute-start.8 = (bf16[2,128,128]{2,1,0:T(8,128)(2,1)S(1)}, bf16[2,128,128]{2,1,0:T(8,128)(2,1)S(1)}, u32[]{:S(2)}, u32[]{:S(2)}) collective-permute-start(bf16[2,128,128]{2,1,0:T(8,128)(2,1)S(1)} %get-tuple-element.40), channel_id=1, source_target_pairs={{0,8},{1,17},{2,10},{3,19},{6,14},{7,23},{4,12},{5,21},{8,0},{9,25... | collective-permute-start | bytes 196616 | tf_op jit(solution)/shard_map/ppermute | solution.py:57
  35.7 0.5 collective-permute-start.9
  36.2 2.8 %collective-permute-done.6 = bf16[2,128,128]{2,1,0:T(8,128)(2,1)S(1)} collective-permute-done((bf16[2,128,128]{2,1,0:T(8,128)(2,1)S(1)}, bf16[2,128,128]{2,1,0:T(8,128)(2,1)S(1)}, u32[]{:S(2)}, u32[]{:S(2)}) %collective-permute-start.6) | collective-permute-done | bytes 65568 | tf_op jit(solution)/shard_map/ppermute | solution.py:57
  39.0 0.5 %collective-permute-done.8 = bf16[2,128,128]{2,1,0:T(8,128)(2,1)S(1)} collective-permute-done((bf16[2,128,128]{2,1,0:T(8,128)(2,1)S(1)}, bf16[2,128,128]{2,1,0:T(8,128)(2,1)S(1)}, u32[]{:S(2)}, u32[]{:S(2)}) %collective-permute-start.8) | collective-permute-done | bytes 65568 | tf_op jit(solution)/shard_map/ppermute | solution.py:57
  39.6 0.4 collective-permute-done.9
  40.1 1.2 %collective-permute-done.10 = f32[1,128,128]{2,1,0:T(8,128)S(1)} collective-permute-done((f32[1,128,128]{2,1,0:T(8,128)S(1)}, f32[1,128,128]{2,1,0:T(8,128)S(1)}, u32[]{:S(2)}, u32[]{:S(2)}) %collective-permute-start.10) | collective-permute-done | bytes 65568 | tf_op jit(solution)/shard_map/ppermute | solution.py:34
  41.4 2.3 %backward.1 = f32[32,4,128]{2,1,0:T(4,128)S(1)} custom-call(f32[1,128,128]{2,1,0:T(8,128)S(1)} %slice_add_fusion.owned_ref, f32[1,128]{1,0:T(1,128)S(1)} %get-tuple-element.42.energy_ref, f32[128,1024]{1,0:T(8,128)S(1)} %get-tuple-element.43.grad_edge_ref, f32[128,1024]{1,0:T(8,128)S(1)} %get-tuple-element.44.dse_ref, ...), custom_call_target="tpu_custom_call" | custom-call | tf_op jit(solution)/shard_map/backward/pallas_call | solution.py:526
  43.7 9.3 %all_to_all.11.moved_ref = f32[32,4,128]{2,1,0:T(4,128)S(1)} all-to-all(f32[32,4,128]{2,1,0:T(4,128)S(1)} %backward.1), channel_id=1, replica_groups=mesh['gx'=4,'gy'=4,'gz'=2] {'gx','gy','gz'}, dimensions={0} | all-to-all | bytes 131072 | tf_op jit(solution)/shard_map/all_to_all | solution.py:626
  53.1 0.7 %finish.1 = (f32[1,1,2,64]{3,2,1,0:T(2,128)}, f32[1,1,2,192]{3,2,1,0:T(2,128)}) custom-call(f32[32,4,128]{2,1,0:T(4,128)S(1)} %all_to_all.11.moved_ref), custom_call_target="tpu_custom_call" | custom-call | tf_op jit(solution)/shard_map/finish/pallas_call | solution.py:526
  (36 shorter events, 0.5 us)
Async XLA Ops:
  0.6 0.7 %copy-start.5 = (s32[1,1,2,512]{3,2,1,0:T(2,128)S(1)}, s32[1,1,2,512]{3,2,1,0:T(2,128)}, u32[]{:S(2)}) copy-start(s32[1,1,2,512]{3,2,1,0:T(2,128)} %nb_ref.1) | copy-start | bytes 12292
  0.6 0.7 %copy-start.9 = (s32[1,1,2,64]{3,2,1,0:T(2,128)S(1)}, s32[1,1,2,64]{3,2,1,0:T(2,128)}, u32[]{:S(2)}) copy-start(s32[1,1,2,64]{3,2,1,0:T(2,128)} %spec_ref.1) | copy-start | bytes 1540
  0.7 0.7 %copy-start.8 = (f32[1,1,2,192]{3,2,1,0:T(2,128)S(1)}, f32[1,1,2,192]{3,2,1,0:T(2,128)}, u32[]{:S(2)}) copy-start(f32[1,1,2,192]{3,2,1,0:T(2,128)} %pos_ref.1) | copy-start | bytes 4612
  0.7 16.1 %copy-start = (bf16[384,128]{1,0:T(8,128)(2,1)S(1)}, bf16[384,128]{1,0:T(8,128)(2,1)}, u32[]{:S(2)}) copy-start(bf16[384,128]{1,0:T(8,128)(2,1)} %upd_ref.1) | copy-start | bytes 294916
  0.7 16.1 %copy-start.2 = (bf16[128,128]{1,0:T(8,128)(2,1)S(1)}, bf16[128,128]{1,0:T(8,128)(2,1)}, u32[]{:S(2)}) copy-start(bf16[128,128]{1,0:T(8,128)(2,1)} %envw_ref.1) | copy-start | bytes 98308
  0.7 16.1 %copy-start.1 = (bf16[128,128]{1,0:T(8,128)(2,1)S(1)}, bf16[128,128]{1,0:T(8,128)(2,1)}, u32[]{:S(2)}) copy-start(bf16[128,128]{1,0:T(8,128)(2,1)} %mix_ref.1) | copy-start | bytes 98308
  0.7 16.1 %copy-start.4 = (bf16[8,128]{1,0:T(8,128)(2,1)S(1)}, bf16[8,128]{1,0:T(8,128)(2,1)}, u32[]{:S(2)}) copy-start(bf16[8,128]{1,0:T(8,128)(2,1)} %radial_ref.1) | copy-start | bytes 6148
  0.7 16.1 %copy-start.7 = (bf16[5,128]{1,0:T(8,128)(2,1)S(1)}, bf16[5,128]{1,0:T(8,128)(2,1)}, u32[]{:S(2)}) copy-start(bf16[5,128]{1,0:T(8,128)(2,1)} %refs_2_.2) | copy-start | bytes 3844
  0.7 16.1 %copy-start.6 = (bf16[5,128]{1,0:T(8,128)(2,1)S(1)}, bf16[5,128]{1,0:T(8,128)(2,1)}, u32[]{:S(2)}) copy-start(bf16[5,128]{1,0:T(8,128)(2,1)} %refs_1_.1) | copy-start | bytes 3844
  0.7 23.7 %copy-start.3 = (bf16[128,128]{1,0:T(8,128)(2,1)S(1)}, bf16[128,128]{1,0:T(8,128)(2,1)}, u32[]{:S(2)}) copy-start(bf16[128,128]{1,0:T(8,128)(2,1)} %refs_7_.1) | copy-start | bytes 98308
  0.7 23.7 %copy-start.10 = (f32[128]{0:T(128)S(1)}, f32[128]{0:T(128)}, u32[]{:S(2)}) copy-start(f32[128]{0:T(128)} %param.21) | copy-start | bytes 1540
  18.8 1.3 %collective-permute-start = (bf16[1,128,128]{2,1,0:T(8,128)(2,1)S(1)}, bf16[1,128,128]{2,1,0:T(8,128)(2,1)S(1)}, u32[]{:S(2)}, u32[]{:S(2)}) collective-permute-start(bf16[1,128,128]{2,1,0:T(8,128)(2,1)S(1)} %get-tuple-element.27), channel_id=1, source_target_pairs={{0,1},{1,0},{2,3},{3,2},{4,5},{5,4},{6,7},{7,6},{8,9},{9,8},{10,11... | collective-permute-start | bytes 98312 | tf_op jit(solution)/shard_map/ppermute | solution.py:34
  20.1 8.7 %collective-permute-start.5 = (f32[128,1024]{1,0:T(8,128)S(1)}, f32[128,1024]{1,0:T(8,128)S(1)}, u32[]{:S(2)}, u32[]{:S(2)}) collective-permute-start(f32[128,1024]{1,0:T(8,128)S(1)} %get-tuple-element.36.refs_10_), channel_id=1, source_target_pairs={{0,1},{1,0},{2,3},{3,2},{4,5},{5,4},{6,7},{7,6},{8,9},{9,8},{10,11... | collective-permute-start | bytes 1572872 | tf_op jit(solution)/shard_map/ppermute | solution.py:34
  20.4 8.2 %collective-permute-start.4 = (bf16[2,128,128]{2,1,0:T(8,128)(2,1)S(1)}, bf16[2,128,128]{2,1,0:T(8,128)(2,1)S(1)}, u32[]{:S(2)}, u32[]{:S(2)}) collective-permute-start(bf16[2,128,128]{2,1,0:T(8,128)(2,1)S(1)} %pad_maximum_fusion.refs_4_), channel_id=1, source_target_pairs={{0,20},{1,19},{2,22},{3,17},{6,18},{7,21},{4,16},{5,23},{8,28},{9,... | collective-permute-start | bytes 196616 | tf_op jit(solution)/shard_map/ppermute | solution.py:57
  21.1 7.5 %collective-permute-start.3 = (bf16[2,128,128]{2,1,0:T(8,128)(2,1)S(1)}, bf16[2,128,128]{2,1,0:T(8,128)(2,1)S(1)}, u32[]{:S(2)}, u32[]{:S(2)}) collective-permute-start(bf16[2,128,128]{2,1,0:T(8,128)(2,1)S(1)} %pad_maximum_fusion.refs_4_), channel_id=1, source_target_pairs={{0,12},{1,11},{2,14},{3,9},{6,10},{7,13},{4,8},{5,15},{8,4},{9,3},... | collective-permute-start | bytes 196616 | tf_op jit(solution)/shard_map/ppermute | solution.py:57
  23.1 5.7 %collective-permute-start.2 = (bf16[2,128,128]{2,1,0:T(8,128)(2,1)S(1)}, bf16[2,128,128]{2,1,0:T(8,128)(2,1)S(1)}, u32[]{:S(2)}, u32[]{:S(2)}) collective-permute-start(bf16[2,128,128]{2,1,0:T(8,128)(2,1)S(1)} %pad_maximum_fusion.refs_4_), channel_id=1, source_target_pairs={{0,8},{1,17},{2,10},{3,19},{6,14},{7,23},{4,12},{5,21},{8,0},{9,25... | collective-permute-start | bytes 196616 | tf_op jit(solution)/shard_map/ppermute | solution.py:57
  24.0 4.8 %collective-permute-start.1 = (bf16[2,128,128]{2,1,0:T(8,128)(2,1)S(1)}, bf16[2,128,128]{2,1,0:T(8,128)(2,1)S(1)}, u32[]{:S(2)}, u32[]{:S(2)}) collective-permute-start(bf16[2,128,128]{2,1,0:T(8,128)(2,1)S(1)} %pad_maximum_fusion.refs_4_), channel_id=1, source_target_pairs={{0,2},{1,5},{2,0},{3,7},{6,4},{7,3},{4,6},{5,1},{8,10},{9,13},{10,... | collective-permute-start | bytes 196616 | tf_op jit(solution)/shard_map/ppermute | solution.py:57
  31.0 8.0 %collective-permute-start.6 = (bf16[2,128,128]{2,1,0:T(8,128)(2,1)S(1)}, bf16[2,128,128]{2,1,0:T(8,128)(2,1)S(1)}, u32[]{:S(2)}, u32[]{:S(2)}) collective-permute-start(bf16[2,128,128]{2,1,0:T(8,128)(2,1)S(1)} %get-tuple-element.38), channel_id=1, source_target_pairs={{0,20},{1,19},{2,22},{3,17},{6,18},{7,21},{4,16},{5,23},{8,28},{9,... | collective-permute-start | bytes 196616 | tf_op jit(solution)/shard_map/ppermute | solution.py:57
  32.8 6.2 %collective-permute-start.7 = (bf16[2,128,128]{2,1,0:T(8,128)(2,1)S(1)}, bf16[2,128,128]{2,1,0:T(8,128)(2,1)S(1)}, u32[]{:S(2)}, u32[]{:S(2)}) collective-permute-start(bf16[2,128,128]{2,1,0:T(8,128)(2,1)S(1)} %get-tuple-element.39), channel_id=1, source_target_pairs={{0,12},{1,11},{2,14},{3,9},{6,10},{7,13},{4,8},{5,15},{8,4},{9,3},... | collective-permute-start | bytes 196616 | tf_op jit(solution)/shard_map/ppermute | solution.py:57
  34.4 5.1 %collective-permute-start.8 = (bf16[2,128,128]{2,1,0:T(8,128)(2,1)S(1)}, bf16[2,128,128]{2,1,0:T(8,128)(2,1)S(1)}, u32[]{:S(2)}, u32[]{:S(2)}) collective-permute-start(bf16[2,128,128]{2,1,0:T(8,128)(2,1)S(1)} %get-tuple-element.40), channel_id=1, source_target_pairs={{0,8},{1,17},{2,10},{3,19},{6,14},{7,23},{4,12},{5,21},{8,0},{9,25... | collective-permute-start | bytes 196616 | tf_op jit(solution)/shard_map/ppermute | solution.py:57
  35.7 4.3 %collective-permute-start.9 = (bf16[2,128,128]{2,1,0:T(8,128)(2,1)S(1)}, bf16[2,128,128]{2,1,0:T(8,128)(2,1)S(1)}, u32[]{:S(2)}, u32[]{:S(2)}) collective-permute-start(bf16[2,128,128]{2,1,0:T(8,128)(2,1)S(1)} %get-tuple-element.41), channel_id=1, source_target_pairs={{0,2},{1,5},{2,0},{3,7},{6,4},{7,3},{4,6},{5,1},{8,10},{9,13},{10,... | collective-permute-start | bytes 196616 | tf_op jit(solution)/shard_map/ppermute | solution.py:57
  36.2 5.2 %collective-permute-start.11 = (f32[136,1024]{1,0:T(8,128)S(1)}, f32[136,1024]{1,0:T(8,128)S(1)}, u32[]{:S(2)}, u32[]{:S(2)}) collective-permute-start(f32[136,1024]{1,0:T(8,128)S(1)} %get-tuple-element.51), channel_id=1, source_target_pairs={{0,1},{1,0},{2,3},{3,2},{4,5},{5,4},{6,7},{7,6},{8,9},{9,8},{10,11... | collective-permute-start | bytes 1671176 | tf_op jit(solution)/shard_map/ppermute | solution.py:34
  40.1 1.3 %collective-permute-start.10 = (f32[1,128,128]{2,1,0:T(8,128)S(1)}, f32[1,128,128]{2,1,0:T(8,128)S(1)}, u32[]{:S(2)}, u32[]{:S(2)}) collective-permute-start(f32[1,128,128]{2,1,0:T(8,128)S(1)} %slice.9), channel_id=1, source_target_pairs={{0,1},{1,0},{2,3},{3,2},{4,5},{5,4},{6,7},{7,6},{8,9},{9,8},{10,11... | collective-permute-start | bytes 196616 | tf_op jit(solution)/shard_map/ppermute | solution.py:34

commit v8 on v7

--- a/solution.py
+++ b/solution.py
@@ -155,7 +155,11 @@
     codes = [refs[0][...]]
     if direct:
         codes.append(listed_codes(refs[1][owner_at(0, 0, 1)][4:8, :]))
-    second_ref, readout_ref, gather_ref, scatter_ref, lane_ref, secondt_ref, rocol_ref, turn_ref = refs[-8:]
+    geo_ref, second_ref, readout_ref, gather_ref, scatter_ref, lane_ref, secondt_ref, rocol_ref = refs[-11:-3]
+    slope_ref, spot_ref, turn_ref = refs[-3:]
+    for k in range(NEIGH):
+        bump, gap, inner, ratio = basis_parts(geo_ref[0, k : k + 1, :])
+        slope_ref[k] = bump * inner * (-2.0 * SHARPNESS * gap * inner - (4.0 / CUTOFF) * ratio)
     secondt_ref[...] = second_ref[...].astype(F32).T.astype(BF16)
     rocol_ref[...] = jnp.broadcast_to(readout_ref[...], (ATOMS, ATOMS)).T
     down = lax.broadcasted_iota(jnp.int32, (ATOMS, ATOMS), 0).astype(F32).astype(BF16)
@@ -166,6 +170,10 @@
     for twin, code in enumerate(codes):
         step_x, step_y, step_z, outside, lane = decode(code, ATOMS // 2)
         chunk = place_direct(step_x, step_y, outside, twin) if direct else place_ring(step_x, step_y, outside)
+        if not twin:
+            spot = outside * 9 + step_y * 3 + step_x + 4
+            for k in range(NEIGH):
+                spot_ref[k] = jnp.broadcast_to(spot[k : k + 1, :], (8, ATOMS))
         lane, chunk = lane.astype(F32), chunk.astype(F32)
         turn_ref[0:NEIGH, :] = lane
         turn_ref[NEIGH : 2 * NEIGH, :] = chunk
@@ -254,8 +262,8 @@
     tables = refs[:parts]
     (
         center_ref, neighbor_ref, radial_ref, mix_ref, envw_ref, upd_ref,
-        table_ref, code_ref, edge_ref, dsb_ref, dsl_ref, dse_ref, env_ref, v_ref, geo_ref,
-        yb_ref, inv_ref, lat_ref, pad_ref,
+        table_ref, code_ref, edge_ref, dsb_ref, dsl_ref, dse_ref, env_ref, v_ref, geo_ref, yb_ref,
+        inv_ref, lat_ref, pad_ref,
     ) = refs[parts:]
     pad_ref[...] = jnp.zeros(pad_ref.shape, F32)
     pad_ref[0:8, :] = radial_ref[...].astype(F32)
@@ -265,7 +273,7 @@
     mixt = mix_ref[...].astype(F32).T.astype(BF16)
     envt = envw_ref[...].astype(F32).T.astype(BF16)
     updt = [upd_ref[p * ATOMS : (p + 1) * ATOMS, :].astype(F32).T.astype(BF16) for p in range(3)]
-    updt = jnp.concatenate(updt, axis=1)
+    updt_alike, updt = updt[0], jnp.concatenate(updt[1:], axis=1)
 
     def chunk_at(far, dx, dy):
         if direct:
@@ -337,14 +345,15 @@
                 out.append(sums)
             halves.append(out)
         for k in range(NEIGH):
-            for p in range(3):
+            for p in range(1, 3):
                 both = jnp.concatenate([halves[0][k][p], halves[1][k][p]], axis=0)
-                inv_ref[p * ATOMS + t * 16 : p * ATOMS + t * 16 + 16, k * ATOMS : (k + 1) * ATOMS] = both.astype(BF16)
+                inv_ref[p * ATOMS - ATOMS + t * 16 : p * ATOMS - ATOMS + t * 16 + 16, k * ATOMS : (k + 1) * ATOMS] = both.astype(BF16)
+    alike = jnp.dot(updt_alike, v_ref[0].astype(BF16), preferred_element_type=F32)
     mean = jnp.zeros((ATOMS, ATOMS), F32)
     for j in range(EDGES // TILE):
         span = slice(j * TILE, (j + 1) * TILE)
         update = jnp.dot(updt, inv_ref[:, span], preferred_element_type=F32)
-        edge, ds = silu_pair(lat_ref[:, span] + update)
+        edge, ds = silu_pair(lat_ref[:, span] + update + jnp.concatenate([alike] * (TILE // ATOMS), axis=1))
         edge_ref[:, span] = edge
         dse_ref[:, span] = ds
         for i in range(TILE // ATOMS):
@@ -398,19 +407,18 @@
 
 
 def backward_kernel(
-    direct, owned_ref, energy_ref, grad_edge_ref, dse_ref, dsl_ref, dsb_ref, env_ref, v_ref, geo_ref, code_ref, lane_ref,
+    direct, owned_ref, energy_ref, grad_edge_ref, dse_ref, dsl_ref, dsb_ref, env_ref, v_ref, geo_ref, yb_ref, slope_ref, spot_ref, lane_ref,
     upd_ref, envw_ref, mix_ref, radial_ref, *refs,
 ):
-    *extra, yb_ref, dinv_ref, denv_ref, dlat_ref, part_ref, force_ref = refs
+    *extra, dinv_ref, denv_ref, dlat_ref, part_ref, force_ref, alike_ref = refs
     energy = energy_ref[...]
     if direct:
         given_ref, *extra = extra
         energy = energy + given_ref[ATOMS : ATOMS + 1, :ATOMS]
     outs = extra
     r, ux, uy, uz = (geo_ref[i] for i in range(4))
-    angular = angular_rows(ux, uy, uz)
-    spread_rows(yb_ref, angular)
     share = owned_ref[0] * 0.125
+    alike = jnp.zeros((ATOMS, ATOMS), F32)
     for j in range(EDGES // TILE):
         span = slice(j * TILE, (j + 1) * TILE)
         d_edge = grad_edge_ref[:, span] + jnp.concatenate([share] * (TILE // ATOMS), axis=1)
@@ -418,7 +426,12 @@
             d_edge = d_edge + given_ref[:ATOMS, span]
         d_pre = d_edge * dse_ref[:, span]
         dlat_ref[:, span] = d_pre
-        dinv_ref[:, span] = jnp.dot(upd_ref[...], d_pre.astype(BF16), preferred_element_type=F32).astype(BF16)
+        dinv_ref[:, span] = jnp.dot(
+            upd_ref[ATOMS:, :], d_pre.astype(BF16), preferred_element_type=F32
+        ).astype(BF16)
+        for i in range(TILE // ATOMS):
+            alike = alike + d_pre[:, i * ATOMS : (i + 1) * ATOMS]
+    alike_ref[...] = jnp.dot(upd_ref[:ATOMS, :], alike.astype(BF16), preferred_element_type=F32)
     part_ref[...] = jnp.zeros(part_ref.shape, F32)
     for t in range(8):
         wide = [
@@ -426,23 +439,20 @@
                 dinv_ref[p * ATOMS + t * 16 : p * ATOMS + t * 16 + 16, k * ATOMS : (k + 1) * ATOMS].astype(F32)
                 for k in range(NEIGH)
             ]
-            for p in range(3)
+            for p in range(2)
         ]
         halves = []
         for h in range(2):
             rows = slice(t * 16 + h * 8, t * 16 + h * 8 + 8)
-            dinv = [[wide[p][k][h * 8 : h * 8 + 8] for k in range(NEIGH)] for p in range(3)]
+            dinv = [[wide[p][k][h * 8 : h * 8 + 8] for k in range(NEIGH)] for p in range(2)]
             env = [env_ref[rows, k * ATOMS : (k + 1) * ATOMS] for k in range(NEIGH)]
-            denv = [None] * NEIGH
-            for m in range(9):
-                down = dinv[PIECE[m]]
-                terms = [down[k] if m == 0 else down[k] * yb_ref[m * NEIGH + k] for k in range(NEIGH)]
+            denv = [alike_ref[rows, :] * 0.125] * NEIGH
+            for m in range(1, 9):
+                down = dinv[PIECE[m] - 1]
+                terms = [down[k] * yb_ref[m * NEIGH + k] for k in range(NEIGH)]
                 while len(terms) > 1:
                     terms = [terms[i] + terms[i + 1] for i in range(0, len(terms), 2)]
                 d_field = terms[0] * 0.125
-                if m == 0:
-                    denv = [d_field] * NEIGH
-                    continue
                 field = v_ref[m, rows, :]
                 for k in range(NEIGH):
                     spot = m * NEIGH + k
@@ -462,9 +472,7 @@
         d_basis = jnp.dot(radial_ref[...], d_before, preferred_element_type=F32).astype(BF16).astype(F32)
         for i in range(TILE // ATOMS):
             k = j * (TILE // ATOMS) + i
-            bump, gap, inner, ratio = basis_parts(r[k : k + 1, :])
-            slope = bump * inner * (-2.0 * SHARPNESS * gap * inner - (4.0 / CUTOFF) * ratio)
-            d_r_rows.append(jnp.sum(slope * d_basis[:, i * ATOMS : (i + 1) * ATOMS], axis=0, keepdims=True))
+            d_r_rows.append(jnp.sum(slope_ref[k] * d_basis[:, i * ATOMS : (i + 1) * ATOMS], axis=0, keepdims=True))
     d_r = jnp.concatenate(d_r_rows, axis=0)
     dy = [None]
     for m in range(1, 9):
@@ -480,13 +488,11 @@
     high = [p.astype(BF16).astype(F32) for p in pull]
     low = [p - h for p, h in zip(pull, high)]
     zero = jnp.zeros((1, ATOMS), F32)
-    step_x, step_y, step_z, outside, lane = decode(code_ref[...], ATOMS // 2)
-    spot = outside * 9 + step_y * 3 + step_x + 4
     rows, spots = [], []
     for k in range(NEIGH):
         parts = [h[k : k + 1, :] for h in high] + [zero] + [q[k : k + 1, :] for q in low] + [zero]
         rows.append(jnp.concatenate(parts, axis=0))
-        spots.append(jnp.broadcast_to(spot[k : k + 1, :], (8, ATOMS)))
+        spots.append(spot_ref[k])
     for c in range(0, CHUNKS, 2):
         for k in range(NEIGH):
             both = [jnp.where(spots[k] == c + i, rows[k], 0.0) for i in range(2)]
@@ -559,33 +565,30 @@
         tables = [lax.all_to_all(copies, EVERY, 0, 0, tiled=True)]
     else:
         tables = ring_gather(packed)
-    table, code, edge, dsb, dsl, dse, env, field, geo = call(
+    table, code, edge, dsb, dsl, dse, env, field, geo, spread = call(
         functools.partial(forward_kernel, len(tables), direct),
         [
             ((1,) + square, BF16), ((NEIGH, ATOMS), jnp.int32), (edges, F32), (edges, F32), (edges, F32),
-            (edges, F32), (edges, F32), ((9,) + square, F32), ((4, NEIGH, ATOMS), F32),
+            (edges, F32), (edges, F32), ((9,) + square, F32), ((4, NEIGH, ATOMS), F32), ((72, 8, ATOMS), F32),
         ],
-        [
-            pltpu.VMEM((72, 8, ATOMS), F32), pltpu.VMEM((3 * ATOMS, EDGES), BF16), pltpu.VMEM(edges, F32),
-            pltpu.VMEM(square, F32),
-        ],
+        [pltpu.VMEM((2 * ATOMS, EDGES), BF16), pltpu.VMEM(edges, F32), pltpu.VMEM(square, F32)],
         name="forward",
     )(*tables, center_table, neighbor_table, radial_weight, mix_weight, env_weight, update_weight)
     chunks, sets = (10, 2) if direct else (CHUNKS, 1)
     sent = edge
     if direct:
         both = jnp.concatenate([table, shifted(table, "gz", 1)], axis=0)
-        both, sent, code = lax.optimization_barrier((both, edge, code))
-    gather, scatter, lanes, secondt, rocol = call(
+        both, sent, code, geo = lax.optimization_barrier((both, edge, code, geo))
+    gather, scatter, lanes, secondt, rocol, slope, spot = call(
         functools.partial(onehot_kernel, direct),
         [
             ((chunks * ATOMS, sets * EDGES), BF16), ((sets * EDGES, chunks * ATOMS), BF16), (edges, BF16),
-            (square, BF16), (square, F32),
+            (square, BF16), (square, F32), ((NEIGH, 8, ATOMS), F32), ((NEIGH, 8, ATOMS), jnp.int32),
         ],
         [pltpu.VMEM(square, F32)],
         name="onehot",
         cost=pl.CostEstimate(flops=1 << 30, bytes_accessed=8 << 20, transcendentals=0),
-    )(code, *(tables if direct else ()), second_weight, readout)
+    )(code, *(tables if direct else ()), geo, second_weight, readout)
     if direct:
         tables = [swapped(both, slot) for slot in range(4)] + [both]
         order = [(array, row) for array in range(5) for row in range(2)]
@@ -615,12 +618,12 @@
         functools.partial(backward_kernel, direct),
         [((devices, 4, ATOMS), F32)] if direct else [((9, 4, ATOMS), F32)] * 2,
         [
-            pltpu.VMEM((72, 8, ATOMS), F32), pltpu.VMEM((3 * ATOMS, EDGES), BF16), pltpu.VMEM(edges, BF16),
-            pltpu.VMEM(edges, F32), pltpu.VMEM((72, 8, ATOMS), F32), pltpu.VMEM((CHUNKS * 8, EDGES), BF16),
+            pltpu.VMEM((2 * ATOMS, EDGES), BF16), pltpu.VMEM(edges, BF16), pltpu.VMEM(edges, F32),
+            pltpu.VMEM((72, 8, ATOMS), F32), pltpu.VMEM((CHUNKS * 8, EDGES), BF16), pltpu.VMEM(square, F32),
         ],
         name="backward",
     )(
-        owned, energy, grad_edge, dse, dsl, dsb, env, field, geo, code, lanes, update_weight, env_weight, mix_weight,
+        owned, energy, grad_edge, dse, dsl, dsb, env, field, geo, spread, slope, spot, lanes, update_weight, env_weight, mix_weight,
         radial_weight, *given,
     )
     moved = lax.all_to_all(moved[0], EVERY, 0, 0, tiled=True) if direct else ring_reduce(*moved)

time: 54 us -> 53.7 us (level)
  no operation moved by 1% of the time
where the time goes in v8:
time: 53.7 us; the launch traced here: 53.5 us
  blocking collectives  24.6 us (46%)
  starting transfers between devices  9.83 us (18%)
  Pallas kernels  9.77 us (18%)
  waiting for transfers between devices  7.72 us (14%)
  between operations  0.83 us (2%)
  local copies, waits for them, and re-layouts  0.65 us (1%)
    all_to_all x1, blocking collectives, on_device(): tables = [lax.all_to_all(copies, EVERY, 0, 0, tiled=True)]  15.3 us
    pallas_call x7, Pallas kernels, run(): pl.pallas_call(kernel, out_shape=shapes, in_specs=[pl.BlockSpec(memory_sp...  9.77 us
    all_to_all x1, blocking collectives, on_device(): lax.all_to_all(moved[0], EVERY, 0, 0, tiled=True)  9.31 us
    ppermute x8, starting transfers between devices, swapped(): return lax.ppermute(value, EVERY, pairs)  9.2 us
    ppermute x8, waiting for transfers between devices, swapped(): return lax.ppermute(value, EVERY, pairs)  5.48 us
    ppermute x4, waiting for transfers between devices, shifted(): lax.ppermute(value, axis, [(i, (i + step) % count) for i in range(count)])  2.24 us
  transfers between devices with their start and end apart: 12, of which 7 were waited for; matrix products, arithmetic and copies ran while one was open for 0% of the time, Pallas kernels for 5%

profile of v8, /device:TPU:0, one launch (start us, length us, event | category | flops | bytes accessed | tf_op | source)
XLA Modules:
  0.0 53.5 jit_solution(17920695355880172457)
XLA Ops:
  0.8 0.6 %copy-done.5 = s32[1,1,2,512]{3,2,1,0:T(2,128)S(1)} copy-done((s32[1,1,2,512]{3,2,1,0:T(2,128)S(1)}, s32[1,1,2,512]{3,2,1,0:T(2,128)}, u32[]{:S(2)}) %copy-start.5) | copy-done | bytes 4120
  1.4 15.3 %all_to_all.10.refs_0_.refs_1_ = f32[32,8,128]{2,1,0:T(8,128)S(1)} all-to-all(f32[32,8,128]{2,1,0:T(8,128)S(1)} %broadcast_in_dim.8), channel_id=1, replica_groups=mesh['gx'=4,'gy'=4,'gz'=2] {'gx','gy','gz'}, dimensions={0} | all-to-all | bytes 262144 | tf_op jit(solution)/shard_map/all_to_all | solution.py:565
  16.8 1.9 %forward.1 = (bf16[1,128,128]{2,1,0:T(8,128)(2,1)S(1)}, s32[8,128]{1,0:T(8,128)S(1)}, f32[128,1024]{1,0:T(8,128)S(1)}, f32[128,1024]{1,0:T(8,128)S(1)}, f32[128,...) custom-call(f32[32,8,128]{2,1,0:T(8,128)S(1)} %all_to_all.10.refs_0_, ...), custom_call_target="tpu_custom_call" | custom-call | tf_op jit(solution)/shard_map/forward/pallas_call | solution.py:532
  18.7 0.3 collective-permute-start
  19.0 1.0 %collective-permute-done = bf16[1,128,128]{2,1,0:T(8,128)(2,1)S(1)} collective-permute-done((bf16[1,128,128]{2,1,0:T(8,128)(2,1)S(1)}, bf16[1,128,128]{2,1,0:T(8,128)(2,1)S(1)}, u32[]{:S(2)}, u32[]{:S(2)}) %collective-permute-start) | collective-permute-done | bytes 32800 | tf_op jit(solution)/shard_map/ppermute | solution.py:34
  20.0 0.3 collective-permute-start.5
  20.3 0.7 %collective-permute-start.4 = (bf16[2,128,128]{2,1,0:T(8,128)(2,1)S(1)}, bf16[2,128,128]{2,1,0:T(8,128)(2,1)S(1)}, u32[]{:S(2)}, u32[]{:S(2)}) collective-permute-start(bf16[2,128,128]{2,1,0:T(8,128)(2,1)S(1)} %pad_maximum_fusion.refs_4_), channel_id=1, source_target_pairs={{0,20},{1,19},{2,22},{3,17},{6,18},{7,21},{4,16},{5,23},{8,28},{9,... | collective-permute-start | bytes 196616 | tf_op jit(solution)/shard_map/ppermute | solution.py:57
  21.0 2.0 %collective-permute-start.3 = (bf16[2,128,128]{2,1,0:T(8,128)(2,1)S(1)}, bf16[2,128,128]{2,1,0:T(8,128)(2,1)S(1)}, u32[]{:S(2)}, u32[]{:S(2)}) collective-permute-start(bf16[2,128,128]{2,1,0:T(8,128)(2,1)S(1)} %pad_maximum_fusion.refs_4_), channel_id=1, source_target_pairs={{0,12},{1,11},{2,14},{3,9},{6,10},{7,13},{4,8},{5,15},{8,4},{9,3},... | collective-permute-start | bytes 196616 | tf_op jit(solution)/shard_map/ppermute | solution.py:57
  23.0 0.9 %collective-permute-start.2 = (bf16[2,128,128]{2,1,0:T(8,128)(2,1)S(1)}, bf16[2,128,128]{2,1,0:T(8,128)(2,1)S(1)}, u32[]{:S(2)}, u32[]{:S(2)}) collective-permute-start(bf16[2,128,128]{2,1,0:T(8,128)(2,1)S(1)} %pad_maximum_fusion.refs_4_), channel_id=1, source_target_pairs={{0,8},{1,17},{2,10},{3,19},{6,14},{7,23},{4,12},{5,21},{8,0},{9,25... | collective-permute-start | bytes 196616 | tf_op jit(solution)/shard_map/ppermute | solution.py:57
  23.9 0.4 collective-permute-start.1
  24.3 2.7 %onehot.1 = (bf16[1280,2048]{1,0:T(8,128)(2,1)S(1)}, bf16[2048,1280]{1,0:T(8,128)(2,1)S(1)}, bf16[128,1024]{1,0:T(8,128)(2,1)S(1)}, bf16[128,128]{1,0:T(8,128)(2...) custom-call(s32[8,128]{1,0:T(8,128)S(1)} %get-tuple-element.36.refs_0_, ...), custom_call_target="tpu_custom_call" | custom-call | flops 1073741824 | bytes 8388608 | tf_op jit(solution)/shard_map/onehot/pallas_call | solution.py:532
  27.0 1.5 %collective-permute-done.4.refs_3_ = bf16[2,128,128]{2,1,0:T(8,128)(2,1)S(1)} collective-permute-done((bf16[2,128,128]{2,1,0:T(8,128)(2,1)S(1)}, bf16[2,128,128]{2,1,0:T(8,128)(2,1)S(1)}, u32[]{:S(2)}, u32[]{:S(2)}) %collective-permute-start.4) | collective-permute-done | bytes 65568 | tf_op jit(solution)/shard_map/ppermute | solution.py:57
  28.7 2.2 %second.1 = (f32[1,128]{1,0:T(1,128)S(1)}, f32[128,1024]{1,0:T(8,128)S(1)}, f32[136,1024]{1,0:T(8,128)S(1)}, bf16[2,128,128]{2,1,0:T(8,128)(2,1)S(1)}, bf16[2,12...) custom-call(bf16[2,128,128]{2,1,0:T(8,128)(2,1)S(1)} %collective-per, ...), custom_call_target="tpu_custom_call" | custom-call | tf_op jit(solution)/shard_map/second/pallas_call | solution.py:532
  31.0 1.8 %collective-permute-start.6 = (bf16[2,128,128]{2,1,0:T(8,128)(2,1)S(1)}, bf16[2,128,128]{2,1,0:T(8,128)(2,1)S(1)}, u32[]{:S(2)}, u32[]{:S(2)}) collective-permute-start(bf16[2,128,128]{2,1,0:T(8,128)(2,1)S(1)} %get-tuple-element.44), channel_id=1, source_target_pairs={{0,20},{1,19},{2,22},{3,17},{6,18},{7,21},{4,16},{5,23},{8,28},{9,... | collective-permute-start | bytes 196616 | tf_op jit(solution)/shard_map/ppermute | solution.py:57
  32.7 1.6 %collective-permute-start.7 = (bf16[2,128,128]{2,1,0:T(8,128)(2,1)S(1)}, bf16[2,128,128]{2,1,0:T(8,128)(2,1)S(1)}, u32[]{:S(2)}, u32[]{:S(2)}) collective-permute-start(bf16[2,128,128]{2,1,0:T(8,128)(2,1)S(1)} %get-tuple-element.45), channel_id=1, source_target_pairs={{0,12},{1,11},{2,14},{3,9},{6,10},{7,13},{4,8},{5,15},{8,4},{9,3},... | collective-permute-start | bytes 196616 | tf_op jit(solution)/shard_map/ppermute | solution.py:57
  34.3 1.3 %collective-permute-start.8 = (bf16[2,128,128]{2,1,0:T(8,128)(2,1)S(1)}, bf16[2,128,128]{2,1,0:T(8,128)(2,1)S(1)}, u32[]{:S(2)}, u32[]{:S(2)}) collective-permute-start(bf16[2,128,128]{2,1,0:T(8,128)(2,1)S(1)} %get-tuple-element.46), channel_id=1, source_target_pairs={{0,8},{1,17},{2,10},{3,19},{6,14},{7,23},{4,12},{5,21},{8,0},{9,25... | collective-permute-start | bytes 196616 | tf_op jit(solution)/shard_map/ppermute | solution.py:57
  35.6 0.5 collective-permute-start.9
  36.2 2.8 %collective-permute-done.6 = bf16[2,128,128]{2,1,0:T(8,128)(2,1)S(1)} collective-permute-done((bf16[2,128,128]{2,1,0:T(8,128)(2,1)S(1)}, bf16[2,128,128]{2,1,0:T(8,128)(2,1)S(1)}, u32[]{:S(2)}, u32[]{:S(2)}) %collective-permute-start.6) | collective-permute-done | bytes 65568 | tf_op jit(solution)/shard_map/ppermute | solution.py:57
  38.9 0.5 %collective-permute-done.8 = bf16[2,128,128]{2,1,0:T(8,128)(2,1)S(1)} collective-permute-done((bf16[2,128,128]{2,1,0:T(8,128)(2,1)S(1)}, bf16[2,128,128]{2,1,0:T(8,128)(2,1)S(1)}, u32[]{:S(2)}, u32[]{:S(2)}) %collective-permute-start.8) | collective-permute-done | bytes 65568 | tf_op jit(solution)/shard_map/ppermute | solution.py:57
  39.5 0.4 collective-permute-done.9
  40.1 1.2 %collective-permute-done.10 = f32[1,128,128]{2,1,0:T(8,128)S(1)} collective-permute-done((f32[1,128,128]{2,1,0:T(8,128)S(1)}, f32[1,128,128]{2,1,0:T(8,128)S(1)}, u32[]{:S(2)}, u32[]{:S(2)}) %collective-permute-start.10) | collective-permute-done | bytes 65568 | tf_op jit(solution)/shard_map/ppermute | solution.py:34
  41.3 2.2 %backward.1 = f32[32,4,128]{2,1,0:T(4,128)S(1)} custom-call(f32[1,128,128]{2,1,0:T(8,128)S(1)} %slice_add_fusion.owned_ref, f32[1,128]{1,0:T(1,128)S(1)} %get-tuple-element.48.energy_ref, f32[128,1024]{1,0:T(8,128)S(1)} %get-tuple-element.49.grad_edge_ref, f32[128,1024]{1,0:T(8,128)S(1)} %get-tuple-element.50.dse_ref, ...), custom_call_target="tpu_custom_call" | custom-call | tf_op jit(solution)/shard_map/backward/pallas_call | solution.py:532
  43.5 9.3 %all_to_all.11.moved_ref = f32[32,4,128]{2,1,0:T(4,128)S(1)} all-to-all(f32[32,4,128]{2,1,0:T(4,128)S(1)} %backward.1), channel_id=1, replica_groups=mesh['gx'=4,'gy'=4,'gz'=2] {'gx','gy','gz'}, dimensions={0} | all-to-all | bytes 131072 | tf_op jit(solution)/shard_map/all_to_all | solution.py:629
  52.8 0.7 %finish.1 = (f32[1,1,2,64]{3,2,1,0:T(2,128)}, f32[1,1,2,192]{3,2,1,0:T(2,128)}) custom-call(f32[32,4,128]{2,1,0:T(4,128)S(1)} %all_to_all.11.moved_ref), custom_call_target="tpu_custom_call" | custom-call | tf_op jit(solution)/shard_map/finish/pallas_call | solution.py:532
  (36 shorter events, 0.5 us)
Async XLA Ops:
  0.6 0.7 %copy-start.5 = (s32[1,1,2,512]{3,2,1,0:T(2,128)S(1)}, s32[1,1,2,512]{3,2,1,0:T(2,128)}, u32[]{:S(2)}) copy-start(s32[1,1,2,512]{3,2,1,0:T(2,128)} %nb_ref.1) | copy-start | bytes 12292
  0.6 0.7 %copy-start.9 = (s32[1,1,2,64]{3,2,1,0:T(2,128)S(1)}, s32[1,1,2,64]{3,2,1,0:T(2,128)}, u32[]{:S(2)}) copy-start(s32[1,1,2,64]{3,2,1,0:T(2,128)} %spec_ref.1) | copy-start | bytes 1540
  0.7 0.7 %copy-start.8 = (f32[1,1,2,192]{3,2,1,0:T(2,128)S(1)}, f32[1,1,2,192]{3,2,1,0:T(2,128)}, u32[]{:S(2)}) copy-start(f32[1,1,2,192]{3,2,1,0:T(2,128)} %pos_ref.1) | copy-start | bytes 4612
  0.7 16.1 %copy-start = (bf16[384,128]{1,0:T(8,128)(2,1)S(1)}, bf16[384,128]{1,0:T(8,128)(2,1)}, u32[]{:S(2)}) copy-start(bf16[384,128]{1,0:T(8,128)(2,1)} %upd_ref.1) | copy-start | bytes 294916
  0.7 16.1 %copy-start.2 = (bf16[128,128]{1,0:T(8,128)(2,1)S(1)}, bf16[128,128]{1,0:T(8,128)(2,1)}, u32[]{:S(2)}) copy-start(bf16[128,128]{1,0:T(8,128)(2,1)} %envw_ref.1) | copy-start | bytes 98308
  0.7 16.1 %copy-start.1 = (bf16[128,128]{1,0:T(8,128)(2,1)S(1)}, bf16[128,128]{1,0:T(8,128)(2,1)}, u32[]{:S(2)}) copy-start(bf16[128,128]{1,0:T(8,128)(2,1)} %mix_ref.1) | copy-start | bytes 98308
  0.7 16.1 %copy-start.4 = (bf16[8,128]{1,0:T(8,128)(2,1)S(1)}, bf16[8,128]{1,0:T(8,128)(2,1)}, u32[]{:S(2)}) copy-start(bf16[8,128]{1,0:T(8,128)(2,1)} %radial_ref.1) | copy-start | bytes 6148
  0.7 16.1 %copy-start.7 = (bf16[5,128]{1,0:T(8,128)(2,1)S(1)}, bf16[5,128]{1,0:T(8,128)(2,1)}, u32[]{:S(2)}) copy-start(bf16[5,128]{1,0:T(8,128)(2,1)} %refs_2_.1) | copy-start | bytes 3844
  0.7 16.1 %copy-start.6 = (bf16[5,128]{1,0:T(8,128)(2,1)S(1)}, bf16[5,128]{1,0:T(8,128)(2,1)}, u32[]{:S(2)}) copy-start(bf16[5,128]{1,0:T(8,128)(2,1)} %refs_1_.1) | copy-start | bytes 3844
  0.7 23.6 %copy-start.3 = (bf16[128,128]{1,0:T(8,128)(2,1)S(1)}, bf16[128,128]{1,0:T(8,128)(2,1)}, u32[]{:S(2)}) copy-start(bf16[128,128]{1,0:T(8,128)(2,1)} %refs_7_.1) | copy-start | bytes 98308
  0.7 23.6 %copy-start.10 = (f32[128]{0:T(128)S(1)}, f32[128]{0:T(128)}, u32[]{:S(2)}) copy-start(f32[128]{0:T(128)} %param.21) | copy-start | bytes 1540
  18.7 1.3 %collective-permute-start = (bf16[1,128,128]{2,1,0:T(8,128)(2,1)S(1)}, bf16[1,128,128]{2,1,0:T(8,128)(2,1)S(1)}, u32[]{:S(2)}, u32[]{:S(2)}) collective-permute-start(bf16[1,128,128]{2,1,0:T(8,128)(2,1)S(1)} %get-tuple-element.31), channel_id=1, source_target_pairs={{0,1},{1,0},{2,3},{3,2},{4,5},{5,4},{6,7},{7,6},{8,9},{9,8},{10,11... | collective-permute-start | bytes 98312 | tf_op jit(solution)/shard_map/ppermute | solution.py:34
  20.0 8.7 %collective-permute-start.5 = (f32[128,1024]{1,0:T(8,128)S(1)}, f32[128,1024]{1,0:T(8,128)S(1)}, u32[]{:S(2)}, u32[]{:S(2)}) collective-permute-start(f32[128,1024]{1,0:T(8,128)S(1)} %get-tuple-element.42.refs_10_), channel_id=1, source_target_pairs={{0,1},{1,0},{2,3},{3,2},{4,5},{5,4},{6,7},{7,6},{8,9},{9,8},{10,11... | collective-permute-start | bytes 1572872 | tf_op jit(solution)/shard_map/ppermute | solution.py:34
  20.3 8.2 %collective-permute-start.4 = (bf16[2,128,128]{2,1,0:T(8,128)(2,1)S(1)}, bf16[2,128,128]{2,1,0:T(8,128)(2,1)S(1)}, u32[]{:S(2)}, u32[]{:S(2)}) collective-permute-start(bf16[2,128,128]{2,1,0:T(8,128)(2,1)S(1)} %pad_maximum_fusion.refs_4_), channel_id=1, source_target_pairs={{0,20},{1,19},{2,22},{3,17},{6,18},{7,21},{4,16},{5,23},{8,28},{9,... | collective-permute-start | bytes 196616 | tf_op jit(solution)/shard_map/ppermute | solution.py:57
  21.0 7.5 %collective-permute-start.3 = (bf16[2,128,128]{2,1,0:T(8,128)(2,1)S(1)}, bf16[2,128,128]{2,1,0:T(8,128)(2,1)S(1)}, u32[]{:S(2)}, u32[]{:S(2)}) collective-permute-start(bf16[2,128,128]{2,1,0:T(8,128)(2,1)S(1)} %pad_maximum_fusion.refs_4_), channel_id=1, source_target_pairs={{0,12},{1,11},{2,14},{3,9},{6,10},{7,13},{4,8},{5,15},{8,4},{9,3},... | collective-permute-start | bytes 196616 | tf_op jit(solution)/shard_map/ppermute | solution.py:57
  23.0 5.7 %collective-permute-start.2 = (bf16[2,128,128]{2,1,0:T(8,128)(2,1)S(1)}, bf16[2,128,128]{2,1,0:T(8,128)(2,1)S(1)}, u32[]{:S(2)}, u32[]{:S(2)}) collective-permute-start(bf16[2,128,128]{2,1,0:T(8,128)(2,1)S(1)} %pad_maximum_fusion.refs_4_), channel_id=1, source_target_pairs={{0,8},{1,17},{2,10},{3,19},{6,14},{7,23},{4,12},{5,21},{8,0},{9,25... | collective-permute-start | bytes 196616 | tf_op jit(solution)/shard_map/ppermute | solution.py:57
  23.9 4.8 %collective-permute-start.1 = (bf16[2,128,128]{2,1,0:T(8,128)(2,1)S(1)}, bf16[2,128,128]{2,1,0:T(8,128)(2,1)S(1)}, u32[]{:S(2)}, u32[]{:S(2)}) collective-permute-start(bf16[2,128,128]{2,1,0:T(8,128)(2,1)S(1)} %pad_maximum_fusion.refs_4_), channel_id=1, source_target_pairs={{0,2},{1,5},{2,0},{3,7},{6,4},{7,3},{4,6},{5,1},{8,10},{9,13},{10,... | collective-permute-start | bytes 196616 | tf_op jit(solution)/shard_map/ppermute | solution.py:57
  31.0 8.0 %collective-permute-start.6 = (bf16[2,128,128]{2,1,0:T(8,128)(2,1)S(1)}, bf16[2,128,128]{2,1,0:T(8,128)(2,1)S(1)}, u32[]{:S(2)}, u32[]{:S(2)}) collective-permute-start(bf16[2,128,128]{2,1,0:T(8,128)(2,1)S(1)} %get-tuple-element.44), channel_id=1, source_target_pairs={{0,20},{1,19},{2,22},{3,17},{6,18},{7,21},{4,16},{5,23},{8,28},{9,... | collective-permute-start | bytes 196616 | tf_op jit(solution)/shard_map/ppermute | solution.py:57
  32.7 6.2 %collective-permute-start.7 = (bf16[2,128,128]{2,1,0:T(8,128)(2,1)S(1)}, bf16[2,128,128]{2,1,0:T(8,128)(2,1)S(1)}, u32[]{:S(2)}, u32[]{:S(2)}) collective-permute-start(bf16[2,128,128]{2,1,0:T(8,128)(2,1)S(1)} %get-tuple-element.45), channel_id=1, source_target_pairs={{0,12},{1,11},{2,14},{3,9},{6,10},{7,13},{4,8},{5,15},{8,4},{9,3},... | collective-permute-start | bytes 196616 | tf_op jit(solution)/shard_map/ppermute | solution.py:57
  34.3 5.1 %collective-permute-start.8 = (bf16[2,128,128]{2,1,0:T(8,128)(2,1)S(1)}, bf16[2,128,128]{2,1,0:T(8,128)(2,1)S(1)}, u32[]{:S(2)}, u32[]{:S(2)}) collective-permute-start(bf16[2,128,128]{2,1,0:T(8,128)(2,1)S(1)} %get-tuple-element.46), channel_id=1, source_target_pairs={{0,8},{1,17},{2,10},{3,19},{6,14},{7,23},{4,12},{5,21},{8,0},{9,25... | collective-permute-start | bytes 196616 | tf_op jit(solution)/shard_map/ppermute | solution.py:57
  35.6 4.3 %collective-permute-start.9 = (bf16[2,128,128]{2,1,0:T(8,128)(2,1)S(1)}, bf16[2,128,128]{2,1,0:T(8,128)(2,1)S(1)}, u32[]{:S(2)}, u32[]{:S(2)}) collective-permute-start(bf16[2,128,128]{2,1,0:T(8,128)(2,1)S(1)} %get-tuple-element.47), channel_id=1, source_target_pairs={{0,2},{1,5},{2,0},{3,7},{6,4},{7,3},{4,6},{5,1},{8,10},{9,13},{10,... | collective-permute-start | bytes 196616 | tf_op jit(solution)/shard_map/ppermute | solution.py:57
  36.2 5.2 %collective-permute-start.11 = (f32[136,1024]{1,0:T(8,128)S(1)}, f32[136,1024]{1,0:T(8,128)S(1)}, u32[]{:S(2)}, u32[]{:S(2)}) collective-permute-start(f32[136,1024]{1,0:T(8,128)S(1)} %get-tuple-element.59), channel_id=1, source_target_pairs={{0,1},{1,0},{2,3},{3,2},{4,5},{5,4},{6,7},{7,6},{8,9},{9,8},{10,11... | collective-permute-start | bytes 1671176 | tf_op jit(solution)/shard_map/ppermute | solution.py:34
  40.0 1.3 %collective-permute-start.10 = (f32[1,128,128]{2,1,0:T(8,128)S(1)}, f32[1,128,128]{2,1,0:T(8,128)S(1)}, u32[]{:S(2)}, u32[]{:S(2)}) collective-permute-start(f32[1,128,128]{2,1,0:T(8,128)S(1)} %slice.9), channel_id=1, source_target_pairs={{0,1},{1,0},{2,3},{3,2},{4,5},{5,4},{6,7},{7,6},{8,9},{9,8},{10,11... | collective-permute-start | bytes 196616 | tf_op jit(solution)/shard_map/ppermute | solution.py:34

commit v9 on v8

--- a/solution.py
+++ b/solution.py
@@ -369,7 +369,10 @@
     other_ref, grad_ref = refs[-2:]
     table = jnp.concatenate([refs[array][row] for array, row in order], axis=1)
     rocol = rocol_ref[...]
-    other_ref[...] = jnp.dot(table, gather_ref[...], preferred_element_type=F32)
+    for own in range(sets):
+        depth = table.shape[1] - 2 * ATOMS * own
+        span = slice(own * EDGES, (own + 1) * EDGES)
+        other_ref[:, span] = jnp.dot(table[:, :depth], gather_ref[:depth, span], preferred_element_type=F32)
     wide = 2 * ATOMS
     if sets == 2:
         give_ref = outs.pop(0)
@@ -400,7 +403,10 @@
             give_ref[ATOMS : ATOMS + 1, :ATOMS] = energy
     places = [(ref, row) for ref in outs for row in range(ref.shape[0])]
     for c in range(0, len(places), 2):
-        back = jnp.dot(grad_ref[...], scatter_ref[:, c * ATOMS : (c + 2) * ATOMS], preferred_element_type=F32)
+        depth = EDGES if c + 2 == len(places) else sets * EDGES
+        back = jnp.dot(
+            grad_ref[:, :depth], scatter_ref[:depth, c * ATOMS : (c + 2) * ATOMS], preferred_element_type=F32
+        )
         for i in range(2):
             ref, row = places[c + i]
             ref[row] = back[:, i * ATOMS : (i + 1) * ATOMS].astype(ref.dtype)

time: 53.7 us -> 53.5 us (level)
  no operation moved by 1% of the time
where the time goes in v9:
time: 53.5 us; the launch traced here: 53.3 us
  blocking collectives  24.6 us (46%)
  starting transfers between devices  9.84 us (18%)
  Pallas kernels  9.57 us (18%)
  waiting for transfers between devices  7.73 us (14%)
  between operations  0.83 us (2%)
  local copies, waits for them, and re-layouts  0.65 us (1%)
    all_to_all x1, blocking collectives, on_device(): tables = [lax.all_to_all(copies, EVERY, 0, 0, tiled=True)]  15.3 us
    pallas_call x7, Pallas kernels, run(): pl.pallas_call(kernel, out_shape=shapes, in_specs=[pl.BlockSpec(memory_sp...  9.57 us
    all_to_all x1, blocking collectives, on_device(): lax.all_to_all(moved[0], EVERY, 0, 0, tiled=True)  9.31 us
    ppermute x8, starting transfers between devices, swapped(): return lax.ppermute(value, EVERY, pairs)  9.21 us
    ppermute x8, waiting for transfers between devices, swapped(): return lax.ppermute(value, EVERY, pairs)  5.49 us
    ppermute x4, waiting for transfers between devices, shifted(): lax.ppermute(value, axis, [(i, (i + step) % count) for i in range(count)])  2.24 us
  transfers between devices with their start and end apart: 12, of which 7 were waited for; matrix products, arithmetic and copies ran while one was open for 0% of the time, Pallas kernels for 5%

profile of v9, /device:TPU:0, one launch (start us, length us, event | category | flops | bytes accessed | tf_op | source)
XLA Modules:
  0.0 53.3 jit_solution(4012901841440852399)
XLA Ops:
  0.8 0.6 %copy-done.5 = s32[1,1,2,512]{3,2,1,0:T(2,128)S(1)} copy-done((s32[1,1,2,512]{3,2,1,0:T(2,128)S(1)}, s32[1,1,2,512]{3,2,1,0:T(2,128)}, u32[]{:S(2)}) %copy-start.5) | copy-done | bytes 4120
  1.4 15.3 %all_to_all.10.refs_0_.refs_1_ = f32[32,8,128]{2,1,0:T(8,128)S(1)} all-to-all(f32[32,8,128]{2,1,0:T(8,128)S(1)} %broadcast_in_dim.8), channel_id=1, replica_groups=mesh['gx'=4,'gy'=4,'gz'=2] {'gx','gy','gz'}, dimensions={0} | all-to-all | bytes 262144 | tf_op jit(solution)/shard_map/all_to_all | solution.py:571
  16.8 1.9 %forward.1 = (bf16[1,128,128]{2,1,0:T(8,128)(2,1)S(1)}, s32[8,128]{1,0:T(8,128)S(1)}, f32[128,1024]{1,0:T(8,128)S(1)}, f32[128,1024]{1,0:T(8,128)S(1)}, f32[128,...) custom-call(f32[32,8,128]{2,1,0:T(8,128)S(1)} %all_to_all.10.refs_0_, ...), custom_call_target="tpu_custom_call" | custom-call | tf_op jit(solution)/shard_map/forward/pallas_call | solution.py:538
  18.7 0.3 collective-permute-start
  19.0 1.0 %collective-permute-done = bf16[1,128,128]{2,1,0:T(8,128)(2,1)S(1)} collective-permute-done((bf16[1,128,128]{2,1,0:T(8,128)(2,1)S(1)}, bf16[1,128,128]{2,1,0:T(8,128)(2,1)S(1)}, u32[]{:S(2)}, u32[]{:S(2)}) %collective-permute-start) | collective-permute-done | bytes 32800 | tf_op jit(solution)/shard_map/ppermute | solution.py:34
  20.0 0.3 collective-permute-start.5
  20.3 0.7 %collective-permute-start.4 = (bf16[2,128,128]{2,1,0:T(8,128)(2,1)S(1)}, bf16[2,128,128]{2,1,0:T(8,128)(2,1)S(1)}, u32[]{:S(2)}, u32[]{:S(2)}) collective-permute-start(bf16[2,128,128]{2,1,0:T(8,128)(2,1)S(1)} %pad_maximum_fusion.refs_4_), channel_id=1, source_target_pairs={{0,20},{1,19},{2,22},{3,17},{6,18},{7,21},{4,16},{5,23},{8,28},{9,... | collective-permute-start | bytes 196616 | tf_op jit(solution)/shard_map/ppermute | solution.py:57
  21.0 2.0 %collective-permute-start.3 = (bf16[2,128,128]{2,1,0:T(8,128)(2,1)S(1)}, bf16[2,128,128]{2,1,0:T(8,128)(2,1)S(1)}, u32[]{:S(2)}, u32[]{:S(2)}) collective-permute-start(bf16[2,128,128]{2,1,0:T(8,128)(2,1)S(1)} %pad_maximum_fusion.refs_4_), channel_id=1, source_target_pairs={{0,12},{1,11},{2,14},{3,9},{6,10},{7,13},{4,8},{5,15},{8,4},{9,3},... | collective-permute-start | bytes 196616 | tf_op jit(solution)/shard_map/ppermute | solution.py:57
  23.0 0.9 %collective-permute-start.2 = (bf16[2,128,128]{2,1,0:T(8,128)(2,1)S(1)}, bf16[2,128,128]{2,1,0:T(8,128)(2,1)S(1)}, u32[]{:S(2)}, u32[]{:S(2)}) collective-permute-start(bf16[2,128,128]{2,1,0:T(8,128)(2,1)S(1)} %pad_maximum_fusion.refs_4_), channel_id=1, source_target_pairs={{0,8},{1,17},{2,10},{3,19},{6,14},{7,23},{4,12},{5,21},{8,0},{9,25... | collective-permute-start | bytes 196616 | tf_op jit(solution)/shard_map/ppermute | solution.py:57
  23.9 0.4 collective-permute-start.1
  24.3 2.7 %onehot.1 = (bf16[1280,2048]{1,0:T(8,128)(2,1)S(1)}, bf16[2048,1280]{1,0:T(8,128)(2,1)S(1)}, bf16[128,1024]{1,0:T(8,128)(2,1)S(1)}, bf16[128,128]{1,0:T(8,128)(2...) custom-call(s32[8,128]{1,0:T(8,128)S(1)} %get-tuple-element.36.refs_0_, ...), custom_call_target="tpu_custom_call" | custom-call | flops 1073741824 | bytes 8388608 | tf_op jit(solution)/shard_map/onehot/pallas_call | solution.py:538
  27.0 1.5 %collective-permute-done.4.refs_3_ = bf16[2,128,128]{2,1,0:T(8,128)(2,1)S(1)} collective-permute-done((bf16[2,128,128]{2,1,0:T(8,128)(2,1)S(1)}, bf16[2,128,128]{2,1,0:T(8,128)(2,1)S(1)}, u32[]{:S(2)}, u32[]{:S(2)}) %collective-permute-start.4) | collective-permute-done | bytes 65568 | tf_op jit(solution)/shard_map/ppermute | solution.py:57
  28.7 2.0 %second.1 = (f32[1,128]{1,0:T(1,128)S(1)}, f32[128,1024]{1,0:T(8,128)S(1)}, f32[136,1024]{1,0:T(8,128)S(1)}, bf16[2,128,128]{2,1,0:T(8,128)(2,1)S(1)}, bf16[2,12...) custom-call(bf16[2,128,128]{2,1,0:T(8,128)(2,1)S(1)} %collective-per, ...), custom_call_target="tpu_custom_call" | custom-call | tf_op jit(solution)/shard_map/second/pallas_call | solution.py:538
  30.8 1.8 %collective-permute-start.6 = (bf16[2,128,128]{2,1,0:T(8,128)(2,1)S(1)}, bf16[2,128,128]{2,1,0:T(8,128)(2,1)S(1)}, u32[]{:S(2)}, u32[]{:S(2)}) collective-permute-start(bf16[2,128,128]{2,1,0:T(8,128)(2,1)S(1)} %get-tuple-element.44), channel_id=1, source_target_pairs={{0,20},{1,19},{2,22},{3,17},{6,18},{7,21},{4,16},{5,23},{8,28},{9,... | collective-permute-start | bytes 196616 | tf_op jit(solution)/shard_map/ppermute | solution.py:57
  32.5 1.6 %collective-permute-start.7 = (bf16[2,128,128]{2,1,0:T(8,128)(2,1)S(1)}, bf16[2,128,128]{2,1,0:T(8,128)(2,1)S(1)}, u32[]{:S(2)}, u32[]{:S(2)}) collective-permute-start(bf16[2,128,128]{2,1,0:T(8,128)(2,1)S(1)} %get-tuple-element.45), channel_id=1, source_target_pairs={{0,12},{1,11},{2,14},{3,9},{6,10},{7,13},{4,8},{5,15},{8,4},{9,3},... | collective-permute-start | bytes 196616 | tf_op jit(solution)/shard_map/ppermute | solution.py:57
  34.1 1.3 %collective-permute-start.8 = (bf16[2,128,128]{2,1,0:T(8,128)(2,1)S(1)}, bf16[2,128,128]{2,1,0:T(8,128)(2,1)S(1)}, u32[]{:S(2)}, u32[]{:S(2)}) collective-permute-start(bf16[2,128,128]{2,1,0:T(8,128)(2,1)S(1)} %get-tuple-element.46), channel_id=1, source_target_pairs={{0,8},{1,17},{2,10},{3,19},{6,14},{7,23},{4,12},{5,21},{8,0},{9,25... | collective-permute-start | bytes 196616 | tf_op jit(solution)/shard_map/ppermute | solution.py:57
  35.5 0.5 collective-permute-start.9
  36.0 2.8 %collective-permute-done.6 = bf16[2,128,128]{2,1,0:T(8,128)(2,1)S(1)} collective-permute-done((bf16[2,128,128]{2,1,0:T(8,128)(2,1)S(1)}, bf16[2,128,128]{2,1,0:T(8,128)(2,1)S(1)}, u32[]{:S(2)}, u32[]{:S(2)}) %collective-permute-start.6) | collective-permute-done | bytes 65568 | tf_op jit(solution)/shard_map/ppermute | solution.py:57
  38.7 0.6 %collective-permute-done.8 = bf16[2,128,128]{2,1,0:T(8,128)(2,1)S(1)} collective-permute-done((bf16[2,128,128]{2,1,0:T(8,128)(2,1)S(1)}, bf16[2,128,128]{2,1,0:T(8,128)(2,1)S(1)}, u32[]{:S(2)}, u32[]{:S(2)}) %collective-permute-start.8) | collective-permute-done | bytes 65568 | tf_op jit(solution)/shard_map/ppermute | solution.py:57
  39.3 0.4 collective-permute-done.9
  39.9 1.2 %collective-permute-done.10 = f32[1,128,128]{2,1,0:T(8,128)S(1)} collective-permute-done((f32[1,128,128]{2,1,0:T(8,128)S(1)}, f32[1,128,128]{2,1,0:T(8,128)S(1)}, u32[]{:S(2)}, u32[]{:S(2)}) %collective-permute-start.10) | collective-permute-done | bytes 65568 | tf_op jit(solution)/shard_map/ppermute | solution.py:34
  41.1 2.2 %backward.1 = f32[32,4,128]{2,1,0:T(4,128)S(1)} custom-call(f32[1,128,128]{2,1,0:T(8,128)S(1)} %slice_add_fusion.owned_ref, f32[1,128]{1,0:T(1,128)S(1)} %get-tuple-element.48.energy_ref, f32[128,1024]{1,0:T(8,128)S(1)} %get-tuple-element.49.grad_edge_ref, f32[128,1024]{1,0:T(8,128)S(1)} %get-tuple-element.50.dse_ref, ...), custom_call_target="tpu_custom_call" | custom-call | tf_op jit(solution)/shard_map/backward/pallas_call | solution.py:538
  43.3 9.3 %all_to_all.11.moved_ref = f32[32,4,128]{2,1,0:T(4,128)S(1)} all-to-all(f32[32,4,128]{2,1,0:T(4,128)S(1)} %backward.1), channel_id=1, replica_groups=mesh['gx'=4,'gy'=4,'gz'=2] {'gx','gy','gz'}, dimensions={0} | all-to-all | bytes 131072 | tf_op jit(solution)/shard_map/all_to_all | solution.py:635
  52.6 0.7 %finish.1 = (f32[1,1,2,64]{3,2,1,0:T(2,128)}, f32[1,1,2,192]{3,2,1,0:T(2,128)}) custom-call(f32[32,4,128]{2,1,0:T(4,128)S(1)} %all_to_all.11.moved_ref), custom_call_target="tpu_custom_call" | custom-call | tf_op jit(solution)/shard_map/finish/pallas_call | solution.py:538
  (36 shorter events, 0.5 us)
Async XLA Ops:
  0.6 0.7 %copy-start.5 = (s32[1,1,2,512]{3,2,1,0:T(2,128)S(1)}, s32[1,1,2,512]{3,2,1,0:T(2,128)}, u32[]{:S(2)}) copy-start(s32[1,1,2,512]{3,2,1,0:T(2,128)} %nb_ref.1) | copy-start | bytes 12292
  0.6 0.7 %copy-start.9 = (s32[1,1,2,64]{3,2,1,0:T(2,128)S(1)}, s32[1,1,2,64]{3,2,1,0:T(2,128)}, u32[]{:S(2)}) copy-start(s32[1,1,2,64]{3,2,1,0:T(2,128)} %spec_ref.1) | copy-start | bytes 1540
  0.7 0.7 %copy-start.8 = (f32[1,1,2,192]{3,2,1,0:T(2,128)S(1)}, f32[1,1,2,192]{3,2,1,0:T(2,128)}, u32[]{:S(2)}) copy-start(f32[1,1,2,192]{3,2,1,0:T(2,128)} %pos_ref.1) | copy-start | bytes 4612
  0.7 16.1 %copy-start = (bf16[384,128]{1,0:T(8,128)(2,1)S(1)}, bf16[384,128]{1,0:T(8,128)(2,1)}, u32[]{:S(2)}) copy-start(bf16[384,128]{1,0:T(8,128)(2,1)} %upd_ref.1) | copy-start | bytes 294916
  0.7 16.1 %copy-start.2 = (bf16[128,128]{1,0:T(8,128)(2,1)S(1)}, bf16[128,128]{1,0:T(8,128)(2,1)}, u32[]{:S(2)}) copy-start(bf16[128,128]{1,0:T(8,128)(2,1)} %envw_ref.1) | copy-start | bytes 98308
  0.7 16.1 %copy-start.1 = (bf16[128,128]{1,0:T(8,128)(2,1)S(1)}, bf16[128,128]{1,0:T(8,128)(2,1)}, u32[]{:S(2)}) copy-start(bf16[128,128]{1,0:T(8,128)(2,1)} %mix_ref.1) | copy-start | bytes 98308
  0.7 16.1 %copy-start.4 = (bf16[8,128]{1,0:T(8,128)(2,1)S(1)}, bf16[8,128]{1,0:T(8,128)(2,1)}, u32[]{:S(2)}) copy-start(bf16[8,128]{1,0:T(8,128)(2,1)} %radial_ref.1) | copy-start | bytes 6148
  0.7 16.1 %copy-start.7 = (bf16[5,128]{1,0:T(8,128)(2,1)S(1)}, bf16[5,128]{1,0:T(8,128)(2,1)}, u32[]{:S(2)}) copy-start(bf16[5,128]{1,0:T(8,128)(2,1)} %refs_2_.1) | copy-start | bytes 3844
  0.7 16.1 %copy-start.6 = (bf16[5,128]{1,0:T(8,128)(2,1)S(1)}, bf16[5,128]{1,0:T(8,128)(2,1)}, u32[]{:S(2)}) copy-start(bf16[5,128]{1,0:T(8,128)(2,1)} %refs_1_.1) | copy-start | bytes 3844
  0.7 23.6 %copy-start.3 = (bf16[128,128]{1,0:T(8,128)(2,1)S(1)}, bf16[128,128]{1,0:T(8,128)(2,1)}, u32[]{:S(2)}) copy-start(bf16[128,128]{1,0:T(8,128)(2,1)} %refs_7_.1) | copy-start | bytes 98308
  0.7 23.6 %copy-start.10 = (f32[128]{0:T(128)S(1)}, f32[128]{0:T(128)}, u32[]{:S(2)}) copy-start(f32[128]{0:T(128)} %param.21) | copy-start | bytes 1540
  18.7 1.3 %collective-permute-start = (bf16[1,128,128]{2,1,0:T(8,128)(2,1)S(1)}, bf16[1,128,128]{2,1,0:T(8,128)(2,1)S(1)}, u32[]{:S(2)}, u32[]{:S(2)}) collective-permute-start(bf16[1,128,128]{2,1,0:T(8,128)(2,1)S(1)} %get-tuple-element.31), channel_id=1, source_target_pairs={{0,1},{1,0},{2,3},{3,2},{4,5},{5,4},{6,7},{7,6},{8,9},{9,8},{10,11... | collective-permute-start | bytes 98312 | tf_op jit(solution)/shard_map/ppermute | solution.py:34
  20.0 8.7 %collective-permute-start.5 = (f32[128,1024]{1,0:T(8,128)S(1)}, f32[128,1024]{1,0:T(8,128)S(1)}, u32[]{:S(2)}, u32[]{:S(2)}) collective-permute-start(f32[128,1024]{1,0:T(8,128)S(1)} %get-tuple-element.42.refs_10_), channel_id=1, source_target_pairs={{0,1},{1,0},{2,3},{3,2},{4,5},{5,4},{6,7},{7,6},{8,9},{9,8},{10,11... | collective-permute-start | bytes 1572872 | tf_op jit(solution)/shard_map/ppermute | solution.py:34
  20.3 8.2 %collective-permute-start.4 = (bf16[2,128,128]{2,1,0:T(8,128)(2,1)S(1)}, bf16[2,128,128]{2,1,0:T(8,128)(2,1)S(1)}, u32[]{:S(2)}, u32[]{:S(2)}) collective-permute-start(bf16[2,128,128]{2,1,0:T(8,128)(2,1)S(1)} %pad_maximum_fusion.refs_4_), channel_id=1, source_target_pairs={{0,20},{1,19},{2,22},{3,17},{6,18},{7,21},{4,16},{5,23},{8,28},{9,... | collective-permute-start | bytes 196616 | tf_op jit(solution)/shard_map/ppermute | solution.py:57
  21.0 7.5 %collective-permute-start.3 = (bf16[2,128,128]{2,1,0:T(8,128)(2,1)S(1)}, bf16[2,128,128]{2,1,0:T(8,128)(2,1)S(1)}, u32[]{:S(2)}, u32[]{:S(2)}) collective-permute-start(bf16[2,128,128]{2,1,0:T(8,128)(2,1)S(1)} %pad_maximum_fusion.refs_4_), channel_id=1, source_target_pairs={{0,12},{1,11},{2,14},{3,9},{6,10},{7,13},{4,8},{5,15},{8,4},{9,3},... | collective-permute-start | bytes 196616 | tf_op jit(solution)/shard_map/ppermute | solution.py:57
  23.0 5.7 %collective-permute-start.2 = (bf16[2,128,128]{2,1,0:T(8,128)(2,1)S(1)}, bf16[2,128,128]{2,1,0:T(8,128)(2,1)S(1)}, u32[]{:S(2)}, u32[]{:S(2)}) collective-permute-start(bf16[2,128,128]{2,1,0:T(8,128)(2,1)S(1)} %pad_maximum_fusion.refs_4_), channel_id=1, source_target_pairs={{0,8},{1,17},{2,10},{3,19},{6,14},{7,23},{4,12},{5,21},{8,0},{9,25... | collective-permute-start | bytes 196616 | tf_op jit(solution)/shard_map/ppermute | solution.py:57
  23.9 4.8 %collective-permute-start.1 = (bf16[2,128,128]{2,1,0:T(8,128)(2,1)S(1)}, bf16[2,128,128]{2,1,0:T(8,128)(2,1)S(1)}, u32[]{:S(2)}, u32[]{:S(2)}) collective-permute-start(bf16[2,128,128]{2,1,0:T(8,128)(2,1)S(1)} %pad_maximum_fusion.refs_4_), channel_id=1, source_target_pairs={{0,2},{1,5},{2,0},{3,7},{6,4},{7,3},{4,6},{5,1},{8,10},{9,13},{10,... | collective-permute-start | bytes 196616 | tf_op jit(solution)/shard_map/ppermute | solution.py:57
  30.8 8.0 %collective-permute-start.6 = (bf16[2,128,128]{2,1,0:T(8,128)(2,1)S(1)}, bf16[2,128,128]{2,1,0:T(8,128)(2,1)S(1)}, u32[]{:S(2)}, u32[]{:S(2)}) collective-permute-start(bf16[2,128,128]{2,1,0:T(8,128)(2,1)S(1)} %get-tuple-element.44), channel_id=1, source_target_pairs={{0,20},{1,19},{2,22},{3,17},{6,18},{7,21},{4,16},{5,23},{8,28},{9,... | collective-permute-start | bytes 196616 | tf_op jit(solution)/shard_map/ppermute | solution.py:57
  32.5 6.2 %collective-permute-start.7 = (bf16[2,128,128]{2,1,0:T(8,128)(2,1)S(1)}, bf16[2,128,128]{2,1,0:T(8,128)(2,1)S(1)}, u32[]{:S(2)}, u32[]{:S(2)}) collective-permute-start(bf16[2,128,128]{2,1,0:T(8,128)(2,1)S(1)} %get-tuple-element.45), channel_id=1, source_target_pairs={{0,12},{1,11},{2,14},{3,9},{6,10},{7,13},{4,8},{5,15},{8,4},{9,3},... | collective-permute-start | bytes 196616 | tf_op jit(solution)/shard_map/ppermute | solution.py:57
  34.1 5.2 %collective-permute-start.8 = (bf16[2,128,128]{2,1,0:T(8,128)(2,1)S(1)}, bf16[2,128,128]{2,1,0:T(8,128)(2,1)S(1)}, u32[]{:S(2)}, u32[]{:S(2)}) collective-permute-start(bf16[2,128,128]{2,1,0:T(8,128)(2,1)S(1)} %get-tuple-element.46), channel_id=1, source_target_pairs={{0,8},{1,17},{2,10},{3,19},{6,14},{7,23},{4,12},{5,21},{8,0},{9,25... | collective-permute-start | bytes 196616 | tf_op jit(solution)/shard_map/ppermute | solution.py:57
  35.5 4.3 %collective-permute-start.9 = (bf16[2,128,128]{2,1,0:T(8,128)(2,1)S(1)}, bf16[2,128,128]{2,1,0:T(8,128)(2,1)S(1)}, u32[]{:S(2)}, u32[]{:S(2)}) collective-permute-start(bf16[2,128,128]{2,1,0:T(8,128)(2,1)S(1)} %get-tuple-element.47), channel_id=1, source_target_pairs={{0,2},{1,5},{2,0},{3,7},{6,4},{7,3},{4,6},{5,1},{8,10},{9,13},{10,... | collective-permute-start | bytes 196616 | tf_op jit(solution)/shard_map/ppermute | solution.py:57
  36.0 5.2 %collective-permute-start.11 = (f32[136,1024]{1,0:T(8,128)S(1)}, f32[136,1024]{1,0:T(8,128)S(1)}, u32[]{:S(2)}, u32[]{:S(2)}) collective-permute-start(f32[136,1024]{1,0:T(8,128)S(1)} %get-tuple-element.59), channel_id=1, source_target_pairs={{0,1},{1,0},{2,3},{3,2},{4,5},{5,4},{6,7},{7,6},{8,9},{9,8},{10,11... | collective-permute-start | bytes 1671176 | tf_op jit(solution)/shard_map/ppermute | solution.py:34
  39.8 1.3 %collective-permute-start.10 = (f32[1,128,128]{2,1,0:T(8,128)S(1)}, f32[1,128,128]{2,1,0:T(8,128)S(1)}, u32[]{:S(2)}, u32[]{:S(2)}) collective-permute-start(f32[1,128,128]{2,1,0:T(8,128)S(1)} %slice.9), channel_id=1, source_target_pairs={{0,1},{1,0},{2,3},{3,2},{4,5},{5,4},{6,7},{7,6},{8,9},{9,8},{10,11... | collective-permute-start | bytes 196616 | tf_op jit(solution)/shard_map/ppermute | solution.py:34
